TPU v7x, 32 devices: a whole 2x2x4 slice. The times are simulated.
32 devices in a mesh: section: 4 (over y, x), ctx: 4 (over z), tp: 2 (over core).
Axes of the slice: x: 2, y: 2, z: 4, core: 2. Of those that a mesh axis runs over, the one named last changes fastest.
Arguments:
- hidden: bfloat16 [4, 512, 8192], P('section', 'ctx', 'tp')
- gain: bfloat16 [4, 8192], P('section', 'tp'), may hold values from 0.5 to 1.5
- queries: bfloat16 [4, 512, 32, 128], P('section', 'ctx', 'tp')
- key_value_weight: bfloat16 [4, 8192, 4, 2, 128], P('section', 'ctx', 'tp')
- adapt_down: bfloat16 [4, 16, 4096], P('section', None, 'tp'), may hold values from -1 to 1
- adapt_up: bfloat16 [4, 16, 8192], P('section', None, 'tp'), may hold values from -0.75 to 0.75
- out_grad: bfloat16 [4, 512, 8192], P('section', 'ctx', 'tp'), may hold values from -6 to 6
- doc_ids: int32 [512], P('ctx'), may hold values from 0 to 7, never falling along the last dimension, each value on 1 to 384 neighbouring positions
Outputs:
- attention_out: bfloat16 [4, 512, 4096], P('section', 'ctx', 'tp')
- adapter_out: bfloat16 [4, 512, 8192], P('section', 'ctx', 'tp')
- grad_down: float32 [4, 16, 4096], P('section', None, 'tp')
- grad_up: float32 [4, 16, 8192], P('section', None, 'tp')
Inputs may be any that keep to these rules, and one draw needn't show every extreme that they name: doc_ids never falls along the sequence; a document spans at most three quarters of 512 tokens, and one spans exactly that.
All inputs are finite; a program needn't handle non-finite values.
Results may differ from a plain program's by a relative error of at most 0.022.
Values may be sent and summed in bfloat16 or wider, within the bound.
No kernel may reach another device: no remote copies, remote signals or barrier semaphores. Data moves between devices by JAX's collectives and lax.ppermute only.
A program may use at most 128 MiB of HBM per device.

v0:
```python
import math

import jax
import jax.numpy as jnp
from jax import lax
from jax.sharding import PartitionSpec as P


def rotate(head_values, positions):
    half_width = head_values.shape[-1] // 2
    freqs = 1000000.0 ** (-jnp.arange(half_width, dtype=jnp.float32) * 2.0 / head_values.shape[-1])
    angles = positions.astype(jnp.float32)[:, None] * freqs[None, :]
    cosine = jnp.cos(angles)[:, None, :]
    sine_table = jnp.sin(angles)[:, None, :]
    first_half = head_values[..., :half_width]
    second_half = head_values[..., half_width:]
    return jnp.concatenate(
        [
            first_half * cosine - second_half * sine_table,
            second_half * cosine + first_half * sine_table,
        ],
        axis=-1,
    )


def per_device(hidden, gain, queries, key_value_weight, adapt_down, adapt_up, out_grad, doc_ids):
    tp_count = lax.axis_size("tp")
    row_count = hidden.shape[1]
    local_width = hidden.shape[2]
    head_dim = key_value_weight.shape[-1]
    kv_count = key_value_weight.shape[2]
    head_count = queries.shape[2]
    group_size = head_count // kv_count
    local_query = head_count * head_dim
    rank_size = adapt_down.shape[1]
    key_block = 1024
    full_rows, full_gain = (
        lax.all_gather(hidden, "tp", axis=2, tiled=True),
        lax.all_gather(gain, "tp", axis=1, tiled=True),
    )
    widened = full_rows[0].astype(jnp.float32)
    normalized_rows = (
        widened
        * lax.rsqrt(jnp.mean(widened * widened, axis=1, keepdims=True) + 1e-06)
        * full_gain[0].astype(jnp.float32)
    ).astype(jnp.bfloat16)
    kv_local = key_value_weight.reshape(1, key_value_weight.shape[1], kv_count * 2 * head_dim)
    keyval_raw = jnp.dot(
        normalized_rows,
        lax.all_gather(kv_local, "ctx", axis=1, tiled=True)[0],
        preferred_element_type=jnp.float32,
    )
    positions = lax.axis_index("ctx") * row_count + jnp.arange(row_count, dtype=jnp.int32)
    key_value_rows = keyval_raw.reshape(row_count, kv_count, 2, head_dim)
    rotated_keys = rotate(key_value_rows[:, :, 0], positions).astype(jnp.bfloat16)
    value_rows = key_value_rows[:, :, 1].astype(jnp.bfloat16)
    rotated_query = rotate(queries[0].astype(jnp.float32), positions).astype(jnp.bfloat16)
    stacked = (
        rotated_query.reshape(row_count, kv_count, group_size, head_dim)
        .transpose(1, 2, 0, 3)
        .reshape(kv_count, group_size * row_count, head_dim)
    )
    query_pos = jnp.tile(positions, group_size)
    query_doc = jnp.tile(doc_ids, group_size).astype(jnp.float32)
    score_scale = head_dim ** (-0.5)
    start_state = (
        jnp.full((kv_count, group_size * row_count), -1e30, jnp.float32),
        jnp.zeros((kv_count, group_size * row_count), jnp.float32),
        jnp.zeros((kv_count, group_size * row_count, head_dim), jnp.float32),
    )
    carried = start_state
    first_row = jnp.int32(0)
    piece_keys = lax.all_gather(rotated_keys, "ctx", axis=0, tiled=True)
    piece_values = lax.all_gather(value_rows, "ctx", axis=0, tiled=True)
    piece_docs = lax.all_gather(doc_ids.astype(jnp.bfloat16), "ctx", axis=0, tiled=True)
    key_total = piece_keys.shape[0]
    for block_start in range(0, key_total, key_block):
        block_stop = min(key_total, block_start + key_block)
        block_keys = piece_keys[block_start:block_stop]
        block_values = piece_values[block_start:block_stop]
        key_pos = first_row + block_start + jnp.arange(block_keys.shape[0], dtype=jnp.int32)
        key_doc = piece_docs[block_start:block_stop].astype(jnp.float32)
        running_top, running_sum, running_acc = carried
        scores = (
            jnp.einsum("gqd,kgd->gqk", stacked, block_keys, preferred_element_type=jnp.float32)
            * score_scale
        )
        allowed = (
            (key_pos[None, :] <= query_pos[:, None]) & (key_doc[None, :] == query_doc[:, None])
        )[None]
        scores = jnp.where(allowed, scores, -1e30)
        new_top = jnp.maximum(running_top, jnp.max(scores, axis=2))
        weights = jnp.where(allowed, jnp.exp(scores - new_top[:, :, None]), 0.0)
        shrink = jnp.exp(running_top - new_top)
        new_acc = running_acc * shrink[:, :, None] + jnp.einsum(
            "gqk,kgd->gqd",
            weights.astype(jnp.bfloat16),
            block_values,
            preferred_element_type=jnp.float32,
        )
        carried = (new_top, running_sum * shrink + jnp.sum(weights, axis=2), new_acc)
    final_top, final_sum, final_acc = carried
    attended = (
        (final_acc / final_sum[:, :, None])
        .reshape(kv_count, group_size, row_count, head_dim)
        .transpose(2, 0, 1, 3)
        .reshape(row_count, local_query)
        .astype(jnp.bfloat16)
    )
    low_part = jnp.dot(attended, adapt_down[0].T, preferred_element_type=jnp.float32)
    back_part = jnp.dot(out_grad[0], adapt_up[0].T, preferred_element_type=jnp.float32)
    low_sum, back_sum = lax.psum((low_part, back_part), "tp")
    low_rows = low_sum.astype(jnp.bfloat16)
    back_rows = back_sum.astype(jnp.bfloat16)
    adapter_rows = jnp.dot(low_rows, adapt_up[0], preferred_element_type=jnp.float32).astype(
        jnp.bfloat16
    )
    up_part = jnp.dot(low_rows.T, out_grad[0], preferred_element_type=jnp.float32)
    down_part = jnp.dot(back_rows.T, attended, preferred_element_type=jnp.float32)
    ceiling = 0.5 * math.sqrt(
        lax.axis_size("section") * rank_size * (local_query + local_width) * tp_count
    )
    up_total, down_total = (
        lax.psum(up_part.astype(jnp.bfloat16), "ctx").astype(jnp.float32),
        lax.psum(down_part.astype(jnp.bfloat16), "ctx").astype(jnp.float32),
    )
    local_squares = jnp.sum(up_total * up_total) + jnp.sum(down_total * down_total)
    squares = lax.psum(local_squares, ("section", "tp"))
    factor = jnp.minimum(1.0, ceiling / (jnp.sqrt(squares) + 1e-06))
    grad_up = up_total * factor
    grad_down = down_total * factor
    return (attended[None], adapter_rows[None], grad_down[None], grad_up[None])


def solution(mesh):
    return jax.shard_map(
        per_device,
        mesh=mesh,
        in_specs=(
            P("section", "ctx", "tp"),
            P("section", "tp"),
            P("section", "ctx", "tp", None),
            P("section", "ctx", "tp", None, None),
            P("section", None, "tp"),
            P("section", None, "tp"),
            P("section", "ctx", "tp"),
            P("ctx"),
        ),
        out_specs=(
            P("section", "ctx", "tp"),
            P("section", "ctx", "tp"),
            P("section", None, "tp"),
            P("section", None, "tp"),
        ),
        check_vma=False,
    )
```

profile of v0, /device:TPU:0, one launch (start us, length us, event | category | flops | bytes accessed | tf_op | source)
XLA Modules:
  0.0 279.8 jit_solution(38250694187567348)
XLA Ops:
  7.2 0.7 all-gather.5.cloned.1.call-update
  8.0 6.2 %copy.45 = bf16[1,2048,2,2,128]{1,4,3,2,0:T(8,128)(2,1)} copy(bf16[1,2048,2,2,128]{4,3,2,1,0:T(2,128)(2,1)} %param.11) | data formatting | bytes 4194304 | tf_op jit(solution)/shard_map/reshape | solution.py:47
  14.3 12.6 %all-gather.1 = bf16[4,1,128]{2,1,0:T(2,128)(2,1)S(1)} all-gather(bf16[1,1,128]{2,1,0:T(2,128)(2,1)S(1)} %get-tuple-element.24), channel_id=1, replica_groups=mesh['section'=4,'ctx'=4,'tp'=2] {'ctx'}, dimensions={0}, use_global_device_ids=true | all-gather | bytes 1280 | tf_op jit(solution)/shard_map/all_gather | solution.py:75
  26.8 0.2 multiply_cosine_fusion
  27.3 0.6 fusion.24
  27.9 0.1 copy.34
  28.1 0.1 copy.33
  28.2 1.8 all_gather.20
  30.1 0.3 pad_maximum_fusion
  30.4 0.5 fusion.14
  30.9 0.4 fusion.20
  31.3 2.4 fusion.1
  33.7 141.6 %all-gather.7.cloned.1.call-done = bf16[1,8192,512]{1,2,0:T(8,128)(2,1)} async-done(((bf16[1,2048,512]{1,2,0:T(8,128)(2,1)}), bf16[1,8192,512]{1,2,0:T(8,128)(2,1)}) %all-gather.7.cloned.1.call-update) | async-done | bytes 8388624 | tf_op jit(solution)/shard_map/all_gather | solution.py:50
  175.3 6.4 %fusion.8 = f32[128,2,2,128]{0,3,2,1:T(8,128)S(1)} fusion(bf16[2,2,128,8192]{3,2,1,0:T(8,128)(2,1)} %bitcast.77, bf16[1,128,8192]{2,1,0:T(8,128)(2,1)} %all-gather.5.cloned.1.call-done, f32[8192]{0:T(1024)S(1)} %bitcast.75, f32[128]{0:T(128)S(1)} %add_rsqrt_fusion), kind=kOutput, calls=%fused_computation.15 | convolution fusion | flops 1077936128 | bytes 10781184 | tf_op jit(solution)/shard_map/dot_general | solution.py:48
  181.8 13.3 %all_gather.22 = bf16[512,2,128]{0,2,1:T(8,128)(2,1)S(1)} all-gather(bf16[128,2,128]{0,2,1:T(8,128)(2,1)S(1)} %pad_maximum_fusion.1), channel_id=1, replica_groups=mesh['section'=4,'ctx'=4,'tp'=2] {'ctx'}, dimensions={0}, use_global_device_ids=true | all-gather | bytes 327680 | tf_op jit(solution)/shard_map/all_gather | solution.py:73
  195.1 1.1 fusion.4
  196.2 1.1 fusion.5
  197.4 12.8 %all-gather = bf16[512,2,1,128]{0,3,2,1:T(8,128)(2,1)S(1)} all-gather(bf16[128,2,1,128]{0,3,2,1:T(8,128)(2,1)S(1)} %slice.49), channel_id=2, replica_groups=mesh['section'=4,'ctx'=4,'tp'=2] {'ctx'}, dimensions={0}, use_global_device_ids=true | all-gather | bytes 327680 | tf_op jit(solution)/shard_map/all_gather | solution.py:74
  210.2 2.1 divide_convert_fusion
  212.3 0.3 copy.39
  212.6 0.2 fusion.33
  212.8 3.3 %all-reduce = (bf16[128,16]{0,1:T(8,128)(2,1)S(1)}, bf16[128,16]{0,1:T(8,128)(2,1)S(1)}) all-reduce(f32[128,16]{0,1:T(8,128)S(1)} %fusion.33, f32[128,16]{0,1:T(8,128)S(1)} %fusion.20), channel_id=1, replica_groups=mesh['section'=4,'ctx'=4,'tp'=2] {'tp'}, use_global_device_ids=true, to_apply=%region_3.4 | all-reduce | flops 4096 | bytes 24576 | tf_op jit(solution)/shard_map/psum | solution.py:112
  216.1 0.9 convolution_convert_fusion.2
  216.9 0.9 convolution_convert_fusion.1
  217.9 1.4 fusion
  219.3 32.1 %all-reduce.4.cloned.1.call-done = (bf16[16,2048]{1,0:T(8,128)(2,1)}, bf16[16,4096]{1,0:T(8,128)(2,1)}) async-done(((bf16[16,2048]{1,0:T(8,128)(2,1)}, bf16[16,4096]{1,0:T(8,128)(2,1)}), (bf16[16,2048]{1,0:T(8,128)(2,1)}, bf16[16,4096]{1,0:T(8,128)(2,1)})) %all-reduce.4.cloned.1.call-update) | async-done | bytes 196624 | tf_op jit(solution)/shard_map/psum | solution.py:125
  251.4 1.6 fusion.26
  252.9 1.5 fusion.29
  255.7 1.0 copy.40
  256.7 12.7 %psum.39 = f32[]{:T(128)} all-reduce(f32[]{:T(128)S(6)} %add.65), channel_id=1, replica_groups=mesh['section'=4,'ctx'=4,'tp'=2] {'section','tp'}, use_global_device_ids=true, to_apply=%region_9.10 | all-reduce | flops 1 | bytes 8 | tf_op jit(solution)/shard_map/psum | solution.py:128
  270.2 1.5 fusion.30
  271.7 1.6 fusion.27
  (36 shorter events, 0.6 us)
Async XLA Ops:
  7.2 23.7 %copy-start = (bf16[1,128,4096]{2,1,0:T(8,128)(2,1)S(1)}, bf16[1,128,4096]{2,1,0:T(8,128)(2,1)}, u32[]{:S(2)}) copy-start(bf16[1,128,4096]{2,1,0:T(8,128)(2,1)} %param.14) | copy-start | bytes 3145732
  7.2 7.1 %copy-start.5 = (s32[128]{0:T(128)S(1)}, s32[128]{0:T(128)}, u32[]{:S(2)}) copy-start(s32[128]{0:T(128)} %param.15) | copy-start | bytes 1540
  7.2 20.1 %copy-start.1 = (bf16[1,128,16,128]{3,2,1,0:T(8,128)(2,1)S(1)}, bf16[1,128,16,128]{3,2,1,0:T(8,128)(2,1)}, u32[]{:S(2)}) copy-start(bf16[1,128,16,128]{3,2,1,0:T(8,128)(2,1)} %param.10) | copy-start | bytes 1572868
  7.2 24.1 %all-gather.5.cloned.1.call-start = ((), (), s32[]{:S(2)}) async-start(), calls=%async_computation | async-start | bytes 3145728 | tf_op jit(solution)/shard_map/all_gather | solution.py:38
  7.9 167.4 %all-gather.7.cloned.1.call-start = ((), (), s32[]{:S(2)}) async-start(), calls=%async_computation.1 | async-start | bytes 10485760 | tf_op jit(solution)/shard_map/all_gather | solution.py:50
  14.2 14.0 %copy-start.4 = (bf16[1,4096]{1,0:T(2,128)(2,1)S(1)}, bf16[1,4096]{1,0:T(2,128)(2,1)}, u32[]{:S(2)}) copy-start(bf16[1,4096]{1,0:T(2,128)(2,1)} %param.9) | copy-start | bytes 24580
  14.2 237.2 %all-reduce.4.cloned.1.call-start = ((), (), s32[]{:S(2)}) async-start(), calls=%async_computation.2 | async-start | bytes 393216 | tf_op jit(solution)/shard_map/psum | solution.py:125
  27.3 3.6 %copy-start.2 = (bf16[1,16,4096]{2,1,0:T(8,128)(2,1)S(1)}, bf16[1,16,4096]{2,1,0:T(8,128)(2,1)}, u32[]{:S(2)}) copy-start(bf16[1,16,4096]{2,1,0:T(8,128)(2,1)} %param.13) | copy-start | bytes 393220
  210.2 2.4 copy-start.3
Sparse Core Ops, SparseCore 0:
  9.6 13.2 all-gather.4
  24.5 150.7 all-gather.6
  218.0 33.3 all-reduce.3
where the time goes:
time: 280 us
  waiting for transfers between devices  174 us (62%)
  blocking collectives  56.5 us (20%)
  between operations  16 us (6%)
  matrix products  13.4 us (5%)
  other arithmetic  11.4 us (4%)
  local copies, waits for them, and re-layouts  8 us (3%)
    all_gather x1, waiting for transfers between devices, per_device(): lax.all_gather(kv_local, 'ctx', axis=1, tiled=True)[0]  142 us
    psum x1, waiting for transfers between devices, per_device(): lax.psum(down_part.astype(jnp.bfloat16), 'ctx').astype(jnp.float32)  32.1 us
    all_gather x1, blocking collectives, per_device(): piece_keys = lax.all_gather(rotated_keys, 'ctx', axis=0, tiled=True)  13.3 us
    all_gather x1, blocking collectives, per_device(): piece_values = lax.all_gather(value_rows, 'ctx', axis=0, tiled=True)  12.8 us
    psum x1, blocking collectives, per_device(): squares = lax.psum(local_squares, ('section', 'tp'))  12.7 us
    all_gather x1, blocking collectives, per_device(): lax.all_gather(doc_ids.astype(jnp.bfloat16), 'ctx', axis=0, tiled=True)  12.6 us
    dot_general x1, matrix products, per_device(): jnp.dot(normalized_rows, lax.all_gather(kv_local, 'ctx', axis=1, tiled=Tr...  6.42 us
    reshape x1, local copies, waits for them, and re-layouts, per_device(): key_value_weight.reshape(1, key_value_weight.shape[1], kv_count * 2 * hea...  6.18 us
  transfers between devices with their start and end apart: 3, of which 2 were waited for; matrix products, arithmetic and copies ran while one was open for 4% of the time, Pallas kernels for 0%

commit v1 on v0

--- a/solution.py
+++ b/solution.py
@@ -23,7 +23,7 @@
     )
 
 
-def per_device(hidden, gain, queries, key_value_weight, adapt_down, adapt_up, out_grad, doc_ids):
+def gathered_weights(hidden, gain, queries, key_value_weight, adapt_down, adapt_up, out_grad, doc_ids):
     tp_count = lax.axis_size("tp")
     row_count = hidden.shape[1]
     local_width = hidden.shape[2]
@@ -132,6 +132,187 @@
     return (attended[None], adapter_rows[None], grad_down[None], grad_up[None])
 
 
+def swap(value, axis, distance):
+    count = lax.axis_size(axis)
+    return lax.ppermute(value, axis, [(i, i ^ distance) for i in range(count)])
+
+
+def send(value, axis, pairs):
+    return lax.ppermute(value, axis, pairs)
+
+
+def split_model_width(
+    hidden, gain, queries, key_value_weight, adapt_down, adapt_up, out_grad, doc_ids
+):
+    f32, bf16 = jnp.float32, jnp.bfloat16
+    place = lax.axis_index("ctx")
+    core = lax.axis_index("tp")
+    row_count = hidden.shape[1]
+    local_width = hidden.shape[2]
+    slice_width = key_value_weight.shape[1]
+    kv_count, head_dim = key_value_weight.shape[2], key_value_weight.shape[-1]
+    head_count = queries.shape[2]
+    group_size = head_count // kv_count
+    local_query = head_count * head_dim
+    rank_size = adapt_down.shape[1]
+    kv_width = kv_count * 2 * head_dim
+
+    widened = hidden[0].astype(f32)
+    part_square = jnp.sum(widened * widened, axis=1)
+    mean_square = (part_square + swap(part_square, "tp", 1)) / (2 * local_width)
+    normed = (
+        widened * lax.rsqrt(mean_square + 1e-06)[:, None] * gain[0].astype(f32)
+    ).astype(bf16)
+
+    home = place // 2 == core
+    parity = place % 2
+    even_half = lax.dynamic_slice_in_dim(normed, parity * slice_width, slice_width, 1)
+    odd_half = lax.dynamic_slice_in_dim(normed, (1 - parity) * slice_width, slice_width, 1)
+
+    def device(chip, which):
+        return chip * 2 + which
+
+    axes = ("ctx", "tp")
+    pairs_1 = [(device(a, a // 2), device(a ^ 1, 1 - a // 2)) for a in range(4)]
+    pairs_3 = [(device(a, 1 - a // 2), device(a ^ 3, a // 2)) for a in range(4)]
+    pairs_2 = [(device(a, 1 - a // 2), device(a ^ 2, 1 - a // 2)) for a in range(4)]
+    home_to_away = [(device(a, a // 2), device(a, 1 - a // 2)) for a in range(4)]
+    away_to_home = [(j, i) for i, j in home_to_away]
+    got_1 = send(odd_half, axes, pairs_1)
+    got_3 = send(odd_half, axes, pairs_3)
+    got_2 = send(even_half, axes, pairs_2)
+    weight = key_value_weight[0].reshape(slice_width, kv_width)
+    near = jnp.where(home, even_half, got_1)
+    near_other = swap(near, "tp", 1)
+    far_3 = send(got_3, axes, away_to_home)
+    far_2 = send(got_2, axes, home_to_away)
+
+    def project(rows):
+        return jnp.dot(rows, weight, preferred_element_type=f32)
+
+    near_mine, near_theirs = project(near), project(near_other)
+    part_0 = jnp.where(home, near_mine, near_theirs)
+    part_1 = jnp.where(home, near_theirs, near_mine)
+    part_3 = project(jnp.where(home, far_3, got_3))
+    part_2 = project(jnp.where(home, got_2, far_2))
+
+    def pack(value):
+        heads = value.reshape(row_count, kv_count, 2, head_dim)
+        keys, values = heads[:, :, 0], heads[:, :, 1]
+        high = lax.reduce_precision(keys, 8, 7)
+        pieces = (high.astype(bf16), (keys - high).astype(bf16), values.astype(bf16))
+        return jnp.concatenate([p.reshape(row_count, -1) for p in pieces], axis=1)
+
+    def unpack(sent):
+        high, low, values = [
+            p.astype(f32).reshape(row_count, kv_count, head_dim) for p in jnp.split(sent, 3, axis=1)
+        ]
+        return jnp.stack([high + low, values], axis=2).reshape(row_count, kv_width)
+
+    def finish(value, d):
+        heads = value.reshape(row_count, kv_count, 2, head_dim)
+        where = (place ^ d) * row_count + jnp.arange(row_count, dtype=jnp.int32)
+        return jnp.concatenate(
+            [rotate(heads[:, :, 0], where).astype(bf16), heads[:, :, 1].astype(bf16)], axis=1
+        ).reshape(row_count, kv_width)
+
+    own_side = part_0 + unpack(swap(pack(part_1), "ctx", 1))
+    own_sent = pack(own_side)
+    side_next = unpack(send(own_sent, "ctx", [(0, 1), (2, 3)]))
+    early_far = unpack(send(own_sent, "ctx", [(0, 2), (1, 3)]))
+    far_side = part_2 + unpack(swap(pack(part_3), "ctx", 1))
+    far_sent = pack(far_side)
+    block_2 = finish(far_side + early_far, 2)
+    block_3 = send(block_2, "ctx", [(2, 3), (3, 2)])
+    block_0 = finish(own_side + unpack(swap(far_sent, "ctx", 2)), 0)
+    block_1 = finish(side_next + unpack(send(far_sent, "ctx", [(0, 3), (2, 1)])), 1)
+
+    positions = place * row_count + jnp.arange(row_count, dtype=jnp.int32)
+    rotated_query = rotate(queries[0].astype(f32), positions).astype(bf16)
+    stacked = (
+        rotated_query.reshape(row_count, kv_count, group_size, head_dim)
+        .transpose(1, 2, 0, 3)
+        .reshape(kv_count, group_size * row_count, head_dim)
+    )
+    docs = doc_ids.astype(bf16)
+    doc_blocks = [docs] + [swap(docs, "ctx", d) for d in (1, 2, 3)]
+    block_positions = [
+        (place ^ d) * row_count + jnp.arange(row_count, dtype=jnp.int32) for d in range(4)
+    ]
+    blocks = [
+        value.reshape(row_count, 2, kv_count, head_dim)
+        for value in (block_0, block_1, block_2, block_3)
+    ]
+    order = (2, 3, 0, 1)
+    keys = jnp.concatenate([blocks[d][:, 0] for d in order], axis=0)
+    values = jnp.concatenate([blocks[d][:, 1] for d in order], axis=0)
+    key_pos = jnp.concatenate([block_positions[d] for d in order])
+    key_doc = jnp.concatenate([doc_blocks[d] for d in order])
+    allowed = (key_pos[None, :] <= positions[:, None]) & (key_doc[None, :] == docs[:, None])
+    allowed = jnp.tile(allowed, (group_size, 1))[None]
+    scores = jnp.einsum("gqd,kgd->gqk", stacked, keys, preferred_element_type=f32)
+    scores = jnp.where(allowed, scores * head_dim ** (-0.5), -1e30)
+    top = jnp.max(scores, axis=2, keepdims=True)
+    weights = jnp.where(allowed, jnp.exp(scores - top), 0.0)
+    weight_sum = jnp.sum(weights, axis=2, keepdims=True)
+    attended = jnp.einsum("gqk,kgd->gqd", weights.astype(bf16), values, preferred_element_type=f32)
+    attended = (
+        (attended / weight_sum)
+        .reshape(kv_count, group_size, row_count, head_dim)
+        .transpose(2, 0, 1, 3)
+        .reshape(row_count, local_query)
+        .astype(bf16)
+    )
+
+    back_part = jnp.dot(out_grad[0], adapt_up[0].T, preferred_element_type=f32)
+    back_rows = (back_part + swap(back_part, "tp", 1)).astype(bf16)
+    low_part = jnp.dot(attended, adapt_down[0].T, preferred_element_type=f32)
+    low_rows = (low_part + swap(low_part, "tp", 1)).astype(bf16)
+    adapter_rows = jnp.dot(low_rows, adapt_up[0], preferred_element_type=f32).astype(bf16)
+    up_part = jnp.dot(low_rows.T, out_grad[0], preferred_element_type=f32)
+    down_part = jnp.dot(back_rows.T, attended, preferred_element_type=f32)
+
+    up_step, down_step = local_width // 4, local_query // 4
+
+    def chunk(d):
+        index = place ^ d
+        return jnp.concatenate(
+            [
+                lax.dynamic_slice_in_dim(up_part, index * up_step, up_step, 1),
+                lax.dynamic_slice_in_dim(down_part, index * down_step, down_step, 1),
+            ],
+            axis=1,
+        )
+
+    total = chunk(0)
+    for d in (1, 2, 3):
+        total = total + swap(chunk(d).astype(bf16), "ctx", d).astype(f32)
+    sent_total = total.astype(bf16)
+    others = [sent_total] + [swap(sent_total, "ctx", d) for d in (1, 2, 3)]
+    squares = jnp.sum(total * total).reshape(1, 1)
+    squares = squares + sum(swap(squares, "section", d) for d in (1, 2, 3))
+    squares = squares + sum(swap(squares, "ctx", d) for d in (1, 2, 3))
+    squares = squares + swap(squares, "tp", 1)
+    ceiling = 0.5 * math.sqrt(
+        lax.axis_size("section") * rank_size * (local_query + local_width) * 2
+    )
+    factor = jnp.minimum(1.0, ceiling / (jnp.sqrt(squares) + 1e-06))
+    gathered = jnp.stack(others)
+    ordered = [
+        lax.dynamic_index_in_dim(gathered, place ^ j, 0, keepdims=False).astype(f32) * factor
+        for j in range(4)
+    ]
+    grad_up = jnp.concatenate([piece[:, :up_step] for piece in ordered], axis=1)
+    grad_down = jnp.concatenate([piece[:, up_step:] for piece in ordered], axis=1)
+    return (attended[None], adapter_rows[None], grad_down[None], grad_up[None])
+
+
+def per_device(*arrays):
+    if lax.axis_size("ctx") == 4 and lax.axis_size("tp") == 2 and lax.axis_size("section") == 4:
+        return split_model_width(*arrays)
+    return gathered_weights(*arrays)
+
+
 def solution(mesh):
     return jax.shard_map(
         per_device,

time: 280 us -> 166 us (0.59)
  waiting for transfers between devices: 174 us -> 21.5 us
  starting transfers between devices: 0.12 us -> 74.4 us
  blocking collectives: 56.5 us -> 0 us
  local copies, waits for them, and re-layouts: 8 us -> 26.7 us
  other arithmetic: 11.4 us -> 22.8 us
  between operations: 16 us -> 6.99 us
    all_gather x2 -> x0, waiting for transfers between devices: 142 us -> none  [the longest x1 142 us: per_device(): lax.all_gather(kv_local, 'ctx', axis=1, tiled=True)[0]]
    ppermute x0 -> x32, starting transfers between devices: none -> 74.4 us  [the longest x23 44.7 us: swap(): return lax.ppermute(value, axis, [(i, i ^ distance) for i in range(count)])]
    all_gather x4 -> x0, blocking collectives: 40.5 us -> none  [the longest x1 13.3 us: per_device(): piece_keys = lax.all_gather(rotated_keys, 'ctx', axis=0, tiled=True)]
    psum x1 -> x0, waiting for transfers between devices: 32.1 us -> none  [per_device(): lax.psum(down_part.astype(jnp.bfloat16), 'ctx').astype(jnp.float32)]
    ppermute x0 -> x32, waiting for transfers between devices: none -> 21.5 us  [the longest x9 11.8 us: send(): return lax.ppermute(value, axis, pairs)]
    psum x2 -> x0, blocking collectives: 16 us -> none  [the longest x1 12.7 us: per_device(): squares = lax.psum(local_squares, ('section', 'tp'))]
    convert_element_type x2 -> x8, other arithmetic: 0.08 us -> 5.14 us  [the longest x4 1.64 us: pack(): high.astype(bf16)]
    slice x1 -> x24, local copies, waits for them, and re-layouts: 0.01 us -> 4.67 us  [the longest x11 4.16 us: pack(): keys, values = (heads[:, :, 0], heads[:, :, 1])]
  transfers between devices with their start and end apart: 3 -> 32, of which waited for: 2 -> 10; matrix products, arithmetic and copies ran while one was open for 4% -> 35% of each run, Pallas kernels for 0% -> 0%
where the time goes in v1:
time: 166 us; the launch traced here: 165 us
  starting transfers between devices  74.4 us (45%)
  local copies, waits for them, and re-layouts  26.7 us (16%)
  other arithmetic  22.8 us (14%)
  waiting for transfers between devices  21.5 us (13%)
  matrix products  12.5 us (8%)
  between operations  6.99 us (4%)
    ppermute x23, starting transfers between devices, swap(): return lax.ppermute(value, axis, [(i, i ^ distance) for i in range(count)])  44.7 us
    ppermute x9, starting transfers between devices, send(): return lax.ppermute(value, axis, pairs)  29.7 us
    ppermute x9, waiting for transfers between devices, send(): return lax.ppermute(value, axis, pairs)  11.8 us
    ppermute x23, waiting for transfers between devices, swap(): return lax.ppermute(value, axis, [(i, i ^ distance) for i in range(count)])  9.75 us
    slice x11, local copies, waits for them, and re-layouts, pack(): keys, values = (heads[:, :, 0], heads[:, :, 1])  4.16 us
    dot_general x4, matrix products, project(): return jnp.dot(rows, weight, preferred_element_type=f32)  3.89 us
    unnamed x45, local copies, waits for them, and re-layouts  3.76 us
    sub x1, matrix products, split_model_width(): weights = jnp.where(allowed, jnp.exp(scores - top), 0.0)  3.55 us
  transfers between devices with their start and end apart: 32, of which 10 were waited for; matrix products, arithmetic and copies ran while one was open for 35% of the time, Pallas kernels for 0%

profile of v1, /device:TPU:0, one launch (start us, length us, event | category | flops | bytes accessed | tf_op | source)
XLA Modules:
  0.0 165.0 jit_solution(9271077587695929920)
XLA Ops:
  1.4 4.0 %collective-permute-start = (bf16[128]{0:T(256)(128)(2,1)S(1)}, bf16[128]{0:T(256)(128)(2,1)S(1)}, u32[]{:S(2)}, u32[]{:S(2)}) collective-permute-start(bf16[128]{0:T(256)(128)(2,1)S(1)} %convert_element_type.223), channel_id=1, source_target_pairs={{0,4},{2,6},{4,0},{6,2},{1,5},{3,7},{5,1},{7,3},{8,12},{10,14},{12... | collective-permute-start | bytes 776 | tf_op jit(solution)/shard_map/ppermute | solution.py:137
  7.0 1.5 fusion.3
  9.5 2.8 %reshape_squeeze.3 = bf16[2048,512]{1,0:T(8,128)(2,1)S(1)} reshape(bf16[1,2048,2,2,128]{4,3,2,1,0:T(2,128)(2,1)} %param.11) | data formatting | bytes 4194304 | tf_op jit(solution)/shard_map/reshape;squeeze | solution.py:184
  12.2 2.4 %copy.86 = bf16[512,2048]{1,0:T(8,128)(2,1)} copy(bf16[512,2048]{0,1:T(8,128)(2,1)S(1)} %bitcast.149) | data formatting | bytes 4194304 | tf_op jit(solution)/shard_map/dot_general | solution.py:191
  21.3 1.6 fusion.5
  24.8 4.5 %collective-permute-start.9 = (bf16[128,2048]{1,0:T(8,128)(2,1)}, bf16[128,2048]{1,0:T(8,128)(2,1)}, u32[]{:S(2)}, u32[]{:S(2)}) collective-permute-start(bf16[128,2048]{1,0:T(8,128)(2,1)} %constant_dynamic-slice_fusion.2), channel_id=1, source_target_pairs={{0,3},{2,1},{5,6},{7,4},{8,11},{10,9},{13,14},{15,12},{16,19},{18,... | collective-permute-start | bytes 1572872 | tf_op jit(solution)/shard_map/ppermute | solution.py:141
  29.3 1.5 collective-permute-start.6
  35.1 4.1 %collective-permute-done.9 = bf16[128,2048]{1,0:T(8,128)(2,1)} collective-permute-done((bf16[128,2048]{1,0:T(8,128)(2,1)}, bf16[128,2048]{1,0:T(8,128)(2,1)}, u32[]{:S(2)}, u32[]{:S(2)}) %collective-permute-start.9) | collective-permute-done | bytes 524320 | tf_op jit(solution)/shard_map/ppermute | solution.py:141
  39.2 2.0 %broadcast_select_fusion = (bf16[128,2048]{1,0:T(8,128)(2,1)S(1)}, bf16[128,2048]{1,0:T(8,128)(2,1)}) fusion(bf16[128,2048]{1,0:T(8,128)(2,1)} %collective-permute-done.9, pred[]{:T(512)S(6)} %eq.25, bf16[128,4096]{1,0:T(8,128)(2,1)} %copy-done.2, s32[]{:T(128)S(6)} %select_n.92), kind=kLoop, calls=%fused_computation.34 | loop fusion | flops 262144 | bytes 2097157 | tf_op jit(solution)/shard_map/jit(_where)/select_n | solution.py:185
  41.2 5.7 %collective-permute-start.10 = (bf16[128,2048]{1,0:T(8,128)(2,1)S(1)}, bf16[128,2048]{1,0:T(8,128)(2,1)S(1)}, u32[]{:S(2)}, u32[]{:S(2)}) collective-permute-start(bf16[128,2048]{1,0:T(8,128)(2,1)S(1)} %get-tuple-element.18), channel_id=1, source_target_pairs={{0,1},{1,0},{2,3},{3,2},{4,5},{5,4},{6,7},{7,6},{8,9},{9,8},{10,11... | collective-permute-start | bytes 1572872 | tf_op jit(solution)/shard_map/ppermute | solution.py:137
  54.8 1.5 pad_maximum_fusion.6
  57.6 7.2 %collective-permute-done.4 = bf16[128,2048]{1,0:T(8,128)(2,1)} collective-permute-done((bf16[128,2048]{1,0:T(8,128)(2,1)}, bf16[128,2048]{1,0:T(8,128)(2,1)}, u32[]{:S(2)}, u32[]{:S(2)}) %collective-permute-start.4) | collective-permute-done | bytes 524320 | tf_op jit(solution)/shard_map/ppermute | solution.py:141
  64.9 2.1 %collective-permute-start.5 = (bf16[128,2048]{1,0:T(8,128)(2,1)}, bf16[128,2048]{1,0:T(8,128)(2,1)}, u32[]{:S(2)}, u32[]{:S(2)}) collective-permute-start(bf16[128,2048]{1,0:T(8,128)(2,1)} %collective-permute-done.4), channel_id=1, source_target_pairs={{0,1},{2,3},{5,4},{7,6},{8,9},{10,11},{13,12},{15,14},{16,17},{18,... | collective-permute-start | bytes 1572872 | tf_op jit(solution)/shard_map/ppermute | solution.py:141
  68.8 1.5 pad_maximum_fusion.7
  75.8 1.6 convolution_add_fusion
  80.6 6.9 %collective-permute-start.16 = (bf16[128,768]{0,1:T(8,128)(2,1)S(1)}, bf16[128,768]{0,1:T(8,128)(2,1)}, u32[]{:S(2)}, u32[]{:S(2)}) collective-permute-start(bf16[128,768]{0,1:T(8,128)(2,1)S(1)} %pad_maximum_fusion.9), channel_id=1, source_target_pairs={{0,6},{4,2},{1,7},{5,3},{8,14},{12,10},{9,15},{13,11},{16,22},{20,... | collective-permute-start | bytes 589832 | tf_op jit(solution)/shard_map/ppermute | solution.py:141
  87.5 1.7 %collective-permute-done.14 = bf16[128,768]{0,1:T(8,128)(2,1)S(1)} collective-permute-done((bf16[128,768]{0,1:T(8,128)(2,1)S(1)}, bf16[128,768]{0,1:T(8,128)(2,1)S(1)}, u32[]{:S(2)}, u32[]{:S(2)}) %collective-permute-start.14) | collective-permute-done | bytes 196640 | tf_op jit(solution)/shard_map/ppermute | solution.py:137
  91.3 1.5 collective-permute-start.12
  92.7 9.9 %collective-permute-start.15 = (bf16[128,768]{0,1:T(8,128)(2,1)S(1)}, bf16[128,768]{0,1:T(8,128)(2,1)S(1)}, u32[]{:S(2)}, u32[]{:S(2)}) collective-permute-start(bf16[128,768]{0,1:T(8,128)(2,1)S(1)} %pad_maximum_fusion.8), channel_id=1, source_target_pairs={{0,2},{4,6},{1,3},{5,7},{8,10},{12,14},{9,11},{13,15},{16,18},{20,... | collective-permute-start | bytes 589832 | tf_op jit(solution)/shard_map/ppermute | solution.py:141
  108.2 3.6 %fusion.66 = (f32[2,1024]{1,0:T(2,128)S(1)}, bf16[2,1024,512]{1,2,0:T(8,128)(2,1)}) fusion(pred[1024,512]{0,1:T(8,128)(4,1)S(1)} %bitcast.159, bf16[2,1024,128]{2,1,0:T(8,128)(2,1)S(1)} %bitcast.158, bf16[128,2,128]{2,0,1:T(8,128)(2,1)S(1)} %get-tuple-element.47, bf16[128,2,128]{2,0,1:T(8,128)(2,1)S(1)} %get-tuple-element.45, ...), kind=kOutput, calls=%fused_computation.158 | convolution fusion | flops 275776000 | bytes 3416064 | tf_op jit(solution)/shard_map/sub | solution.py:256
  111.7 2.6 %fusion.14 = bf16[2,1024,128]{2,1,0:T(8,128)(2,1)S(1)} fusion(bf16[2,1024,512]{1,2,0:T(8,128)(2,1)} %get-tuple-element.69, f32[2,1024]{1,0:T(2,128)S(1)} %get-tuple-element.68, bf16[128,2,128]{2,0,1:T(8,128)(2,1)S(1)} %get-tuple-element.46, bf16[128,2,128]{2,0,1:T(8,128)(2,1)S(1)} %get-tuple-element.44, bf16[128,2,128]{2,0,1:T(8,128)(2,1)S(1)} %bitcast.185, ...), kind=kOutput, calls=%fused_computation.18 | convolution fusion | flops 270008320 | bytes 2891776 | tf_op jit(solution)/shard_map/gqk,kgd->gqd/dot_general | solution.py:258
  116.5 2.5 %collective-permute-start.19 = (bf16[16,1536]{1,0:T(8,128)(2,1)S(1)}, bf16[16,1536]{1,0:T(8,128)(2,1)S(1)}, u32[]{:S(2)}, u32[]{:S(2)}) collective-permute-start(bf16[16,1536]{1,0:T(8,128)(2,1)S(1)} %pad_maximum_fusion.14), channel_id=1, source_target_pairs={{0,2},{2,0},{4,6},{6,4},{1,3},{3,1},{5,7},{7,5},{8,10},{10,8},{12,... | collective-permute-start | bytes 147464 | tf_op jit(solution)/shard_map/ppermute | solution.py:137
  119.1 9.8 %collective-permute-start.20 = (bf16[16,1536]{1,0:T(8,128)(2,1)S(1)}, bf16[16,1536]{1,0:T(8,128)(2,1)S(1)}, u32[]{:S(2)}, u32[]{:S(2)}) collective-permute-start(bf16[16,1536]{1,0:T(8,128)(2,1)S(1)} %pad_maximum_fusion.15), channel_id=1, source_target_pairs={{0,4},{2,6},{4,0},{6,2},{1,5},{3,7},{5,1},{7,3},{8,12},{10,14},{12... | collective-permute-start | bytes 147464 | tf_op jit(solution)/shard_map/ppermute | solution.py:137
  128.9 3.3 %collective-permute-done.20 = bf16[16,1536]{1,0:T(8,128)(2,1)S(1)} collective-permute-done((bf16[16,1536]{1,0:T(8,128)(2,1)S(1)}, bf16[16,1536]{1,0:T(8,128)(2,1)S(1)}, u32[]{:S(2)}, u32[]{:S(2)}) %collective-permute-start.20) | collective-permute-done | bytes 49184 | tf_op jit(solution)/shard_map/ppermute | solution.py:137
  132.3 2.5 %collective-permute-done.21 = bf16[16,1536]{1,0:T(8,128)(2,1)S(1)} collective-permute-done((bf16[16,1536]{1,0:T(8,128)(2,1)S(1)}, bf16[16,1536]{1,0:T(8,128)(2,1)S(1)}, u32[]{:S(2)}, u32[]{:S(2)}) %collective-permute-start.21) | collective-permute-done | bytes 49184 | tf_op jit(solution)/shard_map/ppermute | solution.py:137
  135.4 1.9 %collective-permute-start.23 = (bf16[16,1536]{1,0:T(8,128)(2,1)S(1)}, bf16[16,1536]{1,0:T(8,128)(2,1)S(1)}, u32[]{:S(2)}, u32[]{:S(2)}) collective-permute-start(bf16[16,1536]{1,0:T(8,128)(2,1)S(1)} %get-tuple-element.30), channel_id=1, source_target_pairs={{0,4},{2,6},{4,0},{6,2},{1,5},{3,7},{5,1},{7,3},{8,12},{10,14},{12... | collective-permute-start | bytes 147464 | tf_op jit(solution)/shard_map/ppermute | solution.py:137
  137.3 2.5 %collective-permute-start.24 = (bf16[16,1536]{1,0:T(8,128)(2,1)S(1)}, bf16[16,1536]{1,0:T(8,128)(2,1)S(1)}, u32[]{:S(2)}, u32[]{:S(2)}) collective-permute-start(bf16[16,1536]{1,0:T(8,128)(2,1)S(1)} %get-tuple-element.30), channel_id=1, source_target_pairs={{0,6},{2,4},{4,2},{6,0},{1,7},{3,5},{5,3},{7,1},{8,14},{10,12},{12... | collective-permute-start | bytes 147464 | tf_op jit(solution)/shard_map/ppermute | solution.py:137
  141.2 1.5 collective-permute-start.25
  142.7 1.5 collective-permute-start.26
  145.0 2.5 %collective-permute-start.27 = (f32[1,1]{1,0:T(1,128)}, f32[1,1]{1,0:T(1,128)}, u32[]{:S(2)}, u32[]{:S(2)}) collective-permute-start(f32[1,1]{1,0:T(1,128)} %bitcast.65), channel_id=1, source_target_pairs={{0,24},{8,16},{16,8},{24,0},{1,25},{9,17},{17,9},{25,1},{2,26},{10... | collective-permute-start | bytes 20 | tf_op jit(solution)/shard_map/ppermute | solution.py:137
  152.3 3.2 %collective-permute-start.29 = (f32[1,1]{1,0:T(1,128)}, f32[1,1]{1,0:T(1,128)}, u32[]{:S(2)}, u32[]{:S(2)}) collective-permute-start(f32[1,1]{1,0:T(1,128)} %add.300), channel_id=1, source_target_pairs={{0,4},{2,6},{4,0},{6,2},{1,5},{3,7},{5,1},{7,3},{8,12},{10,14},{12... | collective-permute-start | bytes 20 | tf_op jit(solution)/shard_map/ppermute | solution.py:137
  155.4 3.8 %collective-permute-start.30 = (f32[1,1]{1,0:T(1,128)}, f32[1,1]{1,0:T(1,128)}, u32[]{:S(2)}, u32[]{:S(2)}) collective-permute-start(f32[1,1]{1,0:T(1,128)} %add.300), channel_id=1, source_target_pairs={{0,6},{2,4},{4,2},{6,0},{1,7},{3,5},{5,3},{7,1},{8,14},{10,12},{12... | collective-permute-start | bytes 20 | tf_op jit(solution)/shard_map/ppermute | solution.py:137
  (213 shorter events, 52.7 us)
Async XLA Ops:
  1.4 30.5 %collective-permute-start = (bf16[128]{0:T(256)(128)(2,1)S(1)}, bf16[128]{0:T(256)(128)(2,1)S(1)}, u32[]{:S(2)}, u32[]{:S(2)}) collective-permute-start(bf16[128]{0:T(256)(128)(2,1)S(1)} %convert_element_type.223), channel_id=1, source_target_pairs={{0,4},{2,6},{4,0},{6,2},{1,5},{3,7},{5,1},{7,3},{8,12},{10,14},{12... | collective-permute-start | bytes 776 | tf_op jit(solution)/shard_map/ppermute | solution.py:137
  5.4 26.7 %collective-permute-start.1 = (bf16[128]{0:T(256)(128)(2,1)S(1)}, bf16[128]{0:T(256)(128)(2,1)S(1)}, u32[]{:S(2)}, u32[]{:S(2)}) collective-permute-start(bf16[128]{0:T(256)(128)(2,1)S(1)} %convert_element_type.223), channel_id=1, source_target_pairs={{0,6},{2,4},{4,2},{6,0},{1,7},{3,5},{5,3},{7,1},{8,14},{10,12},{12... | collective-permute-start | bytes 776 | tf_op jit(solution)/shard_map/ppermute | solution.py:137
  6.8 25.4 %collective-permute-start.2 = (bf16[128]{0:T(256)(128)(2,1)S(1)}, bf16[128]{0:T(256)(128)(2,1)S(1)}, u32[]{:S(2)}, u32[]{:S(2)}) collective-permute-start(bf16[128]{0:T(256)(128)(2,1)S(1)} %convert_element_type.223), channel_id=1, source_target_pairs={{0,2},{2,0},{4,6},{6,4},{1,3},{3,1},{5,7},{7,5},{8,10},{10,8},{12,... | collective-permute-start | bytes 776 | tf_op jit(solution)/shard_map/ppermute | solution.py:137
  8.5 12.8 %collective-permute-start.3 = (f32[128]{0:T(128)S(1)}, f32[128]{0:T(128)S(1)}, u32[]{:S(2)}, u32[]{:S(2)}) collective-permute-start(f32[128]{0:T(128)S(1)} %fusion.3), channel_id=1, source_target_pairs={{0,1},{1,0},{2,3},{3,2},{4,5},{5,4},{6,7},{7,6},{8,9},{9,8},{10,11... | collective-permute-start | bytes 1544 | tf_op jit(solution)/shard_map/ppermute | solution.py:137
  24.8 14.4 %collective-permute-start.9 = (bf16[128,2048]{1,0:T(8,128)(2,1)}, bf16[128,2048]{1,0:T(8,128)(2,1)}, u32[]{:S(2)}, u32[]{:S(2)}) collective-permute-start(bf16[128,2048]{1,0:T(8,128)(2,1)} %constant_dynamic-slice_fusion.2), channel_id=1, source_target_pairs={{0,3},{2,1},{5,6},{7,4},{8,11},{10,9},{13,14},{15,12},{16,19},{18,... | collective-permute-start | bytes 1572872 | tf_op jit(solution)/shard_map/ppermute | solution.py:141
  29.3 4.4 %collective-permute-start.6 = (bf16[128,2048]{1,0:T(8,128)(2,1)}, bf16[128,2048]{1,0:T(8,128)(2,1)}, u32[]{:S(2)}, u32[]{:S(2)}) collective-permute-start(bf16[128,2048]{1,0:T(8,128)(2,1)} %constant_dynamic-slice_fusion.2), channel_id=1, source_target_pairs={{1,6},{3,4},{4,3},{6,1},{9,14},{11,12},{12,11},{14,9},{17,22},{19,... | collective-permute-start | bytes 1572872 | tf_op jit(solution)/shard_map/ppermute | solution.py:141
  31.9 83.0 %collective-permute-start.18 = (f32[128,16]{0,1:T(8,128)S(1)}, f32[128,16]{0,1:T(8,128)S(1)}, u32[]{:S(2)}, u32[]{:S(2)}) collective-permute-start(f32[128,16]{0,1:T(8,128)S(1)} %fusion.17), channel_id=1, source_target_pairs={{0,1},{1,0},{2,3},{3,2},{4,5},{5,4},{6,7},{7,6},{8,9},{9,8},{10,11... | collective-permute-start | bytes 24584 | tf_op jit(solution)/shard_map/ppermute | solution.py:137
  33.7 14.9 %collective-permute-start.7 = (bf16[128,2048]{1,0:T(8,128)(2,1)}, bf16[128,2048]{1,0:T(8,128)(2,1)S(1)}, u32[]{:S(2)}, u32[]{:S(2)}) collective-permute-start(bf16[128,2048]{1,0:T(8,128)(2,1)} %collective-permute-done.6), channel_id=1, source_target_pairs={{1,0},{3,2},{4,5},{6,7},{9,8},{11,10},{12,13},{14,15},{17,16},{19,... | collective-permute-start | bytes 1572872 | tf_op jit(solution)/shard_map/ppermute | solution.py:141
  41.2 9.5 %collective-permute-start.10 = (bf16[128,2048]{1,0:T(8,128)(2,1)S(1)}, bf16[128,2048]{1,0:T(8,128)(2,1)S(1)}, u32[]{:S(2)}, u32[]{:S(2)}) collective-permute-start(bf16[128,2048]{1,0:T(8,128)(2,1)S(1)} %get-tuple-element.18), channel_id=1, source_target_pairs={{0,1},{1,0},{2,3},{3,2},{4,5},{5,4},{6,7},{7,6},{8,9},{9,8},{10,11... | collective-permute-start | bytes 1572872 | tf_op jit(solution)/shard_map/ppermute | solution.py:137
  46.9 18.0 %collective-permute-start.4 = (bf16[128,2048]{1,0:T(8,128)(2,1)}, bf16[128,2048]{1,0:T(8,128)(2,1)}, u32[]{:S(2)}, u32[]{:S(2)}) collective-permute-start(bf16[128,2048]{1,0:T(8,128)(2,1)} %get-tuple-element.19), channel_id=1, source_target_pairs={{1,5},{3,7},{4,0},{6,2},{9,13},{11,15},{12,8},{14,10},{17,21},{19,... | collective-permute-start | bytes 1572872 | tf_op jit(solution)/shard_map/ppermute | solution.py:141
  56.3 14.1 %collective-permute-start.8 = (bf16[128,768]{0,1:T(8,128)(2,1)}, bf16[128,768]{0,1:T(8,128)(2,1)}, u32[]{:S(2)}, u32[]{:S(2)}) collective-permute-start(bf16[128,768]{0,1:T(8,128)(2,1)} %pad_maximum_fusion.6), channel_id=1, source_target_pairs={{0,2},{2,0},{4,6},{6,4},{1,3},{3,1},{5,7},{7,5},{8,10},{10,8},{12,... | collective-permute-start | bytes 589832 | tf_op jit(solution)/shard_map/ppermute | solution.py:137
  64.9 10.9 %collective-permute-start.5 = (bf16[128,2048]{1,0:T(8,128)(2,1)}, bf16[128,2048]{1,0:T(8,128)(2,1)}, u32[]{:S(2)}, u32[]{:S(2)}) collective-permute-start(bf16[128,2048]{1,0:T(8,128)(2,1)} %collective-permute-done.4), channel_id=1, source_target_pairs={{0,1},{2,3},{5,4},{7,6},{8,9},{10,11},{13,12},{15,14},{16,17},{18,... | collective-permute-start | bytes 1572872 | tf_op jit(solution)/shard_map/ppermute | solution.py:141
  70.4 7.8 %collective-permute-start.11 = (bf16[128,768]{0,1:T(8,128)(2,1)}, bf16[128,768]{0,1:T(8,128)(2,1)}, u32[]{:S(2)}, u32[]{:S(2)}) collective-permute-start(bf16[128,768]{0,1:T(8,128)(2,1)} %pad_maximum_fusion.7), channel_id=1, source_target_pairs={{0,2},{2,0},{4,6},{6,4},{1,3},{3,1},{5,7},{7,5},{8,10},{10,8},{12,... | collective-permute-start | bytes 589832 | tf_op jit(solution)/shard_map/ppermute | solution.py:137
  78.1 11.2 %collective-permute-start.14 = (bf16[128,768]{0,1:T(8,128)(2,1)S(1)}, bf16[128,768]{0,1:T(8,128)(2,1)S(1)}, u32[]{:S(2)}, u32[]{:S(2)}) collective-permute-start(bf16[128,768]{0,1:T(8,128)(2,1)S(1)} %pad_maximum_fusion.9), channel_id=1, source_target_pairs={{0,4},{2,6},{4,0},{6,2},{1,5},{3,7},{5,1},{7,3},{8,12},{10,14},{12... | collective-permute-start | bytes 589832 | tf_op jit(solution)/shard_map/ppermute | solution.py:137
  80.6 22.3 %collective-permute-start.16 = (bf16[128,768]{0,1:T(8,128)(2,1)S(1)}, bf16[128,768]{0,1:T(8,128)(2,1)}, u32[]{:S(2)}, u32[]{:S(2)}) collective-permute-start(bf16[128,768]{0,1:T(8,128)(2,1)S(1)} %pad_maximum_fusion.9), channel_id=1, source_target_pairs={{0,6},{4,2},{1,7},{5,3},{8,14},{12,10},{9,15},{13,11},{16,22},{20,... | collective-permute-start | bytes 589832 | tf_op jit(solution)/shard_map/ppermute | solution.py:141
  91.3 13.4 %collective-permute-start.12 = (bf16[128,768]{0,1:T(8,128)(2,1)S(1)}, bf16[128,768]{0,1:T(8,128)(2,1)S(1)}, u32[]{:S(2)}, u32[]{:S(2)}) collective-permute-start(bf16[128,768]{0,1:T(8,128)(2,1)S(1)} %pad_maximum_fusion.8), channel_id=1, source_target_pairs={{0,4},{2,6},{1,5},{3,7},{8,12},{10,14},{9,13},{11,15},{16,20},{18,... | collective-permute-start | bytes 589832 | tf_op jit(solution)/shard_map/ppermute | solution.py:141
  92.7 13.6 %collective-permute-start.15 = (bf16[128,768]{0,1:T(8,128)(2,1)S(1)}, bf16[128,768]{0,1:T(8,128)(2,1)S(1)}, u32[]{:S(2)}, u32[]{:S(2)}) collective-permute-start(bf16[128,768]{0,1:T(8,128)(2,1)S(1)} %pad_maximum_fusion.8), channel_id=1, source_target_pairs={{0,2},{4,6},{1,3},{5,7},{8,10},{12,14},{9,11},{13,15},{16,18},{20,... | collective-permute-start | bytes 589832 | tf_op jit(solution)/shard_map/ppermute | solution.py:141
  106.9 0.9 collective-permute-start.13
  114.8 1.4 collective-permute-start.17
  116.5 12.4 %collective-permute-start.19 = (bf16[16,1536]{1,0:T(8,128)(2,1)S(1)}, bf16[16,1536]{1,0:T(8,128)(2,1)S(1)}, u32[]{:S(2)}, u32[]{:S(2)}) collective-permute-start(bf16[16,1536]{1,0:T(8,128)(2,1)S(1)} %pad_maximum_fusion.14), channel_id=1, source_target_pairs={{0,2},{2,0},{4,6},{6,4},{1,3},{3,1},{5,7},{7,5},{8,10},{10,8},{12,... | collective-permute-start | bytes 147464 | tf_op jit(solution)/shard_map/ppermute | solution.py:137
  119.1 13.2 %collective-permute-start.20 = (bf16[16,1536]{1,0:T(8,128)(2,1)S(1)}, bf16[16,1536]{1,0:T(8,128)(2,1)S(1)}, u32[]{:S(2)}, u32[]{:S(2)}) collective-permute-start(bf16[16,1536]{1,0:T(8,128)(2,1)S(1)} %pad_maximum_fusion.15), channel_id=1, source_target_pairs={{0,4},{2,6},{4,0},{6,2},{1,5},{3,7},{5,1},{7,3},{8,12},{10,14},{12... | collective-permute-start | bytes 147464 | tf_op jit(solution)/shard_map/ppermute | solution.py:137
  128.9 5.9 %collective-permute-start.21 = (bf16[16,1536]{1,0:T(8,128)(2,1)S(1)}, bf16[16,1536]{1,0:T(8,128)(2,1)S(1)}, u32[]{:S(2)}, u32[]{:S(2)}) collective-permute-start(bf16[16,1536]{1,0:T(8,128)(2,1)S(1)} %pad_maximum_fusion.16), channel_id=1, source_target_pairs={{0,6},{2,4},{4,2},{6,0},{1,7},{3,5},{5,3},{7,1},{8,14},{10,12},{12... | collective-permute-start | bytes 147464 | tf_op jit(solution)/shard_map/ppermute | solution.py:137
  135.4 28.0 %collective-permute-start.22 = (bf16[16,1536]{1,0:T(8,128)(2,1)S(1)}, bf16[16,1536]{1,0:T(8,128)(2,1)S(1)}, u32[]{:S(2)}, u32[]{:S(2)}) collective-permute-start(bf16[16,1536]{1,0:T(8,128)(2,1)S(1)} %get-tuple-element.30), channel_id=1, source_target_pairs={{0,2},{2,0},{4,6},{6,4},{1,3},{3,1},{5,7},{7,5},{8,10},{10,8},{12,... | collective-permute-start | bytes 147464 | tf_op jit(solution)/shard_map/ppermute | solution.py:137
  135.4 28.0 %collective-permute-start.23 = (bf16[16,1536]{1,0:T(8,128)(2,1)S(1)}, bf16[16,1536]{1,0:T(8,128)(2,1)S(1)}, u32[]{:S(2)}, u32[]{:S(2)}) collective-permute-start(bf16[16,1536]{1,0:T(8,128)(2,1)S(1)} %get-tuple-element.30), channel_id=1, source_target_pairs={{0,4},{2,6},{4,0},{6,2},{1,5},{3,7},{5,1},{7,3},{8,12},{10,14},{12... | collective-permute-start | bytes 147464 | tf_op jit(solution)/shard_map/ppermute | solution.py:137
  137.3 26.1 %collective-permute-start.24 = (bf16[16,1536]{1,0:T(8,128)(2,1)S(1)}, bf16[16,1536]{1,0:T(8,128)(2,1)S(1)}, u32[]{:S(2)}, u32[]{:S(2)}) collective-permute-start(bf16[16,1536]{1,0:T(8,128)(2,1)S(1)} %get-tuple-element.30), channel_id=1, source_target_pairs={{0,6},{2,4},{4,2},{6,0},{1,7},{3,5},{5,3},{7,1},{8,14},{10,12},{12... | collective-permute-start | bytes 147464 | tf_op jit(solution)/shard_map/ppermute | solution.py:137
  141.2 3.8 %collective-permute-start.25 = (f32[1,1]{1,0:T(1,128)}, f32[1,1]{1,0:T(1,128)}, u32[]{:S(2)}, u32[]{:S(2)}) collective-permute-start(f32[1,1]{1,0:T(1,128)} %bitcast.65), channel_id=1, source_target_pairs={{0,8},{8,0},{16,24},{24,16},{1,9},{9,1},{17,25},{25,17},{2,10},{10... | collective-permute-start | bytes 20 | tf_op jit(solution)/shard_map/ppermute | solution.py:137
  142.7 4.7 %collective-permute-start.26 = (f32[1,1]{1,0:T(1,128)}, f32[1,1]{1,0:T(1,128)}, u32[]{:S(2)}, u32[]{:S(2)}) collective-permute-start(f32[1,1]{1,0:T(1,128)} %bitcast.65), channel_id=1, source_target_pairs={{0,16},{8,24},{16,0},{24,8},{1,17},{9,25},{17,1},{25,9},{2,18},{10... | collective-permute-start | bytes 20 | tf_op jit(solution)/shard_map/ppermute | solution.py:137
  145.0 4.5 %collective-permute-start.27 = (f32[1,1]{1,0:T(1,128)}, f32[1,1]{1,0:T(1,128)}, u32[]{:S(2)}, u32[]{:S(2)}) collective-permute-start(f32[1,1]{1,0:T(1,128)} %bitcast.65), channel_id=1, source_target_pairs={{0,24},{8,16},{16,8},{24,0},{1,25},{9,17},{17,9},{25,1},{2,26},{10... | collective-permute-start | bytes 20 | tf_op jit(solution)/shard_map/ppermute | solution.py:137
  150.9 4.5 %collective-permute-start.28 = (f32[1,1]{1,0:T(1,128)}, f32[1,1]{1,0:T(1,128)}, u32[]{:S(2)}, u32[]{:S(2)}) collective-permute-start(f32[1,1]{1,0:T(1,128)} %add.300), channel_id=1, source_target_pairs={{0,2},{2,0},{4,6},{6,4},{1,3},{3,1},{5,7},{7,5},{8,10},{10,8},{12,... | collective-permute-start | bytes 20 | tf_op jit(solution)/shard_map/ppermute | solution.py:137
  152.3 7.0 %collective-permute-start.29 = (f32[1,1]{1,0:T(1,128)}, f32[1,1]{1,0:T(1,128)}, u32[]{:S(2)}, u32[]{:S(2)}) collective-permute-start(f32[1,1]{1,0:T(1,128)} %add.300), channel_id=1, source_target_pairs={{0,4},{2,6},{4,0},{6,2},{1,5},{3,7},{5,1},{7,3},{8,12},{10,14},{12... | collective-permute-start | bytes 20 | tf_op jit(solution)/shard_map/ppermute | solution.py:137
  155.4 5.3 %collective-permute-start.30 = (f32[1,1]{1,0:T(1,128)}, f32[1,1]{1,0:T(1,128)}, u32[]{:S(2)}, u32[]{:S(2)}) collective-permute-start(f32[1,1]{1,0:T(1,128)} %add.300), channel_id=1, source_target_pairs={{0,6},{2,4},{4,2},{6,0},{1,7},{3,5},{5,3},{7,1},{8,14},{10,12},{12... | collective-permute-start | bytes 20 | tf_op jit(solution)/shard_map/ppermute | solution.py:137
  161.4 1.3 collective-permute-start.31
  (17 other events, 122.4 us)

commit v2 on v0

--- a/solution.py
+++ b/solution.py
@@ -1,8 +1,11 @@
+import functools
 import math
 
 import jax
 import jax.numpy as jnp
 from jax import lax
+from jax.experimental import pallas as pl
+from jax.experimental.pallas import tpu as pltpu
 from jax.sharding import PartitionSpec as P
 
 
@@ -23,7 +26,7 @@
     )
 
 
-def per_device(hidden, gain, queries, key_value_weight, adapt_down, adapt_up, out_grad, doc_ids):
+def gathered_weights(hidden, gain, queries, key_value_weight, adapt_down, adapt_up, out_grad, doc_ids):
     tp_count = lax.axis_size("tp")
     row_count = hidden.shape[1]
     local_width = hidden.shape[2]
@@ -132,6 +135,422 @@
     return (attended[None], adapter_rows[None], grad_down[None], grad_up[None])
 
 
+F32, BF16 = jnp.float32, jnp.bfloat16
+VMEM = pl.BlockSpec(memory_space=pltpu.VMEM)
+LIMIT = 48 * 1024 * 1024
+
+
+def swap(value, axis, distance):
+    count = lax.axis_size(axis)
+    return lax.ppermute(value, axis, [(i, i ^ distance) for i in range(count)])
+
+
+def call(kernel, outs, *operands, flops=0, scratch=()):
+    shapes = [jax.ShapeDtypeStruct(shape, dtype) for shape, dtype in outs]
+    moved = sum(math.prod(x.shape) * x.dtype.itemsize for x in (*operands, *shapes))
+    return pl.pallas_call(
+        kernel,
+        out_shape=shapes,
+        in_specs=[VMEM] * len(operands),
+        out_specs=[VMEM] * len(shapes),
+        scratch_shapes=scratch,
+        compiler_params=pltpu.CompilerParams(vmem_limit_bytes=LIMIT),
+        cost_estimate=pl.CostEstimate(flops=flops, bytes_accessed=moved, transcendentals=0),
+    )(*operands)
+
+
+def times(left, right):
+    return lax.dot_general(left, right, (((1,), (0,)), ((), ())), preferred_element_type=F32)
+
+
+def times_transposed(left, right):
+    return lax.dot_general(left, right, (((1,), (1,)), ((), ())), preferred_element_type=F32)
+
+
+def transposed_times(left, right):
+    return lax.dot_general(left, right, (((0,), (0,)), ((), ())), preferred_element_type=F32)
+
+
+def square_kernel(hidden_ref, out_ref):
+    rows = hidden_ref[...].astype(F32)
+    out_ref[...] = jnp.broadcast_to(jnp.sum(rows * rows, axis=1, keepdims=True), out_ref.shape)
+
+
+def norm_kernel(hidden_ref, gain_ref, mine_ref, other_ref, even_ref, odd_ref):
+    width = even_ref.shape[1]
+    mean = (mine_ref[:, :1] + other_ref[:, :1]) / (4 * width)
+    scale = lax.rsqrt(mean + 1e-06)
+    parity = lax.axis_index("ctx") % 2
+    for out_ref, half in ((even_ref, parity), (odd_ref, 1 - parity)):
+        columns = pl.ds(pl.multiple_of(half * width, width), width)
+        rows = hidden_ref[:, columns].astype(F32)
+        out_ref[...] = (rows * scale * gain_ref[:, columns].astype(F32)).astype(BF16)
+
+
+def at_home():
+    return lax.axis_index("ctx") // 2 == lax.axis_index("tp")
+
+
+def split_heads(value, head):
+    count = value.shape[1] // (2 * head)
+    pieces = [value[:, i * head : (i + 1) * head] for i in range(2 * count)]
+    return jnp.concatenate(pieces[0::2], axis=1), jnp.concatenate(pieces[1::2], axis=1)
+
+
+def pack(value, out_ref, head):
+    keys, values = split_heads(value, head)
+    width = keys.shape[1]
+    high = keys.astype(BF16)
+    out_ref[:, :width] = high
+    out_ref[:, width : 2 * width] = (keys - high.astype(F32)).astype(BF16)
+    out_ref[:, 2 * width :] = values.astype(BF16)
+
+
+def unpack(ref):
+    width = ref.shape[1] // 3
+    keys = ref[:, :width].astype(F32) + ref[:, width : 2 * width].astype(F32)
+    return keys, ref[:, 2 * width :].astype(F32)
+
+
+def near_kernel(head, even_ref, fwd_0_ref, got_1_ref, fwd_1_ref, weight_ref, part_0_ref, sent_ref):
+    home = at_home()
+    rows_1 = jnp.where(home, fwd_1_ref[...], got_1_ref[...])
+    pack(times(rows_1, weight_ref[...]), sent_ref, head)
+    rows_0 = jnp.where(home, even_ref[...], fwd_0_ref[...])
+    keys, values = split_heads(times(rows_0, weight_ref[...]), head)
+    part_0_ref[...] = jnp.concatenate([keys, values], axis=1)
+
+
+def side_kernel(part_0_ref, got_ref, own_ref, sent_ref):
+    keys, values = unpack(got_ref)
+    width = keys.shape[1]
+    keys = part_0_ref[:, :width] + keys
+    values = part_0_ref[:, width:] + values
+    store_sum(keys, values, own_ref, sent_ref)
+
+
+def store_sum(keys, values, sum_ref, sent_ref):
+    width = keys.shape[1]
+    sum_ref[:, :width] = keys
+    sum_ref[:, width:] = values
+    high = keys.astype(BF16)
+    sent_ref[:, :width] = high
+    sent_ref[:, width : 2 * width] = (keys - high.astype(F32)).astype(BF16)
+    sent_ref[:, 2 * width :] = values.astype(BF16)
+
+
+def far_3_kernel(head, got_ref, fwd_ref, weight_ref, sent_ref):
+    rows = jnp.where(at_home(), fwd_ref[...], got_ref[...])
+    pack(times(rows, weight_ref[...]), sent_ref, head)
+
+
+def far_2_kernel(head, got_ref, fwd_ref, weight_ref, arrived_ref, sum_ref, sent_ref):
+    rows = jnp.where(at_home(), got_ref[...], fwd_ref[...])
+    keys, values = split_heads(times(rows, weight_ref[...]), head)
+    add_keys, add_values = unpack(arrived_ref)
+    store_sum(keys + add_keys, values + add_values, sum_ref, sent_ref)
+
+
+def turn(value, cosine, sine):
+    head = cosine.shape[1]
+    pieces = []
+    for i in range(value.shape[1] // head):
+        piece = value[:, i * head : (i + 1) * head]
+        pieces.append(piece * cosine + pltpu.roll(piece, head // 2, 1) * sine)
+    return jnp.concatenate(pieces, axis=1)
+
+
+def query_kernel(query_ref, cosine_ref, sine_ref, out_ref):
+    out_ref[...] = turn(query_ref[...].astype(F32), cosine_ref[0], sine_ref[0]).astype(BF16)
+
+
+def finish(sum_ref, arrived_ref, cosine, sine):
+    keys, values = unpack(arrived_ref)
+    width = keys.shape[1]
+    keys = turn(sum_ref[:, :width] + keys, cosine, sine).astype(BF16)
+    return keys, (sum_ref[:, width:] + values).astype(BF16)
+
+
+def block_kernel(sum_ref, arrived_ref, cosine_ref, sine_ref, out_ref):
+    keys, values = finish(sum_ref, arrived_ref, cosine_ref[2], sine_ref[2])
+    width = keys.shape[1]
+    out_ref[:, :width] = keys
+    out_ref[:, width:] = values
+
+
+def attention_kernel(
+    head,
+    query_ref,
+    own_ref,
+    own_far_ref,
+    next_ref,
+    next_far_ref,
+    block_2_ref,
+    block_3_ref,
+    cosine_ref,
+    sine_ref,
+    mask_ref,
+    down_ref,
+    out_ref,
+    low_ref,
+):
+    keys_0, values_0 = finish(own_ref, own_far_ref, cosine_ref[0], sine_ref[0])
+    next_keys, next_values = unpack(next_ref)
+    width = next_keys.shape[1]
+    far_keys, far_values = unpack(next_far_ref)
+    keys_1 = turn(next_keys + far_keys, cosine_ref[1], sine_ref[1]).astype(BF16)
+    values_1 = (next_values + far_values).astype(BF16)
+    keys = jnp.concatenate(
+        [keys_0, keys_1, block_2_ref[:, :width], block_3_ref[:, :width]], axis=0
+    )
+    values = jnp.concatenate(
+        [values_0, values_1, block_2_ref[:, width:], block_3_ref[:, width:]], axis=0
+    )
+    allowed = mask_ref[...] > 0
+    heads = query_ref.shape[1] // head
+    group = heads // (width // head)
+    scale = head ** (-0.5)
+    for index in range(heads):
+        first = index // group * head
+        columns = slice(index * head, (index + 1) * head)
+        scores = times_transposed(query_ref[:, columns], keys[:, first : first + head])
+        scores = jnp.where(allowed, scores * scale, -1e30)
+        weights = jnp.exp(scores - jnp.max(scores, axis=1, keepdims=True))
+        total = jnp.sum(weights, axis=1, keepdims=True)
+        mixed = times(weights.astype(BF16), values[:, first : first + head])
+        out_ref[:, columns] = (mixed / total).astype(BF16)
+    low_ref[...] = times_transposed(out_ref[...], down_ref[...])
+
+
+def back_kernel(grad_ref, up_ref, out_ref):
+    out_ref[...] = times_transposed(grad_ref[...], up_ref[...])
+
+
+def grads_kernel(
+    low_ref,
+    low_other_ref,
+    back_ref,
+    back_other_ref,
+    grad_ref,
+    attended_ref,
+    own_ref,
+    sent_1_ref,
+    sent_2_ref,
+    sent_3_ref,
+):
+    low = (low_ref[...] + low_other_ref[...]).astype(BF16)
+    back = (back_ref[...] + back_other_ref[...]).astype(BF16)
+    place = lax.axis_index("ctx")
+    up_step, down_step = grad_ref.shape[1] // 4, attended_ref.shape[1] // 4
+    for d, out in ((2, sent_2_ref), (3, sent_3_ref), (1, sent_1_ref), (0, own_ref)):
+        index = place ^ d
+        columns = pl.ds(pl.multiple_of(index * up_step, up_step), up_step)
+        out[:, :up_step] = transposed_times(low, grad_ref[:, columns]).astype(out.dtype)
+        columns = pl.ds(pl.multiple_of(index * down_step, down_step), down_step)
+        out[:, up_step:] = transposed_times(back, attended_ref[:, columns]).astype(out.dtype)
+
+
+def adapter_kernel(low_ref, low_other_ref, up_ref, out_ref):
+    low = (low_ref[...] + low_other_ref[...]).astype(BF16)
+    out_ref[...] = times(low, up_ref[...]).astype(BF16)
+
+
+def total_kernel(own_ref, got_1_ref, got_2_ref, got_3_ref, out_ref, square_ref):
+    total = own_ref[...]
+    for ref in (got_1_ref, got_2_ref, got_3_ref):
+        total = total + ref[...].astype(F32)
+    out_ref[...] = total.astype(BF16)
+    square_ref[...] = jnp.broadcast_to(jnp.sum(total * total).reshape(1, 1), square_ref.shape)
+
+
+def clip_kernel(ceiling, square_ref, other_ref, own_ref, got_1, got_2, got_3, up_ref, down_ref):
+    squares = square_ref[:1, :1] + other_ref[:1, :1]
+    factor = jnp.minimum(1.0, ceiling / (jnp.sqrt(squares) + 1e-06))
+    place = lax.axis_index("ctx")
+    up_step, down_step = up_ref.shape[1] // 4, down_ref.shape[1] // 4
+    for d, ref in enumerate((own_ref, got_1, got_2, got_3)):
+        index = place ^ d
+        columns = pl.ds(pl.multiple_of(index * up_step, up_step), up_step)
+        up_ref[:, columns] = ref[:, :up_step].astype(F32) * factor
+        columns = pl.ds(pl.multiple_of(index * down_step, down_step), down_step)
+        down_ref[:, columns] = ref[:, up_step:].astype(F32) * factor
+
+
+def split_model_width(
+    hidden, gain, queries, key_value_weight, adapt_down, adapt_up, out_grad, doc_ids
+):
+    place = lax.axis_index("ctx")
+    rows = hidden.shape[1]
+    local_width = hidden.shape[2]
+    slice_width = key_value_weight.shape[1]
+    kv_count, head = key_value_weight.shape[2], key_value_weight.shape[-1]
+    head_count = queries.shape[2]
+    local_query = head_count * head
+    rank = adapt_down.shape[1]
+    kv_width = kv_count * 2 * head
+    sent_width = kv_count * 3 * head
+
+    (squares,) = call(square_kernel, [((rows, 128), F32)], hidden[0])
+    even, odd = call(
+        norm_kernel,
+        [((rows, slice_width), BF16)] * 2,
+        hidden[0],
+        gain,
+        squares,
+        swap(squares, "tp", 1),
+    )
+
+    def device(chip, which):
+        return chip * 2 + which
+
+    axes = ("ctx", "tp")
+    pairs_1 = [(device(a, a // 2), device(a ^ 1, 1 - a // 2)) for a in range(4)]
+    pairs_3 = [(device(a, 1 - a // 2), device(a ^ 3, a // 2)) for a in range(4)]
+    pairs_2 = [(device(a, 1 - a // 2), device(a ^ 2, 1 - a // 2)) for a in range(4)]
+    home_to_away = [(device(a, a // 2), device(a, 1 - a // 2)) for a in range(4)]
+    away_to_home = [(j, i) for i, j in home_to_away]
+    got_1 = lax.ppermute(odd, axes, pairs_1)
+    got_3 = lax.ppermute(odd, axes, pairs_3)
+    got_2 = lax.ppermute(even, axes, pairs_2)
+    fwd_0 = lax.ppermute(even, axes, home_to_away)
+
+    key_value_weight, queries, out_grad, doc_ids, even, odd = lax.optimization_barrier(
+        (key_value_weight, queries, out_grad, doc_ids, even, odd)
+    )
+    weight = key_value_weight[0].reshape(slice_width, kv_width)
+    freqs = 1000000.0 ** (-jnp.arange(head // 2, dtype=F32) * 2.0 / head)
+    positions = jnp.stack(
+        [(place ^ d) * rows + jnp.arange(rows, dtype=jnp.int32) for d in range(4)]
+    )
+    angles = positions.astype(F32)[:, :, None] * freqs
+    cosine, sine = jnp.cos(angles), jnp.sin(angles)
+    cosine = jnp.concatenate([cosine, cosine], axis=2)
+    sine = jnp.concatenate([-sine, sine], axis=2)
+    (query,) = call(
+        query_kernel,
+        [((rows, local_query), BF16)],
+        queries[0].reshape(rows, local_query),
+        cosine,
+        sine,
+    )
+    (back_part,) = call(
+        back_kernel,
+        [((rows, rank), F32)],
+        out_grad[0],
+        adapt_up[0],
+        flops=2 * rows * local_width * rank,
+    )
+    back_other = swap(back_part, "tp", 1)
+    docs = doc_ids.astype(F32).reshape(1, rows)
+    key_docs = jnp.stack([docs] + [swap(docs, "ctx", d) for d in (1, 2, 3)])
+    allowed = (positions[:, None, :] <= positions[0][None, :, None]) & (
+        key_docs == doc_ids.astype(F32)[None, :, None]
+    )
+    mask = allowed.astype(F32).transpose(1, 0, 2).reshape(rows, 4 * rows)
+
+    fwd_1 = lax.ppermute(got_1, axes, away_to_home)
+    part_flops = 2 * rows * slice_width * kv_width
+    packed = ((rows, sent_width), BF16)
+    summed = ((rows, kv_width), F32)
+    part_0, sent_1 = call(
+        functools.partial(near_kernel, head),
+        [summed, packed],
+        even,
+        fwd_0,
+        got_1,
+        fwd_1,
+        weight,
+        flops=2 * part_flops,
+    )
+    own_side, own_sent = call(side_kernel, [summed, packed], part_0, swap(sent_1, "ctx", 1))
+    side_next = lax.ppermute(own_sent, "ctx", [(0, 1), (2, 3)])
+    early_far = lax.ppermute(own_sent, "ctx", [(0, 2), (1, 3)])
+    fwd_3 = lax.ppermute(got_3, axes, away_to_home)
+    (sent_3,) = call(
+        functools.partial(far_3_kernel, head), [packed], got_3, fwd_3, weight, flops=part_flops
+    )
+    arrived_3 = swap(sent_3, "ctx", 1)
+    fwd_2 = lax.ppermute(got_2, axes, home_to_away)
+    far_side, far_sent = call(
+        functools.partial(far_2_kernel, head),
+        [summed, packed],
+        got_2,
+        fwd_2,
+        weight,
+        arrived_3,
+        flops=part_flops,
+    )
+    own_far = swap(far_sent, "ctx", 2)
+    next_far = lax.ppermute(far_sent, "ctx", [(0, 3), (2, 1)])
+    (block_2,) = call(
+        block_kernel, [((rows, kv_width), BF16)], far_side, early_far, cosine, sine
+    )
+    block_3 = lax.ppermute(block_2, "ctx", [(2, 3), (3, 2)])
+
+    attended, low_part = call(
+        functools.partial(attention_kernel, head),
+        [((rows, local_query), BF16), ((rows, rank), F32)],
+        query,
+        own_side,
+        own_far,
+        side_next,
+        next_far,
+        block_2,
+        block_3,
+        cosine,
+        sine,
+        mask,
+        adapt_down[0],
+        flops=16 * rows * rows * local_query,
+    )
+    low_other = swap(low_part, "tp", 1)
+    up_step, down_step = local_width // 4, local_query // 4
+    piece = (rank, up_step + down_step)
+    own, sent_1, sent_2, sent_3 = call(
+        grads_kernel,
+        [(piece, F32), (piece, BF16), (piece, BF16), (piece, BF16)],
+        low_part,
+        low_other,
+        back_part,
+        back_other,
+        out_grad[0],
+        attended,
+        flops=2 * rows * rank * (local_width + local_query),
+    )
+    (adapter_rows,) = call(
+        adapter_kernel,
+        [((rows, local_width), BF16)],
+        low_part,
+        low_other,
+        adapt_up[0],
+        flops=2 * rows * rank * local_width,
+    )
+    total, squares = call(
+        total_kernel,
+        [(piece, BF16), ((8, 128), F32)],
+        own,
+        *(swap(sent, "ctx", d) for d, sent in ((1, sent_1), (2, sent_2), (3, sent_3))),
+    )
+    totals = [total] + [swap(total, "ctx", d) for d in (1, 2, 3)]
+    squares = squares + sum(swap(squares, "section", d) for d in (1, 2, 3))
+    squares = squares + sum(swap(squares, "ctx", d) for d in (1, 2, 3))
+    ceiling = 0.5 * math.sqrt(lax.axis_size("section") * rank * (local_query + local_width) * 2)
+    grad_up, grad_down = call(
+        functools.partial(clip_kernel, ceiling),
+        [((rank, local_width), F32), ((rank, local_query), F32)],
+        squares,
+        swap(squares, "tp", 1),
+        *totals,
+    )
+    return (attended[None], adapter_rows[None], grad_down[None], grad_up[None])
+
+
+def per_device(*arrays):
+    if lax.axis_size("ctx") == 4 and lax.axis_size("tp") == 2 and lax.axis_size("section") == 4:
+        return split_model_width(*arrays)
+    return gathered_weights(*arrays)
+
+
 def solution(mesh):
     return jax.shard_map(
         per_device,

time: 280 us -> 120 us (0.43)
  waiting for transfers between devices: 174 us -> 37 us
  starting transfers between devices: 0.12 us -> 59.4 us
  blocking collectives: 56.5 us -> 0 us
  between operations: 16 us -> 0.96 us
  Pallas kernels: 0 us -> 14.7 us
  matrix products: 13.4 us -> 0 us
  other arithmetic: 11.4 us -> 1.42 us
    all_gather x2 -> x0, waiting for transfers between devices: 142 us -> none  [the longest x1 142 us: per_device(): lax.all_gather(kv_local, 'ctx', axis=1, tiled=True)[0]]
    ppermute x0 -> x33, starting transfers between devices: none -> 59.4 us  [the longest x22 31.1 us: swap(): return lax.ppermute(value, axis, [(i, i ^ distance) for i in range(count)])]
    all_gather x4 -> x0, blocking collectives: 40.5 us -> none  [the longest x1 13.3 us: per_device(): piece_keys = lax.all_gather(rotated_keys, 'ctx', axis=0, tiled=True)]
    ppermute x0 -> x33, waiting for transfers between devices: none -> 37 us  [the longest x22 23.9 us: swap(): return lax.ppermute(value, axis, [(i, i ^ distance) for i in range(count)])]
    psum x1 -> x0, waiting for transfers between devices: 32.1 us -> none  [per_device(): lax.psum(down_part.astype(jnp.bfloat16), 'ctx').astype(jnp.float32)]
    psum x2 -> x0, blocking collectives: 16 us -> none  [the longest x1 12.7 us: per_device(): squares = lax.psum(local_squares, ('section', 'tp'))]
    pallas_call x0 -> x14, Pallas kernels: none -> 14.7 us  [call(): pl.pallas_call(kernel, out_shape=shapes, in_specs=[VMEM] * len(operands),...]
    dot_general x8 -> x0, matrix products: 13.4 us -> none  [the longest x1 6.42 us: per_device(): jnp.dot(normalized_rows, lax.all_gather(kv_local, 'ctx', axis=1, tiled=Tr...]
  transfers between devices with their start and end apart: 3 -> 33, of which waited for: 2 -> 15; matrix products, arithmetic and copies ran while one was open for 4% -> 4% of each run, Pallas kernels for 0% -> 10%
where the time goes in v2:
time: 120 us; the launch traced here: 119 us
  starting transfers between devices  59.4 us (50%)
  waiting for transfers between devices  37 us (31%)
  Pallas kernels  14.7 us (12%)
  local copies, waits for them, and re-layouts  5.89 us (5%)
  other arithmetic  1.42 us (1%)
    ppermute x22, starting transfers between devices, swap(): return lax.ppermute(value, axis, [(i, i ^ distance) for i in range(count)])  31.1 us
    ppermute x22, waiting for transfers between devices, swap(): return lax.ppermute(value, axis, [(i, i ^ distance) for i in range(count)])  23.9 us
    pallas_call x14, Pallas kernels, call(): pl.pallas_call(kernel, out_shape=shapes, in_specs=[VMEM] * len(operands),...  14.7 us
    ppermute x1, waiting for transfers between devices, split_model_width(): got_2 = lax.ppermute(even, axes, pairs_2)  10.8 us
    ppermute x1, starting transfers between devices, split_model_width(): side_next = lax.ppermute(own_sent, 'ctx', [(0, 1), (2, 3)])  5.71 us
    ppermute x1, starting transfers between devices, split_model_width(): got_1 = lax.ppermute(odd, axes, pairs_1)  5.39 us
    ppermute x1, starting transfers between devices, split_model_width(): early_far = lax.ppermute(own_sent, 'ctx', [(0, 2), (1, 3)])  4.47 us
    ppermute x1, starting transfers between devices, split_model_width(): fwd_0 = lax.ppermute(even, axes, home_to_away)  4.17 us
  transfers between devices with their start and end apart: 33, of which 15 were waited for; matrix products, arithmetic and copies ran while one was open for 4% of the time, Pallas kernels for 10%

profile of v2, /device:TPU:0, one launch (start us, length us, event | category | flops | bytes accessed | tf_op | source)
XLA Modules:
  0.0 119.4 jit_solution(12820379440772050587)
XLA Ops:
  5.3 5.4 %collective-permute-start.2 = (bf16[128,2048]{1,0:T(8,128)(2,1)S(1)}, bf16[128,2048]{1,0:T(8,128)(2,1)}, u32[]{:S(2)}, u32[]{:S(2)}) collective-permute-start(bf16[128,2048]{1,0:T(8,128)(2,1)S(1)} %get-tuple-element.28), channel_id=1, source_target_pairs={{0,3},{2,1},{5,6},{7,4},{8,11},{10,9},{13,14},{15,12},{16,19},{18,... | collective-permute-start | bytes 1572872 | tf_op jit(solution)/shard_map/ppermute | solution.py:412
  10.7 1.4 %collective-permute-start.7 = (bf16[128,2048]{1,0:T(8,128)(2,1)S(1)}, bf16[128,2048]{1,0:T(8,128)(2,1)}, u32[]{:S(2)}, u32[]{:S(2)}) collective-permute-start(bf16[128,2048]{1,0:T(8,128)(2,1)S(1)} %get-tuple-element.28), channel_id=1, source_target_pairs={{1,6},{3,4},{4,3},{6,1},{9,14},{11,12},{12,11},{14,9},{17,22},{19,... | collective-permute-start | bytes 1572872 | tf_op jit(solution)/shard_map/ppermute | solution.py:413
  12.2 4.2 %collective-permute-start.1 = (bf16[128,2048]{1,0:T(8,128)(2,1)}, bf16[128,2048]{1,0:T(8,128)(2,1)}, u32[]{:S(2)}, u32[]{:S(2)}) collective-permute-start(bf16[128,2048]{1,0:T(8,128)(2,1)} %get-tuple-element.30.even_ref), channel_id=1, source_target_pairs={{0,1},{2,3},{5,4},{7,6},{8,9},{10,11},{13,12},{15,14},{16,17},{18,... | collective-permute-start | bytes 1572872 | tf_op jit(solution)/shard_map/ppermute | solution.py:415
  17.6 1.5 %collective-permute-done.2.got_1_ref = bf16[128,2048]{1,0:T(8,128)(2,1)} collective-permute-done((bf16[128,2048]{1,0:T(8,128)(2,1)S(1)}, bf16[128,2048]{1,0:T(8,128)(2,1)}, u32[]{:S(2)}, u32[]{:S(2)}) %collective-permute-start.2) | collective-permute-done | bytes 524320 | tf_op jit(solution)/shard_map/ppermute | solution.py:412
  23.0 2.8 %reshape_squeeze.7.weight_ref = bf16[2048,512]{1,0:T(8,128)(2,1)S(1)} reshape(bf16[1,2048,2,2,128]{4,3,2,1,0:T(2,128)(2,1)} %param.11) | data formatting | bytes 4194304 | tf_op jit(solution)/shard_map/reshape;squeeze | solution.py:420
  25.8 10.8 %collective-permute-done.5.got_ref = bf16[128,2048]{1,0:T(8,128)(2,1)S(1)} collective-permute-done((bf16[128,2048]{1,0:T(8,128)(2,1)}, bf16[128,2048]{1,0:T(8,128)(2,1)S(1)}, u32[]{:S(2)}, u32[]{:S(2)}) %collective-permute-start.5) | collective-permute-done | bytes 524320 | tf_op jit(solution)/shard_map/ppermute | solution.py:414
  38.0 2.2 %shard_map.114 = (f32[128,512]{1,0:T(8,128)S(1)}, bf16[128,768]{1,0:T(8,128)(2,1)S(1)}) custom-call(bf16[128,2048]{1,0:T(8,128)(2,1)} %get-tuple-element.30.even_ref, bf16[128,2048]{1,0:T(8,128)(2,1)} %collective-permute-done.1.fwd_0_ref, bf16[128,2048]{1,0:T(8,128)(2,1)} %collective-permute-done.2.got_1_ref, ...), custom_call_target="tpu_custom_call" | custom-call | flops 536870912 | bytes 4653056 | tf_op jit(solution)/shard_map/pallas_call | solution.py:151
  40.3 1.7 %collective-permute-start.4 = (bf16[128,768]{1,0:T(8,128)(2,1)S(1)}, bf16[128,768]{1,0:T(8,128)(2,1)S(1)}, u32[]{:S(2)}, u32[]{:S(2)}) collective-permute-start(bf16[128,768]{1,0:T(8,128)(2,1)S(1)} %get-tuple-element.33), channel_id=1, source_target_pairs={{0,2},{2,0},{4,6},{6,4},{1,3},{3,1},{5,7},{7,5},{8,10},{10,8},{12,... | collective-permute-start | bytes 589832 | tf_op jit(solution)/shard_map/ppermute | solution.py:145
  42.4 1.6 %shard_map.116 = bf16[128,768]{1,0:T(8,128)(2,1)S(1)} custom-call(bf16[128,2048]{1,0:T(8,128)(2,1)} %collective-permute-done.7.got_ref, bf16[128,2048]{1,0:T(8,128)(2,1)} %collective-permute-done.8.fwd_ref, bf16[2048,512]{1,0:T(8,128)(2,1)S(1)} %reshape_squeeze.7.weight_ref), custom_call_target="tpu_custom_call" | custom-call | flops 268435456 | bytes 3342336 | tf_op jit(solution)/shard_map/pallas_call | solution.py:151
  44.1 1.7 %collective-permute-start.9 = (bf16[128,768]{1,0:T(8,128)(2,1)S(1)}, bf16[128,768]{1,0:T(8,128)(2,1)S(1)}, u32[]{:S(2)}, u32[]{:S(2)}) collective-permute-start(bf16[128,768]{1,0:T(8,128)(2,1)S(1)} %shard_map.116), channel_id=1, source_target_pairs={{0,2},{2,0},{4,6},{6,4},{1,3},{3,1},{5,7},{7,5},{8,10},{10,8},{12,... | collective-permute-start | bytes 589832 | tf_op jit(solution)/shard_map/ppermute | solution.py:145
  45.8 1.4 %collective-permute-done.4.got_ref = bf16[128,768]{1,0:T(8,128)(2,1)S(1)} collective-permute-done((bf16[128,768]{1,0:T(8,128)(2,1)S(1)}, bf16[128,768]{1,0:T(8,128)(2,1)S(1)}, u32[]{:S(2)}, u32[]{:S(2)}) %collective-permute-start.4) | collective-permute-done | bytes 196640 | tf_op jit(solution)/shard_map/ppermute | solution.py:145
  47.3 4.5 %collective-permute-start.13 = (bf16[128,768]{1,0:T(8,128)(2,1)S(1)}, bf16[128,768]{1,0:T(8,128)(2,1)S(1)}, u32[]{:S(2)}, u32[]{:S(2)}) collective-permute-start(bf16[128,768]{1,0:T(8,128)(2,1)S(1)} %get-tuple-element.36), channel_id=1, source_target_pairs={{0,4},{2,6},{1,5},{3,7},{8,12},{10,14},{9,13},{11,15},{16,20},{18,... | collective-permute-start | bytes 589832 | tf_op jit(solution)/shard_map/ppermute | solution.py:467
  51.9 2.1 %collective-permute-start.17 = (f32[1,128]{1,0:T(1,128)S(1)}, f32[1,128]{1,0:T(1,128)S(1)}, u32[]{:S(2)}, u32[]{:S(2)}) collective-permute-start(f32[1,128]{1,0:T(1,128)S(1)} %get-tuple-element.57), channel_id=1, source_target_pairs={{0,6},{2,4},{4,2},{6,0},{1,7},{3,5},{5,3},{7,1},{8,14},{10,12},{12... | collective-permute-start | bytes 1544 | tf_op jit(solution)/shard_map/ppermute | solution.py:145
  54.9 1.8 %collective-permute-done.16 = f32[1,128]{1,0:T(1,128)S(1)} collective-permute-done((f32[1,128]{1,0:T(1,128)S(1)}, f32[1,128]{1,0:T(1,128)S(1)}, u32[]{:S(2)}, u32[]{:S(2)}) %collective-permute-start.16) | collective-permute-done | bytes 544 | tf_op jit(solution)/shard_map/ppermute | solution.py:145
  57.3 5.7 %collective-permute-start.11 = (bf16[128,768]{1,0:T(8,128)(2,1)S(1)}, bf16[128,768]{1,0:T(8,128)(2,1)S(1)}, u32[]{:S(2)}, u32[]{:S(2)}) collective-permute-start(bf16[128,768]{1,0:T(8,128)(2,1)S(1)} %get-tuple-element.36), channel_id=1, source_target_pairs={{0,2},{4,6},{1,3},{5,7},{8,10},{12,14},{9,11},{13,15},{16,18},{20,... | collective-permute-start | bytes 589832 | tf_op jit(solution)/shard_map/ppermute | solution.py:466
  63.5 3.5 %collective-permute-start.10 = (bf16[128,768]{1,0:T(8,128)(2,1)S(1)}, bf16[128,768]{1,0:T(8,128)(2,1)S(1)}, u32[]{:S(2)}, u32[]{:S(2)}) collective-permute-start(bf16[128,768]{1,0:T(8,128)(2,1)S(1)} %get-tuple-element.35), channel_id=1, source_target_pairs={{0,4},{2,6},{4,0},{6,2},{1,5},{3,7},{5,1},{7,3},{8,12},{10,14},{12... | collective-permute-start | bytes 589832 | tf_op jit(solution)/shard_map/ppermute | solution.py:145
  69.2 6.4 %collective-permute-done.10.own_far_ref = bf16[128,768]{1,0:T(8,128)(2,1)S(1)} collective-permute-done((bf16[128,768]{1,0:T(8,128)(2,1)S(1)}, bf16[128,768]{1,0:T(8,128)(2,1)S(1)}, u32[]{:S(2)}, u32[]{:S(2)}) %collective-permute-start.10) | collective-permute-done | bytes 196640 | tf_op jit(solution)/shard_map/ppermute | solution.py:145
  76.3 5.5 %shard_map.119 = (bf16[128,2048]{1,0:T(8,128)(2,1)}, f32[128,16]{1,0:T(8,128)S(1)}) custom-call(bf16[128,2048]{1,0:T(8,128)(2,1)S(1)} %shard_map.113.query_ref, f32[128,512]{1,0:T(8,128)S(1)} %get-tuple-element.34.own_ref, bf16[128,768]{1,0:T(8,128)(2,1)S(1)} %collective-permute-done.10.own_far_ref, bf16[128,768]{1,0:T(8,128)(2,1)S(1)} %collective-permute-done.11.next_ref, ...), custom_call_target="tpu_custom_call" | custom-call | flops 536870912 | bytes 3022848 | tf_op jit(solution)/shard_map/pallas_call | solution.py:151
  84.4 4.1 %collective-permute-start.20 = (bf16[16,1536]{1,0:T(8,128)(2,1)S(1)}, bf16[16,1536]{1,0:T(8,128)(2,1)S(1)}, u32[]{:S(2)}, u32[]{:S(2)}) collective-permute-start(bf16[16,1536]{1,0:T(8,128)(2,1)S(1)} %get-tuple-element.43), channel_id=1, source_target_pairs={{0,2},{2,0},{4,6},{6,4},{1,3},{3,1},{5,7},{7,5},{8,10},{10,8},{12,... | collective-permute-start | bytes 147464 | tf_op jit(solution)/shard_map/ppermute | solution.py:145
  88.5 4.6 %collective-permute-start.21 = (bf16[16,1536]{1,0:T(8,128)(2,1)S(1)}, bf16[16,1536]{1,0:T(8,128)(2,1)S(1)}, u32[]{:S(2)}, u32[]{:S(2)}) collective-permute-start(bf16[16,1536]{1,0:T(8,128)(2,1)S(1)} %get-tuple-element.44), channel_id=1, source_target_pairs={{0,4},{2,6},{4,0},{6,2},{1,5},{3,7},{5,1},{7,3},{8,12},{10,14},{12... | collective-permute-start | bytes 147464 | tf_op jit(solution)/shard_map/ppermute | solution.py:145
  93.1 3.2 %collective-permute-done.21.got_2_ref = bf16[16,1536]{1,0:T(8,128)(2,1)S(1)} collective-permute-done((bf16[16,1536]{1,0:T(8,128)(2,1)S(1)}, bf16[16,1536]{1,0:T(8,128)(2,1)S(1)}, u32[]{:S(2)}, u32[]{:S(2)}) %collective-permute-start.21) | collective-permute-done | bytes 49184 | tf_op jit(solution)/shard_map/ppermute | solution.py:145
  96.3 2.7 %collective-permute-done.22.got_3_ref = bf16[16,1536]{1,0:T(8,128)(2,1)S(1)} collective-permute-done((bf16[16,1536]{1,0:T(8,128)(2,1)S(1)}, bf16[16,1536]{1,0:T(8,128)(2,1)S(1)}, u32[]{:S(2)}, u32[]{:S(2)}) %collective-permute-start.22) | collective-permute-done | bytes 49184 | tf_op jit(solution)/shard_map/ppermute | solution.py:145
  99.1 1.6 %collective-permute-start.23 = (f32[8,128]{1,0:T(8,128)S(1)}, f32[8,128]{1,0:T(8,128)S(1)}, u32[]{:S(2)}, u32[]{:S(2)}) collective-permute-start(f32[8,128]{1,0:T(8,128)S(1)} %get-tuple-element.46), channel_id=1, source_target_pairs={{0,8},{8,0},{16,24},{24,16},{1,9},{9,1},{17,25},{25,17},{2,10},{10... | collective-permute-start | bytes 12296 | tf_op jit(solution)/shard_map/ppermute | solution.py:145
  100.7 1.5 %collective-permute-start.24 = (f32[8,128]{1,0:T(8,128)S(1)}, f32[8,128]{1,0:T(8,128)S(1)}, u32[]{:S(2)}, u32[]{:S(2)}) collective-permute-start(f32[8,128]{1,0:T(8,128)S(1)} %get-tuple-element.46), channel_id=1, source_target_pairs={{0,16},{8,24},{16,0},{24,8},{1,17},{9,25},{17,1},{25,9},{2,18},{10... | collective-permute-start | bytes 12296 | tf_op jit(solution)/shard_map/ppermute | solution.py:145
  102.8 1.5 %collective-permute-done.24 = f32[8,128]{1,0:T(8,128)S(1)} collective-permute-done((f32[8,128]{1,0:T(8,128)S(1)}, f32[8,128]{1,0:T(8,128)S(1)}, u32[]{:S(2)}, u32[]{:S(2)}) %collective-permute-start.24) | collective-permute-done | bytes 4128 | tf_op jit(solution)/shard_map/ppermute | solution.py:145
  104.3 2.4 %collective-permute-done.25 = f32[8,128]{1,0:T(8,128)S(1)} collective-permute-done((f32[8,128]{1,0:T(8,128)S(1)}, f32[8,128]{1,0:T(8,128)S(1)}, u32[]{:S(2)}, u32[]{:S(2)}) %collective-permute-start.25) | collective-permute-done | bytes 4128 | tf_op jit(solution)/shard_map/ppermute | solution.py:145
  106.7 1.5 %collective-permute-start.27 = (f32[8,128]{1,0:T(8,128)S(1)}, f32[8,128]{1,0:T(8,128)S(1)}, u32[]{:S(2)}, u32[]{:S(2)}) collective-permute-start(f32[8,128]{1,0:T(8,128)S(1)} %add_add_fusion.1), channel_id=1, source_target_pairs={{0,4},{2,6},{4,0},{6,2},{1,5},{3,7},{5,1},{7,3},{8,12},{10,14},{12... | collective-permute-start | bytes 12296 | tf_op jit(solution)/shard_map/ppermute | solution.py:145
  108.3 2.9 %collective-permute-start.28 = (f32[8,128]{1,0:T(8,128)S(1)}, f32[8,128]{1,0:T(8,128)S(1)}, u32[]{:S(2)}, u32[]{:S(2)}) collective-permute-start(f32[8,128]{1,0:T(8,128)S(1)} %add_add_fusion.1), channel_id=1, source_target_pairs={{0,6},{2,4},{4,2},{6,0},{1,7},{3,5},{5,3},{7,1},{8,14},{10,12},{12... | collective-permute-start | bytes 12296 | tf_op jit(solution)/shard_map/ppermute | solution.py:145
  111.1 1.5 %collective-permute-start.31 = (bf16[16,1536]{1,0:T(8,128)(2,1)S(1)}, bf16[16,1536]{1,0:T(8,128)(2,1)S(1)}, u32[]{:S(2)}, u32[]{:S(2)}) collective-permute-start(bf16[16,1536]{1,0:T(8,128)(2,1)S(1)} %get-tuple-element.47.own_ref), channel_id=1, source_target_pairs={{0,4},{2,6},{4,0},{6,2},{1,5},{3,7},{5,1},{7,3},{8,12},{10,14},{12... | collective-permute-start | bytes 147464 | tf_op jit(solution)/shard_map/ppermute | solution.py:145
  112.7 2.9 %collective-permute-start.32 = (bf16[16,1536]{1,0:T(8,128)(2,1)S(1)}, bf16[16,1536]{1,0:T(8,128)(2,1)S(1)}, u32[]{:S(2)}, u32[]{:S(2)}) collective-permute-start(bf16[16,1536]{1,0:T(8,128)(2,1)S(1)} %get-tuple-element.47.own_ref), channel_id=1, source_target_pairs={{0,6},{2,4},{4,2},{6,0},{1,7},{3,5},{5,3},{7,1},{8,14},{10,12},{12... | collective-permute-start | bytes 147464 | tf_op jit(solution)/shard_map/ppermute | solution.py:145
  115.6 1.4 %shard_map.120 = bf16[128,4096]{1,0:T(8,128)(2,1)} custom-call(f32[128,16]{1,0:T(8,128)S(1)} %get-tuple-element.40.low_ref, f32[128,16]{1,0:T(8,128)S(1)} %collective-permute-done.18.low_other_ref, bf16[16,4096]{1,0:T(8,128)(2,1)S(1)} %bitcast.30), custom_call_target="tpu_custom_call" | custom-call | flops 16777216 | bytes 1196032 | tf_op jit(solution)/shard_map/pallas_call | solution.py:151
  117.0 1.5 %collective-permute-done.32.got_3 = bf16[16,1536]{1,0:T(8,128)(2,1)S(1)} collective-permute-done((bf16[16,1536]{1,0:T(8,128)(2,1)S(1)}, bf16[16,1536]{1,0:T(8,128)(2,1)S(1)}, u32[]{:S(2)}, u32[]{:S(2)}) %collective-permute-start.32) | collective-permute-done | bytes 49184 | tf_op jit(solution)/shard_map/ppermute | solution.py:145
  (79 shorter events, 20.9 us)
Async XLA Ops:
  2.1 1.4 %collective-permute-start = (f32[128,128]{1,0:T(8,128)S(1)}, f32[128,128]{1,0:T(8,128)S(1)}, u32[]{:S(2)}, u32[]{:S(2)}) collective-permute-start(f32[128,128]{1,0:T(8,128)S(1)} %shard_map.111.mine_ref), channel_id=1, source_target_pairs={{0,1},{1,0},{2,3},{3,2},{4,5},{5,4},{6,7},{7,6},{8,9},{9,8},{10,11... | collective-permute-start | bytes 196616 | tf_op jit(solution)/shard_map/ppermute | solution.py:145
  5.3 13.8 %collective-permute-start.2 = (bf16[128,2048]{1,0:T(8,128)(2,1)S(1)}, bf16[128,2048]{1,0:T(8,128)(2,1)}, u32[]{:S(2)}, u32[]{:S(2)}) collective-permute-start(bf16[128,2048]{1,0:T(8,128)(2,1)S(1)} %get-tuple-element.28), channel_id=1, source_target_pairs={{0,3},{2,1},{5,6},{7,4},{8,11},{10,9},{13,14},{15,12},{16,19},{18,... | collective-permute-start | bytes 1572872 | tf_op jit(solution)/shard_map/ppermute | solution.py:412
  10.7 9.7 %collective-permute-start.7 = (bf16[128,2048]{1,0:T(8,128)(2,1)S(1)}, bf16[128,2048]{1,0:T(8,128)(2,1)}, u32[]{:S(2)}, u32[]{:S(2)}) collective-permute-start(bf16[128,2048]{1,0:T(8,128)(2,1)S(1)} %get-tuple-element.28), channel_id=1, source_target_pairs={{1,6},{3,4},{4,3},{6,1},{9,14},{11,12},{12,11},{14,9},{17,22},{19,... | collective-permute-start | bytes 1572872 | tf_op jit(solution)/shard_map/ppermute | solution.py:413
  12.2 25.8 %collective-permute-start.1 = (bf16[128,2048]{1,0:T(8,128)(2,1)}, bf16[128,2048]{1,0:T(8,128)(2,1)}, u32[]{:S(2)}, u32[]{:S(2)}) collective-permute-start(bf16[128,2048]{1,0:T(8,128)(2,1)} %get-tuple-element.30.even_ref), channel_id=1, source_target_pairs={{0,1},{2,3},{5,4},{7,6},{8,9},{10,11},{13,12},{15,14},{16,17},{18,... | collective-permute-start | bytes 1572872 | tf_op jit(solution)/shard_map/ppermute | solution.py:415
  16.3 20.3 %collective-permute-start.5 = (bf16[128,2048]{1,0:T(8,128)(2,1)}, bf16[128,2048]{1,0:T(8,128)(2,1)S(1)}, u32[]{:S(2)}, u32[]{:S(2)}) collective-permute-start(bf16[128,2048]{1,0:T(8,128)(2,1)} %get-tuple-element.30.even_ref), channel_id=1, source_target_pairs={{1,5},{3,7},{4,0},{6,2},{9,13},{11,15},{12,8},{14,10},{17,21},{19,... | collective-permute-start | bytes 1572872 | tf_op jit(solution)/shard_map/ppermute | solution.py:414
  19.2 18.8 %collective-permute-start.3 = (bf16[128,2048]{1,0:T(8,128)(2,1)}, bf16[128,2048]{1,0:T(8,128)(2,1)}, u32[]{:S(2)}, u32[]{:S(2)}) collective-permute-start(bf16[128,2048]{1,0:T(8,128)(2,1)} %collective-permute-done.2.got_1_ref), channel_id=1, source_target_pairs={{1,0},{3,2},{4,5},{6,7},{9,8},{11,10},{12,13},{14,15},{17,16},{19,... | collective-permute-start | bytes 1572872 | tf_op jit(solution)/shard_map/ppermute | solution.py:451
  20.5 22.0 %collective-permute-start.8 = (bf16[128,2048]{1,0:T(8,128)(2,1)}, bf16[128,2048]{1,0:T(8,128)(2,1)}, u32[]{:S(2)}, u32[]{:S(2)}) collective-permute-start(bf16[128,2048]{1,0:T(8,128)(2,1)} %collective-permute-done.7.got_ref), channel_id=1, source_target_pairs={{1,0},{3,2},{4,5},{6,7},{9,8},{11,10},{12,13},{14,15},{17,16},{19,... | collective-permute-start | bytes 1572872 | tf_op jit(solution)/shard_map/ppermute | solution.py:468
  36.7 26.3 %collective-permute-start.6 = (bf16[128,2048]{1,0:T(8,128)(2,1)S(1)}, bf16[128,2048]{1,0:T(8,128)(2,1)S(1)}, u32[]{:S(2)}, u32[]{:S(2)}) collective-permute-start(bf16[128,2048]{1,0:T(8,128)(2,1)S(1)} %collective-permute-done.5.got_ref), channel_id=1, source_target_pairs={{0,1},{2,3},{5,4},{7,6},{8,9},{10,11},{13,12},{15,14},{16,17},{18,... | collective-permute-start | bytes 1572872 | tf_op jit(solution)/shard_map/ppermute | solution.py:473
  40.3 7.0 %collective-permute-start.4 = (bf16[128,768]{1,0:T(8,128)(2,1)S(1)}, bf16[128,768]{1,0:T(8,128)(2,1)S(1)}, u32[]{:S(2)}, u32[]{:S(2)}) collective-permute-start(bf16[128,768]{1,0:T(8,128)(2,1)S(1)} %get-tuple-element.33), channel_id=1, source_target_pairs={{0,2},{2,0},{4,6},{6,4},{1,3},{3,1},{5,7},{7,5},{8,10},{10,8},{12,... | collective-permute-start | bytes 589832 | tf_op jit(solution)/shard_map/ppermute | solution.py:145
  42.0 9.9 %collective-permute-start.15 = (f32[1,128]{1,0:T(1,128)S(1)}, f32[1,128]{1,0:T(1,128)S(1)}, u32[]{:S(2)}, u32[]{:S(2)}) collective-permute-start(f32[1,128]{1,0:T(1,128)S(1)} %get-tuple-element.57), channel_id=1, source_target_pairs={{0,2},{2,0},{4,6},{6,4},{1,3},{3,1},{5,7},{7,5},{8,10},{10,8},{12,... | collective-permute-start | bytes 1544 | tf_op jit(solution)/shard_map/ppermute | solution.py:145
  44.1 18.9 %collective-permute-start.9 = (bf16[128,768]{1,0:T(8,128)(2,1)S(1)}, bf16[128,768]{1,0:T(8,128)(2,1)S(1)}, u32[]{:S(2)}, u32[]{:S(2)}) collective-permute-start(bf16[128,768]{1,0:T(8,128)(2,1)S(1)} %shard_map.116), channel_id=1, source_target_pairs={{0,2},{2,0},{4,6},{6,4},{1,3},{3,1},{5,7},{7,5},{8,10},{10,8},{12,... | collective-permute-start | bytes 589832 | tf_op jit(solution)/shard_map/ppermute | solution.py:145
  47.3 21.0 %collective-permute-start.13 = (bf16[128,768]{1,0:T(8,128)(2,1)S(1)}, bf16[128,768]{1,0:T(8,128)(2,1)S(1)}, u32[]{:S(2)}, u32[]{:S(2)}) collective-permute-start(bf16[128,768]{1,0:T(8,128)(2,1)S(1)} %get-tuple-element.36), channel_id=1, source_target_pairs={{0,4},{2,6},{1,5},{3,7},{8,12},{10,14},{9,13},{11,15},{16,20},{18,... | collective-permute-start | bytes 589832 | tf_op jit(solution)/shard_map/ppermute | solution.py:467
  51.8 4.9 %collective-permute-start.16 = (f32[1,128]{1,0:T(1,128)S(1)}, f32[1,128]{1,0:T(1,128)S(1)}, u32[]{:S(2)}, u32[]{:S(2)}) collective-permute-start(f32[1,128]{1,0:T(1,128)S(1)} %get-tuple-element.57), channel_id=1, source_target_pairs={{0,4},{2,6},{4,0},{6,2},{1,5},{3,7},{5,1},{7,3},{8,12},{10,14},{12... | collective-permute-start | bytes 1544 | tf_op jit(solution)/shard_map/ppermute | solution.py:145
  51.9 5.4 %collective-permute-start.17 = (f32[1,128]{1,0:T(1,128)S(1)}, f32[1,128]{1,0:T(1,128)S(1)}, u32[]{:S(2)}, u32[]{:S(2)}) collective-permute-start(f32[1,128]{1,0:T(1,128)S(1)} %get-tuple-element.57), channel_id=1, source_target_pairs={{0,6},{2,4},{4,2},{6,0},{1,7},{3,5},{5,3},{7,1},{8,14},{10,12},{12... | collective-permute-start | bytes 1544 | tf_op jit(solution)/shard_map/ppermute | solution.py:145
  56.6 25.2 %collective-permute-start.19 = (f32[128,16]{1,0:T(8,128)S(1)}, f32[128,16]{1,0:T(8,128)S(1)}, u32[]{:S(2)}, u32[]{:S(2)}) collective-permute-start(f32[128,16]{1,0:T(8,128)S(1)} %shard_map.121.back_ref), channel_id=1, source_target_pairs={{0,1},{1,0},{2,3},{3,2},{4,5},{5,4},{6,7},{7,6},{8,9},{9,8},{10,11... | collective-permute-start | bytes 24584 | tf_op jit(solution)/shard_map/ppermute | solution.py:145
  57.3 11.9 %collective-permute-start.11 = (bf16[128,768]{1,0:T(8,128)(2,1)S(1)}, bf16[128,768]{1,0:T(8,128)(2,1)S(1)}, u32[]{:S(2)}, u32[]{:S(2)}) collective-permute-start(bf16[128,768]{1,0:T(8,128)(2,1)S(1)} %get-tuple-element.36), channel_id=1, source_target_pairs={{0,2},{4,6},{1,3},{5,7},{8,10},{12,14},{9,11},{13,15},{16,18},{20,... | collective-permute-start | bytes 589832 | tf_op jit(solution)/shard_map/ppermute | solution.py:466
  63.5 12.1 %collective-permute-start.10 = (bf16[128,768]{1,0:T(8,128)(2,1)S(1)}, bf16[128,768]{1,0:T(8,128)(2,1)S(1)}, u32[]{:S(2)}, u32[]{:S(2)}) collective-permute-start(bf16[128,768]{1,0:T(8,128)(2,1)S(1)} %get-tuple-element.35), channel_id=1, source_target_pairs={{0,4},{2,6},{4,0},{6,2},{1,5},{3,7},{5,1},{7,3},{8,12},{10,14},{12... | collective-permute-start | bytes 589832 | tf_op jit(solution)/shard_map/ppermute | solution.py:145
  67.0 9.4 %collective-permute-start.12 = (bf16[128,768]{1,0:T(8,128)(2,1)S(1)}, bf16[128,768]{1,0:T(8,128)(2,1)S(1)}, u32[]{:S(2)}, u32[]{:S(2)}) collective-permute-start(bf16[128,768]{1,0:T(8,128)(2,1)S(1)} %get-tuple-element.35), channel_id=1, source_target_pairs={{0,6},{4,2},{1,7},{5,3},{8,14},{12,10},{9,15},{13,11},{16,22},{20,... | collective-permute-start | bytes 589832 | tf_op jit(solution)/shard_map/ppermute | solution.py:484
  68.4 8.0 %collective-permute-start.14 = (bf16[128,512]{1,0:T(8,128)(2,1)S(1)}, bf16[128,512]{1,0:T(8,128)(2,1)S(1)}, u32[]{:S(2)}, u32[]{:S(2)}) collective-permute-start(bf16[128,512]{1,0:T(8,128)(2,1)S(1)} %shard_map.118.block_2_ref), channel_id=1, source_target_pairs={{4,6},{6,4},{5,7},{7,5},{12,14},{14,12},{13,15},{15,13},{20,22},{2... | collective-permute-start | bytes 393224 | tf_op jit(solution)/shard_map/ppermute | solution.py:488
  84.4 8.6 %collective-permute-start.20 = (bf16[16,1536]{1,0:T(8,128)(2,1)S(1)}, bf16[16,1536]{1,0:T(8,128)(2,1)S(1)}, u32[]{:S(2)}, u32[]{:S(2)}) collective-permute-start(bf16[16,1536]{1,0:T(8,128)(2,1)S(1)} %get-tuple-element.43), channel_id=1, source_target_pairs={{0,2},{2,0},{4,6},{6,4},{1,3},{3,1},{5,7},{7,5},{8,10},{10,8},{12,... | collective-permute-start | bytes 147464 | tf_op jit(solution)/shard_map/ppermute | solution.py:145
  88.5 7.8 %collective-permute-start.21 = (bf16[16,1536]{1,0:T(8,128)(2,1)S(1)}, bf16[16,1536]{1,0:T(8,128)(2,1)S(1)}, u32[]{:S(2)}, u32[]{:S(2)}) collective-permute-start(bf16[16,1536]{1,0:T(8,128)(2,1)S(1)} %get-tuple-element.44), channel_id=1, source_target_pairs={{0,4},{2,6},{4,0},{6,2},{1,5},{3,7},{5,1},{7,3},{8,12},{10,14},{12... | collective-permute-start | bytes 147464 | tf_op jit(solution)/shard_map/ppermute | solution.py:145
  93.1 5.9 %collective-permute-start.22 = (bf16[16,1536]{1,0:T(8,128)(2,1)S(1)}, bf16[16,1536]{1,0:T(8,128)(2,1)S(1)}, u32[]{:S(2)}, u32[]{:S(2)}) collective-permute-start(bf16[16,1536]{1,0:T(8,128)(2,1)S(1)} %get-tuple-element.45), channel_id=1, source_target_pairs={{0,6},{2,4},{4,2},{6,0},{1,7},{3,5},{5,3},{7,1},{8,14},{10,12},{12... | collective-permute-start | bytes 147464 | tf_op jit(solution)/shard_map/ppermute | solution.py:145
  99.1 3.7 %collective-permute-start.23 = (f32[8,128]{1,0:T(8,128)S(1)}, f32[8,128]{1,0:T(8,128)S(1)}, u32[]{:S(2)}, u32[]{:S(2)}) collective-permute-start(f32[8,128]{1,0:T(8,128)S(1)} %get-tuple-element.46), channel_id=1, source_target_pairs={{0,8},{8,0},{16,24},{24,16},{1,9},{9,1},{17,25},{25,17},{2,10},{10... | collective-permute-start | bytes 12296 | tf_op jit(solution)/shard_map/ppermute | solution.py:145
  100.7 3.6 %collective-permute-start.24 = (f32[8,128]{1,0:T(8,128)S(1)}, f32[8,128]{1,0:T(8,128)S(1)}, u32[]{:S(2)}, u32[]{:S(2)}) collective-permute-start(f32[8,128]{1,0:T(8,128)S(1)} %get-tuple-element.46), channel_id=1, source_target_pairs={{0,16},{8,24},{16,0},{24,8},{1,17},{9,25},{17,1},{25,9},{2,18},{10... | collective-permute-start | bytes 12296 | tf_op jit(solution)/shard_map/ppermute | solution.py:145
  102.2 4.5 %collective-permute-start.25 = (f32[8,128]{1,0:T(8,128)S(1)}, f32[8,128]{1,0:T(8,128)S(1)}, u32[]{:S(2)}, u32[]{:S(2)}) collective-permute-start(f32[8,128]{1,0:T(8,128)S(1)} %get-tuple-element.46), channel_id=1, source_target_pairs={{0,24},{8,16},{16,8},{24,0},{1,25},{9,17},{17,9},{25,1},{2,26},{10... | collective-permute-start | bytes 12296 | tf_op jit(solution)/shard_map/ppermute | solution.py:145
  106.7 5.9 %collective-permute-start.26 = (f32[8,128]{1,0:T(8,128)S(1)}, f32[8,128]{1,0:T(8,128)S(1)}, u32[]{:S(2)}, u32[]{:S(2)}) collective-permute-start(f32[8,128]{1,0:T(8,128)S(1)} %add_add_fusion.1), channel_id=1, source_target_pairs={{0,2},{2,0},{4,6},{6,4},{1,3},{3,1},{5,7},{7,5},{8,10},{10,8},{12,... | collective-permute-start | bytes 12296 | tf_op jit(solution)/shard_map/ppermute | solution.py:145
  106.7 8.8 %collective-permute-start.27 = (f32[8,128]{1,0:T(8,128)S(1)}, f32[8,128]{1,0:T(8,128)S(1)}, u32[]{:S(2)}, u32[]{:S(2)}) collective-permute-start(f32[8,128]{1,0:T(8,128)S(1)} %add_add_fusion.1), channel_id=1, source_target_pairs={{0,4},{2,6},{4,0},{6,2},{1,5},{3,7},{5,1},{7,3},{8,12},{10,14},{12... | collective-permute-start | bytes 12296 | tf_op jit(solution)/shard_map/ppermute | solution.py:145
  108.3 7.3 %collective-permute-start.28 = (f32[8,128]{1,0:T(8,128)S(1)}, f32[8,128]{1,0:T(8,128)S(1)}, u32[]{:S(2)}, u32[]{:S(2)}) collective-permute-start(f32[8,128]{1,0:T(8,128)S(1)} %add_add_fusion.1), channel_id=1, source_target_pairs={{0,6},{2,4},{4,2},{6,0},{1,7},{3,5},{5,3},{7,1},{8,14},{10,12},{12... | collective-permute-start | bytes 12296 | tf_op jit(solution)/shard_map/ppermute | solution.py:145
  111.1 5.9 %collective-permute-start.30 = (bf16[16,1536]{1,0:T(8,128)(2,1)S(1)}, bf16[16,1536]{1,0:T(8,128)(2,1)S(1)}, u32[]{:S(2)}, u32[]{:S(2)}) collective-permute-start(bf16[16,1536]{1,0:T(8,128)(2,1)S(1)} %get-tuple-element.47.own_ref), channel_id=1, source_target_pairs={{0,2},{2,0},{4,6},{6,4},{1,3},{3,1},{5,7},{7,5},{8,10},{10,8},{12,... | collective-permute-start | bytes 147464 | tf_op jit(solution)/shard_map/ppermute | solution.py:145
  111.1 5.9 %collective-permute-start.31 = (bf16[16,1536]{1,0:T(8,128)(2,1)S(1)}, bf16[16,1536]{1,0:T(8,128)(2,1)S(1)}, u32[]{:S(2)}, u32[]{:S(2)}) collective-permute-start(bf16[16,1536]{1,0:T(8,128)(2,1)S(1)} %get-tuple-element.47.own_ref), channel_id=1, source_target_pairs={{0,4},{2,6},{4,0},{6,2},{1,5},{3,7},{5,1},{7,3},{8,12},{10,14},{12... | collective-permute-start | bytes 147464 | tf_op jit(solution)/shard_map/ppermute | solution.py:145
  112.7 5.9 %collective-permute-start.32 = (bf16[16,1536]{1,0:T(8,128)(2,1)S(1)}, bf16[16,1536]{1,0:T(8,128)(2,1)S(1)}, u32[]{:S(2)}, u32[]{:S(2)}) collective-permute-start(bf16[16,1536]{1,0:T(8,128)(2,1)S(1)} %get-tuple-element.47.own_ref), channel_id=1, source_target_pairs={{0,6},{2,4},{4,2},{6,0},{1,7},{3,5},{5,3},{7,1},{8,14},{10,12},{12... | collective-permute-start | bytes 147464 | tf_op jit(solution)/shard_map/ppermute | solution.py:145
  115.5 1.5 %collective-permute-start.29 = (f32[8,128]{1,0:T(8,128)S(1)}, f32[8,128]{1,0:T(8,128)S(1)}, u32[]{:S(2)}, u32[]{:S(2)}) collective-permute-start(f32[8,128]{1,0:T(8,128)S(1)} %add_add_fusion.square_ref), channel_id=1, source_target_pairs={{0,1},{1,0},{2,3},{3,2},{4,5},{5,4},{6,7},{7,6},{8,9},{9,8},{10,11... | collective-permute-start | bytes 12296 | tf_op jit(solution)/shard_map/ppermute | solution.py:145
  (9 other events, 79.5 us)

commit v3 on v0

--- a/solution.py
+++ b/solution.py
@@ -1,8 +1,11 @@
+import functools
 import math
 
 import jax
 import jax.numpy as jnp
 from jax import lax
+from jax.experimental import pallas as pl
+from jax.experimental.pallas import tpu as pltpu
 from jax.sharding import PartitionSpec as P
 
 
@@ -23,7 +26,7 @@
     )
 
 
-def per_device(hidden, gain, queries, key_value_weight, adapt_down, adapt_up, out_grad, doc_ids):
+def gathered_weights(hidden, gain, queries, key_value_weight, adapt_down, adapt_up, out_grad, doc_ids):
     tp_count = lax.axis_size("tp")
     row_count = hidden.shape[1]
     local_width = hidden.shape[2]
@@ -130,6 +133,466 @@
     grad_up = up_total * factor
     grad_down = down_total * factor
     return (attended[None], adapter_rows[None], grad_down[None], grad_up[None])
+
+
+F32, BF16 = jnp.float32, jnp.bfloat16
+VMEM = pl.BlockSpec(memory_space=pltpu.VMEM)
+LIMIT = 20 * 1024 * 1024
+
+
+def swap(value, axis, distance):
+    count = lax.axis_size(axis)
+    return lax.ppermute(value, axis, [(i, i ^ distance) for i in range(count)])
+
+
+def call(kernel, outs, *operands, flops=0, scratch=()):
+    shapes = [jax.ShapeDtypeStruct(shape, dtype) for shape, dtype in outs]
+    moved = sum(math.prod(x.shape) * x.dtype.itemsize for x in (*operands, *shapes))
+    return pl.pallas_call(
+        kernel,
+        out_shape=shapes,
+        in_specs=[VMEM] * len(operands),
+        out_specs=[VMEM] * len(shapes),
+        scratch_shapes=scratch,
+        compiler_params=pltpu.CompilerParams(vmem_limit_bytes=LIMIT),
+        cost_estimate=pl.CostEstimate(flops=flops, bytes_accessed=moved, transcendentals=0),
+    )(*operands)
+
+
+def times(left, right):
+    return lax.dot_general(left, right, (((1,), (0,)), ((), ())), preferred_element_type=F32)
+
+
+def times_transposed(left, right):
+    return lax.dot_general(left, right, (((1,), (1,)), ((), ())), preferred_element_type=F32)
+
+
+def transposed_times(left, right):
+    return lax.dot_general(left, right, (((0,), (0,)), ((), ())), preferred_element_type=F32)
+
+
+def norm_kernel(mine_ref, other_ref, gain_ref, gain_other_ref, *outs):
+    width = outs[0].shape[1]
+    place, core = lax.axis_index("ctx"), lax.axis_index("tp")
+    mine, other = mine_ref[...].astype(F32), other_ref[...].astype(F32)
+    squares = [jnp.sum(rows * rows, axis=1, keepdims=True) for rows in (mine, other)]
+    scale = lax.rsqrt((squares[0] + squares[1]) / (4 * width) + 1e-06)
+    for d, out_ref in enumerate(outs):
+        chip = place ^ d
+        columns = pl.ds(pl.multiple_of(chip % 2 * width, width), width)
+
+        def write(rows_ref, weights_ref, out_ref=out_ref, columns=columns):
+            rows = rows_ref[:, columns].astype(F32) * scale
+            out_ref[...] = (rows * weights_ref[:, columns].astype(F32)).astype(BF16)
+
+        pl.when(chip // 2 == core)(functools.partial(write, mine_ref, gain_ref))
+        pl.when(chip // 2 != core)(functools.partial(write, other_ref, gain_other_ref))
+
+
+def join_rows(mine_ref, other_ref, out_ref):
+    count = mine_ref.shape[0]
+    core = lax.axis_index("tp")
+    out_ref[pl.ds(pl.multiple_of(core * count, count), count)] = mine_ref[...]
+    out_ref[pl.ds(pl.multiple_of((1 - core) * count, count), count)] = other_ref[...]
+
+
+def split_heads(value, head):
+    count = value.shape[1] // (2 * head)
+    pieces = [value[:, i * head : (i + 1) * head] for i in range(2 * count)]
+    return jnp.concatenate(pieces[0::2], axis=1), jnp.concatenate(pieces[1::2], axis=1)
+
+
+def pack(value, out_ref, head):
+    keys, values = split_heads(value, head)
+    store_packed(keys, values, out_ref)
+
+
+def store_packed(keys, values, out_ref):
+    rows, width = keys.shape
+    high = keys.astype(BF16)
+    out_ref[:rows, :width] = high
+    out_ref[:rows, width : 2 * width] = (keys - high.astype(F32)).astype(BF16)
+    out_ref[:rows, 2 * width :] = values.astype(BF16)
+
+
+def unpack(ref, rows):
+    width = ref.shape[1] // 3
+    keys = ref[:rows, :width].astype(F32) + ref[:rows, width : 2 * width].astype(F32)
+    return keys, ref[:rows, 2 * width :].astype(F32)
+
+
+def store_docs(docs, out_ref):
+    rows = docs.shape[1]
+    out_ref[rows:, :rows] = jnp.broadcast_to(docs, (16, rows)).astype(BF16)
+
+
+def load_docs(ref):
+    return ref[-16:, : ref.shape[0] - 16].astype(F32)[:1]
+
+
+def parts_kernel(
+    head,
+    got_1_ref,
+    got_1_other_ref,
+    got_3_ref,
+    got_3_other_ref,
+    even_ref,
+    even_other_ref,
+    weight_ref,
+    sent_1_ref,
+    sent_3_ref,
+    own_ref,
+    rows_ref,
+):
+    count = sent_1_ref.shape[0]
+    pairs = ((got_1_ref, got_1_other_ref), (got_3_ref, got_3_other_ref), (even_ref, even_other_ref))
+    for index, (mine_ref, other_ref) in enumerate(pairs):
+        join_rows(mine_ref, other_ref, rows_ref.at[index * count : (index + 1) * count])
+    product = times(rows_ref[...], weight_ref[...])
+    pack(product[:count], sent_1_ref, head)
+    pack(product[count : 2 * count], sent_3_ref, head)
+    own_ref[...] = jnp.concatenate(split_heads(product[2 * count :], head), axis=1)
+
+
+def far_kernel(head, got_ref, got_other_ref, weight_ref, sent_ref, rows_ref):
+    join_rows(got_ref, got_other_ref, rows_ref)
+    pack(times(rows_ref[...], weight_ref[...]), sent_ref, head)
+
+
+def turn(value, cosine, sine):
+    head = cosine.shape[1]
+    pieces = []
+    for i in range(value.shape[1] // head):
+        piece = value[:, i * head : (i + 1) * head]
+        pieces.append(piece * cosine + pltpu.roll(piece, head // 2, 1) * sine)
+    return jnp.concatenate(pieces, axis=1)
+
+
+def query_kernel(query_ref, cosine_ref, sine_ref, out_ref):
+    rows, head = cosine_ref.shape
+    for index in range(query_ref.shape[1] // head):
+        piece = query_ref[:, index * head : (index + 1) * head].astype(F32)
+        out_ref[index * rows : (index + 1) * rows] = turn(
+            piece, cosine_ref[...], sine_ref[...]
+        ).astype(BF16)
+
+
+def finish_kernel(own_ref, got_1_ref, got_2_ref, got_3_ref, docs_ref, cosine_ref, sine_ref, out_ref):
+    rows = own_ref.shape[0]
+    width = own_ref.shape[1] // 2
+    keys, values = own_ref[:, :width], own_ref[:, width:]
+    for ref in (got_1_ref, got_2_ref, got_3_ref):
+        more_keys, more_values = unpack(ref, rows)
+        keys, values = keys + more_keys, values + more_values
+    out_ref[:rows, :width] = turn(keys, cosine_ref[...], sine_ref[...]).astype(BF16)
+    out_ref[:rows, width:] = values.astype(BF16)
+    store_docs(docs_ref[...], out_ref)
+
+
+def allowed_pairs(own_docs, key_docs, distance):
+    rows = own_docs.shape[1]
+    place = lax.axis_index("ctx")
+    query_docs = jnp.broadcast_to(own_docs, (rows, rows)).T
+    query_at = place * rows + lax.broadcasted_iota(jnp.int32, (rows, rows), 0)
+    key_at = (place ^ distance) * rows + lax.broadcasted_iota(jnp.int32, (rows, rows), 1)
+    return (key_at <= query_at) & (key_docs == query_docs)
+
+
+def group_scores(query_ref, keys, allowed, head, group):
+    rows = allowed.shape[0]
+    groups = keys.shape[1] // head
+    count = query_ref.shape[0] // groups
+    scores = times_transposed(
+        query_ref[group * count : (group + 1) * count], keys[:, group * head : (group + 1) * head]
+    ) * head ** (-0.5)
+    scores = scores.reshape(count // rows, rows, scores.shape[1])
+    return jnp.where(allowed[None], scores, -1e30).reshape(count, scores.shape[2])
+
+
+def first_attention_kernel(
+    head, query_ref, block_0_ref, block_1_ref, block_2_ref, mixed_ref, state_ref
+):
+    rows = block_0_ref.shape[0] - 16
+    width = block_0_ref.shape[1] // 2
+    blocks = (block_0_ref, block_1_ref, block_2_ref)
+    keys = jnp.concatenate([ref[:rows, :width] for ref in blocks], axis=0)
+    values = jnp.concatenate([ref[:rows, width:] for ref in blocks], axis=0)
+    allowed = jnp.concatenate(
+        [allowed_pairs(load_docs(block_0_ref), load_docs(ref), d) for d, ref in enumerate(blocks)],
+        axis=1,
+    )
+    groups = width // head
+    count = query_ref.shape[0] // groups
+    for group in range(groups):
+        scores = group_scores(query_ref, keys, allowed, head, group)
+        top = jnp.max(scores, axis=1, keepdims=True)
+        weights = jnp.exp(scores - top)
+        total = jnp.sum(weights, axis=1, keepdims=True)
+        place = slice(group * count, (group + 1) * count)
+        left = lax.broadcasted_iota(jnp.int32, (count, state_ref.shape[1]), 1) < 64
+        state_ref[place] = jnp.where(left, top, total)
+        mixed_ref[place] = times(
+            weights.astype(BF16), values[:, group * head : (group + 1) * head]
+        )
+
+
+def last_attention_kernel(
+    head,
+    query_ref,
+    block_0_ref,
+    block_3_ref,
+    mixed_ref,
+    state_ref,
+    down_ref,
+    back_ref,
+    back_other_ref,
+    out_ref,
+    low_ref,
+    grad_ref,
+):
+    rows = block_3_ref.shape[0] - 16
+    width = block_3_ref.shape[1] // 2
+    allowed = allowed_pairs(load_docs(block_0_ref), load_docs(block_3_ref), 3)
+    keys, values = block_3_ref[:rows, :width], block_3_ref[:rows, width:]
+    groups = width // head
+    count = query_ref.shape[0] // groups
+    for group in range(groups):
+        scores = group_scores(query_ref, keys, allowed, head, group)
+        place = slice(group * count, (group + 1) * count)
+        before = state_ref[place, :1]
+        top = jnp.maximum(before, jnp.max(scores, axis=1, keepdims=True))
+        weights = jnp.exp(scores - top)
+        shrink = jnp.exp(before - top)
+        total = state_ref[place, 64:65] * shrink + jnp.sum(weights, axis=1, keepdims=True)
+        mixed = mixed_ref[place] * shrink + times(
+            weights.astype(BF16), values[:, group * head : (group + 1) * head]
+        )
+        mixed = (mixed / total).astype(BF16)
+        for index in range(count // rows):
+            column = group * count // rows * head + index * head
+            out_ref[:, column : column + head] = mixed[index * rows : (index + 1) * rows]
+    attended = out_ref[...]
+    low_ref[...] = times_transposed(attended, down_ref[...])
+    back = (back_ref[...] + back_other_ref[...]).astype(BF16)
+    grad_ref[...] = transposed_times(back, attended)
+
+
+def back_kernel(grad_ref, up_ref, out_ref):
+    out_ref[...] = times_transposed(grad_ref[...], up_ref[...])
+
+
+def grads_kernel(low_ref, low_other_ref, grad_ref, down_ref, own_ref, sent_ref):
+    low = (low_ref[...] + low_other_ref[...]).astype(BF16)
+    parity = lax.axis_index("ctx") % 2
+    up_step, down_step = grad_ref.shape[1] // 2, down_ref.shape[1] // 2
+    for index, out in ((1 - parity, sent_ref), (parity, own_ref)):
+        columns = pl.ds(pl.multiple_of(index * up_step, up_step), up_step)
+        out[:, :up_step] = transposed_times(low, grad_ref[:, columns]).astype(out.dtype)
+        columns = pl.ds(pl.multiple_of(index * down_step, down_step), down_step)
+        out[:, up_step:] = down_ref[:, columns].astype(out.dtype)
+
+
+def adapter_kernel(low_ref, low_other_ref, up_ref, out_ref):
+    low = (low_ref[...] + low_other_ref[...]).astype(BF16)
+    out_ref[...] = times(low, up_ref[...]).astype(BF16)
+
+
+def add_kernel(own_ref, got_ref, out_ref):
+    out_ref[...] = (own_ref[...].astype(F32) + got_ref[...].astype(F32)).astype(BF16)
+
+
+def square_sum_kernel(own_ref, got_ref, out_ref):
+    parity = lax.axis_index("ctx") % 2
+    own, got = [jnp.sum(jnp.square(ref[...].astype(F32))).reshape(1, 1) for ref in (own_ref, got_ref)]
+    total = jnp.where(parity == 0, own + got, got + own)
+    out_ref[...] = jnp.broadcast_to(total, out_ref.shape)
+
+
+def clip_kernel(ceiling, square_ref, other_ref, own_ref, got_ref, up_ref, down_ref):
+    squares = square_ref[:1, :1] + other_ref[:1, :1]
+    factor = jnp.minimum(1.0, ceiling / (jnp.sqrt(squares) + 1e-06))
+    parity = lax.axis_index("ctx") % 2
+    up_step, down_step = up_ref.shape[1] // 2, down_ref.shape[1] // 2
+    for index, ref in ((parity, own_ref), (1 - parity, got_ref)):
+        columns = pl.ds(pl.multiple_of(index * up_step, up_step), up_step)
+        up_ref[:, columns] = ref[:, :up_step].astype(F32) * factor
+        columns = pl.ds(pl.multiple_of(index * down_step, down_step), down_step)
+        down_ref[:, columns] = ref[:, up_step:].astype(F32) * factor
+
+
+def split_model_width(
+    hidden, gain, queries, key_value_weight, adapt_down, adapt_up, out_grad, doc_ids
+):
+    place = lax.axis_index("ctx")
+    rows = hidden.shape[1]
+    local_width = hidden.shape[2]
+    slice_width = key_value_weight.shape[1]
+    kv_count, head = key_value_weight.shape[2], key_value_weight.shape[-1]
+    head_count = queries.shape[2]
+    local_query = head_count * head
+    rank = adapt_down.shape[1]
+    kv_width = kv_count * 2 * head
+    sent_width = kv_count * 3 * head
+
+    half = rows // 2
+    core = lax.axis_index("tp")
+    mine = lax.dynamic_slice_in_dim(hidden[0], core * half, half, 0)
+    theirs = lax.dynamic_slice_in_dim(hidden[0], (1 - core) * half, half, 0)
+    part = ((half, slice_width), BF16)
+    slices = call(
+        norm_kernel, [part] * 4, mine, swap(theirs, "tp", 1), gain, swap(gain, "tp", 1)
+    )
+
+    got_1 = swap(slices[1], "ctx", 1)
+    got_3 = swap(slices[3], "ctx", 3)
+    got_2 = swap(slices[2], "ctx", 2)
+    part_flops = 2 * rows * slice_width * kv_width
+    packed = ((rows, sent_width), BF16)
+    summed = ((rows, kv_width), F32)
+    final = ((rows + 16, kv_width), BF16)
+
+    def step(function, *operands):
+        shapes = jax.eval_shape(function, *operands)
+        return lax.cond(
+            place < 4,
+            function,
+            lambda *_: jax.tree.map(lambda x: jnp.zeros(x.shape, x.dtype), shapes),
+            *operands,
+        )
+
+    def prepare(even, key_value_weight, queries, out_grad, adapt_up, doc_ids):
+        even_other = swap(even, "tp", 1)
+        weight = key_value_weight[0].reshape(slice_width, kv_width)
+        docs = doc_ids.astype(F32).reshape(1, rows)
+        freqs = 1000000.0 ** (-jnp.arange(head // 2, dtype=F32) * 2.0 / head)
+        positions = place * rows + jnp.arange(rows, dtype=jnp.int32)
+        angles = positions.astype(F32)[:, None] * freqs
+        cosine, sine = jnp.cos(angles), jnp.sin(angles)
+        cosine = jnp.concatenate([cosine, cosine], axis=1)
+        sine = jnp.concatenate([-sine, sine], axis=1)
+        (query,) = call(
+            query_kernel,
+            [((head_count * rows, head), BF16)],
+            queries[0].reshape(rows, local_query),
+            cosine,
+            sine,
+        )
+        (back_part,) = call(
+            back_kernel,
+            [((rows, rank), F32)],
+            out_grad[0],
+            adapt_up[0],
+            flops=2 * rows * local_width * rank,
+        )
+        back_other = swap(back_part, "tp", 1)
+        return weight, docs, cosine, sine, query, back_part, back_other, even_other
+
+    weight, docs, cosine, sine, query, back_part, back_other, even_other = step(
+        prepare, slices[0], key_value_weight, queries, out_grad, adapt_up, doc_ids
+    )
+    got_1, got_3, even_other = lax.optimization_barrier((got_1, got_3, even_other))
+
+    def near_parts(got_1, got_3, even, even_other, weight):
+        return call(
+            functools.partial(parts_kernel, head),
+            [packed, packed, summed],
+            got_1,
+            swap(got_1, "tp", 1),
+            got_3,
+            swap(got_3, "tp", 1),
+            even,
+            even_other,
+            weight,
+            flops=3 * part_flops,
+            scratch=[pltpu.VMEM((3 * rows, slice_width), BF16)],
+        )
+
+    sent_1, sent_3, part_0 = step(near_parts, got_1, got_3, slices[0], even_other, weight)
+    arrived_1 = swap(sent_1, "ctx", 1)
+    arrived_3 = swap(sent_3, "ctx", 3)
+    got_2, part_0 = lax.optimization_barrier((got_2, part_0))
+    (sent_2,) = call(
+        functools.partial(far_kernel, head),
+        [packed],
+        got_2,
+        swap(got_2, "tp", 1),
+        weight,
+        flops=part_flops,
+        scratch=[pltpu.VMEM((rows, slice_width), BF16)],
+    )
+    arrived_2 = swap(sent_2, "ctx", 2)
+    (block_0,) = call(
+        finish_kernel, [final], part_0, arrived_1, arrived_2, arrived_3, docs, cosine, sine
+    )
+    block_1 = swap(block_0, "ctx", 1)
+    block_2 = swap(block_0, "ctx", 2)
+    block_3 = swap(block_0, "ctx", 3)
+
+    state = ((head_count * rows, 128), F32)
+    mixed, state = call(
+        functools.partial(first_attention_kernel, head),
+        [state, state],
+        query,
+        block_0,
+        block_1,
+        block_2,
+        flops=12 * rows * rows * local_query,
+    )
+    attended, low_part, down_part = call(
+        functools.partial(last_attention_kernel, head),
+        [((rows, local_query), BF16), ((rows, rank), F32), ((rank, local_query), F32)],
+        query,
+        block_0,
+        block_3,
+        mixed,
+        state,
+        adapt_down[0],
+        back_part,
+        back_other,
+        flops=4 * rows * rows * local_query,
+    )
+    low_other = swap(low_part, "tp", 1)
+    piece = (rank, (local_width + local_query) // 2)
+    own, sent = call(
+        grads_kernel,
+        [(piece, F32), (piece, BF16)],
+        low_part,
+        low_other,
+        out_grad[0],
+        down_part,
+        flops=2 * rows * rank * local_width,
+    )
+    (adapter_rows,) = call(
+        adapter_kernel,
+        [((rows, local_width), BF16)],
+        low_part,
+        low_other,
+        adapt_up[0],
+        flops=2 * rows * rank * local_width,
+    )
+    (pair_sum,) = call(add_kernel, [(piece, BF16)], own, swap(sent, "ctx", 1))
+    (total,) = call(add_kernel, [(piece, BF16)], pair_sum, swap(pair_sum, "ctx", 2))
+    total_other = swap(total, "ctx", 1)
+    total_other, adapter_rows = lax.optimization_barrier((total_other, adapter_rows))
+    (squares,) = call(square_sum_kernel, [((8, 128), F32)], total, total_other)
+    squares = squares + swap(squares, "section", 1)
+    squares = squares + swap(squares, "section", 2)
+    ceiling = 0.5 * math.sqrt(lax.axis_size("section") * rank * (local_query + local_width) * 2)
+    grad_up, grad_down = call(
+        functools.partial(clip_kernel, ceiling),
+        [((rank, local_width), F32), ((rank, local_query), F32)],
+        squares,
+        swap(squares, "tp", 1),
+        total,
+        total_other,
+    )
+    return (attended[None], adapter_rows[None], grad_down[None], grad_up[None])
+
+
+def per_device(*arrays):
+    if lax.axis_size("ctx") == 4 and lax.axis_size("tp") == 2 and lax.axis_size("section") == 4:
+        return split_model_width(*arrays)
+    return gathered_weights(*arrays)
 
 
 def solution(mesh):

time: 280 us -> 103 us (0.37)
  waiting for transfers between devices: 174 us -> 54.4 us
  blocking collectives: 56.5 us -> 0 us
  starting transfers between devices: 0.12 us -> 23.5 us
  Pallas kernels: 0 us -> 17.4 us
  between operations: 16 us -> 0.79 us
  matrix products: 13.4 us -> 0 us
  other arithmetic: 11.4 us -> 1.1 us
    all_gather x2 -> x0, waiting for transfers between devices: 142 us -> none  [the longest x1 142 us: per_device(): lax.all_gather(kv_local, 'ctx', axis=1, tiled=True)[0]]
    ppermute x0 -> x23, waiting for transfers between devices: none -> 54.4 us  [swap(): return lax.ppermute(value, axis, [(i, i ^ distance) for i in range(count)])]
    all_gather x4 -> x0, blocking collectives: 40.5 us -> none  [the longest x1 13.3 us: per_device(): piece_keys = lax.all_gather(rotated_keys, 'ctx', axis=0, tiled=True)]
    psum x1 -> x0, waiting for transfers between devices: 32.1 us -> none  [per_device(): lax.psum(down_part.astype(jnp.bfloat16), 'ctx').astype(jnp.float32)]
    ppermute x0 -> x23, starting transfers between devices: none -> 23.5 us  [swap(): return lax.ppermute(value, axis, [(i, i ^ distance) for i in range(count)])]
    pallas_call x0 -> x14, Pallas kernels: none -> 17.4 us  [call(): pl.pallas_call(kernel, out_shape=shapes, in_specs=[VMEM] * len(operands),...]
    psum x2 -> x0, blocking collectives: 16 us -> none  [the longest x1 12.7 us: per_device(): squares = lax.psum(local_squares, ('section', 'tp'))]
    dot_general x8 -> x0, matrix products: 13.4 us -> none  [the longest x1 6.42 us: per_device(): jnp.dot(normalized_rows, lax.all_gather(kv_local, 'ctx', axis=1, tiled=Tr...]
  transfers between devices with their start and end apart: 3 -> 23, of which waited for: 2 -> 17; matrix products, arithmetic and copies ran while one was open for 4% -> 5% of each run, Pallas kernels for 0% -> 10%
where the time goes in v3:
time: 103 us
  waiting for transfers between devices  54.4 us (53%)
  starting transfers between devices  23.5 us (23%)
  Pallas kernels  17.4 us (17%)
  local copies, waits for them, and re-layouts  5.63 us (5%)
  other arithmetic  1.1 us (1%)
    ppermute x23, waiting for transfers between devices, swap(): return lax.ppermute(value, axis, [(i, i ^ distance) for i in range(count)])  54.4 us
    ppermute x23, starting transfers between devices, swap(): return lax.ppermute(value, axis, [(i, i ^ distance) for i in range(count)])  23.5 us
    pallas_call x14, Pallas kernels, call(): pl.pallas_call(kernel, out_shape=shapes, in_specs=[VMEM] * len(operands),...  17.4 us
    squeeze x1, local copies, waits for them, and re-layouts, prepare(): weight = key_value_weight[0].reshape(slice_width, kv_width)  4.11 us
  transfers between devices with their start and end apart: 23, of which 17 were waited for; matrix products, arithmetic and copies ran while one was open for 5% of the time, Pallas kernels for 10%

profile of v3, /device:TPU:0, one launch (start us, length us, event | category | flops | bytes accessed | tf_op | source)
XLA Modules:
  0.0 102.8 jit_solution(9141345399110497181)
XLA Ops:
  0.7 1.4 %dynamic-slice_bitcast_fusion = (bf16[64,4096]{1,0:T(8,128)(2,1)S(1)}, bf16[64,4096]{1,0:T(8,128)(2,1)S(1)}) fusion(bf16[1,128,4096]{2,1,0:T(8,128)(2,1)} %param.12, s32[]{:T(128)S(6)} %select_n.7, s32[]{:T(128)S(6)} %select_n.6), kind=kLoop, calls=%fused_computation.9 | loop fusion | bytes 2097160 | tf_op jit(solution)/shard_map/dynamic_slice | solution.py:440
  2.7 1.5 %collective-permute-done.5.gain_other_ref = bf16[1,4096]{1,0:T(2,128)(2,1)S(1)} collective-permute-done((bf16[1,4096]{1,0:T(2,128)(2,1)S(1)}, bf16[1,4096]{1,0:T(2,128)(2,1)S(1)}, u32[]{:S(2)}, u32[]{:S(2)}) %collective-permute-start.5) | collective-permute-done | bytes 8224 | tf_op jit(solution)/shard_map/ppermute | solution.py:145
  4.7 3.0 %collective-permute-start.7 = (bf16[64,2048]{1,0:T(8,128)(2,1)S(1)}, bf16[64,2048]{1,0:T(8,128)(2,1)}, u32[]{:S(2)}, u32[]{:S(2)}) collective-permute-start(bf16[64,2048]{1,0:T(8,128)(2,1)S(1)} %get-tuple-element.74), channel_id=1, source_target_pairs={{0,2},{2,0},{4,6},{6,4},{1,3},{3,1},{5,7},{7,5},{8,10},{10,8},{12,... | collective-permute-start | bytes 786440 | tf_op jit(solution)/shard_map/ppermute | solution.py:145
  7.7 2.5 %collective-permute-start.8 = (bf16[64,2048]{1,0:T(8,128)(2,1)S(1)}, bf16[64,2048]{1,0:T(8,128)(2,1)}, u32[]{:S(2)}, u32[]{:S(2)}) collective-permute-start(bf16[64,2048]{1,0:T(8,128)(2,1)S(1)} %get-tuple-element.75), channel_id=1, source_target_pairs={{0,6},{2,4},{4,2},{6,0},{1,7},{3,5},{5,3},{7,1},{8,14},{10,12},{12... | collective-permute-start | bytes 786440 | tf_op jit(solution)/shard_map/ppermute | solution.py:145
  10.4 8.1 %conditional.2 = (bf16[2048,512]{1,0:T(8,128)(2,1)}, f32[1,128]{1,0:T(1,128)S(1)}, f32[128,128]{1,0:T(8,128)}, f32[128,128]{1,0:T(8,128)}, bf16[2048,128]{1,0:T(...) conditional(s32[]{:T(128)} %convert_element_type.14, () %tuple.26, ...), branch_computations={%region_0.0_spmd, %region_1.0_spmd} | conditional | flops 16826880 | bytes 11119292 | solution.py:456
  13.2 4.1 %squeeze.3 = bf16[2048,512]{1,0:T(8,128)(2,1)} reshape(bf16[1,2048,2,2,128]{4,3,2,1,0:T(2,128)(2,1)} %get-tuple-element.105) | data formatting | bytes 4194304 | tf_op jit(solution)/shard_map/cond/branch_1_fun/reshape;cond/branch_1_fun/squeeze | solution.py:465
  18.4 4.7 %collective-permute-done.8 = bf16[64,2048]{1,0:T(8,128)(2,1)} collective-permute-done((bf16[64,2048]{1,0:T(8,128)(2,1)S(1)}, bf16[64,2048]{1,0:T(8,128)(2,1)}, u32[]{:S(2)}, u32[]{:S(2)}) %collective-permute-start.8) | collective-permute-done | bytes 262176 | tf_op jit(solution)/shard_map/ppermute | solution.py:145
  23.2 5.0 %conditional.3 = ((bf16[128,768]{1,0:T(8,128)(2,1)S(1)}, bf16[128,768]{1,0:T(8,128)(2,1)S(1)}, f32[128,512]{1,0:T(8,128)S(1)})) conditional(s32[]{:T(128)} %convert_element_type.14, () %tuple.28, (bf16[64,2048]{1,0:T(8,128)(2,1)}, bf16[64,2048]{1,0:T(8,128)(2,1)}, bf16[64,2048]{1,0:T(8,128)(2,1)S(1)}, bf16[64,2048]{1,0:T(8,128)(2,1)}, ...), branch_computations={%region_2.0_spmd, %region_3.0_spmd} | conditional | flops 805306368 | bytes 6422616 | solution.py:456
  23.7 1.2 %collective-permute-done.got_1_other_ref = bf16[64,2048]{1,0:T(8,128)(2,1)S(1)} collective-permute-done((bf16[64,2048]{1,0:T(8,128)(2,1)}, bf16[64,2048]{1,0:T(8,128)(2,1)S(1)}, u32[]{:S(2)}, u32[]{:S(2)}) %collective-permute-start) | collective-permute-done | bytes 262176 | tf_op jit(solution)/shard_map/cond/branch_1_fun/ppermute | solution.py:145
  25.3 2.8 %branch_1_fun.5 = (bf16[128,768]{1,0:T(8,128)(2,1)S(1)}, bf16[128,768]{1,0:T(8,128)(2,1)S(1)}, f32[128,512]{1,0:T(8,128)S(1)}) custom-call(bf16[64,2048]{1,0:T(8,128)(2,1)} %get-tuple-element.31.got_1_ref, bf16[64,2048]{1,0:T(8,128)(2,1)S(1)} %collective-permute-done.got_1_other_ref, bf16[64,2048]{1,0:T(8,128)(2,1)} %get-tuple-element.32.got_3_ref, ...), custom_call_target="tpu_custom_call" | custom-call | flops 805306368 | bytes 4325376 | tf_op jit(solution)/shard_map/cond/branch_1_fun/pallas_call | solution.py:151
  28.1 5.4 %collective-permute-done.6.got_ref = bf16[64,2048]{1,0:T(8,128)(2,1)S(1)} collective-permute-done((bf16[64,2048]{1,0:T(8,128)(2,1)S(1)}, bf16[64,2048]{1,0:T(8,128)(2,1)S(1)}, u32[]{:S(2)}, u32[]{:S(2)}) %collective-permute-start.6) | collective-permute-done | bytes 262176 | tf_op jit(solution)/shard_map/ppermute | solution.py:145
  34.6 3.0 %collective-permute-start.12 = (bf16[128,768]{1,0:T(8,128)(2,1)S(1)}, bf16[128,768]{1,0:T(8,128)(2,1)S(1)}, u32[]{:S(2)}, u32[]{:S(2)}) collective-permute-start(bf16[128,768]{1,0:T(8,128)(2,1)S(1)} %get-tuple-element.85), channel_id=1, source_target_pairs={{0,6},{2,4},{4,2},{6,0},{1,7},{3,5},{5,3},{7,1},{8,14},{10,12},{12... | collective-permute-start | bytes 589832 | tf_op jit(solution)/shard_map/ppermute | solution.py:145
  37.5 2.0 %shard_map.115 = bf16[128,768]{1,0:T(8,128)(2,1)S(1)} custom-call(bf16[64,2048]{1,0:T(8,128)(2,1)S(1)} %collective-permute-done.6.got_ref, bf16[64,2048]{1,0:T(8,128)(2,1)S(1)} %collective-permute-done.10.got_other_ref, bf16[2048,512]{1,0:T(8,128)(2,1)} %get-tuple-element.80.weight_ref), custom_call_target="tpu_custom_call" | custom-call | flops 268435456 | bytes 2818048 | tf_op jit(solution)/shard_map/pallas_call | solution.py:151
  39.7 1.2 %collective-permute-done.9.got_1_ref = bf16[128,768]{1,0:T(8,128)(2,1)S(1)} collective-permute-done((bf16[128,768]{1,0:T(8,128)(2,1)S(1)}, bf16[128,768]{1,0:T(8,128)(2,1)S(1)}, u32[]{:S(2)}, u32[]{:S(2)}) %collective-permute-start.9) | collective-permute-done | bytes 196640 | tf_op jit(solution)/shard_map/ppermute | solution.py:145
  40.8 6.7 %collective-permute-done.12.got_3_ref = bf16[128,768]{1,0:T(8,128)(2,1)S(1)} collective-permute-done((bf16[128,768]{1,0:T(8,128)(2,1)S(1)}, bf16[128,768]{1,0:T(8,128)(2,1)S(1)}, u32[]{:S(2)}, u32[]{:S(2)}) %collective-permute-start.12) | collective-permute-done | bytes 196640 | tf_op jit(solution)/shard_map/ppermute | solution.py:145
  47.5 7.6 %collective-permute-done.11.got_2_ref = bf16[128,768]{1,0:T(8,128)(2,1)S(1)} collective-permute-done((bf16[128,768]{1,0:T(8,128)(2,1)S(1)}, bf16[128,768]{1,0:T(8,128)(2,1)S(1)}, u32[]{:S(2)}, u32[]{:S(2)}) %collective-permute-start.11) | collective-permute-done | bytes 196640 | tf_op jit(solution)/shard_map/ppermute | solution.py:145
  56.3 2.7 %collective-permute-start.14 = (bf16[144,512]{1,0:T(8,128)(2,1)S(1)}, bf16[144,512]{1,0:T(8,128)(2,1)S(1)}, u32[]{:S(2)}, u32[]{:S(2)}) collective-permute-start(bf16[144,512]{1,0:T(8,128)(2,1)S(1)} %shard_map.116.block_0_ref), channel_id=1, source_target_pairs={{0,2},{2,0},{4,6},{6,4},{1,3},{3,1},{5,7},{7,5},{8,10},{10,8},{12,... | collective-permute-start | bytes 442376 | tf_op jit(solution)/shard_map/ppermute | solution.py:145
  59.0 1.7 %collective-permute-start.13 = (bf16[144,512]{1,0:T(8,128)(2,1)S(1)}, bf16[144,512]{1,0:T(8,128)(2,1)S(1)}, u32[]{:S(2)}, u32[]{:S(2)}) collective-permute-start(bf16[144,512]{1,0:T(8,128)(2,1)S(1)} %shard_map.116.block_0_ref), channel_id=1, source_target_pairs={{0,6},{2,4},{4,2},{6,0},{1,7},{3,5},{5,3},{7,1},{8,14},{10,12},{12... | collective-permute-start | bytes 442376 | tf_op jit(solution)/shard_map/ppermute | solution.py:145
  60.6 7.7 %collective-permute-done.15.block_2_ref = bf16[144,512]{1,0:T(8,128)(2,1)S(1)} collective-permute-done((bf16[144,512]{1,0:T(8,128)(2,1)S(1)}, bf16[144,512]{1,0:T(8,128)(2,1)S(1)}, u32[]{:S(2)}, u32[]{:S(2)}) %collective-permute-start.15) | collective-permute-done | bytes 147488 | tf_op jit(solution)/shard_map/ppermute | solution.py:145
  68.4 1.4 %shard_map.117 = (f32[2048,128]{1,0:T(8,128)S(1)}, f32[2048,128]{1,0:T(8,128)S(1)}) custom-call(bf16[2048,128]{1,0:T(8,128)(2,1)S(1)} %get-tuple-element.72.query_ref, bf16[144,512]{1,0:T(8,128)(2,1)S(1)} %shard_map.116.block_0_ref, bf16[144,512]{1,0:T(8,128)(2,1)S(1)} %collective-permute-done.14.block_1_ref, ...), custom_call_target="tpu_custom_call" | custom-call | flops 402653184 | bytes 3063808 | tf_op jit(solution)/shard_map/pallas_call | solution.py:151
  69.9 4.6 %shard_map.118 = (bf16[128,2048]{1,0:T(8,128)(2,1)}, f32[128,16]{1,0:T(8,128)S(1)}, f32[16,2048]{1,0:T(8,128)S(1)}) custom-call(bf16[2048,128]{1,0:T(8,128)(2,1)S(1)} %get-tuple-element.72.query_ref, bf16[144,512]{1,0:T(8,128)(2,1)S(1)} %shard_map.116.block_0_ref, bf16[144,512]{1,0:T(8,128)(2,1)S(1)} %collective-permute-done.13.block_3_ref, ...), custom_call_target="tpu_custom_call" | custom-call | flops 134217728 | bytes 3661824 | tf_op jit(solution)/shard_map/pallas_call | solution.py:151
  74.5 1.3 %collective-permute-done.16.low_other_ref = f32[128,16]{1,0:T(8,128)S(1)} collective-permute-done((f32[128,16]{1,0:T(8,128)S(1)}, f32[128,16]{1,0:T(8,128)S(1)}, u32[]{:S(2)}, u32[]{:S(2)}) %collective-permute-start.16) | collective-permute-done | bytes 8224 | tf_op jit(solution)/shard_map/ppermute | solution.py:145
  76.0 2.1 %collective-permute-start.17 = (bf16[16,3072]{1,0:T(8,128)(2,1)S(1)}, bf16[16,3072]{1,0:T(8,128)(2,1)S(1)}, u32[]{:S(2)}, u32[]{:S(2)}) collective-permute-start(bf16[16,3072]{1,0:T(8,128)(2,1)S(1)} %get-tuple-element.97), channel_id=1, source_target_pairs={{0,2},{2,0},{4,6},{6,4},{1,3},{3,1},{5,7},{7,5},{8,10},{10,8},{12,... | collective-permute-start | bytes 294920 | tf_op jit(solution)/shard_map/ppermute | solution.py:145
  78.1 3.1 %collective-permute-done.17.got_ref = bf16[16,3072]{1,0:T(8,128)(2,1)S(1)} collective-permute-done((bf16[16,3072]{1,0:T(8,128)(2,1)S(1)}, bf16[16,3072]{1,0:T(8,128)(2,1)S(1)}, u32[]{:S(2)}, u32[]{:S(2)}) %collective-permute-start.17) | collective-permute-done | bytes 98336 | tf_op jit(solution)/shard_map/ppermute | solution.py:145
  81.2 2.5 %collective-permute-start.18 = (bf16[16,3072]{1,0:T(8,128)(2,1)S(1)}, bf16[16,3072]{1,0:T(8,128)(2,1)S(1)}, u32[]{:S(2)}, u32[]{:S(2)}) collective-permute-start(bf16[16,3072]{1,0:T(8,128)(2,1)S(1)} %shard_map.120.own_ref), channel_id=1, source_target_pairs={{0,4},{2,6},{4,0},{6,2},{1,5},{3,7},{5,1},{7,3},{8,12},{10,14},{12... | collective-permute-start | bytes 294920 | tf_op jit(solution)/shard_map/ppermute | solution.py:145
  83.7 4.9 %collective-permute-done.18.got_ref = bf16[16,3072]{1,0:T(8,128)(2,1)S(1)} collective-permute-done((bf16[16,3072]{1,0:T(8,128)(2,1)S(1)}, bf16[16,3072]{1,0:T(8,128)(2,1)S(1)}, u32[]{:S(2)}, u32[]{:S(2)}) %collective-permute-start.18) | collective-permute-done | bytes 98336 | tf_op jit(solution)/shard_map/ppermute | solution.py:145
  88.7 1.4 %shard_map.122 = bf16[128,4096]{1,0:T(8,128)(2,1)} custom-call(f32[128,16]{1,0:T(8,128)S(1)} %get-tuple-element.94.low_ref, f32[128,16]{1,0:T(8,128)S(1)} %collective-permute-done.16.low_other_ref, bf16[16,4096]{1,0:T(8,128)(2,1)S(1)} %bitcast.25), custom_call_target="tpu_custom_call" | custom-call | flops 16777216 | bytes 1196032 | tf_op jit(solution)/shard_map/pallas_call | solution.py:151
  90.1 3.2 %collective-permute-done.19.got_ref = bf16[16,3072]{1,0:T(8,128)(2,1)S(1)} collective-permute-done((bf16[16,3072]{1,0:T(8,128)(2,1)S(1)}, bf16[16,3072]{1,0:T(8,128)(2,1)S(1)}, u32[]{:S(2)}, u32[]{:S(2)}) %collective-permute-start.19) | collective-permute-done | bytes 98336 | tf_op jit(solution)/shard_map/ppermute | solution.py:145
  93.5 1.6 %collective-permute-start.20 = (f32[8,128]{1,0:T(8,128)S(1)}, f32[8,128]{1,0:T(8,128)S(1)}, u32[]{:S(2)}, u32[]{:S(2)}) collective-permute-start(f32[8,128]{1,0:T(8,128)S(1)} %shard_map.123), channel_id=1, source_target_pairs={{0,8},{8,0},{16,24},{24,16},{1,9},{9,1},{17,25},{25,17},{2,10},{10... | collective-permute-start | bytes 12296 | tf_op jit(solution)/shard_map/ppermute | solution.py:145
  95.1 2.1 %collective-permute-done.20 = f32[8,128]{1,0:T(8,128)S(1)} collective-permute-done((f32[8,128]{1,0:T(8,128)S(1)}, f32[8,128]{1,0:T(8,128)S(1)}, u32[]{:S(2)}, u32[]{:S(2)}) %collective-permute-start.20) | collective-permute-done | bytes 4128 | tf_op jit(solution)/shard_map/ppermute | solution.py:145
  97.2 1.5 %collective-permute-start.21 = (f32[8,128]{1,0:T(8,128)S(1)}, f32[8,128]{1,0:T(8,128)S(1)}, u32[]{:S(2)}, u32[]{:S(2)}) collective-permute-start(f32[8,128]{1,0:T(8,128)S(1)} %add.24), channel_id=1, source_target_pairs={{0,16},{8,24},{16,0},{24,8},{1,17},{9,25},{17,1},{25,9},{2,18},{10... | collective-permute-start | bytes 12296 | tf_op jit(solution)/shard_map/ppermute | solution.py:145
  98.7 2.1 %collective-permute-done.21 = f32[8,128]{1,0:T(8,128)S(1)} collective-permute-done((f32[8,128]{1,0:T(8,128)S(1)}, f32[8,128]{1,0:T(8,128)S(1)}, u32[]{:S(2)}, u32[]{:S(2)}) %collective-permute-start.21) | collective-permute-done | bytes 4128 | tf_op jit(solution)/shard_map/ppermute | solution.py:145
  (52 shorter events, 11.0 us)
Async XLA Ops:
  0.6 1.9 %copy-start.1 = (bf16[1,4096]{1,0:T(2,128)(2,1)S(1)}, bf16[1,4096]{1,0:T(2,128)(2,1)}, u32[]{:S(2)}) copy-start(bf16[1,4096]{1,0:T(2,128)(2,1)} %gain_ref.1) | copy-start | bytes 24580
  0.6 9.7 %copy-start.2 = (bf16[1,128,4096]{2,1,0:T(8,128)(2,1)S(1)}, bf16[1,128,4096]{2,1,0:T(8,128)(2,1)}, u32[]{:S(2)}) copy-start(bf16[1,128,4096]{2,1,0:T(8,128)(2,1)} %param.18) | copy-start | bytes 3145732
  0.7 9.7 %copy-start.3 = (bf16[1,16,4096]{2,1,0:T(8,128)(2,1)S(1)}, bf16[1,16,4096]{2,1,0:T(8,128)(2,1)}, u32[]{:S(2)}) copy-start(bf16[1,16,4096]{2,1,0:T(8,128)(2,1)} %param.17) | copy-start | bytes 393220
  0.7 9.7 %copy-start.5 = (s32[128]{0:T(128)S(1)}, s32[128]{0:T(128)}, u32[]{:S(2)}) copy-start(s32[128]{0:T(128)} %param.19) | copy-start | bytes 1540
  2.0 2.1 %collective-permute-start.4 = (bf16[64,4096]{1,0:T(8,128)(2,1)S(1)}, bf16[64,4096]{1,0:T(8,128)(2,1)S(1)}, u32[]{:S(2)}, u32[]{:S(2)}) collective-permute-start(bf16[64,4096]{1,0:T(8,128)(2,1)S(1)} %get-tuple-element.113), channel_id=1, source_target_pairs={{0,1},{1,0},{2,3},{3,2},{4,5},{5,4},{6,7},{7,6},{8,9},{9,8},{10,11... | collective-permute-start | bytes 1572872 | tf_op jit(solution)/shard_map/ppermute | solution.py:145
  2.6 1.6 %collective-permute-start.5 = (bf16[1,4096]{1,0:T(2,128)(2,1)S(1)}, bf16[1,4096]{1,0:T(2,128)(2,1)S(1)}, u32[]{:S(2)}, u32[]{:S(2)}) collective-permute-start(bf16[1,4096]{1,0:T(2,128)(2,1)S(1)} %copy-done.1), channel_id=1, source_target_pairs={{0,1},{1,0},{2,3},{3,2},{4,5},{5,4},{6,7},{7,6},{8,9},{9,8},{10,11... | collective-permute-start | bytes 24584 | tf_op jit(solution)/shard_map/ppermute | solution.py:145
  4.7 13.7 %collective-permute-start.7 = (bf16[64,2048]{1,0:T(8,128)(2,1)S(1)}, bf16[64,2048]{1,0:T(8,128)(2,1)}, u32[]{:S(2)}, u32[]{:S(2)}) collective-permute-start(bf16[64,2048]{1,0:T(8,128)(2,1)S(1)} %get-tuple-element.74), channel_id=1, source_target_pairs={{0,2},{2,0},{4,6},{6,4},{1,3},{3,1},{5,7},{7,5},{8,10},{10,8},{12,... | collective-permute-start | bytes 786440 | tf_op jit(solution)/shard_map/ppermute | solution.py:145
  7.7 15.4 %collective-permute-start.8 = (bf16[64,2048]{1,0:T(8,128)(2,1)S(1)}, bf16[64,2048]{1,0:T(8,128)(2,1)}, u32[]{:S(2)}, u32[]{:S(2)}) collective-permute-start(bf16[64,2048]{1,0:T(8,128)(2,1)S(1)} %get-tuple-element.75), channel_id=1, source_target_pairs={{0,6},{2,4},{4,2},{6,0},{1,7},{3,5},{5,3},{7,1},{8,14},{10,12},{12... | collective-permute-start | bytes 786440 | tf_op jit(solution)/shard_map/ppermute | solution.py:145
  10.2 23.3 %collective-permute-start.6 = (bf16[64,2048]{1,0:T(8,128)(2,1)S(1)}, bf16[64,2048]{1,0:T(8,128)(2,1)S(1)}, u32[]{:S(2)}, u32[]{:S(2)}) collective-permute-start(bf16[64,2048]{1,0:T(8,128)(2,1)S(1)} %get-tuple-element.73), channel_id=1, source_target_pairs={{0,4},{2,6},{4,0},{6,2},{1,5},{3,7},{5,1},{7,3},{8,12},{10,14},{12... | collective-permute-start | bytes 786440 | tf_op jit(solution)/shard_map/ppermute | solution.py:145
  10.4 2.7 %copy-start.4 = (bf16[1,128,16,128]{3,2,1,0:T(8,128)(2,1)S(1)}, bf16[1,128,16,128]{3,2,1,0:T(8,128)(2,1)}, u32[]{:S(2)}) copy-start(bf16[1,128,16,128]{3,2,1,0:T(8,128)(2,1)} %get-tuple-element.107) | copy-start | bytes 1572868 | tf_op jit(solution)/shard_map/cond
  11.4 7.0 %collective-permute-start.2 = (f32[128,16]{1,0:T(8,128)}, f32[128,16]{1,0:T(8,128)}, u32[]{:S(2)}, u32[]{:S(2)}) collective-permute-start(f32[128,16]{1,0:T(8,128)} %branch_1_fun.4), channel_id=1, source_target_pairs={{0,1},{1,0},{2,3},{3,2},{4,5},{5,4},{6,7},{7,6},{8,9},{9,8},{10,11... | collective-permute-start | bytes 24584 | tf_op jit(solution)/shard_map/cond/branch_1_fun/ppermute | solution.py:145
  11.4 7.0 %collective-permute-start.3 = (bf16[64,2048]{1,0:T(8,128)(2,1)S(1)}, bf16[64,2048]{1,0:T(8,128)(2,1)}, u32[]{:S(2)}, u32[]{:S(2)}) collective-permute-start(bf16[64,2048]{1,0:T(8,128)(2,1)S(1)} %get-tuple-element.30), channel_id=1, source_target_pairs={{0,1},{1,0},{2,3},{3,2},{4,5},{5,4},{6,7},{7,6},{8,9},{9,8},{10,11... | collective-permute-start | bytes 786440 | tf_op jit(solution)/shard_map/cond/branch_1_fun/ppermute | solution.py:145
  23.2 1.7 %collective-permute-start = (bf16[64,2048]{1,0:T(8,128)(2,1)}, bf16[64,2048]{1,0:T(8,128)(2,1)S(1)}, u32[]{:S(2)}, u32[]{:S(2)}) collective-permute-start(bf16[64,2048]{1,0:T(8,128)(2,1)} %get-tuple-element.31.got_1_ref), channel_id=1, source_target_pairs={{0,1},{1,0},{2,3},{3,2},{4,5},{5,4},{6,7},{7,6},{8,9},{9,8},{10,11... | collective-permute-start | bytes 786440 | tf_op jit(solution)/shard_map/cond/branch_1_fun/ppermute | solution.py:145
  23.2 2.1 %collective-permute-start.1 = (bf16[64,2048]{1,0:T(8,128)(2,1)}, bf16[64,2048]{1,0:T(8,128)(2,1)S(1)}, u32[]{:S(2)}, u32[]{:S(2)}) collective-permute-start(bf16[64,2048]{1,0:T(8,128)(2,1)} %get-tuple-element.32.got_3_ref), channel_id=1, source_target_pairs={{0,1},{1,0},{2,3},{3,2},{4,5},{5,4},{6,7},{7,6},{8,9},{9,8},{10,11... | collective-permute-start | bytes 786440 | tf_op jit(solution)/shard_map/cond/branch_1_fun/ppermute | solution.py:145
  33.5 4.0 %collective-permute-start.10 = (bf16[64,2048]{1,0:T(8,128)(2,1)S(1)}, bf16[64,2048]{1,0:T(8,128)(2,1)S(1)}, u32[]{:S(2)}, u32[]{:S(2)}) collective-permute-start(bf16[64,2048]{1,0:T(8,128)(2,1)S(1)} %collective-permute-done.6.got_ref), channel_id=1, source_target_pairs={{0,1},{1,0},{2,3},{3,2},{4,5},{5,4},{6,7},{7,6},{8,9},{9,8},{10,11... | collective-permute-start | bytes 786440 | tf_op jit(solution)/shard_map/ppermute | solution.py:145
  33.5 7.3 %collective-permute-start.9 = (bf16[128,768]{1,0:T(8,128)(2,1)S(1)}, bf16[128,768]{1,0:T(8,128)(2,1)S(1)}, u32[]{:S(2)}, u32[]{:S(2)}) collective-permute-start(bf16[128,768]{1,0:T(8,128)(2,1)S(1)} %get-tuple-element.83), channel_id=1, source_target_pairs={{0,2},{2,0},{4,6},{6,4},{1,3},{3,1},{5,7},{7,5},{8,10},{10,8},{12,... | collective-permute-start | bytes 589832 | tf_op jit(solution)/shard_map/ppermute | solution.py:145
  34.6 35.3 %copy-start = (bf16[1,16,2048]{2,1,0:T(8,128)(2,1)S(1)}, bf16[1,16,2048]{2,1,0:T(8,128)(2,1)}, u32[]{:S(2)}) copy-start(bf16[1,16,2048]{2,1,0:T(8,128)(2,1)} %param.16) | copy-start | bytes 196612
  34.6 13.0 %collective-permute-start.12 = (bf16[128,768]{1,0:T(8,128)(2,1)S(1)}, bf16[128,768]{1,0:T(8,128)(2,1)S(1)}, u32[]{:S(2)}, u32[]{:S(2)}) collective-permute-start(bf16[128,768]{1,0:T(8,128)(2,1)S(1)} %get-tuple-element.85), channel_id=1, source_target_pairs={{0,6},{2,4},{4,2},{6,0},{1,7},{3,5},{5,3},{7,1},{8,14},{10,12},{12... | collective-permute-start | bytes 589832 | tf_op jit(solution)/shard_map/ppermute | solution.py:145
  39.6 15.6 %collective-permute-start.11 = (bf16[128,768]{1,0:T(8,128)(2,1)S(1)}, bf16[128,768]{1,0:T(8,128)(2,1)S(1)}, u32[]{:S(2)}, u32[]{:S(2)}) collective-permute-start(bf16[128,768]{1,0:T(8,128)(2,1)S(1)} %shard_map.115), channel_id=1, source_target_pairs={{0,4},{2,6},{4,0},{6,2},{1,5},{3,7},{5,1},{7,3},{8,12},{10,14},{12... | collective-permute-start | bytes 589832 | tf_op jit(solution)/shard_map/ppermute | solution.py:145
  56.2 12.1 %collective-permute-start.15 = (bf16[144,512]{1,0:T(8,128)(2,1)S(1)}, bf16[144,512]{1,0:T(8,128)(2,1)S(1)}, u32[]{:S(2)}, u32[]{:S(2)}) collective-permute-start(bf16[144,512]{1,0:T(8,128)(2,1)S(1)} %shard_map.116.block_0_ref), channel_id=1, source_target_pairs={{0,4},{2,6},{4,0},{6,2},{1,5},{3,7},{5,1},{7,3},{8,12},{10,14},{12... | collective-permute-start | bytes 442376 | tf_op jit(solution)/shard_map/ppermute | solution.py:145
  56.3 12.1 %collective-permute-start.14 = (bf16[144,512]{1,0:T(8,128)(2,1)S(1)}, bf16[144,512]{1,0:T(8,128)(2,1)S(1)}, u32[]{:S(2)}, u32[]{:S(2)}) collective-permute-start(bf16[144,512]{1,0:T(8,128)(2,1)S(1)} %shard_map.116.block_0_ref), channel_id=1, source_target_pairs={{0,2},{2,0},{4,6},{6,4},{1,3},{3,1},{5,7},{7,5},{8,10},{10,8},{12,... | collective-permute-start | bytes 442376 | tf_op jit(solution)/shard_map/ppermute | solution.py:145
  59.0 10.9 %collective-permute-start.13 = (bf16[144,512]{1,0:T(8,128)(2,1)S(1)}, bf16[144,512]{1,0:T(8,128)(2,1)S(1)}, u32[]{:S(2)}, u32[]{:S(2)}) collective-permute-start(bf16[144,512]{1,0:T(8,128)(2,1)S(1)} %shard_map.116.block_0_ref), channel_id=1, source_target_pairs={{0,6},{2,4},{4,2},{6,0},{1,7},{3,5},{5,3},{7,1},{8,14},{10,12},{12... | collective-permute-start | bytes 442376 | tf_op jit(solution)/shard_map/ppermute | solution.py:145
  74.5 1.3 %collective-permute-start.16 = (f32[128,16]{1,0:T(8,128)S(1)}, f32[128,16]{1,0:T(8,128)S(1)}, u32[]{:S(2)}, u32[]{:S(2)}) collective-permute-start(f32[128,16]{1,0:T(8,128)S(1)} %get-tuple-element.94.low_ref), channel_id=1, source_target_pairs={{0,1},{1,0},{2,3},{3,2},{4,5},{5,4},{6,7},{7,6},{8,9},{9,8},{10,11... | collective-permute-start | bytes 24584 | tf_op jit(solution)/shard_map/ppermute | solution.py:145
  76.0 5.2 %collective-permute-start.17 = (bf16[16,3072]{1,0:T(8,128)(2,1)S(1)}, bf16[16,3072]{1,0:T(8,128)(2,1)S(1)}, u32[]{:S(2)}, u32[]{:S(2)}) collective-permute-start(bf16[16,3072]{1,0:T(8,128)(2,1)S(1)} %get-tuple-element.97), channel_id=1, source_target_pairs={{0,2},{2,0},{4,6},{6,4},{1,3},{3,1},{5,7},{7,5},{8,10},{10,8},{12,... | collective-permute-start | bytes 294920 | tf_op jit(solution)/shard_map/ppermute | solution.py:145
  81.2 7.4 %collective-permute-start.18 = (bf16[16,3072]{1,0:T(8,128)(2,1)S(1)}, bf16[16,3072]{1,0:T(8,128)(2,1)S(1)}, u32[]{:S(2)}, u32[]{:S(2)}) collective-permute-start(bf16[16,3072]{1,0:T(8,128)(2,1)S(1)} %shard_map.120.own_ref), channel_id=1, source_target_pairs={{0,4},{2,6},{4,0},{6,2},{1,5},{3,7},{5,1},{7,3},{8,12},{10,14},{12... | collective-permute-start | bytes 294920 | tf_op jit(solution)/shard_map/ppermute | solution.py:145
  88.6 4.7 %collective-permute-start.19 = (bf16[16,3072]{1,0:T(8,128)(2,1)S(1)}, bf16[16,3072]{1,0:T(8,128)(2,1)S(1)}, u32[]{:S(2)}, u32[]{:S(2)}) collective-permute-start(bf16[16,3072]{1,0:T(8,128)(2,1)S(1)} %shard_map.121.own_ref), channel_id=1, source_target_pairs={{0,2},{2,0},{4,6},{6,4},{1,3},{3,1},{5,7},{7,5},{8,10},{10,8},{12,... | collective-permute-start | bytes 294920 | tf_op jit(solution)/shard_map/ppermute | solution.py:145
  93.5 3.7 %collective-permute-start.20 = (f32[8,128]{1,0:T(8,128)S(1)}, f32[8,128]{1,0:T(8,128)S(1)}, u32[]{:S(2)}, u32[]{:S(2)}) collective-permute-start(f32[8,128]{1,0:T(8,128)S(1)} %shard_map.123), channel_id=1, source_target_pairs={{0,8},{8,0},{16,24},{24,16},{1,9},{9,1},{17,25},{25,17},{2,10},{10... | collective-permute-start | bytes 12296 | tf_op jit(solution)/shard_map/ppermute | solution.py:145
  97.2 3.6 %collective-permute-start.21 = (f32[8,128]{1,0:T(8,128)S(1)}, f32[8,128]{1,0:T(8,128)S(1)}, u32[]{:S(2)}, u32[]{:S(2)}) collective-permute-start(f32[8,128]{1,0:T(8,128)S(1)} %add.24), channel_id=1, source_target_pairs={{0,16},{8,24},{16,0},{24,8},{1,17},{9,25},{17,1},{25,9},{2,18},{10... | collective-permute-start | bytes 12296 | tf_op jit(solution)/shard_map/ppermute | solution.py:145
  100.8 1.2 %collective-permute-start.22 = (f32[8,128]{1,0:T(8,128)S(1)}, f32[8,128]{1,0:T(8,128)S(1)}, u32[]{:S(2)}, u32[]{:S(2)}) collective-permute-start(f32[8,128]{1,0:T(8,128)S(1)} %add.25.square_ref), channel_id=1, source_target_pairs={{0,1},{1,0},{2,3},{3,2},{4,5},{5,4},{6,7},{7,6},{8,9},{9,8},{10,11... | collective-permute-start | bytes 12296 | tf_op jit(solution)/shard_map/ppermute | solution.py:145

commit v4 on v3

--- a/solution.py
+++ b/solution.py
@@ -137,7 +137,7 @@
 
 F32, BF16 = jnp.float32, jnp.bfloat16
 VMEM = pl.BlockSpec(memory_space=pltpu.VMEM)
-LIMIT = 20 * 1024 * 1024
+LIMIT = 16 * 1024 * 1024
 
 
 def swap(value, axis, distance):
@@ -145,13 +145,13 @@
     return lax.ppermute(value, axis, [(i, i ^ distance) for i in range(count)])
 
 
-def call(kernel, outs, *operands, flops=0, scratch=()):
+def call(kernel, outs, *operands, flops=0, scratch=(), loose=()):
     shapes = [jax.ShapeDtypeStruct(shape, dtype) for shape, dtype in outs]
     moved = sum(math.prod(x.shape) * x.dtype.itemsize for x in (*operands, *shapes))
     return pl.pallas_call(
         kernel,
         out_shape=shapes,
-        in_specs=[VMEM] * len(operands),
+        in_specs=[pl.BlockSpec(memory_space=pl.ANY) if i in loose else VMEM for i in range(len(operands))],
         out_specs=[VMEM] * len(shapes),
         scratch_shapes=scratch,
         compiler_params=pltpu.CompilerParams(vmem_limit_bytes=LIMIT),
@@ -169,6 +169,11 @@
 
 def transposed_times(left, right):
     return lax.dot_general(left, right, (((0,), (0,)), ((), ())), preferred_element_type=F32)
+
+
+def distances():
+    core = lax.axis_index("tp")
+    return 0, jnp.where(core == 0, 1, 3), jnp.where(core == 0, 3, 1), 2
 
 
 def norm_kernel(mine_ref, other_ref, gain_ref, gain_other_ref, *outs):
@@ -177,7 +182,7 @@
     mine, other = mine_ref[...].astype(F32), other_ref[...].astype(F32)
     squares = [jnp.sum(rows * rows, axis=1, keepdims=True) for rows in (mine, other)]
     scale = lax.rsqrt((squares[0] + squares[1]) / (4 * width) + 1e-06)
-    for d, out_ref in enumerate(outs):
+    for d, out_ref in zip(distances(), outs):
         chip = place ^ d
         columns = pl.ds(pl.multiple_of(chip % 2 * width, width), width)
 
@@ -230,33 +235,35 @@
     return ref[-16:, : ref.shape[0] - 16].astype(F32)[:1]
 
 
-def parts_kernel(
-    head,
-    got_1_ref,
-    got_1_other_ref,
-    got_3_ref,
-    got_3_other_ref,
-    even_ref,
-    even_other_ref,
-    weight_ref,
-    sent_1_ref,
-    sent_3_ref,
-    own_ref,
-    rows_ref,
-):
-    count = sent_1_ref.shape[0]
-    pairs = ((got_1_ref, got_1_other_ref), (got_3_ref, got_3_other_ref), (even_ref, even_other_ref))
-    for index, (mine_ref, other_ref) in enumerate(pairs):
-        join_rows(mine_ref, other_ref, rows_ref.at[index * count : (index + 1) * count])
+def own_kernel(head, even_ref, even_other_ref, weight_ref, own_ref, weight_out_ref, rows_ref):
+    weight_out_ref[...] = weight_ref[...]
+    join_rows(even_ref, even_other_ref, rows_ref)
     product = times(rows_ref[...], weight_ref[...])
-    pack(product[:count], sent_1_ref, head)
-    pack(product[count : 2 * count], sent_3_ref, head)
-    own_ref[...] = jnp.concatenate(split_heads(product[2 * count :], head), axis=1)
+    own_ref[...] = jnp.concatenate(split_heads(product, head), axis=1)
 
 
 def far_kernel(head, got_ref, got_other_ref, weight_ref, sent_ref, rows_ref):
     join_rows(got_ref, got_other_ref, rows_ref)
     pack(times(rows_ref[...], weight_ref[...]), sent_ref, head)
+
+
+def near_kernel(
+    head,
+    got_a_ref,
+    got_a_other_ref,
+    got_b_ref,
+    got_b_other_ref,
+    weight_ref,
+    sent_a_ref,
+    sent_b_ref,
+    rows_ref,
+):
+    count = sent_a_ref.shape[0]
+    join_rows(got_a_ref, got_b_other_ref, rows_ref.at[:count])
+    join_rows(got_b_ref, got_a_other_ref, rows_ref.at[count:])
+    product = times(rows_ref[...], weight_ref[...])
+    pack(product[:count], sent_a_ref, head)
+    pack(product[count:], sent_b_ref, head)
 
 
 def turn(value, cosine, sine):
@@ -277,11 +284,26 @@
         ).astype(BF16)
 
 
-def finish_kernel(own_ref, got_1_ref, got_2_ref, got_3_ref, docs_ref, cosine_ref, sine_ref, out_ref):
+def accumulate_kernel(
+    own_ref, got_ref, docs_ref, cosine_ref, sine_ref, out_ref, docs_out_ref, cosine_out_ref, sine_out_ref
+):
+    keys, values = unpack(got_ref, own_ref.shape[0])
+    width = keys.shape[1]
+    out_ref[:, :width] = own_ref[:, :width] + keys
+    out_ref[:, width:] = own_ref[:, width:] + values
+    for ref, copy_ref in (
+        (docs_ref, docs_out_ref),
+        (cosine_ref, cosine_out_ref),
+        (sine_ref, sine_out_ref),
+    ):
+        copy_ref[...] = ref[...]
+
+
+def finish_kernel(own_ref, got_a_ref, got_b_ref, docs_ref, cosine_ref, sine_ref, out_ref):
     rows = own_ref.shape[0]
     width = own_ref.shape[1] // 2
     keys, values = own_ref[:, :width], own_ref[:, width:]
-    for ref in (got_1_ref, got_2_ref, got_3_ref):
+    for ref in (got_a_ref, got_b_ref):
         more_keys, more_values = unpack(ref, rows)
         keys, values = keys + more_keys, values + more_values
     out_ref[:rows, :width] = turn(keys, cosine_ref[...], sine_ref[...]).astype(BF16)
@@ -304,45 +326,17 @@
     count = query_ref.shape[0] // groups
     scores = times_transposed(
         query_ref[group * count : (group + 1) * count], keys[:, group * head : (group + 1) * head]
-    ) * head ** (-0.5)
-    scores = scores.reshape(count // rows, rows, scores.shape[1])
-    return jnp.where(allowed[None], scores, -1e30).reshape(count, scores.shape[2])
-
-
-def first_attention_kernel(
-    head, query_ref, block_0_ref, block_1_ref, block_2_ref, mixed_ref, state_ref
-):
-    rows = block_0_ref.shape[0] - 16
-    width = block_0_ref.shape[1] // 2
-    blocks = (block_0_ref, block_1_ref, block_2_ref)
-    keys = jnp.concatenate([ref[:rows, :width] for ref in blocks], axis=0)
-    values = jnp.concatenate([ref[:rows, width:] for ref in blocks], axis=0)
-    allowed = jnp.concatenate(
-        [allowed_pairs(load_docs(block_0_ref), load_docs(ref), d) for d, ref in enumerate(blocks)],
-        axis=1,
-    )
-    groups = width // head
-    count = query_ref.shape[0] // groups
-    for group in range(groups):
-        scores = group_scores(query_ref, keys, allowed, head, group)
-        top = jnp.max(scores, axis=1, keepdims=True)
-        weights = jnp.exp(scores - top)
-        total = jnp.sum(weights, axis=1, keepdims=True)
-        place = slice(group * count, (group + 1) * count)
-        left = lax.broadcasted_iota(jnp.int32, (count, state_ref.shape[1]), 1) < 64
-        state_ref[place] = jnp.where(left, top, total)
-        mixed_ref[place] = times(
-            weights.astype(BF16), values[:, group * head : (group + 1) * head]
-        )
-
-
-def last_attention_kernel(
+    ).reshape(count // rows, rows, keys.shape[0])
+    return jnp.where(allowed[None], scores, -1e30).reshape(count, keys.shape[0])
+
+
+def attention_kernel(
     head,
     query_ref,
     block_0_ref,
-    block_3_ref,
-    mixed_ref,
-    state_ref,
+    block_a_ref,
+    block_b_ref,
+    block_c_ref,
     down_ref,
     back_ref,
     back_other_ref,
@@ -350,24 +344,25 @@
     low_ref,
     grad_ref,
 ):
-    rows = block_3_ref.shape[0] - 16
-    width = block_3_ref.shape[1] // 2
-    allowed = allowed_pairs(load_docs(block_0_ref), load_docs(block_3_ref), 3)
-    keys, values = block_3_ref[:rows, :width], block_3_ref[:rows, width:]
+    rows = block_0_ref.shape[0] - 16
+    width = block_0_ref.shape[1] // 2
+    blocks = (block_0_ref, block_a_ref, block_b_ref, block_c_ref)
+    keys = jnp.concatenate([ref[:rows, :width] for ref in blocks], axis=0)
+    values = jnp.concatenate([ref[:rows, width:] for ref in blocks], axis=0)
+    own_docs = load_docs(block_0_ref)
+    allowed = jnp.concatenate(
+        [allowed_pairs(own_docs, load_docs(ref), d) for d, ref in zip(distances(), blocks)], axis=1
+    )
     groups = width // head
     count = query_ref.shape[0] // groups
+    scale = head ** (-0.5) * math.log2(math.e)
+    ones = jnp.ones((len(blocks) * rows, head), BF16)
     for group in range(groups):
         scores = group_scores(query_ref, keys, allowed, head, group)
-        place = slice(group * count, (group + 1) * count)
-        before = state_ref[place, :1]
-        top = jnp.maximum(before, jnp.max(scores, axis=1, keepdims=True))
-        weights = jnp.exp(scores - top)
-        shrink = jnp.exp(before - top)
-        total = state_ref[place, 64:65] * shrink + jnp.sum(weights, axis=1, keepdims=True)
-        mixed = mixed_ref[place] * shrink + times(
-            weights.astype(BF16), values[:, group * head : (group + 1) * head]
-        )
-        mixed = (mixed / total).astype(BF16)
+        weights = jnp.exp2((scores - jnp.max(scores, axis=1, keepdims=True)) * scale)
+        group_values = jnp.concatenate([values[:, group * head : (group + 1) * head], ones], axis=1)
+        mixed = times(weights.astype(BF16), group_values)
+        mixed = (mixed[:, :head] / mixed[:, head:]).astype(BF16)
         for index in range(count // rows):
             column = group * count // rows * head + index * head
             out_ref[:, column : column + head] = mixed[index * rows : (index + 1) * rows]
@@ -401,11 +396,10 @@
     out_ref[...] = (own_ref[...].astype(F32) + got_ref[...].astype(F32)).astype(BF16)
 
 
-def square_sum_kernel(own_ref, got_ref, out_ref):
-    parity = lax.axis_index("ctx") % 2
-    own, got = [jnp.sum(jnp.square(ref[...].astype(F32))).reshape(1, 1) for ref in (own_ref, got_ref)]
-    total = jnp.where(parity == 0, own + got, got + own)
-    out_ref[...] = jnp.broadcast_to(total, out_ref.shape)
+def total_kernel(own_ref, got_ref, out_ref, square_ref):
+    add_kernel(own_ref, got_ref, out_ref)
+    squares = jnp.sum(jnp.square(out_ref[...].astype(F32))).reshape(1, 1)
+    square_ref[...] = jnp.broadcast_to(squares, square_ref.shape)
 
 
 def clip_kernel(ceiling, square_ref, other_ref, own_ref, got_ref, up_ref, down_ref):
@@ -443,9 +437,18 @@
         norm_kernel, [part] * 4, mine, swap(theirs, "tp", 1), gain, swap(gain, "tp", 1)
     )
 
-    got_1 = swap(slices[1], "ctx", 1)
-    got_3 = swap(slices[3], "ctx", 3)
-    got_2 = swap(slices[2], "ctx", 2)
+    def send_a(value):
+        return lax.ppermute(
+            value, ("ctx", "tp"), [(2 * a + t, 2 * (a ^ (3 if t else 1)) + t) for a in range(4) for t in range(2)]
+        )
+
+    def send_b(value):
+        return lax.ppermute(
+            value, ("ctx", "tp"), [(2 * a + t, 2 * (a ^ (1 if t else 3)) + t) for a in range(4) for t in range(2)]
+        )
+
+    even, slice_a, slice_b, slice_c = slices
+    got_a, got_b, got_c = send_a(slice_a), send_b(slice_b), swap(slice_c, "ctx", 2)
     part_flops = 2 * rows * slice_width * kv_width
     packed = ((rows, sent_width), BF16)
     summed = ((rows, kv_width), F32)
@@ -460,9 +463,12 @@
             *operands,
         )
 
-    def prepare(even, key_value_weight, queries, out_grad, adapt_up, doc_ids):
-        even_other = swap(even, "tp", 1)
-        weight = key_value_weight[0].reshape(slice_width, kv_width)
+    def prepare(key_value_weight):
+        return key_value_weight[0].reshape(slice_width, kv_width)
+
+    weight = step(prepare, key_value_weight)
+
+    def prepare_attention(queries, out_grad, adapt_up, doc_ids, weight):
         docs = doc_ids.astype(F32).reshape(1, rows)
         freqs = 1000000.0 ** (-jnp.arange(head // 2, dtype=F32) * 2.0 / head)
         positions = place * rows + jnp.arange(rows, dtype=jnp.int32)
@@ -484,72 +490,72 @@
             adapt_up[0],
             flops=2 * rows * local_width * rank,
         )
-        back_other = swap(back_part, "tp", 1)
-        return weight, docs, cosine, sine, query, back_part, back_other, even_other
-
-    weight, docs, cosine, sine, query, back_part, back_other, even_other = step(
-        prepare, slices[0], key_value_weight, queries, out_grad, adapt_up, doc_ids
-    )
-    got_1, got_3, even_other = lax.optimization_barrier((got_1, got_3, even_other))
-
-    def near_parts(got_1, got_3, even, even_other, weight):
-        return call(
-            functools.partial(parts_kernel, head),
-            [packed, packed, summed],
-            got_1,
-            swap(got_1, "tp", 1),
-            got_3,
-            swap(got_3, "tp", 1),
-            even,
-            even_other,
-            weight,
-            flops=3 * part_flops,
-            scratch=[pltpu.VMEM((3 * rows, slice_width), BF16)],
-        )
-
-    sent_1, sent_3, part_0 = step(near_parts, got_1, got_3, slices[0], even_other, weight)
-    arrived_1 = swap(sent_1, "ctx", 1)
-    arrived_3 = swap(sent_3, "ctx", 3)
-    got_2, part_0 = lax.optimization_barrier((got_2, part_0))
-    (sent_2,) = call(
-        functools.partial(far_kernel, head),
-        [packed],
-        got_2,
-        swap(got_2, "tp", 1),
+        return docs, cosine, sine, query, back_part, swap(back_part, "tp", 1)
+
+    docs, cosine, sine, query, back_part, back_other = step(
+        prepare_attention, queries, out_grad, adapt_up, doc_ids, weight
+    )
+    part_0, weight_near = call(
+        functools.partial(own_kernel, head),
+        [summed, (weight.shape, BF16)],
+        even,
+        swap(even, "tp", 1),
         weight,
         flops=part_flops,
         scratch=[pltpu.VMEM((rows, slice_width), BF16)],
     )
-    arrived_2 = swap(sent_2, "ctx", 2)
-    (block_0,) = call(
-        finish_kernel, [final], part_0, arrived_1, arrived_2, arrived_3, docs, cosine, sine
-    )
-    block_1 = swap(block_0, "ctx", 1)
-    block_2 = swap(block_0, "ctx", 2)
-    block_3 = swap(block_0, "ctx", 3)
-
-    state = ((head_count * rows, 128), F32)
-    mixed, state = call(
-        functools.partial(first_attention_kernel, head),
-        [state, state],
-        query,
-        block_0,
-        block_1,
-        block_2,
-        flops=12 * rows * rows * local_query,
-    )
+    got_c, part_0, docs = lax.optimization_barrier((got_c, part_0, docs))
+
+    def far_parts(got_c, weight):
+        return call(
+            functools.partial(far_kernel, head),
+            [packed],
+            got_c,
+            swap(got_c, "tp", 1),
+            weight,
+            flops=part_flops,
+            scratch=[pltpu.VMEM((rows, slice_width), BF16)],
+        )
+
+    (sent_c,) = step(far_parts, got_c, weight)
+    arrived_c = swap(sent_c, "ctx", 2)
+    got_a, got_b, sent_c = lax.optimization_barrier((got_a, got_b, sent_c))
+    sent_a, sent_b = call(
+        functools.partial(near_kernel, head),
+        [packed, packed],
+        got_a,
+        swap(got_a, "tp", 1),
+        got_b,
+        swap(got_b, "tp", 1),
+        weight_near,
+        flops=2 * part_flops,
+        scratch=[pltpu.VMEM((2 * rows, slice_width), BF16)],
+    )
+    arrived_a, arrived_b = send_a(sent_a), send_b(sent_b)
+    part_0, docs, cosine, sine = call(
+        accumulate_kernel,
+        [summed, ((1, rows), F32), ((rows, head), F32), ((rows, head), F32)],
+        part_0,
+        arrived_c,
+        docs,
+        cosine,
+        sine,
+    )
+    arrived_a, arrived_b, part_0 = lax.optimization_barrier((arrived_a, arrived_b, part_0))
+    (block_0,) = call(finish_kernel, [final], part_0, arrived_a, arrived_b, docs, cosine, sine)
+
     attended, low_part, down_part = call(
-        functools.partial(last_attention_kernel, head),
+        functools.partial(attention_kernel, head),
         [((rows, local_query), BF16), ((rows, rank), F32), ((rank, local_query), F32)],
         query,
         block_0,
-        block_3,
-        mixed,
-        state,
+        send_a(block_0),
+        send_b(block_0),
+        swap(block_0, "ctx", 2),
         adapt_down[0],
         back_part,
         back_other,
-        flops=4 * rows * rows * local_query,
+        flops=16 * rows * rows * local_query,
     )
     low_other = swap(low_part, "tp", 1)
     piece = (rank, (local_width + local_query) // 2)
@@ -570,13 +576,21 @@
         adapt_up[0],
         flops=2 * rows * rank * local_width,
     )
-    (pair_sum,) = call(add_kernel, [(piece, BF16)], own, swap(sent, "ctx", 1))
-    (total,) = call(add_kernel, [(piece, BF16)], pair_sum, swap(pair_sum, "ctx", 2))
+    got_sum, adapter_rows = lax.optimization_barrier((swap(sent, "ctx", 1), adapter_rows))
+    (pair_sum,) = call(add_kernel, [(piece, BF16)], own, got_sum)
+    total, squares = call(
+        total_kernel, [(piece, BF16), ((8, 128), F32)], pair_sum, swap(pair_sum, "ctx", 2)
+    )
     total_other = swap(total, "ctx", 1)
-    total_other, adapter_rows = lax.optimization_barrier((total_other, adapter_rows))
-    (squares,) = call(square_sum_kernel, [((8, 128), F32)], total, total_other)
-    squares = squares + swap(squares, "section", 1)
-    squares = squares + swap(squares, "section", 2)
+    squares = squares + swap(squares, "tp", 1)
+    beside = lax.ppermute(
+        squares,
+        ("section", "tp"),
+        [(2 * i + t, 2 * (i ^ (2 if t else 1)) + t) for i in range(4) for t in range(2)],
+    )
+    across = swap(squares, "section", 3)
+    squares = jnp.where(core == 0, squares + across + beside, beside)
+    squares = squares + swap(squares, "ctx", 1)
     ceiling = 0.5 * math.sqrt(lax.axis_size("section") * rank * (local_query + local_width) * 2)
     grad_up, grad_down = call(
         functools.partial(clip_kernel, ceiling),

time: 103 us -> 99.3 us (0.964)
  waiting for transfers between devices: 54.4 us -> 47.1 us
  starting transfers between devices: 23.5 us -> 26.8 us
    ppermute x23 -> x18, waiting for transfers between devices: 54.4 us -> 44.5 us  [swap(): return lax.ppermute(value, axis, [(i, i ^ distance) for i in range(count)])]
    ppermute x0 -> x7, starting transfers between devices: none -> 7.54 us  [the longest x3 4.3 us: send_b(): lax.ppermute(value, ('ctx', 'tp'), [(2 * a + t, 2 * (a ^ (1 if t else 3))...]
    ppermute x23 -> x18, starting transfers between devices: 23.5 us -> 19.2 us  [swap(): return lax.ppermute(value, axis, [(i, i ^ distance) for i in range(count)])]
    ppermute x0 -> x7, waiting for transfers between devices: none -> 2.65 us  [the longest x3 2.03 us: send_a(): lax.ppermute(value, ('ctx', 'tp'), [(2 * a + t, 2 * (a ^ (3 if t else 1))...]
    unnamed x10 -> x20, local copies, waits for them, and re-layouts: 0.02 us -> 2.16 us
    squeeze x1, local copies, waits for them, and re-layouts: 4.11 us -> 2.75 us  [prepare(): return key_value_weight[0].reshape(slice_width, kv_width)]
  transfers between devices with their start and end apart: 23 -> 25, of which waited for: 17 -> 14; matrix products, arithmetic and copies ran while one was open for 5% -> 4% of each run, Pallas kernels for 10% -> 10%
where the time goes in v4:
time: 99.3 us; the launch traced here: 98.9 us
  waiting for transfers between devices  47.1 us (47%)
  starting transfers between devices  26.8 us (27%)
  Pallas kernels  16.6 us (17%)
  local copies, waits for them, and re-layouts  6.44 us (6%)
  other arithmetic  1.08 us (1%)
    ppermute x18, waiting for transfers between devices, swap(): return lax.ppermute(value, axis, [(i, i ^ distance) for i in range(count)])  44.5 us
    ppermute x18, starting transfers between devices, swap(): return lax.ppermute(value, axis, [(i, i ^ distance) for i in range(count)])  19.2 us
    pallas_call x14, Pallas kernels, call(): pl.pallas_call(kernel, out_shape=shapes, in_specs=[pl.BlockSpec(memory_sp...  16.6 us
    ppermute x3, starting transfers between devices, send_b(): lax.ppermute(value, ('ctx', 'tp'), [(2 * a + t, 2 * (a ^ (1 if t else 3))...  4.3 us
    squeeze x1, local copies, waits for them, and re-layouts, prepare(): return key_value_weight[0].reshape(slice_width, kv_width)  2.75 us
    unnamed x20, local copies, waits for them, and re-layouts  2.16 us
    ppermute x3, waiting for transfers between devices, send_a(): lax.ppermute(value, ('ctx', 'tp'), [(2 * a + t, 2 * (a ^ (3 if t else 1))...  2.03 us
  transfers between devices with their start and end apart: 25, of which 14 were waited for; matrix products, arithmetic and copies ran while one was open for 4% of the time, Pallas kernels for 10%

profile of v4, /device:TPU:0, one launch (start us, length us, event | category | flops | bytes accessed | tf_op | source)
XLA Modules:
  0.0 98.9 jit_solution(3566515719062816009)
XLA Ops:
  0.7 1.4 %dynamic-slice_bitcast_fusion = (bf16[64,4096]{1,0:T(8,128)(2,1)S(1)}, bf16[64,4096]{1,0:T(8,128)(2,1)S(1)}) fusion(bf16[1,128,4096]{2,1,0:T(8,128)(2,1)} %param.14, s32[]{:T(128)S(6)} %select_n.15, s32[]{:T(128)S(6)} %select_n.14), kind=kLoop, calls=%fused_computation.9 | loop fusion | bytes 2097160 | tf_op jit(solution)/shard_map/dynamic_slice | solution.py:434
  2.7 1.5 %collective-permute-done.3.gain_other_ref = bf16[1,4096]{1,0:T(2,128)(2,1)S(1)} collective-permute-done((bf16[1,4096]{1,0:T(2,128)(2,1)S(1)}, bf16[1,4096]{1,0:T(2,128)(2,1)S(1)}, u32[]{:S(2)}, u32[]{:S(2)}) %collective-permute-start.3) | collective-permute-done | bytes 8224 | tf_op jit(solution)/shard_map/ppermute | solution.py:145
  4.2 1.5 %shard_map.117 = (bf16[64,2048]{1,0:T(8,128)(2,1)S(1)}, bf16[64,2048]{1,0:T(8,128)(2,1)}, bf16[64,2048]{1,0:T(8,128)(2,1)}, bf16[64,2048]{1,0:T(8,128)(2,1)}) custom-call(bf16[64,4096]{1,0:T(8,128)(2,1)S(1)} %get-tuple-element.118.mine_ref, bf16[64,4096]{1,0:T(8,128)(2,1)S(1)} %collective-permute-done.2.other_ref, bf16[1,4096]{1,0:T(2,128)(2,1)S(1)} %copy-done, ...), custom_call_target="tpu_custom_call" | custom-call | bytes 2113536 | tf_op jit(solution)/shard_map/pallas_call | solution.py:151
  6.0 3.7 %collective-permute-start.6 = (bf16[64,2048]{1,0:T(8,128)(2,1)}, bf16[64,2048]{1,0:T(8,128)(2,1)}, u32[]{:S(2)}, u32[]{:S(2)}) collective-permute-start(bf16[64,2048]{1,0:T(8,128)(2,1)} %get-tuple-element.72), channel_id=1, source_target_pairs={{0,4},{2,6},{4,0},{6,2},{1,5},{3,7},{5,1},{7,3},{8,12},{10,14},{12... | collective-permute-start | bytes 786440 | tf_op jit(solution)/shard_map/ppermute | solution.py:145
  9.8 1.6 %collective-permute-start.4 = (bf16[64,2048]{1,0:T(8,128)(2,1)}, bf16[64,2048]{1,0:T(8,128)(2,1)S(1)}, u32[]{:S(2)}, u32[]{:S(2)}) collective-permute-start(bf16[64,2048]{1,0:T(8,128)(2,1)} %get-tuple-element.70), channel_id=1, source_target_pairs={{0,2},{1,7},{2,0},{3,5},{4,6},{5,3},{6,4},{7,1},{8,10},{9,15},{10,... | collective-permute-start | bytes 786440 | tf_op jit(solution)/shard_map/ppermute | solution.py:441
  11.4 3.4 %conditional.3 = (f32[1,128]{1,0:T(1,128)S(1)}, f32[128,128]{1,0:T(8,128)}, f32[128,128]{1,0:T(8,128)}, bf16[2048,128]{1,0:T(8,128)(2,1)S(1)}, f32[128,16]{1,0:T(8,128)}, /*index=5*/f32[128,16]{1,0:T(8,128)}) conditional(s32[]{:T(128)} %convert_element_type.15, () %tuple.32, (s32[128]{0:T(128)S(1)}, s32[]{:T(128)}, ...), branch_computations={%region_0.0_spmd, %region_1.0_spmd} | conditional | flops 16826880 | bytes 3779176 | solution.py:459
  15.6 2.7 %conditional.4 = (bf16[2048,512]{1,0:T(8,128)(2,1)S(1)}) conditional(s32[]{:T(128)} %convert_element_type.15, () %tuple.35, (bf16[1,2048,2,2,128]{4,3,2,1,0:T(2,128)(2,1)}) %tuple.42), branch_computations={%region_2.0_spmd, %region_3.0_spmd} | conditional | bytes 4194312 | solution.py:459
  15.6 2.7 %squeeze.19 = bf16[2048,512]{1,0:T(8,128)(2,1)S(1)} reshape(bf16[1,2048,2,2,128]{4,3,2,1,0:T(2,128)(2,1)} %get-tuple-element.111) | data formatting | bytes 4194304 | tf_op jit(solution)/shard_map/cond/branch_1_fun/reshape;cond/branch_1_fun/squeeze | solution.py:467
  18.3 1.3 %copy-done.2 = bf16[2048,512]{1,0:T(8,128)(2,1)} copy-done((bf16[2048,512]{1,0:T(8,128)(2,1)}, bf16[2048,512]{1,0:T(8,128)(2,1)S(1)}, u32[]{:S(2)}) %copy-start.2) | copy-done | bytes 2097176
  19.7 2.2 %shard_map.118 = (f32[128,512]{1,0:T(8,128)S(1)}, bf16[2048,512]{1,0:T(8,128)(2,1)S(1)}) custom-call(bf16[64,2048]{1,0:T(8,128)(2,1)S(1)} %get-tuple-element.73.even_ref, bf16[64,2048]{1,0:T(8,128)(2,1)S(1)} %collective-permute-done.7.even_other_ref, bf16[2048,512]{1,0:T(8,128)(2,1)} %copy-done.2), custom_call_target="tpu_custom_call" | custom-call | flops 268435456 | bytes 4980736 | tf_op jit(solution)/shard_map/pallas_call | solution.py:151
  21.8 5.3 %collective-permute-done.6 = bf16[64,2048]{1,0:T(8,128)(2,1)} collective-permute-done((bf16[64,2048]{1,0:T(8,128)(2,1)}, bf16[64,2048]{1,0:T(8,128)(2,1)}, u32[]{:S(2)}, u32[]{:S(2)}) %collective-permute-start.6) | collective-permute-done | bytes 262176 | tf_op jit(solution)/shard_map/ppermute | solution.py:145
  27.2 4.6 %conditional.5 = (bf16[128,768]{1,0:T(8,128)(2,1)}) conditional(s32[]{:T(128)} %convert_element_type.15, () %tuple.34, (bf16[64,2048]{1,0:T(8,128)(2,1)}, bf16[2048,512]{1,0:T(8,128)(2,1)}) %tuple.53), branch_computations={%region_4.0_spmd, %region_5.0_spmd} | conditional | flops 268435456 | bytes 3866672 | solution.py:459
  27.2 1.7 %collective-permute-done.got_other_ref = bf16[64,2048]{1,0:T(8,128)(2,1)S(1)} collective-permute-done((bf16[64,2048]{1,0:T(8,128)(2,1)}, bf16[64,2048]{1,0:T(8,128)(2,1)S(1)}, u32[]{:S(2)}, u32[]{:S(2)}) %collective-permute-start) | collective-permute-done | bytes 262176 | tf_op jit(solution)/shard_map/cond/branch_1_fun/ppermute | solution.py:145
  28.9 2.8 %branch_1_fun.5 = bf16[128,768]{1,0:T(8,128)(2,1)} custom-call(bf16[64,2048]{1,0:T(8,128)(2,1)} %get-tuple-element.26.got_ref, bf16[64,2048]{1,0:T(8,128)(2,1)S(1)} %collective-permute-done.got_other_ref, bf16[2048,512]{1,0:T(8,128)(2,1)} %get-tuple-element.27.weight_ref), custom_call_target="tpu_custom_call" | custom-call | flops 268435456 | bytes 2818048 | tf_op jit(solution)/shard_map/cond/branch_1_fun/pallas_call | solution.py:151
  32.3 4.6 %collective-permute-start.12 = (bf16[128,768]{1,0:T(8,128)(2,1)}, bf16[128,768]{1,0:T(8,128)(2,1)S(1)}, u32[]{:S(2)}, u32[]{:S(2)}) collective-permute-start(bf16[128,768]{1,0:T(8,128)(2,1)} %get-tuple-element.132), channel_id=1, source_target_pairs={{0,4},{2,6},{4,0},{6,2},{1,5},{3,7},{5,1},{7,3},{8,12},{10,14},{12... | collective-permute-start | bytes 589832 | tf_op jit(solution)/shard_map/ppermute | solution.py:145
  37.8 2.7 %collective-permute-start.11 = (bf16[128,768]{1,0:T(8,128)(2,1)S(1)}, bf16[128,768]{1,0:T(8,128)(2,1)S(1)}, u32[]{:S(2)}, u32[]{:S(2)}) collective-permute-start(bf16[128,768]{1,0:T(8,128)(2,1)S(1)} %get-tuple-element.81), channel_id=1, source_target_pairs={{0,6},{1,3},{2,4},{3,1},{4,2},{5,7},{6,0},{7,5},{8,14},{9,11},{10,... | collective-permute-start | bytes 589832 | tf_op jit(solution)/shard_map/ppermute | solution.py:446
  40.5 9.9 %collective-permute-done.12.got_ref = bf16[128,768]{1,0:T(8,128)(2,1)S(1)} collective-permute-done((bf16[128,768]{1,0:T(8,128)(2,1)}, bf16[128,768]{1,0:T(8,128)(2,1)S(1)}, u32[]{:S(2)}, u32[]{:S(2)}) %collective-permute-start.12) | collective-permute-done | bytes 196640 | tf_op jit(solution)/shard_map/ppermute | solution.py:145
  51.3 2.0 %collective-permute-done.10.got_a_ref = bf16[128,768]{1,0:T(8,128)(2,1)S(1)} collective-permute-done((bf16[128,768]{1,0:T(8,128)(2,1)S(1)}, bf16[128,768]{1,0:T(8,128)(2,1)S(1)}, u32[]{:S(2)}, u32[]{:S(2)}) %collective-permute-start.10) | collective-permute-done | bytes 196640 | tf_op jit(solution)/shard_map/ppermute | solution.py:441
  53.4 3.0 %collective-permute-start.15 = (bf16[144,512]{1,0:T(8,128)(2,1)S(1)}, bf16[144,512]{1,0:T(8,128)(2,1)S(1)}, u32[]{:S(2)}, u32[]{:S(2)}) collective-permute-start(bf16[144,512]{1,0:T(8,128)(2,1)S(1)} %shard_map.121.block_0_ref), channel_id=1, source_target_pairs={{0,4},{2,6},{4,0},{6,2},{1,5},{3,7},{5,1},{7,3},{8,12},{10,14},{12... | collective-permute-start | bytes 442376 | tf_op jit(solution)/shard_map/ppermute | solution.py:145
  56.4 1.6 %collective-permute-start.14 = (bf16[144,512]{1,0:T(8,128)(2,1)S(1)}, bf16[144,512]{1,0:T(8,128)(2,1)S(1)}, u32[]{:S(2)}, u32[]{:S(2)}) collective-permute-start(bf16[144,512]{1,0:T(8,128)(2,1)S(1)} %shard_map.121.block_0_ref), channel_id=1, source_target_pairs={{0,6},{1,3},{2,4},{3,1},{4,2},{5,7},{6,0},{7,5},{8,14},{9,11},{10,... | collective-permute-start | bytes 442376 | tf_op jit(solution)/shard_map/ppermute | solution.py:446
  58.0 9.5 %collective-permute-done.15.block_c_ref = bf16[144,512]{1,0:T(8,128)(2,1)S(1)} collective-permute-done((bf16[144,512]{1,0:T(8,128)(2,1)S(1)}, bf16[144,512]{1,0:T(8,128)(2,1)S(1)}, u32[]{:S(2)}, u32[]{:S(2)}) %collective-permute-start.15) | collective-permute-done | bytes 147488 | tf_op jit(solution)/shard_map/ppermute | solution.py:145
  67.5 3.6 %shard_map.122 = (bf16[128,2048]{1,0:T(8,128)(2,1)}, f32[128,16]{1,0:T(8,128)S(1)}, f32[16,2048]{1,0:T(8,128)S(1)}) custom-call(bf16[2048,128]{1,0:T(8,128)(2,1)S(1)} %copy-done.7, bf16[144,512]{1,0:T(8,128)(2,1)S(1)} %shard_map.121.block_0_ref, bf16[144,512]{1,0:T(8,128)(2,1)S(1)} %collective-permute-done.13.block_a_ref, ...), custom_call_target="tpu_custom_call" | custom-call | flops 536870912 | bytes 1859584 | tf_op jit(solution)/shard_map/pallas_call | solution.py:151
  71.1 1.3 %collective-permute-done.16.low_other_ref = f32[128,16]{1,0:T(8,128)S(1)} collective-permute-done((f32[128,16]{1,0:T(8,128)S(1)}, f32[128,16]{1,0:T(8,128)S(1)}, u32[]{:S(2)}, u32[]{:S(2)}) %collective-permute-start.16) | collective-permute-done | bytes 8224 | tf_op jit(solution)/shard_map/ppermute | solution.py:145
  72.6 2.7 %collective-permute-start.17 = (bf16[16,3072]{1,0:T(8,128)(2,1)S(1)}, bf16[16,3072]{1,0:T(8,128)(2,1)S(1)}, u32[]{:S(2)}, u32[]{:S(2)}) collective-permute-start(bf16[16,3072]{1,0:T(8,128)(2,1)S(1)} %get-tuple-element.98), channel_id=1, source_target_pairs={{0,2},{2,0},{4,6},{6,4},{1,3},{3,1},{5,7},{7,5},{8,10},{10,8},{12,... | collective-permute-start | bytes 294920 | tf_op jit(solution)/shard_map/ppermute | solution.py:145
  75.3 1.4 %shard_map.124 = bf16[128,4096]{1,0:T(8,128)(2,1)} custom-call(f32[128,16]{1,0:T(8,128)S(1)} %get-tuple-element.96.low_ref, f32[128,16]{1,0:T(8,128)S(1)} %collective-permute-done.16.low_other_ref, bf16[16,4096]{1,0:T(8,128)(2,1)S(1)} %bitcast.25), custom_call_target="tpu_custom_call" | custom-call | flops 16777216 | bytes 1196032 | tf_op jit(solution)/shard_map/pallas_call | solution.py:151
  76.7 1.7 %collective-permute-done.17.got_ref = bf16[16,3072]{1,0:T(8,128)(2,1)S(1)} collective-permute-done((bf16[16,3072]{1,0:T(8,128)(2,1)S(1)}, bf16[16,3072]{1,0:T(8,128)(2,1)S(1)}, u32[]{:S(2)}, u32[]{:S(2)}) %collective-permute-start.17) | collective-permute-done | bytes 98336 | tf_op jit(solution)/shard_map/ppermute | solution.py:145
  78.4 2.1 %collective-permute-start.18 = (bf16[16,3072]{1,0:T(8,128)(2,1)S(1)}, bf16[16,3072]{1,0:T(8,128)(2,1)S(1)}, u32[]{:S(2)}, u32[]{:S(2)}) collective-permute-start(bf16[16,3072]{1,0:T(8,128)(2,1)S(1)} %shard_map.125.own_ref), channel_id=1, source_target_pairs={{0,4},{2,6},{4,0},{6,2},{1,5},{3,7},{5,1},{7,3},{8,12},{10,14},{12... | collective-permute-start | bytes 294920 | tf_op jit(solution)/shard_map/ppermute | solution.py:145
  80.5 5.3 %collective-permute-done.18.got_ref = bf16[16,3072]{1,0:T(8,128)(2,1)S(1)} collective-permute-done((bf16[16,3072]{1,0:T(8,128)(2,1)S(1)}, bf16[16,3072]{1,0:T(8,128)(2,1)S(1)}, u32[]{:S(2)}, u32[]{:S(2)}) %collective-permute-start.18) | collective-permute-done | bytes 98336 | tf_op jit(solution)/shard_map/ppermute | solution.py:145
  87.3 1.5 %collective-permute-start.21 = (f32[8,128]{1,0:T(8,128)S(1)}, f32[8,128]{1,0:T(8,128)S(1)}, u32[]{:S(2)}, u32[]{:S(2)}) collective-permute-start(f32[8,128]{1,0:T(8,128)S(1)} %add.30), channel_id=1, source_target_pairs={{0,8},{1,17},{8,0},{9,25},{16,24},{17,1},{24,16},{25,9},{2,10},{3,... | collective-permute-start | bytes 12296 | tf_op jit(solution)/shard_map/ppermute | solution.py:586
  88.8 1.5 %collective-permute-start.20 = (f32[8,128]{1,0:T(8,128)S(1)}, f32[8,128]{1,0:T(8,128)S(1)}, u32[]{:S(2)}, u32[]{:S(2)}) collective-permute-start(f32[8,128]{1,0:T(8,128)S(1)} %add.30), channel_id=1, source_target_pairs={{0,24},{8,16},{16,8},{24,0},{1,25},{9,17},{17,9},{25,1},{2,26},{10... | collective-permute-start | bytes 12296 | tf_op jit(solution)/shard_map/ppermute | solution.py:145
  90.9 2.4 %collective-permute-done.20 = f32[8,128]{1,0:T(8,128)S(1)} collective-permute-done((f32[8,128]{1,0:T(8,128)S(1)}, f32[8,128]{1,0:T(8,128)S(1)}, u32[]{:S(2)}, u32[]{:S(2)}) %collective-permute-start.20) | collective-permute-done | bytes 4128 | tf_op jit(solution)/shard_map/ppermute | solution.py:145
  93.3 3.6 %collective-permute-done.22 = f32[8,128]{1,0:T(8,128)S(1)} collective-permute-done((f32[8,128]{1,0:T(8,128)S(1)}, f32[8,128]{1,0:T(8,128)S(1)}, u32[]{:S(2)}, u32[]{:S(2)}) %collective-permute-start.22) | collective-permute-done | bytes 4128 | tf_op jit(solution)/shard_map/ppermute | solution.py:145
  (66 shorter events, 12.0 us)
Async XLA Ops:
  0.6 10.7 %copy-start.3 = (bf16[1,128,4096]{2,1,0:T(8,128)(2,1)S(1)}, bf16[1,128,4096]{2,1,0:T(8,128)(2,1)}, u32[]{:S(2)}) copy-start(bf16[1,128,4096]{2,1,0:T(8,128)(2,1)} %param.20) | copy-start | bytes 3145732
  0.7 10.7 %copy-start.5 = (bf16[1,16,4096]{2,1,0:T(8,128)(2,1)S(1)}, bf16[1,16,4096]{2,1,0:T(8,128)(2,1)}, u32[]{:S(2)}) copy-start(bf16[1,16,4096]{2,1,0:T(8,128)(2,1)} %param.19) | copy-start | bytes 393220
  0.7 10.7 %copy-start.9 = (s32[128]{0:T(128)S(1)}, s32[128]{0:T(128)}, u32[]{:S(2)}) copy-start(s32[128]{0:T(128)} %param.21) | copy-start | bytes 1540
  0.7 10.7 %copy-start.8 = (bf16[1,128,16,128]{3,2,1,0:T(8,128)(2,1)S(1)}, bf16[1,128,16,128]{3,2,1,0:T(8,128)(2,1)}, u32[]{:S(2)}) copy-start(bf16[1,128,16,128]{3,2,1,0:T(8,128)(2,1)} %param.16) | copy-start | bytes 1572868
  2.1 2.1 %collective-permute-start.2 = (bf16[64,4096]{1,0:T(8,128)(2,1)S(1)}, bf16[64,4096]{1,0:T(8,128)(2,1)S(1)}, u32[]{:S(2)}, u32[]{:S(2)}) collective-permute-start(bf16[64,4096]{1,0:T(8,128)(2,1)S(1)} %get-tuple-element.117), channel_id=1, source_target_pairs={{0,1},{1,0},{2,3},{3,2},{4,5},{5,4},{6,7},{7,6},{8,9},{9,8},{10,11... | collective-permute-start | bytes 1572872 | tf_op jit(solution)/shard_map/ppermute | solution.py:145
  2.6 1.6 %collective-permute-start.3 = (bf16[1,4096]{1,0:T(2,128)(2,1)S(1)}, bf16[1,4096]{1,0:T(2,128)(2,1)S(1)}, u32[]{:S(2)}, u32[]{:S(2)}) collective-permute-start(bf16[1,4096]{1,0:T(2,128)(2,1)S(1)} %copy-done), channel_id=1, source_target_pairs={{0,1},{1,0},{2,3},{3,2},{4,5},{5,4},{6,7},{7,6},{8,9},{9,8},{10,11... | collective-permute-start | bytes 24584 | tf_op jit(solution)/shard_map/ppermute | solution.py:145
  5.6 14.0 %collective-permute-start.7 = (bf16[64,2048]{1,0:T(8,128)(2,1)S(1)}, bf16[64,2048]{1,0:T(8,128)(2,1)S(1)}, u32[]{:S(2)}, u32[]{:S(2)}) collective-permute-start(bf16[64,2048]{1,0:T(8,128)(2,1)S(1)} %get-tuple-element.73.even_ref), channel_id=1, source_target_pairs={{0,1},{1,0},{2,3},{3,2},{4,5},{5,4},{6,7},{7,6},{8,9},{9,8},{10,11... | collective-permute-start | bytes 786440 | tf_op jit(solution)/shard_map/ppermute | solution.py:145
  6.0 21.1 %collective-permute-start.6 = (bf16[64,2048]{1,0:T(8,128)(2,1)}, bf16[64,2048]{1,0:T(8,128)(2,1)}, u32[]{:S(2)}, u32[]{:S(2)}) collective-permute-start(bf16[64,2048]{1,0:T(8,128)(2,1)} %get-tuple-element.72), channel_id=1, source_target_pairs={{0,4},{2,6},{4,0},{6,2},{1,5},{3,7},{5,1},{7,3},{8,12},{10,14},{12... | collective-permute-start | bytes 786440 | tf_op jit(solution)/shard_map/ppermute | solution.py:145
  9.8 22.0 %collective-permute-start.4 = (bf16[64,2048]{1,0:T(8,128)(2,1)}, bf16[64,2048]{1,0:T(8,128)(2,1)S(1)}, u32[]{:S(2)}, u32[]{:S(2)}) collective-permute-start(bf16[64,2048]{1,0:T(8,128)(2,1)} %get-tuple-element.70), channel_id=1, source_target_pairs={{0,2},{1,7},{2,0},{3,5},{4,6},{5,3},{6,4},{7,1},{8,10},{9,15},{10,... | collective-permute-start | bytes 786440 | tf_op jit(solution)/shard_map/ppermute | solution.py:441
  11.3 20.4 %collective-permute-start.5 = (bf16[64,2048]{1,0:T(8,128)(2,1)}, bf16[64,2048]{1,0:T(8,128)(2,1)S(1)}, u32[]{:S(2)}, u32[]{:S(2)}) collective-permute-start(bf16[64,2048]{1,0:T(8,128)(2,1)} %get-tuple-element.71), channel_id=1, source_target_pairs={{0,6},{1,3},{2,4},{3,1},{4,2},{5,7},{6,0},{7,5},{8,14},{9,11},{10,... | collective-permute-start | bytes 786440 | tf_op jit(solution)/shard_map/ppermute | solution.py:446
  12.4 2.4 %collective-permute-start.1 = (f32[128,16]{1,0:T(8,128)}, f32[128,16]{1,0:T(8,128)}, u32[]{:S(2)}, u32[]{:S(2)}) collective-permute-start(f32[128,16]{1,0:T(8,128)} %branch_1_fun.4), channel_id=1, source_target_pairs={{0,1},{1,0},{2,3},{3,2},{4,5},{5,4},{6,7},{7,6},{8,9},{9,8},{10,11... | collective-permute-start | bytes 24584 | tf_op jit(solution)/shard_map/cond/branch_1_fun/ppermute | solution.py:145
  27.2 1.7 %collective-permute-start = (bf16[64,2048]{1,0:T(8,128)(2,1)}, bf16[64,2048]{1,0:T(8,128)(2,1)S(1)}, u32[]{:S(2)}, u32[]{:S(2)}) collective-permute-start(bf16[64,2048]{1,0:T(8,128)(2,1)} %get-tuple-element.26.got_ref), channel_id=1, source_target_pairs={{0,1},{1,0},{2,3},{3,2},{4,5},{5,4},{6,7},{7,6},{8,9},{9,8},{10,11... | collective-permute-start | bytes 786440 | tf_op jit(solution)/shard_map/cond/branch_1_fun/ppermute | solution.py:145
  31.7 5.1 %collective-permute-start.8 = (bf16[64,2048]{1,0:T(8,128)(2,1)S(1)}, bf16[64,2048]{1,0:T(8,128)(2,1)S(1)}, u32[]{:S(2)}, u32[]{:S(2)}) collective-permute-start(bf16[64,2048]{1,0:T(8,128)(2,1)S(1)} %collective-permute-done.4.got_a_ref), channel_id=1, source_target_pairs={{0,1},{1,0},{2,3},{3,2},{4,5},{5,4},{6,7},{7,6},{8,9},{9,8},{10,11... | collective-permute-start | bytes 786440 | tf_op jit(solution)/shard_map/ppermute | solution.py:145
  31.9 4.9 %collective-permute-start.9 = (bf16[64,2048]{1,0:T(8,128)(2,1)S(1)}, bf16[64,2048]{1,0:T(8,128)(2,1)S(1)}, u32[]{:S(2)}, u32[]{:S(2)}) collective-permute-start(bf16[64,2048]{1,0:T(8,128)(2,1)S(1)} %collective-permute-done.5.got_b_ref), channel_id=1, source_target_pairs={{0,1},{1,0},{2,3},{3,2},{4,5},{5,4},{6,7},{7,6},{8,9},{9,8},{10,11... | collective-permute-start | bytes 786440 | tf_op jit(solution)/shard_map/ppermute | solution.py:145
  32.3 18.1 %collective-permute-start.12 = (bf16[128,768]{1,0:T(8,128)(2,1)}, bf16[128,768]{1,0:T(8,128)(2,1)S(1)}, u32[]{:S(2)}, u32[]{:S(2)}) collective-permute-start(bf16[128,768]{1,0:T(8,128)(2,1)} %get-tuple-element.132), channel_id=1, source_target_pairs={{0,4},{2,6},{4,0},{6,2},{1,5},{3,7},{5,1},{7,3},{8,12},{10,14},{12... | collective-permute-start | bytes 589832 | tf_op jit(solution)/shard_map/ppermute | solution.py:145
  36.9 30.6 %copy-start.1 = (bf16[1,16,2048]{2,1,0:T(8,128)(2,1)S(1)}, bf16[1,16,2048]{2,1,0:T(8,128)(2,1)}, u32[]{:S(2)}) copy-start(bf16[1,16,2048]{2,1,0:T(8,128)(2,1)} %param.18) | copy-start | bytes 196612
  36.9 30.6 %copy-start.7 = (bf16[2048,128]{1,0:T(8,128)(2,1)S(1)}, bf16[2048,128]{1,0:T(8,128)(2,1)}, u32[]{:S(2)}) copy-start(bf16[2048,128]{1,0:T(8,128)(2,1)} %copy-done.6) | copy-start | bytes 1572868
  37.6 34.7 %copy-start.4 = (bf16[1,128,4096]{2,1,0:T(8,128)(2,1)S(1)}, bf16[1,128,4096]{2,1,0:T(8,128)(2,1)}, u32[]{:S(2)}) copy-start(bf16[1,128,4096]{2,1,0:T(8,128)(2,1)} %param.20) | copy-start | bytes 3145732
  37.6 15.7 %collective-permute-start.10 = (bf16[128,768]{1,0:T(8,128)(2,1)S(1)}, bf16[128,768]{1,0:T(8,128)(2,1)S(1)}, u32[]{:S(2)}, u32[]{:S(2)}) collective-permute-start(bf16[128,768]{1,0:T(8,128)(2,1)S(1)} %get-tuple-element.80), channel_id=1, source_target_pairs={{0,2},{1,7},{2,0},{3,5},{4,6},{5,3},{6,4},{7,1},{8,10},{9,15},{10,... | collective-permute-start | bytes 589832 | tf_op jit(solution)/shard_map/ppermute | solution.py:441
  37.8 15.5 %collective-permute-start.11 = (bf16[128,768]{1,0:T(8,128)(2,1)S(1)}, bf16[128,768]{1,0:T(8,128)(2,1)S(1)}, u32[]{:S(2)}, u32[]{:S(2)}) collective-permute-start(bf16[128,768]{1,0:T(8,128)(2,1)S(1)} %get-tuple-element.81), channel_id=1, source_target_pairs={{0,6},{1,3},{2,4},{3,1},{4,2},{5,7},{6,0},{7,5},{8,14},{9,11},{10,... | collective-permute-start | bytes 589832 | tf_op jit(solution)/shard_map/ppermute | solution.py:446
  53.4 14.0 %collective-permute-start.15 = (bf16[144,512]{1,0:T(8,128)(2,1)S(1)}, bf16[144,512]{1,0:T(8,128)(2,1)S(1)}, u32[]{:S(2)}, u32[]{:S(2)}) collective-permute-start(bf16[144,512]{1,0:T(8,128)(2,1)S(1)} %shard_map.121.block_0_ref), channel_id=1, source_target_pairs={{0,4},{2,6},{4,0},{6,2},{1,5},{3,7},{5,1},{7,3},{8,12},{10,14},{12... | collective-permute-start | bytes 442376 | tf_op jit(solution)/shard_map/ppermute | solution.py:145
  56.4 11.0 %collective-permute-start.14 = (bf16[144,512]{1,0:T(8,128)(2,1)S(1)}, bf16[144,512]{1,0:T(8,128)(2,1)S(1)}, u32[]{:S(2)}, u32[]{:S(2)}) collective-permute-start(bf16[144,512]{1,0:T(8,128)(2,1)S(1)} %shard_map.121.block_0_ref), channel_id=1, source_target_pairs={{0,6},{1,3},{2,4},{3,1},{4,2},{5,7},{6,0},{7,5},{8,14},{9,11},{10,... | collective-permute-start | bytes 442376 | tf_op jit(solution)/shard_map/ppermute | solution.py:446
  58.0 9.5 %collective-permute-start.13 = (bf16[144,512]{1,0:T(8,128)(2,1)S(1)}, bf16[144,512]{1,0:T(8,128)(2,1)S(1)}, u32[]{:S(2)}, u32[]{:S(2)}) collective-permute-start(bf16[144,512]{1,0:T(8,128)(2,1)S(1)} %shard_map.121.block_0_ref), channel_id=1, source_target_pairs={{0,2},{1,7},{2,0},{3,5},{4,6},{5,3},{6,4},{7,1},{8,10},{9,15},{10,... | collective-permute-start | bytes 442376 | tf_op jit(solution)/shard_map/ppermute | solution.py:441
  71.1 1.3 %collective-permute-start.16 = (f32[128,16]{1,0:T(8,128)S(1)}, f32[128,16]{1,0:T(8,128)S(1)}, u32[]{:S(2)}, u32[]{:S(2)}) collective-permute-start(f32[128,16]{1,0:T(8,128)S(1)} %get-tuple-element.96.low_ref), channel_id=1, source_target_pairs={{0,1},{1,0},{2,3},{3,2},{4,5},{5,4},{6,7},{7,6},{8,9},{9,8},{10,11... | collective-permute-start | bytes 24584 | tf_op jit(solution)/shard_map/ppermute | solution.py:145
  72.6 5.8 %collective-permute-start.17 = (bf16[16,3072]{1,0:T(8,128)(2,1)S(1)}, bf16[16,3072]{1,0:T(8,128)(2,1)S(1)}, u32[]{:S(2)}, u32[]{:S(2)}) collective-permute-start(bf16[16,3072]{1,0:T(8,128)(2,1)S(1)} %get-tuple-element.98), channel_id=1, source_target_pairs={{0,2},{2,0},{4,6},{6,4},{1,3},{3,1},{5,7},{7,5},{8,10},{10,8},{12,... | collective-permute-start | bytes 294920 | tf_op jit(solution)/shard_map/ppermute | solution.py:145
  78.4 7.4 %collective-permute-start.18 = (bf16[16,3072]{1,0:T(8,128)(2,1)S(1)}, bf16[16,3072]{1,0:T(8,128)(2,1)S(1)}, u32[]{:S(2)}, u32[]{:S(2)}) collective-permute-start(bf16[16,3072]{1,0:T(8,128)(2,1)S(1)} %shard_map.125.own_ref), channel_id=1, source_target_pairs={{0,4},{2,6},{4,0},{6,2},{1,5},{3,7},{5,1},{7,3},{8,12},{10,14},{12... | collective-permute-start | bytes 294920 | tf_op jit(solution)/shard_map/ppermute | solution.py:145
  86.1 1.2 %collective-permute-start.19 = (f32[8,128]{1,0:T(8,128)S(1)}, f32[8,128]{1,0:T(8,128)S(1)}, u32[]{:S(2)}, u32[]{:S(2)}) collective-permute-start(f32[8,128]{1,0:T(8,128)S(1)} %get-tuple-element.102), channel_id=1, source_target_pairs={{0,1},{1,0},{2,3},{3,2},{4,5},{5,4},{6,7},{7,6},{8,9},{9,8},{10,11... | collective-permute-start | bytes 12296 | tf_op jit(solution)/shard_map/ppermute | solution.py:145
  87.3 3.6 %collective-permute-start.21 = (f32[8,128]{1,0:T(8,128)S(1)}, f32[8,128]{1,0:T(8,128)S(1)}, u32[]{:S(2)}, u32[]{:S(2)}) collective-permute-start(f32[8,128]{1,0:T(8,128)S(1)} %add.30), channel_id=1, source_target_pairs={{0,8},{1,17},{8,0},{9,25},{16,24},{17,1},{24,16},{25,9},{2,10},{3,... | collective-permute-start | bytes 12296 | tf_op jit(solution)/shard_map/ppermute | solution.py:586
  88.8 4.5 %collective-permute-start.20 = (f32[8,128]{1,0:T(8,128)S(1)}, f32[8,128]{1,0:T(8,128)S(1)}, u32[]{:S(2)}, u32[]{:S(2)}) collective-permute-start(f32[8,128]{1,0:T(8,128)S(1)} %add.30), channel_id=1, source_target_pairs={{0,24},{8,16},{16,8},{24,0},{1,25},{9,17},{17,9},{25,1},{2,26},{10... | collective-permute-start | bytes 12296 | tf_op jit(solution)/shard_map/ppermute | solution.py:145
  90.3 7.8 %collective-permute-start.24 = (bf16[16,3072]{1,0:T(8,128)(2,1)S(1)}, bf16[16,3072]{1,0:T(8,128)(2,1)S(1)}, u32[]{:S(2)}, u32[]{:S(2)}) collective-permute-start(bf16[16,3072]{1,0:T(8,128)(2,1)S(1)} %get-tuple-element.103.own_ref), channel_id=1, source_target_pairs={{0,2},{2,0},{4,6},{6,4},{1,3},{3,1},{5,7},{7,5},{8,10},{10,8},{12,... | collective-permute-start | bytes 294920 | tf_op jit(solution)/shard_map/ppermute | solution.py:145
  93.3 3.6 %collective-permute-start.22 = (f32[8,128]{1,0:T(8,128)S(1)}, f32[8,128]{1,0:T(8,128)S(1)}, u32[]{:S(2)}, u32[]{:S(2)}) collective-permute-start(f32[8,128]{1,0:T(8,128)S(1)} %add_select_fusion), channel_id=1, source_target_pairs={{0,2},{2,0},{4,6},{6,4},{1,3},{3,1},{5,7},{7,5},{8,10},{10,8},{12,... | collective-permute-start | bytes 12296 | tf_op jit(solution)/shard_map/ppermute | solution.py:145
  96.9 1.2 %collective-permute-start.23 = (f32[8,128]{1,0:T(8,128)S(1)}, f32[8,128]{1,0:T(8,128)S(1)}, u32[]{:S(2)}, u32[]{:S(2)}) collective-permute-start(f32[8,128]{1,0:T(8,128)S(1)} %add.33.square_ref), channel_id=1, source_target_pairs={{0,1},{1,0},{2,3},{3,2},{4,5},{5,4},{6,7},{7,6},{8,9},{9,8},{10,11... | collective-permute-start | bytes 12296 | tf_op jit(solution)/shard_map/ppermute | solution.py:145
  (3 other events, 4.1 us)

commit v5 on v4

--- a/solution.py
+++ b/solution.py
@@ -138,6 +138,7 @@
 F32, BF16 = jnp.float32, jnp.bfloat16
 VMEM = pl.BlockSpec(memory_space=pltpu.VMEM)
 LIMIT = 16 * 1024 * 1024
+STEPS = 10.0
 
 
 def swap(value, axis, distance):
@@ -173,7 +174,7 @@
 
 def distances():
     core = lax.axis_index("tp")
-    return 0, jnp.where(core == 0, 1, 3), jnp.where(core == 0, 3, 1), 2
+    return 0, jnp.where(core == 0, 1, 2), jnp.where(core == 0, 2, 1), 3
 
 
 def norm_kernel(mine_ref, other_ref, gain_ref, gain_other_ref, *outs):
@@ -215,15 +216,24 @@
 def store_packed(keys, values, out_ref):
     rows, width = keys.shape
     high = keys.astype(BF16)
+    wide = high.astype(F32)
+    size = jnp.abs(wide)
+    steps = jnp.round((keys - wide) * (256.0 * STEPS) / jnp.where(size > 0, size, 1.0))
+    half = width // 2
     out_ref[:rows, :width] = high
-    out_ref[:rows, width : 2 * width] = (keys - high.astype(F32)).astype(BF16)
-    out_ref[:rows, 2 * width :] = values.astype(BF16)
+    out_ref[:rows, width : 2 * width] = values.astype(BF16)
+    pairs = steps[:, :half] * (2.0 * STEPS + 1.0) + steps[:, half:]
+    out_ref[:rows, 2 * width :] = pairs.astype(BF16)
 
 
 def unpack(ref, rows):
-    width = ref.shape[1] // 3
-    keys = ref[:rows, :width].astype(F32) + ref[:rows, width : 2 * width].astype(F32)
-    return keys, ref[:rows, 2 * width :].astype(F32)
+    width = ref.shape[1] * 2 // 5
+    wide = ref[:rows, :width].astype(F32)
+    pairs = ref[:rows, 2 * width :].astype(F32)
+    first = jnp.round(pairs / (2.0 * STEPS + 1.0))
+    steps = jnp.concatenate([first, pairs - first * (2.0 * STEPS + 1.0)], axis=1)
+    keys = wide + jnp.abs(wide) * steps * (1.0 / (256.0 * STEPS))
+    return keys, ref[:rows, width : 2 * width].astype(F32)
 
 
 def store_docs(docs, out_ref):
@@ -426,7 +436,7 @@
     local_query = head_count * head
     rank = adapt_down.shape[1]
     kv_width = kv_count * 2 * head
-    sent_width = kv_count * 3 * head
+    sent_width = kv_count * 5 * head // 2
 
     half = rows // 2
     core = lax.axis_index("tp")
@@ -439,16 +449,16 @@
 
     def send_a(value):
         return lax.ppermute(
-            value, ("ctx", "tp"), [(2 * a + t, 2 * (a ^ (3 if t else 1)) + t) for a in range(4) for t in range(2)]
+            value, ("ctx", "tp"), [(2 * a + t, 2 * (a ^ (2 if t else 1)) + t) for a in range(4) for t in range(2)]
         )
 
     def send_b(value):
         return lax.ppermute(
-            value, ("ctx", "tp"), [(2 * a + t, 2 * (a ^ (1 if t else 3)) + t) for a in range(4) for t in range(2)]
+            value, ("ctx", "tp"), [(2 * a + t, 2 * (a ^ (1 if t else 2)) + t) for a in range(4) for t in range(2)]
         )
 
     even, slice_a, slice_b, slice_c = slices
-    got_a, got_b, got_c = send_a(slice_a), send_b(slice_b), swap(slice_c, "ctx", 2)
+    got_a, got_b, got_c = send_a(slice_a), send_b(slice_b), swap(slice_c, "ctx", 3)
     part_flops = 2 * rows * slice_width * kv_width
     packed = ((rows, sent_width), BF16)
     summed = ((rows, kv_width), F32)
@@ -518,7 +528,7 @@
         )
 
     (sent_c,) = step(far_parts, got_c, weight)
-    arrived_c = swap(sent_c, "ctx", 2)
+    arrived_c = swap(sent_c, "ctx", 3)
     got_a, got_b, sent_c = lax.optimization_barrier((got_a, got_b, sent_c))
     sent_a, sent_b = call(
         functools.partial(near_kernel, head),
@@ -551,7 +561,7 @@
         block_0,
         send_a(block_0),
         send_b(block_0),
-        swap(block_0, "ctx", 2),
+        swap(block_0, "ctx", 3),
         adapt_down[0],
         back_part,
         back_other,

time: 99.3 us -> 95 us (0.957)
  starting transfers between devices: 26.8 us -> 20.7 us
  waiting for transfers between devices: 47.1 us -> 48.8 us
    ppermute x6, waiting for transfers between devices: 2.04 us -> 18.4 us  [the longest x3 14.1 us: send_b(): lax.ppermute(value, ('ctx', 'tp'), [(2 * a + t, 2 * (a ^ (1 if t else 2))...]
    ppermute x18, waiting for transfers between devices: 44.5 us -> 29.8 us  [swap(): return lax.ppermute(value, axis, [(i, i ^ distance) for i in range(count)])]
    ppermute x18, starting transfers between devices: 19.2 us -> 13.8 us  [swap(): return lax.ppermute(value, axis, [(i, i ^ distance) for i in range(count)])]
  transfers between devices with their start and end apart: 25 -> 25, of which waited for: 14 -> 16; matrix products, arithmetic and copies ran while one was open for 4% -> 4% of each run, Pallas kernels for 10% -> 11%
where the time goes in v5:
time: 95 us; the launch traced here: 94.6 us
  waiting for transfers between devices  48.8 us (51%)
  starting transfers between devices  20.7 us (22%)
  Pallas kernels  16.7 us (18%)
  local copies, waits for them, and re-layouts  6.44 us (7%)
  other arithmetic  1.08 us (1%)
    ppermute x18, waiting for transfers between devices, swap(): return lax.ppermute(value, axis, [(i, i ^ distance) for i in range(count)])  29.8 us
    pallas_call x14, Pallas kernels, call(): pl.pallas_call(kernel, out_shape=shapes, in_specs=[pl.BlockSpec(memory_sp...  16.7 us
    ppermute x3, waiting for transfers between devices, send_b(): lax.ppermute(value, ('ctx', 'tp'), [(2 * a + t, 2 * (a ^ (1 if t else 2))...  14.1 us
    ppermute x18, starting transfers between devices, swap(): return lax.ppermute(value, axis, [(i, i ^ distance) for i in range(count)])  13.8 us
    ppermute x3, waiting for transfers between devices, send_a(): lax.ppermute(value, ('ctx', 'tp'), [(2 * a + t, 2 * (a ^ (2 if t else 1))...  4.37 us
    ppermute x3, starting transfers between devices, send_a(): lax.ppermute(value, ('ctx', 'tp'), [(2 * a + t, 2 * (a ^ (2 if t else 1))...  2.89 us
    squeeze x1, local copies, waits for them, and re-layouts, prepare(): return key_value_weight[0].reshape(slice_width, kv_width)  2.75 us
    ppermute x3, starting transfers between devices, send_b(): lax.ppermute(value, ('ctx', 'tp'), [(2 * a + t, 2 * (a ^ (1 if t else 2))...  2.47 us
  transfers between devices with their start and end apart: 25, of which 16 were waited for; matrix products, arithmetic and copies ran while one was open for 4% of the time, Pallas kernels for 11%

profile of v5, /device:TPU:0, one launch (start us, length us, event | category | flops | bytes accessed | tf_op | source)
XLA Modules:
  0.0 94.6 jit_solution(12184391025915953428)
XLA Ops:
  0.7 1.4 %dynamic-slice_bitcast_fusion = (bf16[64,4096]{1,0:T(8,128)(2,1)S(1)}, bf16[64,4096]{1,0:T(8,128)(2,1)S(1)}) fusion(bf16[1,128,4096]{2,1,0:T(8,128)(2,1)} %param.14, s32[]{:T(128)S(6)} %select_n.15, s32[]{:T(128)S(6)} %select_n.14), kind=kLoop, calls=%fused_computation.9 | loop fusion | bytes 2097160 | tf_op jit(solution)/shard_map/dynamic_slice | solution.py:444
  2.7 1.5 %collective-permute-done.3.gain_other_ref = bf16[1,4096]{1,0:T(2,128)(2,1)S(1)} collective-permute-done((bf16[1,4096]{1,0:T(2,128)(2,1)S(1)}, bf16[1,4096]{1,0:T(2,128)(2,1)S(1)}, u32[]{:S(2)}, u32[]{:S(2)}) %collective-permute-start.3) | collective-permute-done | bytes 8224 | tf_op jit(solution)/shard_map/ppermute | solution.py:146
  4.2 1.5 %shard_map.117 = (bf16[64,2048]{1,0:T(8,128)(2,1)S(1)}, bf16[64,2048]{1,0:T(8,128)(2,1)}, bf16[64,2048]{1,0:T(8,128)(2,1)}, bf16[64,2048]{1,0:T(8,128)(2,1)}) custom-call(bf16[64,4096]{1,0:T(8,128)(2,1)S(1)} %get-tuple-element.118.mine_ref, bf16[64,4096]{1,0:T(8,128)(2,1)S(1)} %collective-permute-done.2.other_ref, bf16[1,4096]{1,0:T(2,128)(2,1)S(1)} %copy-done, ...), custom_call_target="tpu_custom_call" | custom-call | bytes 2113536 | tf_op jit(solution)/shard_map/pallas_call | solution.py:152
  6.0 4.7 %collective-permute-start.6 = (bf16[64,2048]{1,0:T(8,128)(2,1)}, bf16[64,2048]{1,0:T(8,128)(2,1)}, u32[]{:S(2)}, u32[]{:S(2)}) collective-permute-start(bf16[64,2048]{1,0:T(8,128)(2,1)} %get-tuple-element.72), channel_id=1, source_target_pairs={{0,6},{2,4},{4,2},{6,0},{1,7},{3,5},{5,3},{7,1},{8,14},{10,12},{12... | collective-permute-start | bytes 786440 | tf_op jit(solution)/shard_map/ppermute | solution.py:146
  11.3 3.4 %conditional.3 = (f32[1,128]{1,0:T(1,128)S(1)}, f32[128,128]{1,0:T(8,128)}, f32[128,128]{1,0:T(8,128)}, bf16[2048,128]{1,0:T(8,128)(2,1)S(1)}, f32[128,16]{1,0:T(8,128)}, /*index=5*/f32[128,16]{1,0:T(8,128)}) conditional(s32[]{:T(128)} %convert_element_type.15, () %tuple.32, (s32[128]{0:T(128)S(1)}, s32[]{:T(128)}, ...), branch_computations={%region_0.0_spmd, %region_1.0_spmd} | conditional | flops 16826880 | bytes 3779176 | solution.py:469
  15.5 2.7 %conditional.4 = (bf16[2048,512]{1,0:T(8,128)(2,1)S(1)}) conditional(s32[]{:T(128)} %convert_element_type.15, () %tuple.35, (bf16[1,2048,2,2,128]{4,3,2,1,0:T(2,128)(2,1)}) %tuple.42), branch_computations={%region_2.0_spmd, %region_3.0_spmd} | conditional | bytes 4194312 | solution.py:469
  15.5 2.7 %squeeze.19 = bf16[2048,512]{1,0:T(8,128)(2,1)S(1)} reshape(bf16[1,2048,2,2,128]{4,3,2,1,0:T(2,128)(2,1)} %get-tuple-element.111) | data formatting | bytes 4194304 | tf_op jit(solution)/shard_map/cond/branch_1_fun/reshape;cond/branch_1_fun/squeeze | solution.py:477
  18.3 1.3 %copy-done.2 = bf16[2048,512]{1,0:T(8,128)(2,1)} copy-done((bf16[2048,512]{1,0:T(8,128)(2,1)}, bf16[2048,512]{1,0:T(8,128)(2,1)S(1)}, u32[]{:S(2)}) %copy-start.2) | copy-done | bytes 2097176
  19.6 2.2 %shard_map.118 = (f32[128,512]{1,0:T(8,128)S(1)}, bf16[2048,512]{1,0:T(8,128)(2,1)S(1)}) custom-call(bf16[64,2048]{1,0:T(8,128)(2,1)S(1)} %get-tuple-element.73.even_ref, bf16[64,2048]{1,0:T(8,128)(2,1)S(1)} %collective-permute-done.7.even_other_ref, bf16[2048,512]{1,0:T(8,128)(2,1)} %copy-done.2), custom_call_target="tpu_custom_call" | custom-call | flops 268435456 | bytes 4980736 | tf_op jit(solution)/shard_map/pallas_call | solution.py:152
  21.8 4.8 %conditional.5 = (bf16[128,640]{1,0:T(8,128)(2,1)}) conditional(s32[]{:T(128)} %convert_element_type.15, () %tuple.34, (bf16[64,2048]{1,0:T(8,128)(2,1)}, bf16[2048,512]{1,0:T(8,128)(2,1)}) %tuple.53), branch_computations={%region_4.0_spmd, %region_5.0_spmd} | conditional | flops 268435456 | bytes 3833904 | solution.py:469
  22.4 1.4 %collective-permute-done.got_other_ref = bf16[64,2048]{1,0:T(8,128)(2,1)S(1)} collective-permute-done((bf16[64,2048]{1,0:T(8,128)(2,1)}, bf16[64,2048]{1,0:T(8,128)(2,1)S(1)}, u32[]{:S(2)}, u32[]{:S(2)}) %collective-permute-start) | collective-permute-done | bytes 262176 | tf_op jit(solution)/shard_map/cond/branch_1_fun/ppermute | solution.py:146
  23.8 2.8 %branch_1_fun.5 = bf16[128,640]{1,0:T(8,128)(2,1)} custom-call(bf16[64,2048]{1,0:T(8,128)(2,1)} %get-tuple-element.26.got_ref, bf16[64,2048]{1,0:T(8,128)(2,1)S(1)} %collective-permute-done.got_other_ref, bf16[2048,512]{1,0:T(8,128)(2,1)} %get-tuple-element.27.weight_ref), custom_call_target="tpu_custom_call" | custom-call | flops 268435456 | bytes 2785280 | tf_op jit(solution)/shard_map/cond/branch_1_fun/pallas_call | solution.py:152
  26.6 7.2 %collective-permute-done.5.got_b_ref = bf16[64,2048]{1,0:T(8,128)(2,1)S(1)} collective-permute-done((bf16[64,2048]{1,0:T(8,128)(2,1)}, bf16[64,2048]{1,0:T(8,128)(2,1)S(1)}, u32[]{:S(2)}, u32[]{:S(2)}) %collective-permute-start.5) | collective-permute-done | bytes 262176 | tf_op jit(solution)/shard_map/ppermute | solution.py:456
  34.3 2.5 %collective-permute-start.12 = (bf16[128,640]{1,0:T(8,128)(2,1)}, bf16[128,640]{1,0:T(8,128)(2,1)S(1)}, u32[]{:S(2)}, u32[]{:S(2)}) collective-permute-start(bf16[128,640]{1,0:T(8,128)(2,1)} %get-tuple-element.132), channel_id=1, source_target_pairs={{0,6},{2,4},{4,2},{6,0},{1,7},{3,5},{5,3},{7,1},{8,14},{10,12},{12... | collective-permute-start | bytes 491528 | tf_op jit(solution)/shard_map/ppermute | solution.py:146
  37.7 1.9 %collective-permute-start.11 = (bf16[128,640]{1,0:T(8,128)(2,1)S(1)}, bf16[128,640]{1,0:T(8,128)(2,1)S(1)}, u32[]{:S(2)}, u32[]{:S(2)}) collective-permute-start(bf16[128,640]{1,0:T(8,128)(2,1)S(1)} %get-tuple-element.81), channel_id=1, source_target_pairs={{0,4},{1,3},{2,6},{3,1},{4,0},{5,7},{6,2},{7,5},{8,12},{9,11},{10,... | collective-permute-start | bytes 491528 | tf_op jit(solution)/shard_map/ppermute | solution.py:456
  39.6 3.9 %collective-permute-done.12.got_ref = bf16[128,640]{1,0:T(8,128)(2,1)S(1)} collective-permute-done((bf16[128,640]{1,0:T(8,128)(2,1)}, bf16[128,640]{1,0:T(8,128)(2,1)S(1)}, u32[]{:S(2)}, u32[]{:S(2)}) %collective-permute-start.12) | collective-permute-done | bytes 163872 | tf_op jit(solution)/shard_map/ppermute | solution.py:146
  44.4 4.4 %collective-permute-done.10.got_a_ref = bf16[128,640]{1,0:T(8,128)(2,1)S(1)} collective-permute-done((bf16[128,640]{1,0:T(8,128)(2,1)S(1)}, bf16[128,640]{1,0:T(8,128)(2,1)S(1)}, u32[]{:S(2)}, u32[]{:S(2)}) %collective-permute-start.10) | collective-permute-done | bytes 163872 | tf_op jit(solution)/shard_map/ppermute | solution.py:451
  48.8 1.6 %collective-permute-done.11.got_b_ref = bf16[128,640]{1,0:T(8,128)(2,1)S(1)} collective-permute-done((bf16[128,640]{1,0:T(8,128)(2,1)S(1)}, bf16[128,640]{1,0:T(8,128)(2,1)S(1)}, u32[]{:S(2)}, u32[]{:S(2)}) %collective-permute-start.11) | collective-permute-done | bytes 163872 | tf_op jit(solution)/shard_map/ppermute | solution.py:456
  50.5 1.6 %collective-permute-start.15 = (bf16[144,512]{1,0:T(8,128)(2,1)S(1)}, bf16[144,512]{1,0:T(8,128)(2,1)S(1)}, u32[]{:S(2)}, u32[]{:S(2)}) collective-permute-start(bf16[144,512]{1,0:T(8,128)(2,1)S(1)} %shard_map.121.block_0_ref), channel_id=1, source_target_pairs={{0,6},{2,4},{4,2},{6,0},{1,7},{3,5},{5,3},{7,1},{8,14},{10,12},{12... | collective-permute-start | bytes 442376 | tf_op jit(solution)/shard_map/ppermute | solution.py:146
  52.2 2.8 %collective-permute-start.13 = (bf16[144,512]{1,0:T(8,128)(2,1)S(1)}, bf16[144,512]{1,0:T(8,128)(2,1)S(1)}, u32[]{:S(2)}, u32[]{:S(2)}) collective-permute-start(bf16[144,512]{1,0:T(8,128)(2,1)S(1)} %shard_map.121.block_0_ref), channel_id=1, source_target_pairs={{0,2},{1,5},{2,0},{3,7},{4,6},{5,1},{6,4},{7,3},{8,10},{9,13},{10,... | collective-permute-start | bytes 442376 | tf_op jit(solution)/shard_map/ppermute | solution.py:451
  55.0 4.2 %collective-permute-done.15.block_c_ref = bf16[144,512]{1,0:T(8,128)(2,1)S(1)} collective-permute-done((bf16[144,512]{1,0:T(8,128)(2,1)S(1)}, bf16[144,512]{1,0:T(8,128)(2,1)S(1)}, u32[]{:S(2)}, u32[]{:S(2)}) %collective-permute-start.15) | collective-permute-done | bytes 147488 | tf_op jit(solution)/shard_map/ppermute | solution.py:146
  59.2 5.2 %collective-permute-done.14.block_b_ref = bf16[144,512]{1,0:T(8,128)(2,1)S(1)} collective-permute-done((bf16[144,512]{1,0:T(8,128)(2,1)S(1)}, bf16[144,512]{1,0:T(8,128)(2,1)S(1)}, u32[]{:S(2)}, u32[]{:S(2)}) %collective-permute-start.14) | collective-permute-done | bytes 147488 | tf_op jit(solution)/shard_map/ppermute | solution.py:456
  64.5 3.6 %shard_map.122 = (bf16[128,2048]{1,0:T(8,128)(2,1)}, f32[128,16]{1,0:T(8,128)S(1)}, f32[16,2048]{1,0:T(8,128)S(1)}) custom-call(bf16[2048,128]{1,0:T(8,128)(2,1)S(1)} %copy-done.7, bf16[144,512]{1,0:T(8,128)(2,1)S(1)} %shard_map.121.block_0_ref, bf16[144,512]{1,0:T(8,128)(2,1)S(1)} %collective-permute-done.13.block_a_ref, ...), custom_call_target="tpu_custom_call" | custom-call | flops 536870912 | bytes 1859584 | tf_op jit(solution)/shard_map/pallas_call | solution.py:152
  68.0 1.3 %collective-permute-done.16.low_other_ref = f32[128,16]{1,0:T(8,128)S(1)} collective-permute-done((f32[128,16]{1,0:T(8,128)S(1)}, f32[128,16]{1,0:T(8,128)S(1)}, u32[]{:S(2)}, u32[]{:S(2)}) %collective-permute-start.16) | collective-permute-done | bytes 8224 | tf_op jit(solution)/shard_map/ppermute | solution.py:146
  69.6 1.4 %shard_map.124 = bf16[128,4096]{1,0:T(8,128)(2,1)} custom-call(f32[128,16]{1,0:T(8,128)S(1)} %get-tuple-element.96.low_ref, f32[128,16]{1,0:T(8,128)S(1)} %collective-permute-done.16.low_other_ref, bf16[16,4096]{1,0:T(8,128)(2,1)S(1)} %bitcast.25), custom_call_target="tpu_custom_call" | custom-call | flops 16777216 | bytes 1196032 | tf_op jit(solution)/shard_map/pallas_call | solution.py:152
  71.0 3.5 %collective-permute-done.17.got_ref = bf16[16,3072]{1,0:T(8,128)(2,1)S(1)} collective-permute-done((bf16[16,3072]{1,0:T(8,128)(2,1)S(1)}, bf16[16,3072]{1,0:T(8,128)(2,1)S(1)}, u32[]{:S(2)}, u32[]{:S(2)}) %collective-permute-start.17) | collective-permute-done | bytes 98336 | tf_op jit(solution)/shard_map/ppermute | solution.py:146
  74.5 1.3 %collective-permute-start.18 = (bf16[16,3072]{1,0:T(8,128)(2,1)S(1)}, bf16[16,3072]{1,0:T(8,128)(2,1)S(1)}, u32[]{:S(2)}, u32[]{:S(2)}) collective-permute-start(bf16[16,3072]{1,0:T(8,128)(2,1)S(1)} %shard_map.125.own_ref), channel_id=1, source_target_pairs={{0,4},{2,6},{4,0},{6,2},{1,5},{3,7},{5,1},{7,3},{8,12},{10,14},{12... | collective-permute-start | bytes 294920 | tf_op jit(solution)/shard_map/ppermute | solution.py:146
  75.8 5.8 %collective-permute-done.18.got_ref = bf16[16,3072]{1,0:T(8,128)(2,1)S(1)} collective-permute-done((bf16[16,3072]{1,0:T(8,128)(2,1)S(1)}, bf16[16,3072]{1,0:T(8,128)(2,1)S(1)}, u32[]{:S(2)}, u32[]{:S(2)}) %collective-permute-start.18) | collective-permute-done | bytes 98336 | tf_op jit(solution)/shard_map/ppermute | solution.py:146
  83.0 1.5 %collective-permute-start.21 = (f32[8,128]{1,0:T(8,128)S(1)}, f32[8,128]{1,0:T(8,128)S(1)}, u32[]{:S(2)}, u32[]{:S(2)}) collective-permute-start(f32[8,128]{1,0:T(8,128)S(1)} %add.30), channel_id=1, source_target_pairs={{0,8},{1,17},{8,0},{9,25},{16,24},{17,1},{24,16},{25,9},{2,10},{3,... | collective-permute-start | bytes 12296 | tf_op jit(solution)/shard_map/ppermute | solution.py:596
  84.5 1.5 %collective-permute-start.20 = (f32[8,128]{1,0:T(8,128)S(1)}, f32[8,128]{1,0:T(8,128)S(1)}, u32[]{:S(2)}, u32[]{:S(2)}) collective-permute-start(f32[8,128]{1,0:T(8,128)S(1)} %add.30), channel_id=1, source_target_pairs={{0,24},{8,16},{16,8},{24,0},{1,25},{9,17},{17,9},{25,1},{2,26},{10... | collective-permute-start | bytes 12296 | tf_op jit(solution)/shard_map/ppermute | solution.py:146
  86.6 2.4 %collective-permute-done.20 = f32[8,128]{1,0:T(8,128)S(1)} collective-permute-done((f32[8,128]{1,0:T(8,128)S(1)}, f32[8,128]{1,0:T(8,128)S(1)}, u32[]{:S(2)}, u32[]{:S(2)}) %collective-permute-start.20) | collective-permute-done | bytes 4128 | tf_op jit(solution)/shard_map/ppermute | solution.py:146
  89.0 3.6 %collective-permute-done.22 = f32[8,128]{1,0:T(8,128)S(1)} collective-permute-done((f32[8,128]{1,0:T(8,128)S(1)}, f32[8,128]{1,0:T(8,128)S(1)}, u32[]{:S(2)}, u32[]{:S(2)}) %collective-permute-start.22) | collective-permute-done | bytes 4128 | tf_op jit(solution)/shard_map/ppermute | solution.py:146
  (66 shorter events, 13.1 us)
Async XLA Ops:
  0.6 10.7 %copy-start.3 = (bf16[1,128,4096]{2,1,0:T(8,128)(2,1)S(1)}, bf16[1,128,4096]{2,1,0:T(8,128)(2,1)}, u32[]{:S(2)}) copy-start(bf16[1,128,4096]{2,1,0:T(8,128)(2,1)} %param.20) | copy-start | bytes 3145732
  0.7 10.7 %copy-start.5 = (bf16[1,16,4096]{2,1,0:T(8,128)(2,1)S(1)}, bf16[1,16,4096]{2,1,0:T(8,128)(2,1)}, u32[]{:S(2)}) copy-start(bf16[1,16,4096]{2,1,0:T(8,128)(2,1)} %param.19) | copy-start | bytes 393220
  0.7 10.7 %copy-start.9 = (s32[128]{0:T(128)S(1)}, s32[128]{0:T(128)}, u32[]{:S(2)}) copy-start(s32[128]{0:T(128)} %param.21) | copy-start | bytes 1540
  0.7 10.7 %copy-start.8 = (bf16[1,128,16,128]{3,2,1,0:T(8,128)(2,1)S(1)}, bf16[1,128,16,128]{3,2,1,0:T(8,128)(2,1)}, u32[]{:S(2)}) copy-start(bf16[1,128,16,128]{3,2,1,0:T(8,128)(2,1)} %param.16) | copy-start | bytes 1572868
  2.1 2.1 %collective-permute-start.2 = (bf16[64,4096]{1,0:T(8,128)(2,1)S(1)}, bf16[64,4096]{1,0:T(8,128)(2,1)S(1)}, u32[]{:S(2)}, u32[]{:S(2)}) collective-permute-start(bf16[64,4096]{1,0:T(8,128)(2,1)S(1)} %get-tuple-element.117), channel_id=1, source_target_pairs={{0,1},{1,0},{2,3},{3,2},{4,5},{5,4},{6,7},{7,6},{8,9},{9,8},{10,11... | collective-permute-start | bytes 1572872 | tf_op jit(solution)/shard_map/ppermute | solution.py:146
  2.6 1.6 %collective-permute-start.3 = (bf16[1,4096]{1,0:T(2,128)(2,1)S(1)}, bf16[1,4096]{1,0:T(2,128)(2,1)S(1)}, u32[]{:S(2)}, u32[]{:S(2)}) collective-permute-start(bf16[1,4096]{1,0:T(2,128)(2,1)S(1)} %copy-done), channel_id=1, source_target_pairs={{0,1},{1,0},{2,3},{3,2},{4,5},{5,4},{6,7},{7,6},{8,9},{9,8},{10,11... | collective-permute-start | bytes 24584 | tf_op jit(solution)/shard_map/ppermute | solution.py:146
  5.6 14.0 %collective-permute-start.7 = (bf16[64,2048]{1,0:T(8,128)(2,1)S(1)}, bf16[64,2048]{1,0:T(8,128)(2,1)S(1)}, u32[]{:S(2)}, u32[]{:S(2)}) collective-permute-start(bf16[64,2048]{1,0:T(8,128)(2,1)S(1)} %get-tuple-element.73.even_ref), channel_id=1, source_target_pairs={{0,1},{1,0},{2,3},{3,2},{4,5},{5,4},{6,7},{7,6},{8,9},{9,8},{10,11... | collective-permute-start | bytes 786440 | tf_op jit(solution)/shard_map/ppermute | solution.py:146
  6.0 15.8 %collective-permute-start.6 = (bf16[64,2048]{1,0:T(8,128)(2,1)}, bf16[64,2048]{1,0:T(8,128)(2,1)}, u32[]{:S(2)}, u32[]{:S(2)}) collective-permute-start(bf16[64,2048]{1,0:T(8,128)(2,1)} %get-tuple-element.72), channel_id=1, source_target_pairs={{0,6},{2,4},{4,2},{6,0},{1,7},{3,5},{5,3},{7,1},{8,14},{10,12},{12... | collective-permute-start | bytes 786440 | tf_op jit(solution)/shard_map/ppermute | solution.py:146
  10.8 15.8 %collective-permute-start.4 = (bf16[64,2048]{1,0:T(8,128)(2,1)}, bf16[64,2048]{1,0:T(8,128)(2,1)S(1)}, u32[]{:S(2)}, u32[]{:S(2)}) collective-permute-start(bf16[64,2048]{1,0:T(8,128)(2,1)} %get-tuple-element.70), channel_id=1, source_target_pairs={{0,2},{1,5},{2,0},{3,7},{4,6},{5,1},{6,4},{7,3},{8,10},{9,13},{10,... | collective-permute-start | bytes 786440 | tf_op jit(solution)/shard_map/ppermute | solution.py:451
  10.8 23.0 %collective-permute-start.5 = (bf16[64,2048]{1,0:T(8,128)(2,1)}, bf16[64,2048]{1,0:T(8,128)(2,1)S(1)}, u32[]{:S(2)}, u32[]{:S(2)}) collective-permute-start(bf16[64,2048]{1,0:T(8,128)(2,1)} %get-tuple-element.71), channel_id=1, source_target_pairs={{0,4},{1,3},{2,6},{3,1},{4,0},{5,7},{6,2},{7,5},{8,12},{9,11},{10,... | collective-permute-start | bytes 786440 | tf_op jit(solution)/shard_map/ppermute | solution.py:456
  12.4 2.4 %collective-permute-start.1 = (f32[128,16]{1,0:T(8,128)}, f32[128,16]{1,0:T(8,128)}, u32[]{:S(2)}, u32[]{:S(2)}) collective-permute-start(f32[128,16]{1,0:T(8,128)} %branch_1_fun.4), channel_id=1, source_target_pairs={{0,1},{1,0},{2,3},{3,2},{4,5},{5,4},{6,7},{7,6},{8,9},{9,8},{10,11... | collective-permute-start | bytes 24584 | tf_op jit(solution)/shard_map/cond/branch_1_fun/ppermute | solution.py:146
  21.8 1.9 %collective-permute-start = (bf16[64,2048]{1,0:T(8,128)(2,1)}, bf16[64,2048]{1,0:T(8,128)(2,1)S(1)}, u32[]{:S(2)}, u32[]{:S(2)}) collective-permute-start(bf16[64,2048]{1,0:T(8,128)(2,1)} %get-tuple-element.26.got_ref), channel_id=1, source_target_pairs={{0,1},{1,0},{2,3},{3,2},{4,5},{5,4},{6,7},{7,6},{8,9},{9,8},{10,11... | collective-permute-start | bytes 786440 | tf_op jit(solution)/shard_map/cond/branch_1_fun/ppermute | solution.py:146
  33.8 3.0 %collective-permute-start.8 = (bf16[64,2048]{1,0:T(8,128)(2,1)S(1)}, bf16[64,2048]{1,0:T(8,128)(2,1)S(1)}, u32[]{:S(2)}, u32[]{:S(2)}) collective-permute-start(bf16[64,2048]{1,0:T(8,128)(2,1)S(1)} %collective-permute-done.4.got_a_ref), channel_id=1, source_target_pairs={{0,1},{1,0},{2,3},{3,2},{4,5},{5,4},{6,7},{7,6},{8,9},{9,8},{10,11... | collective-permute-start | bytes 786440 | tf_op jit(solution)/shard_map/ppermute | solution.py:146
  33.8 3.0 %collective-permute-start.9 = (bf16[64,2048]{1,0:T(8,128)(2,1)S(1)}, bf16[64,2048]{1,0:T(8,128)(2,1)S(1)}, u32[]{:S(2)}, u32[]{:S(2)}) collective-permute-start(bf16[64,2048]{1,0:T(8,128)(2,1)S(1)} %collective-permute-done.5.got_b_ref), channel_id=1, source_target_pairs={{0,1},{1,0},{2,3},{3,2},{4,5},{5,4},{6,7},{7,6},{8,9},{9,8},{10,11... | collective-permute-start | bytes 786440 | tf_op jit(solution)/shard_map/ppermute | solution.py:146
  34.3 9.2 %collective-permute-start.12 = (bf16[128,640]{1,0:T(8,128)(2,1)}, bf16[128,640]{1,0:T(8,128)(2,1)S(1)}, u32[]{:S(2)}, u32[]{:S(2)}) collective-permute-start(bf16[128,640]{1,0:T(8,128)(2,1)} %get-tuple-element.132), channel_id=1, source_target_pairs={{0,6},{2,4},{4,2},{6,0},{1,7},{3,5},{5,3},{7,1},{8,14},{10,12},{12... | collective-permute-start | bytes 491528 | tf_op jit(solution)/shard_map/ppermute | solution.py:146
  36.8 27.6 %copy-start.1 = (bf16[1,16,2048]{2,1,0:T(8,128)(2,1)S(1)}, bf16[1,16,2048]{2,1,0:T(8,128)(2,1)}, u32[]{:S(2)}) copy-start(bf16[1,16,2048]{2,1,0:T(8,128)(2,1)} %param.18) | copy-start | bytes 196612
  36.8 27.6 %copy-start.7 = (bf16[2048,128]{1,0:T(8,128)(2,1)S(1)}, bf16[2048,128]{1,0:T(8,128)(2,1)}, u32[]{:S(2)}) copy-start(bf16[2048,128]{1,0:T(8,128)(2,1)} %copy-done.6) | copy-start | bytes 1572868
  37.6 31.7 %copy-start.4 = (bf16[1,128,4096]{2,1,0:T(8,128)(2,1)S(1)}, bf16[1,128,4096]{2,1,0:T(8,128)(2,1)}, u32[]{:S(2)}) copy-start(bf16[1,128,4096]{2,1,0:T(8,128)(2,1)} %param.20) | copy-start | bytes 3145732
  37.6 11.2 %collective-permute-start.10 = (bf16[128,640]{1,0:T(8,128)(2,1)S(1)}, bf16[128,640]{1,0:T(8,128)(2,1)S(1)}, u32[]{:S(2)}, u32[]{:S(2)}) collective-permute-start(bf16[128,640]{1,0:T(8,128)(2,1)S(1)} %get-tuple-element.80), channel_id=1, source_target_pairs={{0,2},{1,5},{2,0},{3,7},{4,6},{5,1},{6,4},{7,3},{8,10},{9,13},{10,... | collective-permute-start | bytes 491528 | tf_op jit(solution)/shard_map/ppermute | solution.py:451
  37.7 12.7 %collective-permute-start.11 = (bf16[128,640]{1,0:T(8,128)(2,1)S(1)}, bf16[128,640]{1,0:T(8,128)(2,1)S(1)}, u32[]{:S(2)}, u32[]{:S(2)}) collective-permute-start(bf16[128,640]{1,0:T(8,128)(2,1)S(1)} %get-tuple-element.81), channel_id=1, source_target_pairs={{0,4},{1,3},{2,6},{3,1},{4,0},{5,7},{6,2},{7,5},{8,12},{9,11},{10,... | collective-permute-start | bytes 491528 | tf_op jit(solution)/shard_map/ppermute | solution.py:456
  50.5 8.7 %collective-permute-start.15 = (bf16[144,512]{1,0:T(8,128)(2,1)S(1)}, bf16[144,512]{1,0:T(8,128)(2,1)S(1)}, u32[]{:S(2)}, u32[]{:S(2)}) collective-permute-start(bf16[144,512]{1,0:T(8,128)(2,1)S(1)} %shard_map.121.block_0_ref), channel_id=1, source_target_pairs={{0,6},{2,4},{4,2},{6,0},{1,7},{3,5},{5,3},{7,1},{8,14},{10,12},{12... | collective-permute-start | bytes 442376 | tf_op jit(solution)/shard_map/ppermute | solution.py:146
  52.2 12.3 %collective-permute-start.14 = (bf16[144,512]{1,0:T(8,128)(2,1)S(1)}, bf16[144,512]{1,0:T(8,128)(2,1)S(1)}, u32[]{:S(2)}, u32[]{:S(2)}) collective-permute-start(bf16[144,512]{1,0:T(8,128)(2,1)S(1)} %shard_map.121.block_0_ref), channel_id=1, source_target_pairs={{0,4},{1,3},{2,6},{3,1},{4,0},{5,7},{6,2},{7,5},{8,12},{9,11},{10,... | collective-permute-start | bytes 442376 | tf_op jit(solution)/shard_map/ppermute | solution.py:456
  52.2 12.3 %collective-permute-start.13 = (bf16[144,512]{1,0:T(8,128)(2,1)S(1)}, bf16[144,512]{1,0:T(8,128)(2,1)S(1)}, u32[]{:S(2)}, u32[]{:S(2)}) collective-permute-start(bf16[144,512]{1,0:T(8,128)(2,1)S(1)} %shard_map.121.block_0_ref), channel_id=1, source_target_pairs={{0,2},{1,5},{2,0},{3,7},{4,6},{5,1},{6,4},{7,3},{8,10},{9,13},{10,... | collective-permute-start | bytes 442376 | tf_op jit(solution)/shard_map/ppermute | solution.py:451
  68.0 1.3 %collective-permute-start.16 = (f32[128,16]{1,0:T(8,128)S(1)}, f32[128,16]{1,0:T(8,128)S(1)}, u32[]{:S(2)}, u32[]{:S(2)}) collective-permute-start(f32[128,16]{1,0:T(8,128)S(1)} %get-tuple-element.96.low_ref), channel_id=1, source_target_pairs={{0,1},{1,0},{2,3},{3,2},{4,5},{5,4},{6,7},{7,6},{8,9},{9,8},{10,11... | collective-permute-start | bytes 24584 | tf_op jit(solution)/shard_map/ppermute | solution.py:146
  69.6 4.9 %collective-permute-start.17 = (bf16[16,3072]{1,0:T(8,128)(2,1)S(1)}, bf16[16,3072]{1,0:T(8,128)(2,1)S(1)}, u32[]{:S(2)}, u32[]{:S(2)}) collective-permute-start(bf16[16,3072]{1,0:T(8,128)(2,1)S(1)} %get-tuple-element.98), channel_id=1, source_target_pairs={{0,2},{2,0},{4,6},{6,4},{1,3},{3,1},{5,7},{7,5},{8,10},{10,8},{12,... | collective-permute-start | bytes 294920 | tf_op jit(solution)/shard_map/ppermute | solution.py:146
  74.5 7.1 %collective-permute-start.18 = (bf16[16,3072]{1,0:T(8,128)(2,1)S(1)}, bf16[16,3072]{1,0:T(8,128)(2,1)S(1)}, u32[]{:S(2)}, u32[]{:S(2)}) collective-permute-start(bf16[16,3072]{1,0:T(8,128)(2,1)S(1)} %shard_map.125.own_ref), channel_id=1, source_target_pairs={{0,4},{2,6},{4,0},{6,2},{1,5},{3,7},{5,1},{7,3},{8,12},{10,14},{12... | collective-permute-start | bytes 294920 | tf_op jit(solution)/shard_map/ppermute | solution.py:146
  81.8 1.2 %collective-permute-start.19 = (f32[8,128]{1,0:T(8,128)S(1)}, f32[8,128]{1,0:T(8,128)S(1)}, u32[]{:S(2)}, u32[]{:S(2)}) collective-permute-start(f32[8,128]{1,0:T(8,128)S(1)} %get-tuple-element.102), channel_id=1, source_target_pairs={{0,1},{1,0},{2,3},{3,2},{4,5},{5,4},{6,7},{7,6},{8,9},{9,8},{10,11... | collective-permute-start | bytes 12296 | tf_op jit(solution)/shard_map/ppermute | solution.py:146
  83.0 3.6 %collective-permute-start.21 = (f32[8,128]{1,0:T(8,128)S(1)}, f32[8,128]{1,0:T(8,128)S(1)}, u32[]{:S(2)}, u32[]{:S(2)}) collective-permute-start(f32[8,128]{1,0:T(8,128)S(1)} %add.30), channel_id=1, source_target_pairs={{0,8},{1,17},{8,0},{9,25},{16,24},{17,1},{24,16},{25,9},{2,10},{3,... | collective-permute-start | bytes 12296 | tf_op jit(solution)/shard_map/ppermute | solution.py:596
  84.5 4.5 %collective-permute-start.20 = (f32[8,128]{1,0:T(8,128)S(1)}, f32[8,128]{1,0:T(8,128)S(1)}, u32[]{:S(2)}, u32[]{:S(2)}) collective-permute-start(f32[8,128]{1,0:T(8,128)S(1)} %add.30), channel_id=1, source_target_pairs={{0,24},{8,16},{16,8},{24,0},{1,25},{9,17},{17,9},{25,1},{2,26},{10... | collective-permute-start | bytes 12296 | tf_op jit(solution)/shard_map/ppermute | solution.py:146
  86.0 7.8 %collective-permute-start.24 = (bf16[16,3072]{1,0:T(8,128)(2,1)S(1)}, bf16[16,3072]{1,0:T(8,128)(2,1)S(1)}, u32[]{:S(2)}, u32[]{:S(2)}) collective-permute-start(bf16[16,3072]{1,0:T(8,128)(2,1)S(1)} %get-tuple-element.103.own_ref), channel_id=1, source_target_pairs={{0,2},{2,0},{4,6},{6,4},{1,3},{3,1},{5,7},{7,5},{8,10},{10,8},{12,... | collective-permute-start | bytes 294920 | tf_op jit(solution)/shard_map/ppermute | solution.py:146
  89.0 3.6 %collective-permute-start.22 = (f32[8,128]{1,0:T(8,128)S(1)}, f32[8,128]{1,0:T(8,128)S(1)}, u32[]{:S(2)}, u32[]{:S(2)}) collective-permute-start(f32[8,128]{1,0:T(8,128)S(1)} %add_select_fusion), channel_id=1, source_target_pairs={{0,2},{2,0},{4,6},{6,4},{1,3},{3,1},{5,7},{7,5},{8,10},{10,8},{12,... | collective-permute-start | bytes 12296 | tf_op jit(solution)/shard_map/ppermute | solution.py:146
  92.6 1.2 %collective-permute-start.23 = (f32[8,128]{1,0:T(8,128)S(1)}, f32[8,128]{1,0:T(8,128)S(1)}, u32[]{:S(2)}, u32[]{:S(2)}) collective-permute-start(f32[8,128]{1,0:T(8,128)S(1)} %add.33.square_ref), channel_id=1, source_target_pairs={{0,1},{1,0},{2,3},{3,2},{4,5},{5,4},{6,7},{7,6},{8,9},{9,8},{10,11... | collective-permute-start | bytes 12296 | tf_op jit(solution)/shard_map/ppermute | solution.py:146
  (3 other events, 4.1 us)

commit v6 on v5

--- a/solution.py
+++ b/solution.py
@@ -137,6 +137,7 @@
 
 F32, BF16 = jnp.float32, jnp.bfloat16
 VMEM = pl.BlockSpec(memory_space=pltpu.VMEM)
+ANYWHERE = pl.BlockSpec(memory_space=pl.ANY)
 LIMIT = 16 * 1024 * 1024
 STEPS = 10.0
 
@@ -146,14 +147,14 @@
     return lax.ppermute(value, axis, [(i, i ^ distance) for i in range(count)])
 
 
-def call(kernel, outs, *operands, flops=0, scratch=(), loose=()):
+def call(kernel, outs, *operands, flops=0, scratch=(), loose=(), loose_outs=()):
     shapes = [jax.ShapeDtypeStruct(shape, dtype) for shape, dtype in outs]
     moved = sum(math.prod(x.shape) * x.dtype.itemsize for x in (*operands, *shapes))
     return pl.pallas_call(
         kernel,
         out_shape=shapes,
-        in_specs=[pl.BlockSpec(memory_space=pl.ANY) if i in loose else VMEM for i in range(len(operands))],
-        out_specs=[VMEM] * len(shapes),
+        in_specs=[ANYWHERE if i in loose else VMEM for i in range(len(operands))],
+        out_specs=[ANYWHERE if i in loose_outs else VMEM for i in range(len(shapes))],
         scratch_shapes=scratch,
         compiler_params=pltpu.CompilerParams(vmem_limit_bytes=LIMIT),
         cost_estimate=pl.CostEstimate(flops=flops, bytes_accessed=moved, transcendentals=0),
@@ -177,22 +178,30 @@
     return 0, jnp.where(core == 0, 1, 2), jnp.where(core == 0, 2, 1), 3
 
 
-def norm_kernel(mine_ref, other_ref, gain_ref, gain_other_ref, *outs):
+def norm_kernel(mine_ref, other_ref, gain_ref, gain_other_ref, *refs):
+    outs, (held_ref, written) = refs[:4], refs[4:]
     width = outs[0].shape[1]
     place, core = lax.axis_index("ctx"), lax.axis_index("tp")
     mine, other = mine_ref[...].astype(F32), other_ref[...].astype(F32)
     squares = [jnp.sum(rows * rows, axis=1, keepdims=True) for rows in (mine, other)]
     scale = lax.rsqrt((squares[0] + squares[1]) / (4 * width) + 1e-06)
-    for d, out_ref in zip(distances(), outs):
-        chip = place ^ d
+    copies = []
+    for index in (3, 1, 2, 0):
+        chip = place ^ distances()[index]
         columns = pl.ds(pl.multiple_of(chip % 2 * width, width), width)
-
-        def write(rows_ref, weights_ref, out_ref=out_ref, columns=columns):
+        slot = outs[0] if index == 0 else held_ref.at[index - 1]
+
+        def write(rows_ref, weights_ref, slot=slot, columns=columns):
             rows = rows_ref[:, columns].astype(F32) * scale
-            out_ref[...] = (rows * weights_ref[:, columns].astype(F32)).astype(BF16)
+            slot[...] = (rows * weights_ref[:, columns].astype(F32)).astype(BF16)
 
         pl.when(chip // 2 == core)(functools.partial(write, mine_ref, gain_ref))
         pl.when(chip // 2 != core)(functools.partial(write, other_ref, gain_other_ref))
+        if index:
+            copies.append(pltpu.make_async_copy(slot, outs[index], written.at[index - 1]))
+            copies[-1].start()
+    for copy in copies:
+        copy.wait()
 
 
 def join_rows(mine_ref, other_ref, out_ref):
@@ -245,10 +254,14 @@
     return ref[-16:, : ref.shape[0] - 16].astype(F32)[:1]
 
 
-def own_kernel(head, even_ref, even_other_ref, weight_ref, own_ref, weight_out_ref, rows_ref):
-    weight_out_ref[...] = weight_ref[...]
+def own_kernel(
+    head, even_ref, even_other_ref, weight_ref, own_ref, weight_out_ref, rows_ref, arrived
+):
+    copy = pltpu.make_async_copy(weight_ref, weight_out_ref, arrived)
+    copy.start()
     join_rows(even_ref, even_other_ref, rows_ref)
-    product = times(rows_ref[...], weight_ref[...])
+    copy.wait()
+    product = times(rows_ref[...], weight_out_ref[...])
     own_ref[...] = jnp.concatenate(split_heads(product, head), axis=1)
 
 
@@ -294,18 +307,15 @@
         ).astype(BF16)
 
 
-def accumulate_kernel(
-    own_ref, got_ref, docs_ref, cosine_ref, sine_ref, out_ref, docs_out_ref, cosine_out_ref, sine_out_ref
-):
+def accumulate_kernel(own_ref, got_ref, back_ref, back_other_ref, *refs):
+    count = len(refs) // 2
+    out_ref, back_out_ref = refs[count - 1 : count + 1]
     keys, values = unpack(got_ref, own_ref.shape[0])
     width = keys.shape[1]
     out_ref[:, :width] = own_ref[:, :width] + keys
     out_ref[:, width:] = own_ref[:, width:] + values
-    for ref, copy_ref in (
-        (docs_ref, docs_out_ref),
-        (cosine_ref, cosine_out_ref),
-        (sine_ref, sine_out_ref),
-    ):
+    back_out_ref[...] = (back_ref[...] + back_other_ref[...]).astype(BF16)
+    for ref, copy_ref in zip(refs[: count - 1], refs[count + 1 :]):
         copy_ref[...] = ref[...]
 
 
@@ -330,16 +340,6 @@
     return (key_at <= query_at) & (key_docs == query_docs)
 
 
-def group_scores(query_ref, keys, allowed, head, group):
-    rows = allowed.shape[0]
-    groups = keys.shape[1] // head
-    count = query_ref.shape[0] // groups
-    scores = times_transposed(
-        query_ref[group * count : (group + 1) * count], keys[:, group * head : (group + 1) * head]
-    ).reshape(count // rows, rows, keys.shape[0])
-    return jnp.where(allowed[None], scores, -1e30).reshape(count, keys.shape[0])
-
-
 def attention_kernel(
     head,
     query_ref,
@@ -349,10 +349,11 @@
     block_c_ref,
     down_ref,
     back_ref,
-    back_other_ref,
     out_ref,
     low_ref,
     grad_ref,
+    mixed_ref,
+    written,
 ):
     rows = block_0_ref.shape[0] - 16
     width = block_0_ref.shape[1] // 2
@@ -363,23 +364,35 @@
     allowed = jnp.concatenate(
         [allowed_pairs(own_docs, load_docs(ref), d) for d, ref in zip(distances(), blocks)], axis=1
     )
-    groups = width // head
-    count = query_ref.shape[0] // groups
     scale = head ** (-0.5) * math.log2(math.e)
     ones = jnp.ones((len(blocks) * rows, head), BF16)
-    for group in range(groups):
-        scores = group_scores(query_ref, keys, allowed, head, group)
+    groups = width // head
+    pairs = query_ref.shape[0] // (2 * rows)
+    copies = []
+    for pair in range(pairs):
+        shared = slice(pair * groups // pairs * head, (pair * groups // pairs + 1) * head)
+        scores = times_transposed(
+            query_ref[2 * pair * rows : 2 * (pair + 1) * rows], keys[:, shared]
+        ).reshape(2, rows, keys.shape[0])
+        scores = jnp.where(allowed[None], scores, -1e30).reshape(2 * rows, keys.shape[0])
         weights = jnp.exp2((scores - jnp.max(scores, axis=1, keepdims=True)) * scale)
-        group_values = jnp.concatenate([values[:, group * head : (group + 1) * head], ones], axis=1)
-        mixed = times(weights.astype(BF16), group_values)
+        mixed = times(
+            weights.astype(BF16), jnp.concatenate([values[:, shared], ones], axis=1)
+        )
         mixed = (mixed[:, :head] / mixed[:, head:]).astype(BF16)
-        for index in range(count // rows):
-            column = group * count // rows * head + index * head
-            out_ref[:, column : column + head] = mixed[index * rows : (index + 1) * rows]
-    attended = out_ref[...]
+        columns = slice(2 * pair * head, 2 * (pair + 1) * head)
+        mixed_ref[:, columns] = jnp.concatenate([mixed[:rows], mixed[rows:]], axis=1)
+        copies.append(
+            pltpu.make_async_copy(
+                mixed_ref.at[:, columns], out_ref.at[:, columns], written.at[pair]
+            )
+        )
+        copies[-1].start()
+    attended = mixed_ref[...]
     low_ref[...] = times_transposed(attended, down_ref[...])
-    back = (back_ref[...] + back_other_ref[...]).astype(BF16)
-    grad_ref[...] = transposed_times(back, attended)
+    grad_ref[...] = transposed_times(back_ref[...], attended)
+    for copy in copies:
+        copy.wait()
 
 
 def back_kernel(grad_ref, up_ref, out_ref):
@@ -444,7 +457,14 @@
     theirs = lax.dynamic_slice_in_dim(hidden[0], (1 - core) * half, half, 0)
     part = ((half, slice_width), BF16)
     slices = call(
-        norm_kernel, [part] * 4, mine, swap(theirs, "tp", 1), gain, swap(gain, "tp", 1)
+        norm_kernel,
+        [part] * 4,
+        mine,
+        swap(theirs, "tp", 1),
+        gain,
+        swap(gain, "tp", 1),
+        scratch=[pltpu.VMEM((3, half, slice_width), BF16), pltpu.SemaphoreType.DMA((3,))],
+        loose_outs=(1, 2, 3),
     )
 
     def send_a(value):
@@ -512,7 +532,8 @@
         swap(even, "tp", 1),
         weight,
         flops=part_flops,
-        scratch=[pltpu.VMEM((rows, slice_width), BF16)],
+        scratch=[pltpu.VMEM((rows, slice_width), BF16), pltpu.SemaphoreType.DMA],
+        loose=(2,),
     )
     got_c, part_0, docs = lax.optimization_barrier((got_c, part_0, docs))
 
@@ -542,14 +563,24 @@
         scratch=[pltpu.VMEM((2 * rows, slice_width), BF16)],
     )
     arrived_a, arrived_b = send_a(sent_a), send_b(sent_b)
-    part_0, docs, cosine, sine = call(
+    part_0, back_rows, docs, cosine, sine, staged_down = call(
         accumulate_kernel,
-        [summed, ((1, rows), F32), ((rows, head), F32), ((rows, head), F32)],
+        [
+            summed,
+            ((rows, rank), BF16),
+            ((1, rows), F32),
+            ((rows, head), F32),
+            ((rows, head), F32),
+            ((rank, local_query), BF16),
+        ],
         part_0,
         arrived_c,
+        back_part,
+        back_other,
         docs,
         cosine,
         sine,
+        adapt_down[0],
     )
     arrived_a, arrived_b, part_0 = lax.optimization_barrier((arrived_a, arrived_b, part_0))
     (block_0,) = call(finish_kernel, [final], part_0, arrived_a, arrived_b, docs, cosine, sine)
@@ -562,10 +593,14 @@
         send_a(block_0),
         send_b(block_0),
         swap(block_0, "ctx", 3),
-        adapt_down[0],
-        back_part,
-        back_other,
+        staged_down,
+        back_rows,
         flops=16 * rows * rows * local_query,
+        scratch=[
+            pltpu.VMEM((rows, local_query), BF16),
+            pltpu.SemaphoreType.DMA((head_count // 2,)),
+        ],
+        loose_outs=(0,),
     )
     low_other = swap(low_part, "tp", 1)
     piece = (rank, (local_width + local_query) // 2)

time: 95 us -> 93.7 us (0.986)
  Pallas kernels: 16.7 us -> 15.2 us
    pallas_call x14, Pallas kernels: 16.7 us -> 15.2 us  [call(): pl.pallas_call(kernel, out_shape=shapes, in_specs=[ANYWHERE if i in loose...]
where the time goes in v6:
time: 93.7 us; the launch traced here: 93.3 us
  waiting for transfers between devices  48.9 us (52%)
  starting transfers between devices  20.8 us (22%)
  Pallas kernels  15.2 us (16%)
  local copies, waits for them, and re-layouts  6.44 us (7%)
  other arithmetic  1.08 us (1%)
    ppermute x18, waiting for transfers between devices, swap(): return lax.ppermute(value, axis, [(i, i ^ distance) for i in range(count)])  29.8 us
    pallas_call x14, Pallas kernels, call(): pl.pallas_call(kernel, out_shape=shapes, in_specs=[ANYWHERE if i in loose...  15.2 us
    ppermute x3, waiting for transfers between devices, send_b(): lax.ppermute(value, ('ctx', 'tp'), [(2 * a + t, 2 * (a ^ (1 if t else 2))...  14.1 us
    ppermute x18, starting transfers between devices, swap(): return lax.ppermute(value, axis, [(i, i ^ distance) for i in range(count)])  13.9 us
    ppermute x3, waiting for transfers between devices, send_a(): lax.ppermute(value, ('ctx', 'tp'), [(2 * a + t, 2 * (a ^ (2 if t else 1))...  4.32 us
    ppermute x3, starting transfers between devices, send_a(): lax.ppermute(value, ('ctx', 'tp'), [(2 * a + t, 2 * (a ^ (2 if t else 1))...  2.89 us
    squeeze x1, local copies, waits for them, and re-layouts, prepare(): return key_value_weight[0].reshape(slice_width, kv_width)  2.75 us
    ppermute x3, starting transfers between devices, send_b(): lax.ppermute(value, ('ctx', 'tp'), [(2 * a + t, 2 * (a ^ (1 if t else 2))...  2.5 us
  transfers between devices with their start and end apart: 25, of which 16 were waited for; matrix products, arithmetic and copies ran while one was open for 4% of the time, Pallas kernels for 11%

profile of v6, /device:TPU:0, one launch (start us, length us, event | category | flops | bytes accessed | tf_op | source)
XLA Modules:
  0.0 93.3 jit_solution(9795612349691394526)
XLA Ops:
  0.7 1.4 %dynamic-slice_bitcast_fusion = (bf16[64,4096]{1,0:T(8,128)(2,1)S(1)}, bf16[64,4096]{1,0:T(8,128)(2,1)S(1)}) fusion(bf16[1,128,4096]{2,1,0:T(8,128)(2,1)} %param.14, s32[]{:T(128)S(6)} %select_n.15, s32[]{:T(128)S(6)} %select_n.14), kind=kLoop, calls=%fused_computation.9 | loop fusion | bytes 2097160 | tf_op jit(solution)/shard_map/dynamic_slice | solution.py:457
  2.7 1.5 %collective-permute-done.3.gain_other_ref = bf16[1,4096]{1,0:T(2,128)(2,1)S(1)} collective-permute-done((bf16[1,4096]{1,0:T(2,128)(2,1)S(1)}, bf16[1,4096]{1,0:T(2,128)(2,1)S(1)}, u32[]{:S(2)}, u32[]{:S(2)}) %collective-permute-start.3) | collective-permute-done | bytes 8224 | tf_op jit(solution)/shard_map/ppermute | solution.py:147
  4.2 1.3 %shard_map.117 = (bf16[64,2048]{1,0:T(8,128)(2,1)S(1)}, bf16[64,2048]{1,0:T(8,128)(2,1)}, bf16[64,2048]{1,0:T(8,128)(2,1)}, bf16[64,2048]{1,0:T(8,128)(2,1)}) custom-call(bf16[64,4096]{1,0:T(8,128)(2,1)S(1)} %get-tuple-element.122.mine_ref, bf16[64,4096]{1,0:T(8,128)(2,1)S(1)} %collective-permute-done.2.other_ref, bf16[1,4096]{1,0:T(2,128)(2,1)S(1)} %copy-done.1, ...), custom_call_target="tpu_custom_call" | custom-call | bytes 2113536 | tf_op jit(solution)/shard_map/pallas_call | solution.py:153
  5.9 4.8 %collective-permute-start.6 = (bf16[64,2048]{1,0:T(8,128)(2,1)}, bf16[64,2048]{1,0:T(8,128)(2,1)}, u32[]{:S(2)}, u32[]{:S(2)}) collective-permute-start(bf16[64,2048]{1,0:T(8,128)(2,1)} %get-tuple-element.74), channel_id=1, source_target_pairs={{0,6},{2,4},{4,2},{6,0},{1,7},{3,5},{5,3},{7,1},{8,14},{10,12},{12... | collective-permute-start | bytes 786440 | tf_op jit(solution)/shard_map/ppermute | solution.py:147
  11.2 3.4 %conditional.3 = (f32[1,128]{1,0:T(1,128)S(1)}, f32[128,128]{1,0:T(8,128)}, f32[128,128]{1,0:T(8,128)}, bf16[2048,128]{1,0:T(8,128)(2,1)S(1)}, f32[128,16]{1,0:T(8,128)}, /*index=5*/f32[128,16]{1,0:T(8,128)}) conditional(s32[]{:T(128)} %convert_element_type.15, () %tuple.32, (s32[128]{0:T(128)S(1)}, s32[]{:T(128)}, ...), branch_computations={%region_0.0_spmd, %region_1.0_spmd} | conditional | flops 16826880 | bytes 3779176 | solution.py:489
  15.4 2.7 %conditional.4 = (bf16[2048,512]{1,0:T(8,128)(2,1)S(1)}) conditional(s32[]{:T(128)} %convert_element_type.15, () %tuple.35, (bf16[1,2048,2,2,128]{4,3,2,1,0:T(2,128)(2,1)}) %tuple.42), branch_computations={%region_2.0_spmd, %region_3.0_spmd} | conditional | bytes 4194312 | solution.py:489
  15.4 2.7 %squeeze.19 = bf16[2048,512]{1,0:T(8,128)(2,1)S(1)} reshape(bf16[1,2048,2,2,128]{4,3,2,1,0:T(2,128)(2,1)} %get-tuple-element.115) | data formatting | bytes 4194304 | tf_op jit(solution)/shard_map/cond/branch_1_fun/reshape;cond/branch_1_fun/squeeze | solution.py:497
  18.2 1.3 %copy-done.2 = bf16[2048,512]{1,0:T(8,128)(2,1)} copy-done((bf16[2048,512]{1,0:T(8,128)(2,1)}, bf16[2048,512]{1,0:T(8,128)(2,1)S(1)}, u32[]{:S(2)}) %copy-start.2) | copy-done | bytes 2097176
  19.5 2.0 %shard_map.118 = (f32[128,512]{1,0:T(8,128)S(1)}, bf16[2048,512]{1,0:T(8,128)(2,1)S(1)}) custom-call(bf16[64,2048]{1,0:T(8,128)(2,1)S(1)} %get-tuple-element.75.even_ref, bf16[64,2048]{1,0:T(8,128)(2,1)S(1)} %collective-permute-done.7.even_other_ref, bf16[2048,512]{1,0:T(8,128)(2,1)} %copy-done.2), custom_call_target="tpu_custom_call" | custom-call | flops 268435456 | bytes 4980736 | tf_op jit(solution)/shard_map/pallas_call | solution.py:153
  21.6 4.8 %conditional.5 = (bf16[128,640]{1,0:T(8,128)(2,1)}) conditional(s32[]{:T(128)} %convert_element_type.15, () %tuple.34, (bf16[64,2048]{1,0:T(8,128)(2,1)}, bf16[2048,512]{1,0:T(8,128)(2,1)}) %tuple.53), branch_computations={%region_4.0_spmd, %region_5.0_spmd} | conditional | flops 268435456 | bytes 3833904 | solution.py:489
  22.2 1.4 %collective-permute-done.got_other_ref = bf16[64,2048]{1,0:T(8,128)(2,1)S(1)} collective-permute-done((bf16[64,2048]{1,0:T(8,128)(2,1)}, bf16[64,2048]{1,0:T(8,128)(2,1)S(1)}, u32[]{:S(2)}, u32[]{:S(2)}) %collective-permute-start) | collective-permute-done | bytes 262176 | tf_op jit(solution)/shard_map/cond/branch_1_fun/ppermute | solution.py:147
  23.5 2.8 %branch_1_fun.5 = bf16[128,640]{1,0:T(8,128)(2,1)} custom-call(bf16[64,2048]{1,0:T(8,128)(2,1)} %get-tuple-element.26.got_ref, bf16[64,2048]{1,0:T(8,128)(2,1)S(1)} %collective-permute-done.got_other_ref, bf16[2048,512]{1,0:T(8,128)(2,1)} %get-tuple-element.27.weight_ref), custom_call_target="tpu_custom_call" | custom-call | flops 268435456 | bytes 2785280 | tf_op jit(solution)/shard_map/cond/branch_1_fun/pallas_call | solution.py:153
  26.4 7.3 %collective-permute-done.5.got_b_ref = bf16[64,2048]{1,0:T(8,128)(2,1)S(1)} collective-permute-done((bf16[64,2048]{1,0:T(8,128)(2,1)}, bf16[64,2048]{1,0:T(8,128)(2,1)S(1)}, u32[]{:S(2)}, u32[]{:S(2)}) %collective-permute-start.5) | collective-permute-done | bytes 262176 | tf_op jit(solution)/shard_map/ppermute | solution.py:476
  34.2 2.5 %collective-permute-start.12 = (bf16[128,640]{1,0:T(8,128)(2,1)}, bf16[128,640]{1,0:T(8,128)(2,1)S(1)}, u32[]{:S(2)}, u32[]{:S(2)}) collective-permute-start(bf16[128,640]{1,0:T(8,128)(2,1)} %get-tuple-element.136), channel_id=1, source_target_pairs={{0,6},{2,4},{4,2},{6,0},{1,7},{3,5},{5,3},{7,1},{8,14},{10,12},{12... | collective-permute-start | bytes 491528 | tf_op jit(solution)/shard_map/ppermute | solution.py:147
  37.5 1.9 %collective-permute-start.11 = (bf16[128,640]{1,0:T(8,128)(2,1)S(1)}, bf16[128,640]{1,0:T(8,128)(2,1)S(1)}, u32[]{:S(2)}, u32[]{:S(2)}) collective-permute-start(bf16[128,640]{1,0:T(8,128)(2,1)S(1)} %get-tuple-element.83), channel_id=1, source_target_pairs={{0,4},{1,3},{2,6},{3,1},{4,0},{5,7},{6,2},{7,5},{8,12},{9,11},{10,... | collective-permute-start | bytes 491528 | tf_op jit(solution)/shard_map/ppermute | solution.py:476
  39.5 3.9 %collective-permute-done.12.got_ref = bf16[128,640]{1,0:T(8,128)(2,1)S(1)} collective-permute-done((bf16[128,640]{1,0:T(8,128)(2,1)}, bf16[128,640]{1,0:T(8,128)(2,1)S(1)}, u32[]{:S(2)}, u32[]{:S(2)}) %collective-permute-start.12) | collective-permute-done | bytes 163872 | tf_op jit(solution)/shard_map/ppermute | solution.py:147
  44.4 4.3 %collective-permute-done.10.got_a_ref = bf16[128,640]{1,0:T(8,128)(2,1)S(1)} collective-permute-done((bf16[128,640]{1,0:T(8,128)(2,1)S(1)}, bf16[128,640]{1,0:T(8,128)(2,1)S(1)}, u32[]{:S(2)}, u32[]{:S(2)}) %collective-permute-start.10) | collective-permute-done | bytes 163872 | tf_op jit(solution)/shard_map/ppermute | solution.py:471
  48.7 1.5 %collective-permute-done.11.got_b_ref = bf16[128,640]{1,0:T(8,128)(2,1)S(1)} collective-permute-done((bf16[128,640]{1,0:T(8,128)(2,1)S(1)}, bf16[128,640]{1,0:T(8,128)(2,1)S(1)}, u32[]{:S(2)}, u32[]{:S(2)}) %collective-permute-start.11) | collective-permute-done | bytes 163872 | tf_op jit(solution)/shard_map/ppermute | solution.py:476
  50.4 1.6 %collective-permute-start.15 = (bf16[144,512]{1,0:T(8,128)(2,1)S(1)}, bf16[144,512]{1,0:T(8,128)(2,1)S(1)}, u32[]{:S(2)}, u32[]{:S(2)}) collective-permute-start(bf16[144,512]{1,0:T(8,128)(2,1)S(1)} %shard_map.121.block_0_ref), channel_id=1, source_target_pairs={{0,6},{2,4},{4,2},{6,0},{1,7},{3,5},{5,3},{7,1},{8,14},{10,12},{12... | collective-permute-start | bytes 442376 | tf_op jit(solution)/shard_map/ppermute | solution.py:147
  52.0 2.8 %collective-permute-start.13 = (bf16[144,512]{1,0:T(8,128)(2,1)S(1)}, bf16[144,512]{1,0:T(8,128)(2,1)S(1)}, u32[]{:S(2)}, u32[]{:S(2)}) collective-permute-start(bf16[144,512]{1,0:T(8,128)(2,1)S(1)} %shard_map.121.block_0_ref), channel_id=1, source_target_pairs={{0,2},{1,5},{2,0},{3,7},{4,6},{5,1},{6,4},{7,3},{8,10},{9,13},{10,... | collective-permute-start | bytes 442376 | tf_op jit(solution)/shard_map/ppermute | solution.py:471
  54.8 4.2 %collective-permute-done.15.block_c_ref = bf16[144,512]{1,0:T(8,128)(2,1)S(1)} collective-permute-done((bf16[144,512]{1,0:T(8,128)(2,1)S(1)}, bf16[144,512]{1,0:T(8,128)(2,1)S(1)}, u32[]{:S(2)}, u32[]{:S(2)}) %collective-permute-start.15) | collective-permute-done | bytes 147488 | tf_op jit(solution)/shard_map/ppermute | solution.py:147
  59.1 5.2 %collective-permute-done.14.block_b_ref = bf16[144,512]{1,0:T(8,128)(2,1)S(1)} collective-permute-done((bf16[144,512]{1,0:T(8,128)(2,1)S(1)}, bf16[144,512]{1,0:T(8,128)(2,1)S(1)}, u32[]{:S(2)}, u32[]{:S(2)}) %collective-permute-start.14) | collective-permute-done | bytes 147488 | tf_op jit(solution)/shard_map/ppermute | solution.py:476
  64.3 2.3 %shard_map.122 = (bf16[128,2048]{1,0:T(8,128)(2,1)}, f32[128,16]{1,0:T(8,128)S(1)}, f32[16,2048]{1,0:T(8,128)S(1)}) custom-call(bf16[2048,128]{1,0:T(8,128)(2,1)S(1)} %copy-done.7, bf16[144,512]{1,0:T(8,128)(2,1)S(1)} %shard_map.121.block_0_ref, bf16[144,512]{1,0:T(8,128)(2,1)S(1)} %collective-permute-done.13.block_a_ref, ...), custom_call_target="tpu_custom_call" | custom-call | flops 536870912 | bytes 1847296 | tf_op jit(solution)/shard_map/pallas_call | solution.py:153
  66.7 1.2 %collective-permute-done.16.low_other_ref = f32[128,16]{1,0:T(8,128)S(1)} collective-permute-done((f32[128,16]{1,0:T(8,128)S(1)}, f32[128,16]{1,0:T(8,128)S(1)}, u32[]{:S(2)}, u32[]{:S(2)}) %collective-permute-start.16) | collective-permute-done | bytes 8224 | tf_op jit(solution)/shard_map/ppermute | solution.py:147
  68.3 1.4 %shard_map.124 = bf16[128,4096]{1,0:T(8,128)(2,1)} custom-call(f32[128,16]{1,0:T(8,128)S(1)} %get-tuple-element.100.low_ref, f32[128,16]{1,0:T(8,128)S(1)} %collective-permute-done.16.low_other_ref, bf16[16,4096]{1,0:T(8,128)(2,1)S(1)} %bitcast.25), custom_call_target="tpu_custom_call" | custom-call | flops 16777216 | bytes 1196032 | tf_op jit(solution)/shard_map/pallas_call | solution.py:153
  69.7 3.5 %collective-permute-done.17.got_ref = bf16[16,3072]{1,0:T(8,128)(2,1)S(1)} collective-permute-done((bf16[16,3072]{1,0:T(8,128)(2,1)S(1)}, bf16[16,3072]{1,0:T(8,128)(2,1)S(1)}, u32[]{:S(2)}, u32[]{:S(2)}) %collective-permute-start.17) | collective-permute-done | bytes 98336 | tf_op jit(solution)/shard_map/ppermute | solution.py:147
  73.2 1.3 %collective-permute-start.18 = (bf16[16,3072]{1,0:T(8,128)(2,1)S(1)}, bf16[16,3072]{1,0:T(8,128)(2,1)S(1)}, u32[]{:S(2)}, u32[]{:S(2)}) collective-permute-start(bf16[16,3072]{1,0:T(8,128)(2,1)S(1)} %shard_map.125.own_ref), channel_id=1, source_target_pairs={{0,4},{2,6},{4,0},{6,2},{1,5},{3,7},{5,1},{7,3},{8,12},{10,14},{12... | collective-permute-start | bytes 294920 | tf_op jit(solution)/shard_map/ppermute | solution.py:147
  74.5 5.8 %collective-permute-done.18.got_ref = bf16[16,3072]{1,0:T(8,128)(2,1)S(1)} collective-permute-done((bf16[16,3072]{1,0:T(8,128)(2,1)S(1)}, bf16[16,3072]{1,0:T(8,128)(2,1)S(1)}, u32[]{:S(2)}, u32[]{:S(2)}) %collective-permute-start.18) | collective-permute-done | bytes 98336 | tf_op jit(solution)/shard_map/ppermute | solution.py:147
  81.7 1.5 %collective-permute-start.21 = (f32[8,128]{1,0:T(8,128)S(1)}, f32[8,128]{1,0:T(8,128)S(1)}, u32[]{:S(2)}, u32[]{:S(2)}) collective-permute-start(f32[8,128]{1,0:T(8,128)S(1)} %add.30), channel_id=1, source_target_pairs={{0,8},{1,17},{8,0},{9,25},{16,24},{17,1},{24,16},{25,9},{2,10},{3,... | collective-permute-start | bytes 12296 | tf_op jit(solution)/shard_map/ppermute | solution.py:631
  83.2 1.5 %collective-permute-start.20 = (f32[8,128]{1,0:T(8,128)S(1)}, f32[8,128]{1,0:T(8,128)S(1)}, u32[]{:S(2)}, u32[]{:S(2)}) collective-permute-start(f32[8,128]{1,0:T(8,128)S(1)} %add.30), channel_id=1, source_target_pairs={{0,24},{8,16},{16,8},{24,0},{1,25},{9,17},{17,9},{25,1},{2,26},{10... | collective-permute-start | bytes 12296 | tf_op jit(solution)/shard_map/ppermute | solution.py:147
  85.3 2.4 %collective-permute-done.20 = f32[8,128]{1,0:T(8,128)S(1)} collective-permute-done((f32[8,128]{1,0:T(8,128)S(1)}, f32[8,128]{1,0:T(8,128)S(1)}, u32[]{:S(2)}, u32[]{:S(2)}) %collective-permute-start.20) | collective-permute-done | bytes 4128 | tf_op jit(solution)/shard_map/ppermute | solution.py:147
  87.7 3.6 %collective-permute-done.22 = f32[8,128]{1,0:T(8,128)S(1)} collective-permute-done((f32[8,128]{1,0:T(8,128)S(1)}, f32[8,128]{1,0:T(8,128)S(1)}, u32[]{:S(2)}, u32[]{:S(2)}) %collective-permute-start.22) | collective-permute-done | bytes 4128 | tf_op jit(solution)/shard_map/ppermute | solution.py:147
  (66 shorter events, 13.3 us)
Async XLA Ops:
  0.6 10.6 %copy-start.3 = (bf16[1,128,4096]{2,1,0:T(8,128)(2,1)S(1)}, bf16[1,128,4096]{2,1,0:T(8,128)(2,1)}, u32[]{:S(2)}) copy-start(bf16[1,128,4096]{2,1,0:T(8,128)(2,1)} %param.20) | copy-start | bytes 3145732
  0.7 10.5 %copy-start.5 = (bf16[1,16,4096]{2,1,0:T(8,128)(2,1)S(1)}, bf16[1,16,4096]{2,1,0:T(8,128)(2,1)}, u32[]{:S(2)}) copy-start(bf16[1,16,4096]{2,1,0:T(8,128)(2,1)} %param.19) | copy-start | bytes 393220
  0.7 10.5 %copy-start.9 = (s32[128]{0:T(128)S(1)}, s32[128]{0:T(128)}, u32[]{:S(2)}) copy-start(s32[128]{0:T(128)} %param.21) | copy-start | bytes 1540
  0.7 10.5 %copy-start.8 = (bf16[1,128,16,128]{3,2,1,0:T(8,128)(2,1)S(1)}, bf16[1,128,16,128]{3,2,1,0:T(8,128)(2,1)}, u32[]{:S(2)}) copy-start(bf16[1,128,16,128]{3,2,1,0:T(8,128)(2,1)} %param.16) | copy-start | bytes 1572868
  2.1 2.1 %collective-permute-start.2 = (bf16[64,4096]{1,0:T(8,128)(2,1)S(1)}, bf16[64,4096]{1,0:T(8,128)(2,1)S(1)}, u32[]{:S(2)}, u32[]{:S(2)}) collective-permute-start(bf16[64,4096]{1,0:T(8,128)(2,1)S(1)} %get-tuple-element.121), channel_id=1, source_target_pairs={{0,1},{1,0},{2,3},{3,2},{4,5},{5,4},{6,7},{7,6},{8,9},{9,8},{10,11... | collective-permute-start | bytes 1572872 | tf_op jit(solution)/shard_map/ppermute | solution.py:147
  2.6 1.6 %collective-permute-start.3 = (bf16[1,4096]{1,0:T(2,128)(2,1)S(1)}, bf16[1,4096]{1,0:T(2,128)(2,1)S(1)}, u32[]{:S(2)}, u32[]{:S(2)}) collective-permute-start(bf16[1,4096]{1,0:T(2,128)(2,1)S(1)} %copy-done.1), channel_id=1, source_target_pairs={{0,1},{1,0},{2,3},{3,2},{4,5},{5,4},{6,7},{7,6},{8,9},{9,8},{10,11... | collective-permute-start | bytes 24584 | tf_op jit(solution)/shard_map/ppermute | solution.py:147
  5.5 14.1 %collective-permute-start.7 = (bf16[64,2048]{1,0:T(8,128)(2,1)S(1)}, bf16[64,2048]{1,0:T(8,128)(2,1)S(1)}, u32[]{:S(2)}, u32[]{:S(2)}) collective-permute-start(bf16[64,2048]{1,0:T(8,128)(2,1)S(1)} %get-tuple-element.75.even_ref), channel_id=1, source_target_pairs={{0,1},{1,0},{2,3},{3,2},{4,5},{5,4},{6,7},{7,6},{8,9},{9,8},{10,11... | collective-permute-start | bytes 786440 | tf_op jit(solution)/shard_map/ppermute | solution.py:147
  5.9 15.7 %collective-permute-start.6 = (bf16[64,2048]{1,0:T(8,128)(2,1)}, bf16[64,2048]{1,0:T(8,128)(2,1)}, u32[]{:S(2)}, u32[]{:S(2)}) collective-permute-start(bf16[64,2048]{1,0:T(8,128)(2,1)} %get-tuple-element.74), channel_id=1, source_target_pairs={{0,6},{2,4},{4,2},{6,0},{1,7},{3,5},{5,3},{7,1},{8,14},{10,12},{12... | collective-permute-start | bytes 786440 | tf_op jit(solution)/shard_map/ppermute | solution.py:147
  10.6 15.7 %collective-permute-start.4 = (bf16[64,2048]{1,0:T(8,128)(2,1)}, bf16[64,2048]{1,0:T(8,128)(2,1)S(1)}, u32[]{:S(2)}, u32[]{:S(2)}) collective-permute-start(bf16[64,2048]{1,0:T(8,128)(2,1)} %get-tuple-element.72), channel_id=1, source_target_pairs={{0,2},{1,5},{2,0},{3,7},{4,6},{5,1},{6,4},{7,3},{8,10},{9,13},{10,... | collective-permute-start | bytes 786440 | tf_op jit(solution)/shard_map/ppermute | solution.py:471
  10.6 23.0 %collective-permute-start.5 = (bf16[64,2048]{1,0:T(8,128)(2,1)}, bf16[64,2048]{1,0:T(8,128)(2,1)S(1)}, u32[]{:S(2)}, u32[]{:S(2)}) collective-permute-start(bf16[64,2048]{1,0:T(8,128)(2,1)} %get-tuple-element.73), channel_id=1, source_target_pairs={{0,4},{1,3},{2,6},{3,1},{4,0},{5,7},{6,2},{7,5},{8,12},{9,11},{10,... | collective-permute-start | bytes 786440 | tf_op jit(solution)/shard_map/ppermute | solution.py:476
  12.2 2.4 %collective-permute-start.1 = (f32[128,16]{1,0:T(8,128)}, f32[128,16]{1,0:T(8,128)}, u32[]{:S(2)}, u32[]{:S(2)}) collective-permute-start(f32[128,16]{1,0:T(8,128)} %branch_1_fun.4), channel_id=1, source_target_pairs={{0,1},{1,0},{2,3},{3,2},{4,5},{5,4},{6,7},{7,6},{8,9},{9,8},{10,11... | collective-permute-start | bytes 24584 | tf_op jit(solution)/shard_map/cond/branch_1_fun/ppermute | solution.py:147
  21.6 1.9 %collective-permute-start = (bf16[64,2048]{1,0:T(8,128)(2,1)}, bf16[64,2048]{1,0:T(8,128)(2,1)S(1)}, u32[]{:S(2)}, u32[]{:S(2)}) collective-permute-start(bf16[64,2048]{1,0:T(8,128)(2,1)} %get-tuple-element.26.got_ref), channel_id=1, source_target_pairs={{0,1},{1,0},{2,3},{3,2},{4,5},{5,4},{6,7},{7,6},{8,9},{9,8},{10,11... | collective-permute-start | bytes 786440 | tf_op jit(solution)/shard_map/cond/branch_1_fun/ppermute | solution.py:147
  26.4 17.0 %copy-start = (bf16[1,16,2048]{2,1,0:T(8,128)(2,1)S(1)}, bf16[1,16,2048]{2,1,0:T(8,128)(2,1)}, u32[]{:S(2)}) copy-start(bf16[1,16,2048]{2,1,0:T(8,128)(2,1)} %param.18) | copy-start | bytes 196612
  33.7 3.0 %collective-permute-start.8 = (bf16[64,2048]{1,0:T(8,128)(2,1)S(1)}, bf16[64,2048]{1,0:T(8,128)(2,1)S(1)}, u32[]{:S(2)}, u32[]{:S(2)}) collective-permute-start(bf16[64,2048]{1,0:T(8,128)(2,1)S(1)} %collective-permute-done.4.got_a_ref), channel_id=1, source_target_pairs={{0,1},{1,0},{2,3},{3,2},{4,5},{5,4},{6,7},{7,6},{8,9},{9,8},{10,11... | collective-permute-start | bytes 786440 | tf_op jit(solution)/shard_map/ppermute | solution.py:147
  33.7 3.0 %collective-permute-start.9 = (bf16[64,2048]{1,0:T(8,128)(2,1)S(1)}, bf16[64,2048]{1,0:T(8,128)(2,1)S(1)}, u32[]{:S(2)}, u32[]{:S(2)}) collective-permute-start(bf16[64,2048]{1,0:T(8,128)(2,1)S(1)} %collective-permute-done.5.got_b_ref), channel_id=1, source_target_pairs={{0,1},{1,0},{2,3},{3,2},{4,5},{5,4},{6,7},{7,6},{8,9},{9,8},{10,11... | collective-permute-start | bytes 786440 | tf_op jit(solution)/shard_map/ppermute | solution.py:147
  34.2 9.2 %collective-permute-start.12 = (bf16[128,640]{1,0:T(8,128)(2,1)}, bf16[128,640]{1,0:T(8,128)(2,1)S(1)}, u32[]{:S(2)}, u32[]{:S(2)}) collective-permute-start(bf16[128,640]{1,0:T(8,128)(2,1)} %get-tuple-element.136), channel_id=1, source_target_pairs={{0,6},{2,4},{4,2},{6,0},{1,7},{3,5},{5,3},{7,1},{8,14},{10,12},{12... | collective-permute-start | bytes 491528 | tf_op jit(solution)/shard_map/ppermute | solution.py:147
  36.7 27.7 %copy-start.7 = (bf16[2048,128]{1,0:T(8,128)(2,1)S(1)}, bf16[2048,128]{1,0:T(8,128)(2,1)}, u32[]{:S(2)}) copy-start(bf16[2048,128]{1,0:T(8,128)(2,1)} %copy-done.6) | copy-start | bytes 1572868
  37.4 30.6 %copy-start.4 = (bf16[1,128,4096]{2,1,0:T(8,128)(2,1)S(1)}, bf16[1,128,4096]{2,1,0:T(8,128)(2,1)}, u32[]{:S(2)}) copy-start(bf16[1,128,4096]{2,1,0:T(8,128)(2,1)} %param.20) | copy-start | bytes 3145732
  37.4 11.2 %collective-permute-start.10 = (bf16[128,640]{1,0:T(8,128)(2,1)S(1)}, bf16[128,640]{1,0:T(8,128)(2,1)S(1)}, u32[]{:S(2)}, u32[]{:S(2)}) collective-permute-start(bf16[128,640]{1,0:T(8,128)(2,1)S(1)} %get-tuple-element.82), channel_id=1, source_target_pairs={{0,2},{1,5},{2,0},{3,7},{4,6},{5,1},{6,4},{7,3},{8,10},{9,13},{10,... | collective-permute-start | bytes 491528 | tf_op jit(solution)/shard_map/ppermute | solution.py:471
  37.5 12.7 %collective-permute-start.11 = (bf16[128,640]{1,0:T(8,128)(2,1)S(1)}, bf16[128,640]{1,0:T(8,128)(2,1)S(1)}, u32[]{:S(2)}, u32[]{:S(2)}) collective-permute-start(bf16[128,640]{1,0:T(8,128)(2,1)S(1)} %get-tuple-element.83), channel_id=1, source_target_pairs={{0,4},{1,3},{2,6},{3,1},{4,0},{5,7},{6,2},{7,5},{8,12},{9,11},{10,... | collective-permute-start | bytes 491528 | tf_op jit(solution)/shard_map/ppermute | solution.py:476
  50.4 8.7 %collective-permute-start.15 = (bf16[144,512]{1,0:T(8,128)(2,1)S(1)}, bf16[144,512]{1,0:T(8,128)(2,1)S(1)}, u32[]{:S(2)}, u32[]{:S(2)}) collective-permute-start(bf16[144,512]{1,0:T(8,128)(2,1)S(1)} %shard_map.121.block_0_ref), channel_id=1, source_target_pairs={{0,6},{2,4},{4,2},{6,0},{1,7},{3,5},{5,3},{7,1},{8,14},{10,12},{12... | collective-permute-start | bytes 442376 | tf_op jit(solution)/shard_map/ppermute | solution.py:147
  52.0 12.3 %collective-permute-start.14 = (bf16[144,512]{1,0:T(8,128)(2,1)S(1)}, bf16[144,512]{1,0:T(8,128)(2,1)S(1)}, u32[]{:S(2)}, u32[]{:S(2)}) collective-permute-start(bf16[144,512]{1,0:T(8,128)(2,1)S(1)} %shard_map.121.block_0_ref), channel_id=1, source_target_pairs={{0,4},{1,3},{2,6},{3,1},{4,0},{5,7},{6,2},{7,5},{8,12},{9,11},{10,... | collective-permute-start | bytes 442376 | tf_op jit(solution)/shard_map/ppermute | solution.py:476
  52.0 12.3 %collective-permute-start.13 = (bf16[144,512]{1,0:T(8,128)(2,1)S(1)}, bf16[144,512]{1,0:T(8,128)(2,1)S(1)}, u32[]{:S(2)}, u32[]{:S(2)}) collective-permute-start(bf16[144,512]{1,0:T(8,128)(2,1)S(1)} %shard_map.121.block_0_ref), channel_id=1, source_target_pairs={{0,2},{1,5},{2,0},{3,7},{4,6},{5,1},{6,4},{7,3},{8,10},{9,13},{10,... | collective-permute-start | bytes 442376 | tf_op jit(solution)/shard_map/ppermute | solution.py:471
  66.7 1.3 %collective-permute-start.16 = (f32[128,16]{1,0:T(8,128)S(1)}, f32[128,16]{1,0:T(8,128)S(1)}, u32[]{:S(2)}, u32[]{:S(2)}) collective-permute-start(f32[128,16]{1,0:T(8,128)S(1)} %get-tuple-element.100.low_ref), channel_id=1, source_target_pairs={{0,1},{1,0},{2,3},{3,2},{4,5},{5,4},{6,7},{7,6},{8,9},{9,8},{10,11... | collective-permute-start | bytes 24584 | tf_op jit(solution)/shard_map/ppermute | solution.py:147
  68.3 4.9 %collective-permute-start.17 = (bf16[16,3072]{1,0:T(8,128)(2,1)S(1)}, bf16[16,3072]{1,0:T(8,128)(2,1)S(1)}, u32[]{:S(2)}, u32[]{:S(2)}) collective-permute-start(bf16[16,3072]{1,0:T(8,128)(2,1)S(1)} %get-tuple-element.102), channel_id=1, source_target_pairs={{0,2},{2,0},{4,6},{6,4},{1,3},{3,1},{5,7},{7,5},{8,10},{10,8},{12,... | collective-permute-start | bytes 294920 | tf_op jit(solution)/shard_map/ppermute | solution.py:147
  73.2 7.1 %collective-permute-start.18 = (bf16[16,3072]{1,0:T(8,128)(2,1)S(1)}, bf16[16,3072]{1,0:T(8,128)(2,1)S(1)}, u32[]{:S(2)}, u32[]{:S(2)}) collective-permute-start(bf16[16,3072]{1,0:T(8,128)(2,1)S(1)} %shard_map.125.own_ref), channel_id=1, source_target_pairs={{0,4},{2,6},{4,0},{6,2},{1,5},{3,7},{5,1},{7,3},{8,12},{10,14},{12... | collective-permute-start | bytes 294920 | tf_op jit(solution)/shard_map/ppermute | solution.py:147
  80.5 1.2 %collective-permute-start.19 = (f32[8,128]{1,0:T(8,128)S(1)}, f32[8,128]{1,0:T(8,128)S(1)}, u32[]{:S(2)}, u32[]{:S(2)}) collective-permute-start(f32[8,128]{1,0:T(8,128)S(1)} %get-tuple-element.106), channel_id=1, source_target_pairs={{0,1},{1,0},{2,3},{3,2},{4,5},{5,4},{6,7},{7,6},{8,9},{9,8},{10,11... | collective-permute-start | bytes 12296 | tf_op jit(solution)/shard_map/ppermute | solution.py:147
  81.7 3.6 %collective-permute-start.21 = (f32[8,128]{1,0:T(8,128)S(1)}, f32[8,128]{1,0:T(8,128)S(1)}, u32[]{:S(2)}, u32[]{:S(2)}) collective-permute-start(f32[8,128]{1,0:T(8,128)S(1)} %add.30), channel_id=1, source_target_pairs={{0,8},{1,17},{8,0},{9,25},{16,24},{17,1},{24,16},{25,9},{2,10},{3,... | collective-permute-start | bytes 12296 | tf_op jit(solution)/shard_map/ppermute | solution.py:631
  83.2 4.5 %collective-permute-start.20 = (f32[8,128]{1,0:T(8,128)S(1)}, f32[8,128]{1,0:T(8,128)S(1)}, u32[]{:S(2)}, u32[]{:S(2)}) collective-permute-start(f32[8,128]{1,0:T(8,128)S(1)} %add.30), channel_id=1, source_target_pairs={{0,24},{8,16},{16,8},{24,0},{1,25},{9,17},{17,9},{25,1},{2,26},{10... | collective-permute-start | bytes 12296 | tf_op jit(solution)/shard_map/ppermute | solution.py:147
  84.7 7.8 %collective-permute-start.24 = (bf16[16,3072]{1,0:T(8,128)(2,1)S(1)}, bf16[16,3072]{1,0:T(8,128)(2,1)S(1)}, u32[]{:S(2)}, u32[]{:S(2)}) collective-permute-start(bf16[16,3072]{1,0:T(8,128)(2,1)S(1)} %get-tuple-element.107.own_ref), channel_id=1, source_target_pairs={{0,2},{2,0},{4,6},{6,4},{1,3},{3,1},{5,7},{7,5},{8,10},{10,8},{12,... | collective-permute-start | bytes 294920 | tf_op jit(solution)/shard_map/ppermute | solution.py:147
  87.7 3.6 %collective-permute-start.22 = (f32[8,128]{1,0:T(8,128)S(1)}, f32[8,128]{1,0:T(8,128)S(1)}, u32[]{:S(2)}, u32[]{:S(2)}) collective-permute-start(f32[8,128]{1,0:T(8,128)S(1)} %add_select_fusion), channel_id=1, source_target_pairs={{0,2},{2,0},{4,6},{6,4},{1,3},{3,1},{5,7},{7,5},{8,10},{10,8},{12,... | collective-permute-start | bytes 12296 | tf_op jit(solution)/shard_map/ppermute | solution.py:147
  91.3 1.2 %collective-permute-start.23 = (f32[8,128]{1,0:T(8,128)S(1)}, f32[8,128]{1,0:T(8,128)S(1)}, u32[]{:S(2)}, u32[]{:S(2)}) collective-permute-start(f32[8,128]{1,0:T(8,128)S(1)} %add.33.square_ref), channel_id=1, source_target_pairs={{0,1},{1,0},{2,3},{3,2},{4,5},{5,4},{6,7},{7,6},{8,9},{9,8},{10,11... | collective-permute-start | bytes 12296 | tf_op jit(solution)/shard_map/ppermute | solution.py:147
  (3 other events, 4.1 us)

commit v7 on v6

--- a/solution.py
+++ b/solution.py
@@ -139,7 +139,7 @@
 VMEM = pl.BlockSpec(memory_space=pltpu.VMEM)
 ANYWHERE = pl.BlockSpec(memory_space=pl.ANY)
 LIMIT = 16 * 1024 * 1024
-STEPS = 10.0
+LEVELS = (5, 5, 5, 4)
 
 
 def swap(value, axis, distance):
@@ -227,22 +227,32 @@
     high = keys.astype(BF16)
     wide = high.astype(F32)
     size = jnp.abs(wide)
-    steps = jnp.round((keys - wide) * (256.0 * STEPS) / jnp.where(size > 0, size, 1.0))
-    half = width // 2
+    part = (keys - wide) * 256.0 / jnp.where(size > 0, size, 1.0)
     out_ref[:rows, :width] = high
-    out_ref[:rows, width : 2 * width] = values.astype(BF16)
-    pairs = steps[:, :half] * (2.0 * STEPS + 1.0) + steps[:, half:]
-    out_ref[:rows, 2 * width :] = pairs.astype(BF16)
+    out_ref[:rows, width:] = values.astype(BF16)
+    count = rows // len(LEVELS)
+    code, weight = -250.0, 1.0
+    for index, levels in enumerate(LEVELS):
+        level = jnp.floor((part[index * count : (index + 1) * count] + 1.0) * (levels / 2))
+        code = code + jnp.clip(level, 0.0, levels - 1.0) * weight
+        weight *= levels
+    code = jnp.concatenate([code[: count // 2], code[count // 2 :]], axis=1)
+    out_ref[rows:] = code.astype(BF16)
 
 
 def unpack(ref, rows):
-    width = ref.shape[1] * 2 // 5
+    width = ref.shape[1] // 2
     wide = ref[:rows, :width].astype(F32)
-    pairs = ref[:rows, 2 * width :].astype(F32)
-    first = jnp.round(pairs / (2.0 * STEPS + 1.0))
-    steps = jnp.concatenate([first, pairs - first * (2.0 * STEPS + 1.0)], axis=1)
-    keys = wide + jnp.abs(wide) * steps * (1.0 / (256.0 * STEPS))
-    return keys, ref[:rows, width : 2 * width].astype(F32)
+    code = ref[rows:].astype(F32) + 250.0
+    code = jnp.concatenate([code[:, :width], code[:, width:]], axis=0)
+    parts, weight = [], math.prod(LEVELS)
+    for levels in reversed(LEVELS):
+        weight /= levels
+        level = jnp.floor((code + 0.5) / weight)
+        code = code - level * weight
+        parts.append((level * 2.0 + 1.0) / levels - 1.0)
+    part = jnp.concatenate(parts[::-1], axis=0)
+    return wide + jnp.abs(wide) * part * (1.0 / 256.0), ref[:rows, width:].astype(F32)
 
 
 def store_docs(docs, out_ref):
@@ -281,7 +291,7 @@
     sent_b_ref,
     rows_ref,
 ):
-    count = sent_a_ref.shape[0]
+    count = rows_ref.shape[0] // 2
     join_rows(got_a_ref, got_b_other_ref, rows_ref.at[:count])
     join_rows(got_b_ref, got_a_other_ref, rows_ref.at[count:])
     product = times(rows_ref[...], weight_ref[...])
@@ -449,7 +459,6 @@
     local_query = head_count * head
     rank = adapt_down.shape[1]
     kv_width = kv_count * 2 * head
-    sent_width = kv_count * 5 * head // 2
 
     half = rows // 2
     core = lax.axis_index("tp")
@@ -480,7 +489,7 @@
     even, slice_a, slice_b, slice_c = slices
     got_a, got_b, got_c = send_a(slice_a), send_b(slice_b), swap(slice_c, "ctx", 3)
     part_flops = 2 * rows * slice_width * kv_width
-    packed = ((rows, sent_width), BF16)
+    packed = ((rows + rows // 8, kv_width), BF16)
     summed = ((rows, kv_width), F32)
     final = ((rows + 16, kv_width), BF16)
 

time: 93.7 us -> 92.7 us (0.989)
  waiting for transfers between devices: 48.9 us -> 47.8 us
where the time goes in v7:
time: 92.7 us; the launch traced here: 92.3 us
  waiting for transfers between devices  47.8 us (52%)
  starting transfers between devices  20.8 us (22%)
  Pallas kernels  15.3 us (17%)
  local copies, waits for them, and re-layouts  6.44 us (7%)
  other arithmetic  1.08 us (1%)
    ppermute x18, waiting for transfers between devices, swap(): return lax.ppermute(value, axis, [(i, i ^ distance) for i in range(count)])  29.5 us
    pallas_call x14, Pallas kernels, call(): pl.pallas_call(kernel, out_shape=shapes, in_specs=[ANYWHERE if i in loose...  15.3 us
    ppermute x18, starting transfers between devices, swap(): return lax.ppermute(value, axis, [(i, i ^ distance) for i in range(count)])  14.2 us
    ppermute x3, waiting for transfers between devices, send_b(): lax.ppermute(value, ('ctx', 'tp'), [(2 * a + t, 2 * (a ^ (1 if t else 2))...  13.8 us
    ppermute x3, waiting for transfers between devices, send_a(): lax.ppermute(value, ('ctx', 'tp'), [(2 * a + t, 2 * (a ^ (2 if t else 1))...  3.94 us
    squeeze x1, local copies, waits for them, and re-layouts, prepare(): return key_value_weight[0].reshape(slice_width, kv_width)  2.75 us
    ppermute x3, starting transfers between devices, send_a(): lax.ppermute(value, ('ctx', 'tp'), [(2 * a + t, 2 * (a ^ (2 if t else 1))...  2.54 us
    ppermute x3, starting transfers between devices, send_b(): lax.ppermute(value, ('ctx', 'tp'), [(2 * a + t, 2 * (a ^ (1 if t else 2))...  2.5 us
  transfers between devices with their start and end apart: 25, of which 16 were waited for; matrix products, arithmetic and copies ran while one was open for 4% of the time, Pallas kernels for 11%

profile of v7, /device:TPU:0, one launch (start us, length us, event | category | flops | bytes accessed | tf_op | source)
XLA Modules:
  0.0 92.3 jit_solution(4748350116898664957)
XLA Ops:
  0.7 1.4 %dynamic-slice_bitcast_fusion = (bf16[64,4096]{1,0:T(8,128)(2,1)S(1)}, bf16[64,4096]{1,0:T(8,128)(2,1)S(1)}) fusion(bf16[1,128,4096]{2,1,0:T(8,128)(2,1)} %param.14, s32[]{:T(128)S(6)} %select_n.15, s32[]{:T(128)S(6)} %select_n.14), kind=kLoop, calls=%fused_computation.9 | loop fusion | bytes 2097160 | tf_op jit(solution)/shard_map/dynamic_slice | solution.py:466
  2.7 1.5 %collective-permute-done.3.gain_other_ref = bf16[1,4096]{1,0:T(2,128)(2,1)S(1)} collective-permute-done((bf16[1,4096]{1,0:T(2,128)(2,1)S(1)}, bf16[1,4096]{1,0:T(2,128)(2,1)S(1)}, u32[]{:S(2)}, u32[]{:S(2)}) %collective-permute-start.3) | collective-permute-done | bytes 8224 | tf_op jit(solution)/shard_map/ppermute | solution.py:147
  4.2 1.3 %shard_map.117 = (bf16[64,2048]{1,0:T(8,128)(2,1)S(1)}, bf16[64,2048]{1,0:T(8,128)(2,1)}, bf16[64,2048]{1,0:T(8,128)(2,1)}, bf16[64,2048]{1,0:T(8,128)(2,1)}) custom-call(bf16[64,4096]{1,0:T(8,128)(2,1)S(1)} %get-tuple-element.122.mine_ref, bf16[64,4096]{1,0:T(8,128)(2,1)S(1)} %collective-permute-done.2.other_ref, bf16[1,4096]{1,0:T(2,128)(2,1)S(1)} %copy-done.1, ...), custom_call_target="tpu_custom_call" | custom-call | bytes 2113536 | tf_op jit(solution)/shard_map/pallas_call | solution.py:153
  5.9 4.8 %collective-permute-start.6 = (bf16[64,2048]{1,0:T(8,128)(2,1)}, bf16[64,2048]{1,0:T(8,128)(2,1)}, u32[]{:S(2)}, u32[]{:S(2)}) collective-permute-start(bf16[64,2048]{1,0:T(8,128)(2,1)} %get-tuple-element.74), channel_id=1, source_target_pairs={{0,6},{2,4},{4,2},{6,0},{1,7},{3,5},{5,3},{7,1},{8,14},{10,12},{12... | collective-permute-start | bytes 786440 | tf_op jit(solution)/shard_map/ppermute | solution.py:147
  11.2 3.4 %conditional.3 = (f32[1,128]{1,0:T(1,128)S(1)}, f32[128,128]{1,0:T(8,128)}, f32[128,128]{1,0:T(8,128)}, bf16[2048,128]{1,0:T(8,128)(2,1)S(1)}, f32[128,16]{1,0:T(8,128)}, /*index=5*/f32[128,16]{1,0:T(8,128)}) conditional(s32[]{:T(128)} %convert_element_type.15, () %tuple.32, (s32[128]{0:T(128)S(1)}, s32[]{:T(128)}, ...), branch_computations={%region_0.0_spmd, %region_1.0_spmd} | conditional | flops 16826880 | bytes 3779176 | solution.py:498
  15.4 2.7 %conditional.4 = (bf16[2048,512]{1,0:T(8,128)(2,1)S(1)}) conditional(s32[]{:T(128)} %convert_element_type.15, () %tuple.35, (bf16[1,2048,2,2,128]{4,3,2,1,0:T(2,128)(2,1)}) %tuple.42), branch_computations={%region_2.0_spmd, %region_3.0_spmd} | conditional | bytes 4194312 | solution.py:498
  15.4 2.7 %squeeze.19 = bf16[2048,512]{1,0:T(8,128)(2,1)S(1)} reshape(bf16[1,2048,2,2,128]{4,3,2,1,0:T(2,128)(2,1)} %get-tuple-element.115) | data formatting | bytes 4194304 | tf_op jit(solution)/shard_map/cond/branch_1_fun/reshape;cond/branch_1_fun/squeeze | solution.py:506
  18.2 1.3 %copy-done.2 = bf16[2048,512]{1,0:T(8,128)(2,1)} copy-done((bf16[2048,512]{1,0:T(8,128)(2,1)}, bf16[2048,512]{1,0:T(8,128)(2,1)S(1)}, u32[]{:S(2)}) %copy-start.2) | copy-done | bytes 2097176
  19.5 2.0 %shard_map.118 = (f32[128,512]{1,0:T(8,128)S(1)}, bf16[2048,512]{1,0:T(8,128)(2,1)S(1)}) custom-call(bf16[64,2048]{1,0:T(8,128)(2,1)S(1)} %get-tuple-element.75.even_ref, bf16[64,2048]{1,0:T(8,128)(2,1)S(1)} %collective-permute-done.7.even_other_ref, bf16[2048,512]{1,0:T(8,128)(2,1)} %copy-done.2), custom_call_target="tpu_custom_call" | custom-call | flops 268435456 | bytes 4980736 | tf_op jit(solution)/shard_map/pallas_call | solution.py:153
  21.6 4.8 %conditional.5 = (bf16[144,512]{1,0:T(8,128)(2,1)}) conditional(s32[]{:T(128)} %convert_element_type.15, () %tuple.34, (bf16[64,2048]{1,0:T(8,128)(2,1)}, bf16[2048,512]{1,0:T(8,128)(2,1)}) %tuple.53), branch_computations={%region_4.0_spmd, %region_5.0_spmd} | conditional | flops 268435456 | bytes 3817520 | solution.py:498
  22.2 1.4 %collective-permute-done.got_other_ref = bf16[64,2048]{1,0:T(8,128)(2,1)S(1)} collective-permute-done((bf16[64,2048]{1,0:T(8,128)(2,1)}, bf16[64,2048]{1,0:T(8,128)(2,1)S(1)}, u32[]{:S(2)}, u32[]{:S(2)}) %collective-permute-start) | collective-permute-done | bytes 262176 | tf_op jit(solution)/shard_map/cond/branch_1_fun/ppermute | solution.py:147
  23.5 2.8 %branch_1_fun.5 = bf16[144,512]{1,0:T(8,128)(2,1)} custom-call(bf16[64,2048]{1,0:T(8,128)(2,1)} %get-tuple-element.26.got_ref, bf16[64,2048]{1,0:T(8,128)(2,1)S(1)} %collective-permute-done.got_other_ref, bf16[2048,512]{1,0:T(8,128)(2,1)} %get-tuple-element.27.weight_ref), custom_call_target="tpu_custom_call" | custom-call | flops 268435456 | bytes 2768896 | tf_op jit(solution)/shard_map/cond/branch_1_fun/pallas_call | solution.py:153
  26.4 7.3 %collective-permute-done.5.got_b_ref = bf16[64,2048]{1,0:T(8,128)(2,1)S(1)} collective-permute-done((bf16[64,2048]{1,0:T(8,128)(2,1)}, bf16[64,2048]{1,0:T(8,128)(2,1)S(1)}, u32[]{:S(2)}, u32[]{:S(2)}) %collective-permute-start.5) | collective-permute-done | bytes 262176 | tf_op jit(solution)/shard_map/ppermute | solution.py:485
  34.2 2.5 %collective-permute-start.12 = (bf16[144,512]{1,0:T(8,128)(2,1)}, bf16[144,512]{1,0:T(8,128)(2,1)S(1)}, u32[]{:S(2)}, u32[]{:S(2)}) collective-permute-start(bf16[144,512]{1,0:T(8,128)(2,1)} %get-tuple-element.136), channel_id=1, source_target_pairs={{0,6},{2,4},{4,2},{6,0},{1,7},{3,5},{5,3},{7,1},{8,14},{10,12},{12... | collective-permute-start | bytes 442376 | tf_op jit(solution)/shard_map/ppermute | solution.py:147
  37.5 1.9 %collective-permute-start.11 = (bf16[144,512]{1,0:T(8,128)(2,1)S(1)}, bf16[144,512]{1,0:T(8,128)(2,1)S(1)}, u32[]{:S(2)}, u32[]{:S(2)}) collective-permute-start(bf16[144,512]{1,0:T(8,128)(2,1)S(1)} %get-tuple-element.83), channel_id=1, source_target_pairs={{0,4},{1,3},{2,6},{3,1},{4,0},{5,7},{6,2},{7,5},{8,12},{9,11},{10,... | collective-permute-start | bytes 442376 | tf_op jit(solution)/shard_map/ppermute | solution.py:485
  39.5 3.5 %collective-permute-done.12.got_ref = bf16[144,512]{1,0:T(8,128)(2,1)S(1)} collective-permute-done((bf16[144,512]{1,0:T(8,128)(2,1)}, bf16[144,512]{1,0:T(8,128)(2,1)S(1)}, u32[]{:S(2)}, u32[]{:S(2)}) %collective-permute-start.12) | collective-permute-done | bytes 147488 | tf_op jit(solution)/shard_map/ppermute | solution.py:147
  44.0 3.9 %collective-permute-done.10.got_a_ref = bf16[144,512]{1,0:T(8,128)(2,1)S(1)} collective-permute-done((bf16[144,512]{1,0:T(8,128)(2,1)S(1)}, bf16[144,512]{1,0:T(8,128)(2,1)S(1)}, u32[]{:S(2)}, u32[]{:S(2)}) %collective-permute-start.10) | collective-permute-done | bytes 147488 | tf_op jit(solution)/shard_map/ppermute | solution.py:480
  49.0 2.0 %collective-permute-start.15 = (bf16[144,512]{1,0:T(8,128)(2,1)S(1)}, bf16[144,512]{1,0:T(8,128)(2,1)S(1)}, u32[]{:S(2)}, u32[]{:S(2)}) collective-permute-start(bf16[144,512]{1,0:T(8,128)(2,1)S(1)} %shard_map.121.block_0_ref), channel_id=1, source_target_pairs={{0,6},{2,4},{4,2},{6,0},{1,7},{3,5},{5,3},{7,1},{8,14},{10,12},{12... | collective-permute-start | bytes 442376 | tf_op jit(solution)/shard_map/ppermute | solution.py:147
  51.0 2.5 %collective-permute-start.13 = (bf16[144,512]{1,0:T(8,128)(2,1)S(1)}, bf16[144,512]{1,0:T(8,128)(2,1)S(1)}, u32[]{:S(2)}, u32[]{:S(2)}) collective-permute-start(bf16[144,512]{1,0:T(8,128)(2,1)S(1)} %shard_map.121.block_0_ref), channel_id=1, source_target_pairs={{0,2},{1,5},{2,0},{3,7},{4,6},{5,1},{6,4},{7,3},{8,10},{9,13},{10,... | collective-permute-start | bytes 442376 | tf_op jit(solution)/shard_map/ppermute | solution.py:480
  53.5 4.2 %collective-permute-done.15.block_c_ref = bf16[144,512]{1,0:T(8,128)(2,1)S(1)} collective-permute-done((bf16[144,512]{1,0:T(8,128)(2,1)S(1)}, bf16[144,512]{1,0:T(8,128)(2,1)S(1)}, u32[]{:S(2)}, u32[]{:S(2)}) %collective-permute-start.15) | collective-permute-done | bytes 147488 | tf_op jit(solution)/shard_map/ppermute | solution.py:147
  57.7 5.6 %collective-permute-done.14.block_b_ref = bf16[144,512]{1,0:T(8,128)(2,1)S(1)} collective-permute-done((bf16[144,512]{1,0:T(8,128)(2,1)S(1)}, bf16[144,512]{1,0:T(8,128)(2,1)S(1)}, u32[]{:S(2)}, u32[]{:S(2)}) %collective-permute-start.14) | collective-permute-done | bytes 147488 | tf_op jit(solution)/shard_map/ppermute | solution.py:485
  63.3 2.3 %shard_map.122 = (bf16[128,2048]{1,0:T(8,128)(2,1)}, f32[128,16]{1,0:T(8,128)S(1)}, f32[16,2048]{1,0:T(8,128)S(1)}) custom-call(bf16[2048,128]{1,0:T(8,128)(2,1)S(1)} %copy-done.7, bf16[144,512]{1,0:T(8,128)(2,1)S(1)} %shard_map.121.block_0_ref, bf16[144,512]{1,0:T(8,128)(2,1)S(1)} %collective-permute-done.13.block_a_ref, ...), custom_call_target="tpu_custom_call" | custom-call | flops 536870912 | bytes 1847296 | tf_op jit(solution)/shard_map/pallas_call | solution.py:153
  65.7 1.2 %collective-permute-done.16.low_other_ref = f32[128,16]{1,0:T(8,128)S(1)} collective-permute-done((f32[128,16]{1,0:T(8,128)S(1)}, f32[128,16]{1,0:T(8,128)S(1)}, u32[]{:S(2)}, u32[]{:S(2)}) %collective-permute-start.16) | collective-permute-done | bytes 8224 | tf_op jit(solution)/shard_map/ppermute | solution.py:147
  67.3 1.4 %shard_map.124 = bf16[128,4096]{1,0:T(8,128)(2,1)} custom-call(f32[128,16]{1,0:T(8,128)S(1)} %get-tuple-element.100.low_ref, f32[128,16]{1,0:T(8,128)S(1)} %collective-permute-done.16.low_other_ref, bf16[16,4096]{1,0:T(8,128)(2,1)S(1)} %bitcast.25), custom_call_target="tpu_custom_call" | custom-call | flops 16777216 | bytes 1196032 | tf_op jit(solution)/shard_map/pallas_call | solution.py:153
  68.7 3.5 %collective-permute-done.17.got_ref = bf16[16,3072]{1,0:T(8,128)(2,1)S(1)} collective-permute-done((bf16[16,3072]{1,0:T(8,128)(2,1)S(1)}, bf16[16,3072]{1,0:T(8,128)(2,1)S(1)}, u32[]{:S(2)}, u32[]{:S(2)}) %collective-permute-start.17) | collective-permute-done | bytes 98336 | tf_op jit(solution)/shard_map/ppermute | solution.py:147
  72.2 1.2 %collective-permute-start.18 = (bf16[16,3072]{1,0:T(8,128)(2,1)S(1)}, bf16[16,3072]{1,0:T(8,128)(2,1)S(1)}, u32[]{:S(2)}, u32[]{:S(2)}) collective-permute-start(bf16[16,3072]{1,0:T(8,128)(2,1)S(1)} %shard_map.125.own_ref), channel_id=1, source_target_pairs={{0,4},{2,6},{4,0},{6,2},{1,5},{3,7},{5,1},{7,3},{8,12},{10,14},{12... | collective-permute-start | bytes 294920 | tf_op jit(solution)/shard_map/ppermute | solution.py:147
  73.4 5.8 %collective-permute-done.18.got_ref = bf16[16,3072]{1,0:T(8,128)(2,1)S(1)} collective-permute-done((bf16[16,3072]{1,0:T(8,128)(2,1)S(1)}, bf16[16,3072]{1,0:T(8,128)(2,1)S(1)}, u32[]{:S(2)}, u32[]{:S(2)}) %collective-permute-start.18) | collective-permute-done | bytes 98336 | tf_op jit(solution)/shard_map/ppermute | solution.py:147
  80.7 1.5 %collective-permute-start.21 = (f32[8,128]{1,0:T(8,128)S(1)}, f32[8,128]{1,0:T(8,128)S(1)}, u32[]{:S(2)}, u32[]{:S(2)}) collective-permute-start(f32[8,128]{1,0:T(8,128)S(1)} %add.30), channel_id=1, source_target_pairs={{0,8},{1,17},{8,0},{9,25},{16,24},{17,1},{24,16},{25,9},{2,10},{3,... | collective-permute-start | bytes 12296 | tf_op jit(solution)/shard_map/ppermute | solution.py:640
  82.2 1.5 %collective-permute-start.20 = (f32[8,128]{1,0:T(8,128)S(1)}, f32[8,128]{1,0:T(8,128)S(1)}, u32[]{:S(2)}, u32[]{:S(2)}) collective-permute-start(f32[8,128]{1,0:T(8,128)S(1)} %add.30), channel_id=1, source_target_pairs={{0,24},{8,16},{16,8},{24,0},{1,25},{9,17},{17,9},{25,1},{2,26},{10... | collective-permute-start | bytes 12296 | tf_op jit(solution)/shard_map/ppermute | solution.py:147
  84.3 2.4 %collective-permute-done.20 = f32[8,128]{1,0:T(8,128)S(1)} collective-permute-done((f32[8,128]{1,0:T(8,128)S(1)}, f32[8,128]{1,0:T(8,128)S(1)}, u32[]{:S(2)}, u32[]{:S(2)}) %collective-permute-start.20) | collective-permute-done | bytes 4128 | tf_op jit(solution)/shard_map/ppermute | solution.py:147
  86.7 3.6 %collective-permute-done.22 = f32[8,128]{1,0:T(8,128)S(1)} collective-permute-done((f32[8,128]{1,0:T(8,128)S(1)}, f32[8,128]{1,0:T(8,128)S(1)}, u32[]{:S(2)}, u32[]{:S(2)}) %collective-permute-start.22) | collective-permute-done | bytes 4128 | tf_op jit(solution)/shard_map/ppermute | solution.py:147
  90.3 1.2 %collective-permute-done.23.other_ref = f32[8,128]{1,0:T(8,128)S(1)} collective-permute-done((f32[8,128]{1,0:T(8,128)S(1)}, f32[8,128]{1,0:T(8,128)S(1)}, u32[]{:S(2)}, u32[]{:S(2)}) %collective-permute-start.23) | collective-permute-done | bytes 4128 | tf_op jit(solution)/shard_map/ppermute | solution.py:147
  (66 shorter events, 13.1 us)
Async XLA Ops:
  0.6 10.6 %copy-start.3 = (bf16[1,128,4096]{2,1,0:T(8,128)(2,1)S(1)}, bf16[1,128,4096]{2,1,0:T(8,128)(2,1)}, u32[]{:S(2)}) copy-start(bf16[1,128,4096]{2,1,0:T(8,128)(2,1)} %param.20) | copy-start | bytes 3145732
  0.7 10.5 %copy-start.5 = (bf16[1,16,4096]{2,1,0:T(8,128)(2,1)S(1)}, bf16[1,16,4096]{2,1,0:T(8,128)(2,1)}, u32[]{:S(2)}) copy-start(bf16[1,16,4096]{2,1,0:T(8,128)(2,1)} %param.19) | copy-start | bytes 393220
  0.7 10.5 %copy-start.9 = (s32[128]{0:T(128)S(1)}, s32[128]{0:T(128)}, u32[]{:S(2)}) copy-start(s32[128]{0:T(128)} %param.21) | copy-start | bytes 1540
  0.7 10.5 %copy-start.8 = (bf16[1,128,16,128]{3,2,1,0:T(8,128)(2,1)S(1)}, bf16[1,128,16,128]{3,2,1,0:T(8,128)(2,1)}, u32[]{:S(2)}) copy-start(bf16[1,128,16,128]{3,2,1,0:T(8,128)(2,1)} %param.16) | copy-start | bytes 1572868
  2.1 2.1 %collective-permute-start.2 = (bf16[64,4096]{1,0:T(8,128)(2,1)S(1)}, bf16[64,4096]{1,0:T(8,128)(2,1)S(1)}, u32[]{:S(2)}, u32[]{:S(2)}) collective-permute-start(bf16[64,4096]{1,0:T(8,128)(2,1)S(1)} %get-tuple-element.121), channel_id=1, source_target_pairs={{0,1},{1,0},{2,3},{3,2},{4,5},{5,4},{6,7},{7,6},{8,9},{9,8},{10,11... | collective-permute-start | bytes 1572872 | tf_op jit(solution)/shard_map/ppermute | solution.py:147
  2.6 1.6 %collective-permute-start.3 = (bf16[1,4096]{1,0:T(2,128)(2,1)S(1)}, bf16[1,4096]{1,0:T(2,128)(2,1)S(1)}, u32[]{:S(2)}, u32[]{:S(2)}) collective-permute-start(bf16[1,4096]{1,0:T(2,128)(2,1)S(1)} %copy-done.1), channel_id=1, source_target_pairs={{0,1},{1,0},{2,3},{3,2},{4,5},{5,4},{6,7},{7,6},{8,9},{9,8},{10,11... | collective-permute-start | bytes 24584 | tf_op jit(solution)/shard_map/ppermute | solution.py:147
  5.5 14.1 %collective-permute-start.7 = (bf16[64,2048]{1,0:T(8,128)(2,1)S(1)}, bf16[64,2048]{1,0:T(8,128)(2,1)S(1)}, u32[]{:S(2)}, u32[]{:S(2)}) collective-permute-start(bf16[64,2048]{1,0:T(8,128)(2,1)S(1)} %get-tuple-element.75.even_ref), channel_id=1, source_target_pairs={{0,1},{1,0},{2,3},{3,2},{4,5},{5,4},{6,7},{7,6},{8,9},{9,8},{10,11... | collective-permute-start | bytes 786440 | tf_op jit(solution)/shard_map/ppermute | solution.py:147
  5.9 15.7 %collective-permute-start.6 = (bf16[64,2048]{1,0:T(8,128)(2,1)}, bf16[64,2048]{1,0:T(8,128)(2,1)}, u32[]{:S(2)}, u32[]{:S(2)}) collective-permute-start(bf16[64,2048]{1,0:T(8,128)(2,1)} %get-tuple-element.74), channel_id=1, source_target_pairs={{0,6},{2,4},{4,2},{6,0},{1,7},{3,5},{5,3},{7,1},{8,14},{10,12},{12... | collective-permute-start | bytes 786440 | tf_op jit(solution)/shard_map/ppermute | solution.py:147
  10.6 15.7 %collective-permute-start.4 = (bf16[64,2048]{1,0:T(8,128)(2,1)}, bf16[64,2048]{1,0:T(8,128)(2,1)S(1)}, u32[]{:S(2)}, u32[]{:S(2)}) collective-permute-start(bf16[64,2048]{1,0:T(8,128)(2,1)} %get-tuple-element.72), channel_id=1, source_target_pairs={{0,2},{1,5},{2,0},{3,7},{4,6},{5,1},{6,4},{7,3},{8,10},{9,13},{10,... | collective-permute-start | bytes 786440 | tf_op jit(solution)/shard_map/ppermute | solution.py:480
  10.6 23.0 %collective-permute-start.5 = (bf16[64,2048]{1,0:T(8,128)(2,1)}, bf16[64,2048]{1,0:T(8,128)(2,1)S(1)}, u32[]{:S(2)}, u32[]{:S(2)}) collective-permute-start(bf16[64,2048]{1,0:T(8,128)(2,1)} %get-tuple-element.73), channel_id=1, source_target_pairs={{0,4},{1,3},{2,6},{3,1},{4,0},{5,7},{6,2},{7,5},{8,12},{9,11},{10,... | collective-permute-start | bytes 786440 | tf_op jit(solution)/shard_map/ppermute | solution.py:485
  12.2 2.4 %collective-permute-start.1 = (f32[128,16]{1,0:T(8,128)}, f32[128,16]{1,0:T(8,128)}, u32[]{:S(2)}, u32[]{:S(2)}) collective-permute-start(f32[128,16]{1,0:T(8,128)} %branch_1_fun.4), channel_id=1, source_target_pairs={{0,1},{1,0},{2,3},{3,2},{4,5},{5,4},{6,7},{7,6},{8,9},{9,8},{10,11... | collective-permute-start | bytes 24584 | tf_op jit(solution)/shard_map/cond/branch_1_fun/ppermute | solution.py:147
  21.6 1.9 %collective-permute-start = (bf16[64,2048]{1,0:T(8,128)(2,1)}, bf16[64,2048]{1,0:T(8,128)(2,1)S(1)}, u32[]{:S(2)}, u32[]{:S(2)}) collective-permute-start(bf16[64,2048]{1,0:T(8,128)(2,1)} %get-tuple-element.26.got_ref), channel_id=1, source_target_pairs={{0,1},{1,0},{2,3},{3,2},{4,5},{5,4},{6,7},{7,6},{8,9},{9,8},{10,11... | collective-permute-start | bytes 786440 | tf_op jit(solution)/shard_map/cond/branch_1_fun/ppermute | solution.py:147
  26.4 16.6 %copy-start = (bf16[1,16,2048]{2,1,0:T(8,128)(2,1)S(1)}, bf16[1,16,2048]{2,1,0:T(8,128)(2,1)}, u32[]{:S(2)}) copy-start(bf16[1,16,2048]{2,1,0:T(8,128)(2,1)} %param.18) | copy-start | bytes 196612
  33.7 3.0 %collective-permute-start.8 = (bf16[64,2048]{1,0:T(8,128)(2,1)S(1)}, bf16[64,2048]{1,0:T(8,128)(2,1)S(1)}, u32[]{:S(2)}, u32[]{:S(2)}) collective-permute-start(bf16[64,2048]{1,0:T(8,128)(2,1)S(1)} %collective-permute-done.4.got_a_ref), channel_id=1, source_target_pairs={{0,1},{1,0},{2,3},{3,2},{4,5},{5,4},{6,7},{7,6},{8,9},{9,8},{10,11... | collective-permute-start | bytes 786440 | tf_op jit(solution)/shard_map/ppermute | solution.py:147
  33.7 3.0 %collective-permute-start.9 = (bf16[64,2048]{1,0:T(8,128)(2,1)S(1)}, bf16[64,2048]{1,0:T(8,128)(2,1)S(1)}, u32[]{:S(2)}, u32[]{:S(2)}) collective-permute-start(bf16[64,2048]{1,0:T(8,128)(2,1)S(1)} %collective-permute-done.5.got_b_ref), channel_id=1, source_target_pairs={{0,1},{1,0},{2,3},{3,2},{4,5},{5,4},{6,7},{7,6},{8,9},{9,8},{10,11... | collective-permute-start | bytes 786440 | tf_op jit(solution)/shard_map/ppermute | solution.py:147
  34.2 8.8 %collective-permute-start.12 = (bf16[144,512]{1,0:T(8,128)(2,1)}, bf16[144,512]{1,0:T(8,128)(2,1)S(1)}, u32[]{:S(2)}, u32[]{:S(2)}) collective-permute-start(bf16[144,512]{1,0:T(8,128)(2,1)} %get-tuple-element.136), channel_id=1, source_target_pairs={{0,6},{2,4},{4,2},{6,0},{1,7},{3,5},{5,3},{7,1},{8,14},{10,12},{12... | collective-permute-start | bytes 442376 | tf_op jit(solution)/shard_map/ppermute | solution.py:147
  36.7 26.7 %copy-start.7 = (bf16[2048,128]{1,0:T(8,128)(2,1)S(1)}, bf16[2048,128]{1,0:T(8,128)(2,1)}, u32[]{:S(2)}) copy-start(bf16[2048,128]{1,0:T(8,128)(2,1)} %copy-done.6) | copy-start | bytes 1572868
  37.5 29.5 %copy-start.4 = (bf16[1,128,4096]{2,1,0:T(8,128)(2,1)S(1)}, bf16[1,128,4096]{2,1,0:T(8,128)(2,1)}, u32[]{:S(2)}) copy-start(bf16[1,128,4096]{2,1,0:T(8,128)(2,1)} %param.20) | copy-start | bytes 3145732
  37.5 10.5 %collective-permute-start.10 = (bf16[144,512]{1,0:T(8,128)(2,1)S(1)}, bf16[144,512]{1,0:T(8,128)(2,1)S(1)}, u32[]{:S(2)}, u32[]{:S(2)}) collective-permute-start(bf16[144,512]{1,0:T(8,128)(2,1)S(1)} %get-tuple-element.82), channel_id=1, source_target_pairs={{0,2},{1,5},{2,0},{3,7},{4,6},{5,1},{6,4},{7,3},{8,10},{9,13},{10,... | collective-permute-start | bytes 442376 | tf_op jit(solution)/shard_map/ppermute | solution.py:480
  37.5 11.3 %collective-permute-start.11 = (bf16[144,512]{1,0:T(8,128)(2,1)S(1)}, bf16[144,512]{1,0:T(8,128)(2,1)S(1)}, u32[]{:S(2)}, u32[]{:S(2)}) collective-permute-start(bf16[144,512]{1,0:T(8,128)(2,1)S(1)} %get-tuple-element.83), channel_id=1, source_target_pairs={{0,4},{1,3},{2,6},{3,1},{4,0},{5,7},{6,2},{7,5},{8,12},{9,11},{10,... | collective-permute-start | bytes 442376 | tf_op jit(solution)/shard_map/ppermute | solution.py:485
  49.0 8.7 %collective-permute-start.15 = (bf16[144,512]{1,0:T(8,128)(2,1)S(1)}, bf16[144,512]{1,0:T(8,128)(2,1)S(1)}, u32[]{:S(2)}, u32[]{:S(2)}) collective-permute-start(bf16[144,512]{1,0:T(8,128)(2,1)S(1)} %shard_map.121.block_0_ref), channel_id=1, source_target_pairs={{0,6},{2,4},{4,2},{6,0},{1,7},{3,5},{5,3},{7,1},{8,14},{10,12},{12... | collective-permute-start | bytes 442376 | tf_op jit(solution)/shard_map/ppermute | solution.py:147
  51.0 12.3 %collective-permute-start.14 = (bf16[144,512]{1,0:T(8,128)(2,1)S(1)}, bf16[144,512]{1,0:T(8,128)(2,1)S(1)}, u32[]{:S(2)}, u32[]{:S(2)}) collective-permute-start(bf16[144,512]{1,0:T(8,128)(2,1)S(1)} %shard_map.121.block_0_ref), channel_id=1, source_target_pairs={{0,4},{1,3},{2,6},{3,1},{4,0},{5,7},{6,2},{7,5},{8,12},{9,11},{10,... | collective-permute-start | bytes 442376 | tf_op jit(solution)/shard_map/ppermute | solution.py:485
  51.0 12.3 %collective-permute-start.13 = (bf16[144,512]{1,0:T(8,128)(2,1)S(1)}, bf16[144,512]{1,0:T(8,128)(2,1)S(1)}, u32[]{:S(2)}, u32[]{:S(2)}) collective-permute-start(bf16[144,512]{1,0:T(8,128)(2,1)S(1)} %shard_map.121.block_0_ref), channel_id=1, source_target_pairs={{0,2},{1,5},{2,0},{3,7},{4,6},{5,1},{6,4},{7,3},{8,10},{9,13},{10,... | collective-permute-start | bytes 442376 | tf_op jit(solution)/shard_map/ppermute | solution.py:480
  65.7 1.3 %collective-permute-start.16 = (f32[128,16]{1,0:T(8,128)S(1)}, f32[128,16]{1,0:T(8,128)S(1)}, u32[]{:S(2)}, u32[]{:S(2)}) collective-permute-start(f32[128,16]{1,0:T(8,128)S(1)} %get-tuple-element.100.low_ref), channel_id=1, source_target_pairs={{0,1},{1,0},{2,3},{3,2},{4,5},{5,4},{6,7},{7,6},{8,9},{9,8},{10,11... | collective-permute-start | bytes 24584 | tf_op jit(solution)/shard_map/ppermute | solution.py:147
  67.3 4.9 %collective-permute-start.17 = (bf16[16,3072]{1,0:T(8,128)(2,1)S(1)}, bf16[16,3072]{1,0:T(8,128)(2,1)S(1)}, u32[]{:S(2)}, u32[]{:S(2)}) collective-permute-start(bf16[16,3072]{1,0:T(8,128)(2,1)S(1)} %get-tuple-element.102), channel_id=1, source_target_pairs={{0,2},{2,0},{4,6},{6,4},{1,3},{3,1},{5,7},{7,5},{8,10},{10,8},{12,... | collective-permute-start | bytes 294920 | tf_op jit(solution)/shard_map/ppermute | solution.py:147
  72.2 7.1 %collective-permute-start.18 = (bf16[16,3072]{1,0:T(8,128)(2,1)S(1)}, bf16[16,3072]{1,0:T(8,128)(2,1)S(1)}, u32[]{:S(2)}, u32[]{:S(2)}) collective-permute-start(bf16[16,3072]{1,0:T(8,128)(2,1)S(1)} %shard_map.125.own_ref), channel_id=1, source_target_pairs={{0,4},{2,6},{4,0},{6,2},{1,5},{3,7},{5,1},{7,3},{8,12},{10,14},{12... | collective-permute-start | bytes 294920 | tf_op jit(solution)/shard_map/ppermute | solution.py:147
  79.5 1.2 %collective-permute-start.19 = (f32[8,128]{1,0:T(8,128)S(1)}, f32[8,128]{1,0:T(8,128)S(1)}, u32[]{:S(2)}, u32[]{:S(2)}) collective-permute-start(f32[8,128]{1,0:T(8,128)S(1)} %get-tuple-element.106), channel_id=1, source_target_pairs={{0,1},{1,0},{2,3},{3,2},{4,5},{5,4},{6,7},{7,6},{8,9},{9,8},{10,11... | collective-permute-start | bytes 12296 | tf_op jit(solution)/shard_map/ppermute | solution.py:147
  80.7 3.6 %collective-permute-start.21 = (f32[8,128]{1,0:T(8,128)S(1)}, f32[8,128]{1,0:T(8,128)S(1)}, u32[]{:S(2)}, u32[]{:S(2)}) collective-permute-start(f32[8,128]{1,0:T(8,128)S(1)} %add.30), channel_id=1, source_target_pairs={{0,8},{1,17},{8,0},{9,25},{16,24},{17,1},{24,16},{25,9},{2,10},{3,... | collective-permute-start | bytes 12296 | tf_op jit(solution)/shard_map/ppermute | solution.py:640
  82.2 4.5 %collective-permute-start.20 = (f32[8,128]{1,0:T(8,128)S(1)}, f32[8,128]{1,0:T(8,128)S(1)}, u32[]{:S(2)}, u32[]{:S(2)}) collective-permute-start(f32[8,128]{1,0:T(8,128)S(1)} %add.30), channel_id=1, source_target_pairs={{0,24},{8,16},{16,8},{24,0},{1,25},{9,17},{17,9},{25,1},{2,26},{10... | collective-permute-start | bytes 12296 | tf_op jit(solution)/shard_map/ppermute | solution.py:147
  83.7 7.8 %collective-permute-start.24 = (bf16[16,3072]{1,0:T(8,128)(2,1)S(1)}, bf16[16,3072]{1,0:T(8,128)(2,1)S(1)}, u32[]{:S(2)}, u32[]{:S(2)}) collective-permute-start(bf16[16,3072]{1,0:T(8,128)(2,1)S(1)} %get-tuple-element.107.own_ref), channel_id=1, source_target_pairs={{0,2},{2,0},{4,6},{6,4},{1,3},{3,1},{5,7},{7,5},{8,10},{10,8},{12,... | collective-permute-start | bytes 294920 | tf_op jit(solution)/shard_map/ppermute | solution.py:147
  86.7 3.6 %collective-permute-start.22 = (f32[8,128]{1,0:T(8,128)S(1)}, f32[8,128]{1,0:T(8,128)S(1)}, u32[]{:S(2)}, u32[]{:S(2)}) collective-permute-start(f32[8,128]{1,0:T(8,128)S(1)} %add_select_fusion), channel_id=1, source_target_pairs={{0,2},{2,0},{4,6},{6,4},{1,3},{3,1},{5,7},{7,5},{8,10},{10,8},{12,... | collective-permute-start | bytes 12296 | tf_op jit(solution)/shard_map/ppermute | solution.py:147
  90.3 1.2 %collective-permute-start.23 = (f32[8,128]{1,0:T(8,128)S(1)}, f32[8,128]{1,0:T(8,128)S(1)}, u32[]{:S(2)}, u32[]{:S(2)}) collective-permute-start(f32[8,128]{1,0:T(8,128)S(1)} %add.33.square_ref), channel_id=1, source_target_pairs={{0,1},{1,0},{2,3},{3,2},{4,5},{5,4},{6,7},{7,6},{8,9},{9,8},{10,11... | collective-permute-start | bytes 12296 | tf_op jit(solution)/shard_map/ppermute | solution.py:147
  (3 other events, 4.1 us)

commit v8 on v7

--- a/solution.py
+++ b/solution.py
@@ -462,8 +462,9 @@
 
     half = rows // 2
     core = lax.axis_index("tp")
+    theirs = lax.dynamic_slice_in_dim(hidden[0], (1 - core) * half, half, 0)
+    hidden, theirs = lax.optimization_barrier((hidden, theirs))
     mine = lax.dynamic_slice_in_dim(hidden[0], core * half, half, 0)
-    theirs = lax.dynamic_slice_in_dim(hidden[0], (1 - core) * half, half, 0)
     part = ((half, slice_width), BF16)
     slices = call(
         norm_kernel,
@@ -501,6 +502,8 @@
             lambda *_: jax.tree.map(lambda x: jnp.zeros(x.shape, x.dtype), shapes),
             *operands,
         )
+
+    key_value_weight, slice_c = lax.optimization_barrier((key_value_weight, slice_c))
 
     def prepare(key_value_weight):
         return key_value_weight[0].reshape(slice_width, kv_width)

time: 92.7 us -> 92.9 us (level)
  waiting for transfers between devices: 47.8 us -> 43.6 us
  local copies, waits for them, and re-layouts: 6.44 us -> 9.62 us
  Pallas kernels: 15.3 us -> 16.3 us
    ppermute x3, waiting for transfers between devices: 13.8 us -> 10.5 us  [send_b(): lax.ppermute(value, ('ctx', 'tp'), [(2 * a + t, 2 * (a ^ (1 if t else 2))...]
    unnamed x20 -> x32, local copies, waits for them, and re-layouts: 2.16 us -> 5.29 us
    squeeze x1, local copies, waits for them, and re-layouts: 2.75 us -> 4.12 us  [prepare(): return key_value_weight[0].reshape(slice_width, kv_width)]
    dynamic_slice x1, local copies, waits for them, and re-layouts: 1.4 us -> 0.03 us  [split_model_width(): theirs = lax.dynamic_slice_in_dim(hidden[0], (1 - core) * half, half, 0)]
    ppermute x18, waiting for transfers between devices: 29.5 us -> 28.3 us  [swap(): return lax.ppermute(value, axis, [(i, i ^ distance) for i in range(count)])]
    pallas_call x14, Pallas kernels: 15.3 us -> 16.3 us  [call(): pl.pallas_call(kernel, out_shape=shapes, in_specs=[ANYWHERE if i in loose...]
  transfers between devices with their start and end apart: 25 -> 25, of which waited for: 16 -> 16; matrix products, arithmetic and copies ran while one was open for 4% -> 6% of each run, Pallas kernels for 11% -> 12%
where the time goes in v8:
time: 92.9 us; the launch traced here: 92.5 us
  waiting for transfers between devices  43.6 us (47%)
  starting transfers between devices  20.9 us (22%)
  Pallas kernels  16.3 us (18%)
  local copies, waits for them, and re-layouts  9.62 us (10%)
  other arithmetic  1.08 us (1%)
    ppermute x18, waiting for transfers between devices, swap(): return lax.ppermute(value, axis, [(i, i ^ distance) for i in range(count)])  28.3 us
    pallas_call x14, Pallas kernels, call(): pl.pallas_call(kernel, out_shape=shapes, in_specs=[ANYWHERE if i in loose...  16.3 us
    ppermute x18, starting transfers between devices, swap(): return lax.ppermute(value, axis, [(i, i ^ distance) for i in range(count)])  14.2 us
    ppermute x3, waiting for transfers between devices, send_b(): lax.ppermute(value, ('ctx', 'tp'), [(2 * a + t, 2 * (a ^ (1 if t else 2))...  10.5 us
    unnamed x32, local copies, waits for them, and re-layouts  5.29 us
    ppermute x3, waiting for transfers between devices, send_a(): lax.ppermute(value, ('ctx', 'tp'), [(2 * a + t, 2 * (a ^ (2 if t else 1))...  4.21 us
    squeeze x1, local copies, waits for them, and re-layouts, prepare(): return key_value_weight[0].reshape(slice_width, kv_width)  4.12 us
    ppermute x3, starting transfers between devices, send_b(): lax.ppermute(value, ('ctx', 'tp'), [(2 * a + t, 2 * (a ^ (1 if t else 2))...  2.71 us
  transfers between devices with their start and end apart: 25, of which 16 were waited for; matrix products, arithmetic and copies ran while one was open for 6% of the time, Pallas kernels for 12%

profile of v8, /device:TPU:0, one launch (start us, length us, event | category | flops | bytes accessed | tf_op | source)
XLA Modules:
  0.0 92.5 jit_solution(12558996082168454128)
XLA Ops:
  0.7 1.2 %copy-done = bf16[1,128,4096]{2,1,0:T(8,128)(2,1)S(1)} copy-done((bf16[1,128,4096]{2,1,0:T(8,128)(2,1)S(1)}, bf16[1,128,4096]{2,1,0:T(8,128)(2,1)}, u32[]{:S(2)}) %copy-start) | copy-done | bytes 1048600
  2.5 1.7 %collective-permute-done.3.gain_other_ref = bf16[1,4096]{1,0:T(2,128)(2,1)S(1)} collective-permute-done((bf16[1,4096]{1,0:T(2,128)(2,1)}, bf16[1,4096]{1,0:T(2,128)(2,1)S(1)}, u32[]{:S(2)}, u32[]{:S(2)}) %collective-permute-start.3) | collective-permute-done | bytes 8224 | tf_op jit(solution)/shard_map/ppermute | solution.py:147
  4.2 1.3 %shard_map.113 = (bf16[64,2048]{1,0:T(8,128)(2,1)S(1)}, bf16[64,2048]{1,0:T(8,128)(2,1)}, bf16[64,2048]{1,0:T(8,128)(2,1)}, bf16[64,2048]{1,0:T(8,128)(2,1)}) custom-call(bf16[64,4096]{1,0:T(8,128)(2,1)S(1)} %dynamic-slice_bitcast_fusion.mine_ref, bf16[64,4096]{1,0:T(8,128)(2,1)S(1)} %collective-permute-done.2.other_ref, bf16[1,4096]{1,0:T(2,128)(2,1)S(1)} %copy-done.8, ...), custom_call_target="tpu_custom_call" | custom-call | bytes 2113536 | tf_op jit(solution)/shard_map/pallas_call | solution.py:153
  5.9 4.8 %collective-permute-start.6 = (bf16[64,2048]{1,0:T(8,128)(2,1)}, bf16[64,2048]{1,0:T(8,128)(2,1)}, u32[]{:S(2)}, u32[]{:S(2)}) collective-permute-start(bf16[64,2048]{1,0:T(8,128)(2,1)} %get-tuple-element.79), channel_id=1, source_target_pairs={{0,6},{2,4},{4,2},{6,0},{1,7},{3,5},{5,3},{7,1},{8,14},{10,12},{12... | collective-permute-start | bytes 786440 | tf_op jit(solution)/shard_map/ppermute | solution.py:147
  11.2 3.4 %conditional.3 = (f32[1,128]{1,0:T(1,128)S(1)}, f32[128,128]{1,0:T(8,128)}, f32[128,128]{1,0:T(8,128)}, bf16[2048,128]{1,0:T(8,128)(2,1)S(1)}, f32[128,16]{1,0:T(8,128)}, /*index=5*/f32[128,16]{1,0:T(8,128)}) conditional(s32[]{:T(128)} %convert_element_type.15, () %tuple.34, (s32[128]{0:T(128)S(1)}, s32[]{:T(128)}, ...), branch_computations={%region_0.0_spmd, %region_1.0_spmd} | conditional | flops 16826880 | bytes 5876356 | solution.py:499
  15.5 4.1 %conditional.4 = (bf16[2048,512]{1,0:T(8,128)(2,1)}) conditional(s32[]{:T(128)} %convert_element_type.15, () %tuple.38, bf16[1,2048,2,2,128]{4,3,2,1,0:T(2,128)(2,1)} %param.17), branch_computations={%region_2.0_spmd, %region_3.0_spmd} | conditional | bytes 4194312 | solution.py:499
  15.5 4.1 %squeeze.19 = bf16[2048,512]{1,0:T(8,128)(2,1)} reshape(bf16[1,2048,2,2,128]{4,3,2,1,0:T(2,128)(2,1)} %param.3) | data formatting | bytes 4194304 | tf_op jit(solution)/shard_map/cond/branch_1_fun/reshape;cond/branch_1_fun/squeeze | solution.py:509
  22.2 2.0 %shard_map.114 = (f32[128,512]{1,0:T(8,128)S(1)}, bf16[2048,512]{1,0:T(8,128)(2,1)S(1)}) custom-call(bf16[64,2048]{1,0:T(8,128)(2,1)S(1)} %copy-done.2, bf16[64,2048]{1,0:T(8,128)(2,1)S(1)} %copy-done.4, bf16[2048,512]{1,0:T(8,128)(2,1)} %get-tuple-element.137.weight_ref), custom_call_target="tpu_custom_call" | custom-call | flops 268435456 | bytes 4980736 | tf_op jit(solution)/shard_map/pallas_call | solution.py:153
  24.9 4.7 %conditional.5 = (bf16[144,512]{1,0:T(8,128)(2,1)}) conditional(s32[]{:T(128)} %convert_element_type.15, () %tuple.37, (bf16[64,2048]{1,0:T(8,128)(2,1)}, bf16[2048,512]{1,0:T(8,128)(2,1)}) %tuple.41), branch_computations={%region_4.0_spmd, %region_5.0_spmd} | conditional | flops 268435456 | bytes 3817520 | solution.py:499
  25.4 1.4 %collective-permute-done.got_other_ref = bf16[64,2048]{1,0:T(8,128)(2,1)S(1)} collective-permute-done((bf16[64,2048]{1,0:T(8,128)(2,1)}, bf16[64,2048]{1,0:T(8,128)(2,1)S(1)}, u32[]{:S(2)}, u32[]{:S(2)}) %collective-permute-start) | collective-permute-done | bytes 262176 | tf_op jit(solution)/shard_map/cond/branch_1_fun/ppermute | solution.py:147
  26.8 2.8 %branch_1_fun.5 = bf16[144,512]{1,0:T(8,128)(2,1)} custom-call(bf16[64,2048]{1,0:T(8,128)(2,1)} %get-tuple-element.26.got_ref, bf16[64,2048]{1,0:T(8,128)(2,1)S(1)} %collective-permute-done.got_other_ref, bf16[2048,512]{1,0:T(8,128)(2,1)} %get-tuple-element.27.weight_ref), custom_call_target="tpu_custom_call" | custom-call | flops 268435456 | bytes 2768896 | tf_op jit(solution)/shard_map/cond/branch_1_fun/pallas_call | solution.py:153
  29.7 4.2 %collective-permute-done.5.got_b_ref = bf16[64,2048]{1,0:T(8,128)(2,1)} collective-permute-done((bf16[64,2048]{1,0:T(8,128)(2,1)}, bf16[64,2048]{1,0:T(8,128)(2,1)}, u32[]{:S(2)}, u32[]{:S(2)}) %collective-permute-start.5) | collective-permute-done | bytes 262176 | tf_op jit(solution)/shard_map/ppermute | solution.py:486
  34.3 2.5 %collective-permute-start.12 = (bf16[144,512]{1,0:T(8,128)(2,1)}, bf16[144,512]{1,0:T(8,128)(2,1)S(1)}, u32[]{:S(2)}, u32[]{:S(2)}) collective-permute-start(bf16[144,512]{1,0:T(8,128)(2,1)} %get-tuple-element.138), channel_id=1, source_target_pairs={{0,6},{2,4},{4,2},{6,0},{1,7},{3,5},{5,3},{7,1},{8,14},{10,12},{12... | collective-permute-start | bytes 442376 | tf_op jit(solution)/shard_map/ppermute | solution.py:147
  36.8 1.8 %shard_map.115 = (bf16[144,512]{1,0:T(8,128)(2,1)S(1)}, bf16[144,512]{1,0:T(8,128)(2,1)S(1)}) custom-call(bf16[64,2048]{1,0:T(8,128)(2,1)S(1)} %collective-permute-done.4.got_a_ref, bf16[64,2048]{1,0:T(8,128)(2,1)S(1)} %collective-permute-done.8.got_a_other_ref, bf16[64,2048]{1,0:T(8,128)(2,1)} %collective-permute-done.5.got_b_ref, ...), custom_call_target="tpu_custom_call" | custom-call | flops 536870912 | bytes 3440640 | tf_op jit(solution)/shard_map/pallas_call | solution.py:153
  38.7 2.1 %collective-permute-start.11 = (bf16[144,512]{1,0:T(8,128)(2,1)S(1)}, bf16[144,512]{1,0:T(8,128)(2,1)S(1)}, u32[]{:S(2)}, u32[]{:S(2)}) collective-permute-start(bf16[144,512]{1,0:T(8,128)(2,1)S(1)} %get-tuple-element.89), channel_id=1, source_target_pairs={{0,4},{1,3},{2,6},{3,1},{4,0},{5,7},{6,2},{7,5},{8,12},{9,11},{10,... | collective-permute-start | bytes 442376 | tf_op jit(solution)/shard_map/ppermute | solution.py:486
  40.8 2.2 %collective-permute-done.12.got_ref = bf16[144,512]{1,0:T(8,128)(2,1)S(1)} collective-permute-done((bf16[144,512]{1,0:T(8,128)(2,1)}, bf16[144,512]{1,0:T(8,128)(2,1)S(1)}, u32[]{:S(2)}, u32[]{:S(2)}) %collective-permute-start.12) | collective-permute-done | bytes 147488 | tf_op jit(solution)/shard_map/ppermute | solution.py:147
  44.1 4.2 %collective-permute-done.10.got_a_ref = bf16[144,512]{1,0:T(8,128)(2,1)S(1)} collective-permute-done((bf16[144,512]{1,0:T(8,128)(2,1)S(1)}, bf16[144,512]{1,0:T(8,128)(2,1)S(1)}, u32[]{:S(2)}, u32[]{:S(2)}) %collective-permute-start.10) | collective-permute-done | bytes 147488 | tf_op jit(solution)/shard_map/ppermute | solution.py:481
  49.1 2.0 %collective-permute-start.15 = (bf16[144,512]{1,0:T(8,128)(2,1)S(1)}, bf16[144,512]{1,0:T(8,128)(2,1)S(1)}, u32[]{:S(2)}, u32[]{:S(2)}) collective-permute-start(bf16[144,512]{1,0:T(8,128)(2,1)S(1)} %shard_map.117.block_0_ref), channel_id=1, source_target_pairs={{0,6},{2,4},{4,2},{6,0},{1,7},{3,5},{5,3},{7,1},{8,14},{10,12},{12... | collective-permute-start | bytes 442376 | tf_op jit(solution)/shard_map/ppermute | solution.py:147
  51.2 2.4 %collective-permute-start.13 = (bf16[144,512]{1,0:T(8,128)(2,1)S(1)}, bf16[144,512]{1,0:T(8,128)(2,1)S(1)}, u32[]{:S(2)}, u32[]{:S(2)}) collective-permute-start(bf16[144,512]{1,0:T(8,128)(2,1)S(1)} %shard_map.117.block_0_ref), channel_id=1, source_target_pairs={{0,2},{1,5},{2,0},{3,7},{4,6},{5,1},{6,4},{7,3},{8,10},{9,13},{10,... | collective-permute-start | bytes 442376 | tf_op jit(solution)/shard_map/ppermute | solution.py:481
  53.6 4.2 %collective-permute-done.15.block_c_ref = bf16[144,512]{1,0:T(8,128)(2,1)S(1)} collective-permute-done((bf16[144,512]{1,0:T(8,128)(2,1)S(1)}, bf16[144,512]{1,0:T(8,128)(2,1)S(1)}, u32[]{:S(2)}, u32[]{:S(2)}) %collective-permute-start.15) | collective-permute-done | bytes 147488 | tf_op jit(solution)/shard_map/ppermute | solution.py:147
  57.8 5.7 %collective-permute-done.14.block_b_ref = bf16[144,512]{1,0:T(8,128)(2,1)S(1)} collective-permute-done((bf16[144,512]{1,0:T(8,128)(2,1)S(1)}, bf16[144,512]{1,0:T(8,128)(2,1)S(1)}, u32[]{:S(2)}, u32[]{:S(2)}) %collective-permute-start.14) | collective-permute-done | bytes 147488 | tf_op jit(solution)/shard_map/ppermute | solution.py:486
  63.5 2.3 %shard_map.118 = (bf16[128,2048]{1,0:T(8,128)(2,1)}, f32[128,16]{1,0:T(8,128)S(1)}, f32[16,2048]{1,0:T(8,128)S(1)}) custom-call(bf16[2048,128]{1,0:T(8,128)(2,1)S(1)} %copy-done.14, bf16[144,512]{1,0:T(8,128)(2,1)S(1)} %shard_map.117.block_0_ref, bf16[144,512]{1,0:T(8,128)(2,1)S(1)} %collective-permute-done.13.block_a_ref, ...), custom_call_target="tpu_custom_call" | custom-call | flops 536870912 | bytes 1847296 | tf_op jit(solution)/shard_map/pallas_call | solution.py:153
  65.9 1.2 %collective-permute-done.16.low_other_ref = f32[128,16]{1,0:T(8,128)S(1)} collective-permute-done((f32[128,16]{1,0:T(8,128)S(1)}, f32[128,16]{1,0:T(8,128)S(1)}, u32[]{:S(2)}, u32[]{:S(2)}) %collective-permute-start.16) | collective-permute-done | bytes 8224 | tf_op jit(solution)/shard_map/ppermute | solution.py:147
  67.5 1.4 %shard_map.120 = bf16[128,4096]{1,0:T(8,128)(2,1)} custom-call(f32[128,16]{1,0:T(8,128)S(1)} %get-tuple-element.106.low_ref, f32[128,16]{1,0:T(8,128)S(1)} %collective-permute-done.16.low_other_ref, bf16[16,4096]{1,0:T(8,128)(2,1)S(1)} %bitcast.25), custom_call_target="tpu_custom_call" | custom-call | flops 16777216 | bytes 1196032 | tf_op jit(solution)/shard_map/pallas_call | solution.py:153
  68.8 3.5 %collective-permute-done.17.got_ref = bf16[16,3072]{1,0:T(8,128)(2,1)S(1)} collective-permute-done((bf16[16,3072]{1,0:T(8,128)(2,1)S(1)}, bf16[16,3072]{1,0:T(8,128)(2,1)S(1)}, u32[]{:S(2)}, u32[]{:S(2)}) %collective-permute-start.17) | collective-permute-done | bytes 98336 | tf_op jit(solution)/shard_map/ppermute | solution.py:147
  72.3 1.2 %collective-permute-start.18 = (bf16[16,3072]{1,0:T(8,128)(2,1)S(1)}, bf16[16,3072]{1,0:T(8,128)(2,1)S(1)}, u32[]{:S(2)}, u32[]{:S(2)}) collective-permute-start(bf16[16,3072]{1,0:T(8,128)(2,1)S(1)} %shard_map.121.own_ref), channel_id=1, source_target_pairs={{0,4},{2,6},{4,0},{6,2},{1,5},{3,7},{5,1},{7,3},{8,12},{10,14},{12... | collective-permute-start | bytes 294920 | tf_op jit(solution)/shard_map/ppermute | solution.py:147
  73.5 5.9 %collective-permute-done.18.got_ref = bf16[16,3072]{1,0:T(8,128)(2,1)S(1)} collective-permute-done((bf16[16,3072]{1,0:T(8,128)(2,1)S(1)}, bf16[16,3072]{1,0:T(8,128)(2,1)S(1)}, u32[]{:S(2)}, u32[]{:S(2)}) %collective-permute-start.18) | collective-permute-done | bytes 98336 | tf_op jit(solution)/shard_map/ppermute | solution.py:147
  80.9 1.5 %collective-permute-start.21 = (f32[8,128]{1,0:T(8,128)S(1)}, f32[8,128]{1,0:T(8,128)S(1)}, u32[]{:S(2)}, u32[]{:S(2)}) collective-permute-start(f32[8,128]{1,0:T(8,128)S(1)} %add.30), channel_id=1, source_target_pairs={{0,8},{1,17},{8,0},{9,25},{16,24},{17,1},{24,16},{25,9},{2,10},{3,... | collective-permute-start | bytes 12296 | tf_op jit(solution)/shard_map/ppermute | solution.py:643
  82.3 1.5 %collective-permute-start.20 = (f32[8,128]{1,0:T(8,128)S(1)}, f32[8,128]{1,0:T(8,128)S(1)}, u32[]{:S(2)}, u32[]{:S(2)}) collective-permute-start(f32[8,128]{1,0:T(8,128)S(1)} %add.30), channel_id=1, source_target_pairs={{0,24},{8,16},{16,8},{24,0},{1,25},{9,17},{17,9},{25,1},{2,26},{10... | collective-permute-start | bytes 12296 | tf_op jit(solution)/shard_map/ppermute | solution.py:147
  84.5 2.4 %collective-permute-done.20 = f32[8,128]{1,0:T(8,128)S(1)} collective-permute-done((f32[8,128]{1,0:T(8,128)S(1)}, f32[8,128]{1,0:T(8,128)S(1)}, u32[]{:S(2)}, u32[]{:S(2)}) %collective-permute-start.20) | collective-permute-done | bytes 4128 | tf_op jit(solution)/shard_map/ppermute | solution.py:147
  86.9 3.6 %collective-permute-done.22 = f32[8,128]{1,0:T(8,128)S(1)} collective-permute-done((f32[8,128]{1,0:T(8,128)S(1)}, f32[8,128]{1,0:T(8,128)S(1)}, u32[]{:S(2)}, u32[]{:S(2)}) %collective-permute-start.22) | collective-permute-done | bytes 4128 | tf_op jit(solution)/shard_map/ppermute | solution.py:147
  90.5 1.2 %collective-permute-done.23.other_ref = f32[8,128]{1,0:T(8,128)S(1)} collective-permute-done((f32[8,128]{1,0:T(8,128)S(1)}, f32[8,128]{1,0:T(8,128)S(1)}, u32[]{:S(2)}, u32[]{:S(2)}) %collective-permute-start.23) | collective-permute-done | bytes 4128 | tf_op jit(solution)/shard_map/ppermute | solution.py:147
  (81 shorter events, 15.4 us)
Async XLA Ops:
  0.7 10.6 %copy-start.9 = (bf16[1,128,4096]{2,1,0:T(8,128)(2,1)S(1)}, bf16[1,128,4096]{2,1,0:T(8,128)(2,1)}, u32[]{:S(2)}) copy-start(bf16[1,128,4096]{2,1,0:T(8,128)(2,1)} %param.20) | copy-start | bytes 3145732
  0.7 10.6 %copy-start.11 = (bf16[1,16,4096]{2,1,0:T(8,128)(2,1)S(1)}, bf16[1,16,4096]{2,1,0:T(8,128)(2,1)}, u32[]{:S(2)}) copy-start(bf16[1,16,4096]{2,1,0:T(8,128)(2,1)} %param.19) | copy-start | bytes 393220
  1.9 2.3 %collective-permute-start.2 = (bf16[64,4096]{1,0:T(8,128)(2,1)S(1)}, bf16[64,4096]{1,0:T(8,128)(2,1)S(1)}, u32[]{:S(2)}, u32[]{:S(2)}) collective-permute-start(bf16[64,4096]{1,0:T(8,128)(2,1)S(1)} %dynamic-slice_bitcast_fusion.1), channel_id=1, source_target_pairs={{0,1},{1,0},{2,3},{3,2},{4,5},{5,4},{6,7},{7,6},{8,9},{9,8},{10,11... | collective-permute-start | bytes 1572872 | tf_op jit(solution)/shard_map/ppermute | solution.py:147
  2.4 1.8 %collective-permute-start.3 = (bf16[1,4096]{1,0:T(2,128)(2,1)}, bf16[1,4096]{1,0:T(2,128)(2,1)S(1)}, u32[]{:S(2)}, u32[]{:S(2)}) collective-permute-start(bf16[1,4096]{1,0:T(2,128)(2,1)} %gain_ref.1), channel_id=1, source_target_pairs={{0,1},{1,0},{2,3},{3,2},{4,5},{5,4},{6,7},{7,6},{8,9},{9,8},{10,11... | collective-permute-start | bytes 24584 | tf_op jit(solution)/shard_map/ppermute | solution.py:147
  5.5 14.1 %collective-permute-start.7 = (bf16[64,2048]{1,0:T(8,128)(2,1)S(1)}, bf16[64,2048]{1,0:T(8,128)(2,1)S(1)}, u32[]{:S(2)}, u32[]{:S(2)}) collective-permute-start(bf16[64,2048]{1,0:T(8,128)(2,1)S(1)} %get-tuple-element.80.even_ref), channel_id=1, source_target_pairs={{0,1},{1,0},{2,3},{3,2},{4,5},{5,4},{6,7},{7,6},{8,9},{9,8},{10,11... | collective-permute-start | bytes 786440 | tf_op jit(solution)/shard_map/ppermute | solution.py:147
  5.9 19.0 %collective-permute-start.6 = (bf16[64,2048]{1,0:T(8,128)(2,1)}, bf16[64,2048]{1,0:T(8,128)(2,1)}, u32[]{:S(2)}, u32[]{:S(2)}) collective-permute-start(bf16[64,2048]{1,0:T(8,128)(2,1)} %get-tuple-element.79), channel_id=1, source_target_pairs={{0,6},{2,4},{4,2},{6,0},{1,7},{3,5},{5,3},{7,1},{8,14},{10,12},{12... | collective-permute-start | bytes 786440 | tf_op jit(solution)/shard_map/ppermute | solution.py:147
  10.7 19.0 %collective-permute-start.4 = (bf16[64,2048]{1,0:T(8,128)(2,1)}, bf16[64,2048]{1,0:T(8,128)(2,1)S(1)}, u32[]{:S(2)}, u32[]{:S(2)}) collective-permute-start(bf16[64,2048]{1,0:T(8,128)(2,1)} %get-tuple-element.77), channel_id=1, source_target_pairs={{0,2},{1,5},{2,0},{3,7},{4,6},{5,1},{6,4},{7,3},{8,10},{9,13},{10,... | collective-permute-start | bytes 786440 | tf_op jit(solution)/shard_map/ppermute | solution.py:481
  10.7 23.1 %collective-permute-start.5 = (bf16[64,2048]{1,0:T(8,128)(2,1)}, bf16[64,2048]{1,0:T(8,128)(2,1)}, u32[]{:S(2)}, u32[]{:S(2)}) collective-permute-start(bf16[64,2048]{1,0:T(8,128)(2,1)} %get-tuple-element.78), channel_id=1, source_target_pairs={{0,4},{1,3},{2,6},{3,1},{4,0},{5,7},{6,2},{7,5},{8,12},{9,11},{10,... | collective-permute-start | bytes 786440 | tf_op jit(solution)/shard_map/ppermute | solution.py:486
  12.3 2.4 %collective-permute-start.1 = (f32[128,16]{1,0:T(8,128)}, f32[128,16]{1,0:T(8,128)}, u32[]{:S(2)}, u32[]{:S(2)}) collective-permute-start(f32[128,16]{1,0:T(8,128)} %branch_1_fun.4), channel_id=1, source_target_pairs={{0,1},{1,0},{2,3},{3,2},{4,5},{5,4},{6,7},{7,6},{8,9},{9,8},{10,11... | collective-permute-start | bytes 24584 | tf_op jit(solution)/shard_map/cond/branch_1_fun/ppermute | solution.py:147
  24.9 1.9 %collective-permute-start = (bf16[64,2048]{1,0:T(8,128)(2,1)}, bf16[64,2048]{1,0:T(8,128)(2,1)S(1)}, u32[]{:S(2)}, u32[]{:S(2)}) collective-permute-start(bf16[64,2048]{1,0:T(8,128)(2,1)} %get-tuple-element.26.got_ref), channel_id=1, source_target_pairs={{0,1},{1,0},{2,3},{3,2},{4,5},{5,4},{6,7},{7,6},{8,9},{9,8},{10,11... | collective-permute-start | bytes 786440 | tf_op jit(solution)/shard_map/cond/branch_1_fun/ppermute | solution.py:147
  29.6 13.4 %copy-start.7 = (bf16[1,16,2048]{2,1,0:T(8,128)(2,1)S(1)}, bf16[1,16,2048]{2,1,0:T(8,128)(2,1)}, u32[]{:S(2)}) copy-start(bf16[1,16,2048]{2,1,0:T(8,128)(2,1)} %param.18) | copy-start | bytes 196612
  29.7 13.4 %copy-start.6 = (f32[128,512]{1,0:T(8,128)S(1)}, f32[128,512]{1,0:T(8,128)}, u32[]{:S(2)}) copy-start(f32[128,512]{1,0:T(8,128)} %copy-done.5) | copy-start | bytes 786436
  33.8 3.0 %collective-permute-start.8 = (bf16[64,2048]{1,0:T(8,128)(2,1)S(1)}, bf16[64,2048]{1,0:T(8,128)(2,1)S(1)}, u32[]{:S(2)}, u32[]{:S(2)}) collective-permute-start(bf16[64,2048]{1,0:T(8,128)(2,1)S(1)} %collective-permute-done.4.got_a_ref), channel_id=1, source_target_pairs={{0,1},{1,0},{2,3},{3,2},{4,5},{5,4},{6,7},{7,6},{8,9},{9,8},{10,11... | collective-permute-start | bytes 786440 | tf_op jit(solution)/shard_map/ppermute | solution.py:147
  33.8 3.0 %collective-permute-start.9 = (bf16[64,2048]{1,0:T(8,128)(2,1)}, bf16[64,2048]{1,0:T(8,128)(2,1)S(1)}, u32[]{:S(2)}, u32[]{:S(2)}) collective-permute-start(bf16[64,2048]{1,0:T(8,128)(2,1)} %collective-permute-done.5.got_b_ref), channel_id=1, source_target_pairs={{0,1},{1,0},{2,3},{3,2},{4,5},{5,4},{6,7},{7,6},{8,9},{9,8},{10,11... | collective-permute-start | bytes 786440 | tf_op jit(solution)/shard_map/ppermute | solution.py:147
  34.3 8.7 %collective-permute-start.12 = (bf16[144,512]{1,0:T(8,128)(2,1)}, bf16[144,512]{1,0:T(8,128)(2,1)S(1)}, u32[]{:S(2)}, u32[]{:S(2)}) collective-permute-start(bf16[144,512]{1,0:T(8,128)(2,1)} %get-tuple-element.138), channel_id=1, source_target_pairs={{0,6},{2,4},{4,2},{6,0},{1,7},{3,5},{5,3},{7,1},{8,14},{10,12},{12... | collective-permute-start | bytes 442376 | tf_op jit(solution)/shard_map/ppermute | solution.py:147
  36.8 26.7 %copy-start.14 = (bf16[2048,128]{1,0:T(8,128)(2,1)S(1)}, bf16[2048,128]{1,0:T(8,128)(2,1)}, u32[]{:S(2)}) copy-start(bf16[2048,128]{1,0:T(8,128)(2,1)} %copy-done.13) | copy-start | bytes 1572868
  38.6 28.5 %copy-start.10 = (bf16[1,128,4096]{2,1,0:T(8,128)(2,1)S(1)}, bf16[1,128,4096]{2,1,0:T(8,128)(2,1)}, u32[]{:S(2)}) copy-start(bf16[1,128,4096]{2,1,0:T(8,128)(2,1)} %param.20) | copy-start | bytes 3145732
  38.6 9.6 %collective-permute-start.10 = (bf16[144,512]{1,0:T(8,128)(2,1)S(1)}, bf16[144,512]{1,0:T(8,128)(2,1)S(1)}, u32[]{:S(2)}, u32[]{:S(2)}) collective-permute-start(bf16[144,512]{1,0:T(8,128)(2,1)S(1)} %get-tuple-element.88), channel_id=1, source_target_pairs={{0,2},{1,5},{2,0},{3,7},{4,6},{5,1},{6,4},{7,3},{8,10},{9,13},{10,... | collective-permute-start | bytes 442376 | tf_op jit(solution)/shard_map/ppermute | solution.py:481
  38.7 10.2 %collective-permute-start.11 = (bf16[144,512]{1,0:T(8,128)(2,1)S(1)}, bf16[144,512]{1,0:T(8,128)(2,1)S(1)}, u32[]{:S(2)}, u32[]{:S(2)}) collective-permute-start(bf16[144,512]{1,0:T(8,128)(2,1)S(1)} %get-tuple-element.89), channel_id=1, source_target_pairs={{0,4},{1,3},{2,6},{3,1},{4,0},{5,7},{6,2},{7,5},{8,12},{9,11},{10,... | collective-permute-start | bytes 442376 | tf_op jit(solution)/shard_map/ppermute | solution.py:486
  44.0 23.4 %copy-start.12 = (bf16[1,16,4096]{2,1,0:T(8,128)(2,1)S(1)}, bf16[1,16,4096]{2,1,0:T(8,128)(2,1)}, u32[]{:S(2)}) copy-start(bf16[1,16,4096]{2,1,0:T(8,128)(2,1)} %param.19) | copy-start | bytes 393220
  49.1 8.7 %collective-permute-start.15 = (bf16[144,512]{1,0:T(8,128)(2,1)S(1)}, bf16[144,512]{1,0:T(8,128)(2,1)S(1)}, u32[]{:S(2)}, u32[]{:S(2)}) collective-permute-start(bf16[144,512]{1,0:T(8,128)(2,1)S(1)} %shard_map.117.block_0_ref), channel_id=1, source_target_pairs={{0,6},{2,4},{4,2},{6,0},{1,7},{3,5},{5,3},{7,1},{8,14},{10,12},{12... | collective-permute-start | bytes 442376 | tf_op jit(solution)/shard_map/ppermute | solution.py:147
  51.2 12.3 %collective-permute-start.14 = (bf16[144,512]{1,0:T(8,128)(2,1)S(1)}, bf16[144,512]{1,0:T(8,128)(2,1)S(1)}, u32[]{:S(2)}, u32[]{:S(2)}) collective-permute-start(bf16[144,512]{1,0:T(8,128)(2,1)S(1)} %shard_map.117.block_0_ref), channel_id=1, source_target_pairs={{0,4},{1,3},{2,6},{3,1},{4,0},{5,7},{6,2},{7,5},{8,12},{9,11},{10,... | collective-permute-start | bytes 442376 | tf_op jit(solution)/shard_map/ppermute | solution.py:486
  51.2 12.3 %collective-permute-start.13 = (bf16[144,512]{1,0:T(8,128)(2,1)S(1)}, bf16[144,512]{1,0:T(8,128)(2,1)S(1)}, u32[]{:S(2)}, u32[]{:S(2)}) collective-permute-start(bf16[144,512]{1,0:T(8,128)(2,1)S(1)} %shard_map.117.block_0_ref), channel_id=1, source_target_pairs={{0,2},{1,5},{2,0},{3,7},{4,6},{5,1},{6,4},{7,3},{8,10},{9,13},{10,... | collective-permute-start | bytes 442376 | tf_op jit(solution)/shard_map/ppermute | solution.py:481
  65.8 1.3 %collective-permute-start.16 = (f32[128,16]{1,0:T(8,128)S(1)}, f32[128,16]{1,0:T(8,128)S(1)}, u32[]{:S(2)}, u32[]{:S(2)}) collective-permute-start(f32[128,16]{1,0:T(8,128)S(1)} %get-tuple-element.106.low_ref), channel_id=1, source_target_pairs={{0,1},{1,0},{2,3},{3,2},{4,5},{5,4},{6,7},{7,6},{8,9},{9,8},{10,11... | collective-permute-start | bytes 24584 | tf_op jit(solution)/shard_map/ppermute | solution.py:147
  67.4 4.9 %collective-permute-start.17 = (bf16[16,3072]{1,0:T(8,128)(2,1)S(1)}, bf16[16,3072]{1,0:T(8,128)(2,1)S(1)}, u32[]{:S(2)}, u32[]{:S(2)}) collective-permute-start(bf16[16,3072]{1,0:T(8,128)(2,1)S(1)} %get-tuple-element.108), channel_id=1, source_target_pairs={{0,2},{2,0},{4,6},{6,4},{1,3},{3,1},{5,7},{7,5},{8,10},{10,8},{12,... | collective-permute-start | bytes 294920 | tf_op jit(solution)/shard_map/ppermute | solution.py:147
  72.3 7.1 %collective-permute-start.18 = (bf16[16,3072]{1,0:T(8,128)(2,1)S(1)}, bf16[16,3072]{1,0:T(8,128)(2,1)S(1)}, u32[]{:S(2)}, u32[]{:S(2)}) collective-permute-start(bf16[16,3072]{1,0:T(8,128)(2,1)S(1)} %shard_map.121.own_ref), channel_id=1, source_target_pairs={{0,4},{2,6},{4,0},{6,2},{1,5},{3,7},{5,1},{7,3},{8,12},{10,14},{12... | collective-permute-start | bytes 294920 | tf_op jit(solution)/shard_map/ppermute | solution.py:147
  79.6 1.2 %collective-permute-start.19 = (f32[8,128]{1,0:T(8,128)S(1)}, f32[8,128]{1,0:T(8,128)S(1)}, u32[]{:S(2)}, u32[]{:S(2)}) collective-permute-start(f32[8,128]{1,0:T(8,128)S(1)} %get-tuple-element.112), channel_id=1, source_target_pairs={{0,1},{1,0},{2,3},{3,2},{4,5},{5,4},{6,7},{7,6},{8,9},{9,8},{10,11... | collective-permute-start | bytes 12296 | tf_op jit(solution)/shard_map/ppermute | solution.py:147
  80.9 3.6 %collective-permute-start.21 = (f32[8,128]{1,0:T(8,128)S(1)}, f32[8,128]{1,0:T(8,128)S(1)}, u32[]{:S(2)}, u32[]{:S(2)}) collective-permute-start(f32[8,128]{1,0:T(8,128)S(1)} %add.30), channel_id=1, source_target_pairs={{0,8},{1,17},{8,0},{9,25},{16,24},{17,1},{24,16},{25,9},{2,10},{3,... | collective-permute-start | bytes 12296 | tf_op jit(solution)/shard_map/ppermute | solution.py:643
  82.3 4.5 %collective-permute-start.20 = (f32[8,128]{1,0:T(8,128)S(1)}, f32[8,128]{1,0:T(8,128)S(1)}, u32[]{:S(2)}, u32[]{:S(2)}) collective-permute-start(f32[8,128]{1,0:T(8,128)S(1)} %add.30), channel_id=1, source_target_pairs={{0,24},{8,16},{16,8},{24,0},{1,25},{9,17},{17,9},{25,1},{2,26},{10... | collective-permute-start | bytes 12296 | tf_op jit(solution)/shard_map/ppermute | solution.py:147
  83.8 7.8 %collective-permute-start.24 = (bf16[16,3072]{1,0:T(8,128)(2,1)S(1)}, bf16[16,3072]{1,0:T(8,128)(2,1)S(1)}, u32[]{:S(2)}, u32[]{:S(2)}) collective-permute-start(bf16[16,3072]{1,0:T(8,128)(2,1)S(1)} %get-tuple-element.113.own_ref), channel_id=1, source_target_pairs={{0,2},{2,0},{4,6},{6,4},{1,3},{3,1},{5,7},{7,5},{8,10},{10,8},{12,... | collective-permute-start | bytes 294920 | tf_op jit(solution)/shard_map/ppermute | solution.py:147
  86.9 3.6 %collective-permute-start.22 = (f32[8,128]{1,0:T(8,128)S(1)}, f32[8,128]{1,0:T(8,128)S(1)}, u32[]{:S(2)}, u32[]{:S(2)}) collective-permute-start(f32[8,128]{1,0:T(8,128)S(1)} %add_select_fusion), channel_id=1, source_target_pairs={{0,2},{2,0},{4,6},{6,4},{1,3},{3,1},{5,7},{7,5},{8,10},{10,8},{12,... | collective-permute-start | bytes 12296 | tf_op jit(solution)/shard_map/ppermute | solution.py:147
  90.5 1.2 %collective-permute-start.23 = (f32[8,128]{1,0:T(8,128)S(1)}, f32[8,128]{1,0:T(8,128)S(1)}, u32[]{:S(2)}, u32[]{:S(2)}) collective-permute-start(f32[8,128]{1,0:T(8,128)S(1)} %add.33.square_ref), channel_id=1, source_target_pairs={{0,1},{1,0},{2,3},{3,2},{4,5},{5,4},{6,7},{7,6},{8,9},{9,8},{10,11... | collective-permute-start | bytes 12296 | tf_op jit(solution)/shard_map/ppermute | solution.py:147
  (10 other events, 27.3 us)

commit v9 on v7

--- a/solution.py
+++ b/solution.py
@@ -376,6 +376,7 @@
     )
     scale = head ** (-0.5) * math.log2(math.e)
     ones = jnp.ones((len(blocks) * rows, head), BF16)
+    excluded = -1e30 * head**0.5
     groups = width // head
     pairs = query_ref.shape[0] // (2 * rows)
     copies = []
@@ -384,7 +385,7 @@
         scores = times_transposed(
             query_ref[2 * pair * rows : 2 * (pair + 1) * rows], keys[:, shared]
         ).reshape(2, rows, keys.shape[0])
-        scores = jnp.where(allowed[None], scores, -1e30).reshape(2 * rows, keys.shape[0])
+        scores = jnp.where(allowed[None], scores, excluded).reshape(2 * rows, keys.shape[0])
         weights = jnp.exp2((scores - jnp.max(scores, axis=1, keepdims=True)) * scale)
         mixed = times(
             weights.astype(BF16), jnp.concatenate([values[:, shared], ones], axis=1)

time: 92.7 us -> 92.7 us (level)
  no operation moved by 1% of the time
where the time goes in v9:
time: 92.7 us; the launch traced here: 92.3 us
  waiting for transfers between devices  47.8 us (52%)
  starting transfers between devices  20.8 us (22%)
  Pallas kernels  15.3 us (17%)
  local copies, waits for them, and re-layouts  6.44 us (7%)
  other arithmetic  1.08 us (1%)
    ppermute x18, waiting for transfers between devices, swap(): return lax.ppermute(value, axis, [(i, i ^ distance) for i in range(count)])  29.5 us
    pallas_call x14, Pallas kernels, call(): pl.pallas_call(kernel, out_shape=shapes, in_specs=[ANYWHERE if i in loose...  15.3 us
    ppermute x18, starting transfers between devices, swap(): return lax.ppermute(value, axis, [(i, i ^ distance) for i in range(count)])  14.2 us
    ppermute x3, waiting for transfers between devices, send_b(): lax.ppermute(value, ('ctx', 'tp'), [(2 * a + t, 2 * (a ^ (1 if t else 2))...  13.8 us
    ppermute x3, waiting for transfers between devices, send_a(): lax.ppermute(value, ('ctx', 'tp'), [(2 * a + t, 2 * (a ^ (2 if t else 1))...  3.94 us
    squeeze x1, local copies, waits for them, and re-layouts, prepare(): return key_value_weight[0].reshape(slice_width, kv_width)  2.75 us
    ppermute x3, starting transfers between devices, send_a(): lax.ppermute(value, ('ctx', 'tp'), [(2 * a + t, 2 * (a ^ (2 if t else 1))...  2.54 us
    ppermute x3, starting transfers between devices, send_b(): lax.ppermute(value, ('ctx', 'tp'), [(2 * a + t, 2 * (a ^ (1 if t else 2))...  2.5 us
  transfers between devices with their start and end apart: 25, of which 16 were waited for; matrix products, arithmetic and copies ran while one was open for 4% of the time, Pallas kernels for 11%

profile of v9, /device:TPU:0, one launch (start us, length us, event | category | flops | bytes accessed | tf_op | source)
XLA Modules:
  0.0 92.3 jit_solution(1734798768102824341)
XLA Ops:
  0.7 1.4 %dynamic-slice_bitcast_fusion = (bf16[64,4096]{1,0:T(8,128)(2,1)S(1)}, bf16[64,4096]{1,0:T(8,128)(2,1)S(1)}) fusion(bf16[1,128,4096]{2,1,0:T(8,128)(2,1)} %param.14, s32[]{:T(128)S(6)} %select_n.15, s32[]{:T(128)S(6)} %select_n.14), kind=kLoop, calls=%fused_computation.9 | loop fusion | bytes 2097160 | tf_op jit(solution)/shard_map/dynamic_slice | solution.py:467
  2.7 1.5 %collective-permute-done.3.gain_other_ref = bf16[1,4096]{1,0:T(2,128)(2,1)S(1)} collective-permute-done((bf16[1,4096]{1,0:T(2,128)(2,1)S(1)}, bf16[1,4096]{1,0:T(2,128)(2,1)S(1)}, u32[]{:S(2)}, u32[]{:S(2)}) %collective-permute-start.3) | collective-permute-done | bytes 8224 | tf_op jit(solution)/shard_map/ppermute | solution.py:147
  4.2 1.3 %shard_map.117 = (bf16[64,2048]{1,0:T(8,128)(2,1)S(1)}, bf16[64,2048]{1,0:T(8,128)(2,1)}, bf16[64,2048]{1,0:T(8,128)(2,1)}, bf16[64,2048]{1,0:T(8,128)(2,1)}) custom-call(bf16[64,4096]{1,0:T(8,128)(2,1)S(1)} %get-tuple-element.122.mine_ref, bf16[64,4096]{1,0:T(8,128)(2,1)S(1)} %collective-permute-done.2.other_ref, bf16[1,4096]{1,0:T(2,128)(2,1)S(1)} %copy-done.1, ...), custom_call_target="tpu_custom_call" | custom-call | bytes 2113536 | tf_op jit(solution)/shard_map/pallas_call | solution.py:153
  5.9 4.8 %collective-permute-start.6 = (bf16[64,2048]{1,0:T(8,128)(2,1)}, bf16[64,2048]{1,0:T(8,128)(2,1)}, u32[]{:S(2)}, u32[]{:S(2)}) collective-permute-start(bf16[64,2048]{1,0:T(8,128)(2,1)} %get-tuple-element.74), channel_id=1, source_target_pairs={{0,6},{2,4},{4,2},{6,0},{1,7},{3,5},{5,3},{7,1},{8,14},{10,12},{12... | collective-permute-start | bytes 786440 | tf_op jit(solution)/shard_map/ppermute | solution.py:147
  11.2 3.4 %conditional.3 = (f32[1,128]{1,0:T(1,128)S(1)}, f32[128,128]{1,0:T(8,128)}, f32[128,128]{1,0:T(8,128)}, bf16[2048,128]{1,0:T(8,128)(2,1)S(1)}, f32[128,16]{1,0:T(8,128)}, /*index=5*/f32[128,16]{1,0:T(8,128)}) conditional(s32[]{:T(128)} %convert_element_type.15, () %tuple.32, (s32[128]{0:T(128)S(1)}, s32[]{:T(128)}, ...), branch_computations={%region_0.0_spmd, %region_1.0_spmd} | conditional | flops 16826880 | bytes 3779176 | solution.py:499
  15.4 2.7 %conditional.4 = (bf16[2048,512]{1,0:T(8,128)(2,1)S(1)}) conditional(s32[]{:T(128)} %convert_element_type.15, () %tuple.35, (bf16[1,2048,2,2,128]{4,3,2,1,0:T(2,128)(2,1)}) %tuple.42), branch_computations={%region_2.0_spmd, %region_3.0_spmd} | conditional | bytes 4194312 | solution.py:499
  15.4 2.7 %squeeze.19 = bf16[2048,512]{1,0:T(8,128)(2,1)S(1)} reshape(bf16[1,2048,2,2,128]{4,3,2,1,0:T(2,128)(2,1)} %get-tuple-element.115) | data formatting | bytes 4194304 | tf_op jit(solution)/shard_map/cond/branch_1_fun/reshape;cond/branch_1_fun/squeeze | solution.py:507
  18.2 1.3 %copy-done.2 = bf16[2048,512]{1,0:T(8,128)(2,1)} copy-done((bf16[2048,512]{1,0:T(8,128)(2,1)}, bf16[2048,512]{1,0:T(8,128)(2,1)S(1)}, u32[]{:S(2)}) %copy-start.2) | copy-done | bytes 2097176
  19.5 2.0 %shard_map.118 = (f32[128,512]{1,0:T(8,128)S(1)}, bf16[2048,512]{1,0:T(8,128)(2,1)S(1)}) custom-call(bf16[64,2048]{1,0:T(8,128)(2,1)S(1)} %get-tuple-element.75.even_ref, bf16[64,2048]{1,0:T(8,128)(2,1)S(1)} %collective-permute-done.7.even_other_ref, bf16[2048,512]{1,0:T(8,128)(2,1)} %copy-done.2), custom_call_target="tpu_custom_call" | custom-call | flops 268435456 | bytes 4980736 | tf_op jit(solution)/shard_map/pallas_call | solution.py:153
  21.6 4.8 %conditional.5 = (bf16[144,512]{1,0:T(8,128)(2,1)}) conditional(s32[]{:T(128)} %convert_element_type.15, () %tuple.34, (bf16[64,2048]{1,0:T(8,128)(2,1)}, bf16[2048,512]{1,0:T(8,128)(2,1)}) %tuple.53), branch_computations={%region_4.0_spmd, %region_5.0_spmd} | conditional | flops 268435456 | bytes 3817520 | solution.py:499
  22.2 1.4 %collective-permute-done.got_other_ref = bf16[64,2048]{1,0:T(8,128)(2,1)S(1)} collective-permute-done((bf16[64,2048]{1,0:T(8,128)(2,1)}, bf16[64,2048]{1,0:T(8,128)(2,1)S(1)}, u32[]{:S(2)}, u32[]{:S(2)}) %collective-permute-start) | collective-permute-done | bytes 262176 | tf_op jit(solution)/shard_map/cond/branch_1_fun/ppermute | solution.py:147
  23.5 2.8 %branch_1_fun.5 = bf16[144,512]{1,0:T(8,128)(2,1)} custom-call(bf16[64,2048]{1,0:T(8,128)(2,1)} %get-tuple-element.26.got_ref, bf16[64,2048]{1,0:T(8,128)(2,1)S(1)} %collective-permute-done.got_other_ref, bf16[2048,512]{1,0:T(8,128)(2,1)} %get-tuple-element.27.weight_ref), custom_call_target="tpu_custom_call" | custom-call | flops 268435456 | bytes 2768896 | tf_op jit(solution)/shard_map/cond/branch_1_fun/pallas_call | solution.py:153
  26.4 7.3 %collective-permute-done.5.got_b_ref = bf16[64,2048]{1,0:T(8,128)(2,1)S(1)} collective-permute-done((bf16[64,2048]{1,0:T(8,128)(2,1)}, bf16[64,2048]{1,0:T(8,128)(2,1)S(1)}, u32[]{:S(2)}, u32[]{:S(2)}) %collective-permute-start.5) | collective-permute-done | bytes 262176 | tf_op jit(solution)/shard_map/ppermute | solution.py:486
  34.2 2.5 %collective-permute-start.12 = (bf16[144,512]{1,0:T(8,128)(2,1)}, bf16[144,512]{1,0:T(8,128)(2,1)S(1)}, u32[]{:S(2)}, u32[]{:S(2)}) collective-permute-start(bf16[144,512]{1,0:T(8,128)(2,1)} %get-tuple-element.136), channel_id=1, source_target_pairs={{0,6},{2,4},{4,2},{6,0},{1,7},{3,5},{5,3},{7,1},{8,14},{10,12},{12... | collective-permute-start | bytes 442376 | tf_op jit(solution)/shard_map/ppermute | solution.py:147
  37.5 1.9 %collective-permute-start.11 = (bf16[144,512]{1,0:T(8,128)(2,1)S(1)}, bf16[144,512]{1,0:T(8,128)(2,1)S(1)}, u32[]{:S(2)}, u32[]{:S(2)}) collective-permute-start(bf16[144,512]{1,0:T(8,128)(2,1)S(1)} %get-tuple-element.83), channel_id=1, source_target_pairs={{0,4},{1,3},{2,6},{3,1},{4,0},{5,7},{6,2},{7,5},{8,12},{9,11},{10,... | collective-permute-start | bytes 442376 | tf_op jit(solution)/shard_map/ppermute | solution.py:486
  39.5 3.5 %collective-permute-done.12.got_ref = bf16[144,512]{1,0:T(8,128)(2,1)S(1)} collective-permute-done((bf16[144,512]{1,0:T(8,128)(2,1)}, bf16[144,512]{1,0:T(8,128)(2,1)S(1)}, u32[]{:S(2)}, u32[]{:S(2)}) %collective-permute-start.12) | collective-permute-done | bytes 147488 | tf_op jit(solution)/shard_map/ppermute | solution.py:147
  44.0 3.9 %collective-permute-done.10.got_a_ref = bf16[144,512]{1,0:T(8,128)(2,1)S(1)} collective-permute-done((bf16[144,512]{1,0:T(8,128)(2,1)S(1)}, bf16[144,512]{1,0:T(8,128)(2,1)S(1)}, u32[]{:S(2)}, u32[]{:S(2)}) %collective-permute-start.10) | collective-permute-done | bytes 147488 | tf_op jit(solution)/shard_map/ppermute | solution.py:481
  49.0 2.0 %collective-permute-start.15 = (bf16[144,512]{1,0:T(8,128)(2,1)S(1)}, bf16[144,512]{1,0:T(8,128)(2,1)S(1)}, u32[]{:S(2)}, u32[]{:S(2)}) collective-permute-start(bf16[144,512]{1,0:T(8,128)(2,1)S(1)} %shard_map.121.block_0_ref), channel_id=1, source_target_pairs={{0,6},{2,4},{4,2},{6,0},{1,7},{3,5},{5,3},{7,1},{8,14},{10,12},{12... | collective-permute-start | bytes 442376 | tf_op jit(solution)/shard_map/ppermute | solution.py:147
  51.0 2.5 %collective-permute-start.13 = (bf16[144,512]{1,0:T(8,128)(2,1)S(1)}, bf16[144,512]{1,0:T(8,128)(2,1)S(1)}, u32[]{:S(2)}, u32[]{:S(2)}) collective-permute-start(bf16[144,512]{1,0:T(8,128)(2,1)S(1)} %shard_map.121.block_0_ref), channel_id=1, source_target_pairs={{0,2},{1,5},{2,0},{3,7},{4,6},{5,1},{6,4},{7,3},{8,10},{9,13},{10,... | collective-permute-start | bytes 442376 | tf_op jit(solution)/shard_map/ppermute | solution.py:481
  53.5 4.2 %collective-permute-done.15.block_c_ref = bf16[144,512]{1,0:T(8,128)(2,1)S(1)} collective-permute-done((bf16[144,512]{1,0:T(8,128)(2,1)S(1)}, bf16[144,512]{1,0:T(8,128)(2,1)S(1)}, u32[]{:S(2)}, u32[]{:S(2)}) %collective-permute-start.15) | collective-permute-done | bytes 147488 | tf_op jit(solution)/shard_map/ppermute | solution.py:147
  57.7 5.6 %collective-permute-done.14.block_b_ref = bf16[144,512]{1,0:T(8,128)(2,1)S(1)} collective-permute-done((bf16[144,512]{1,0:T(8,128)(2,1)S(1)}, bf16[144,512]{1,0:T(8,128)(2,1)S(1)}, u32[]{:S(2)}, u32[]{:S(2)}) %collective-permute-start.14) | collective-permute-done | bytes 147488 | tf_op jit(solution)/shard_map/ppermute | solution.py:486
  63.3 2.3 %shard_map.122 = (bf16[128,2048]{1,0:T(8,128)(2,1)}, f32[128,16]{1,0:T(8,128)S(1)}, f32[16,2048]{1,0:T(8,128)S(1)}) custom-call(bf16[2048,128]{1,0:T(8,128)(2,1)S(1)} %copy-done.7, bf16[144,512]{1,0:T(8,128)(2,1)S(1)} %shard_map.121.block_0_ref, bf16[144,512]{1,0:T(8,128)(2,1)S(1)} %collective-permute-done.13.block_a_ref, ...), custom_call_target="tpu_custom_call" | custom-call | flops 536870912 | bytes 1847296 | tf_op jit(solution)/shard_map/pallas_call | solution.py:153
  65.7 1.2 %collective-permute-done.16.low_other_ref = f32[128,16]{1,0:T(8,128)S(1)} collective-permute-done((f32[128,16]{1,0:T(8,128)S(1)}, f32[128,16]{1,0:T(8,128)S(1)}, u32[]{:S(2)}, u32[]{:S(2)}) %collective-permute-start.16) | collective-permute-done | bytes 8224 | tf_op jit(solution)/shard_map/ppermute | solution.py:147
  67.3 1.4 %shard_map.124 = bf16[128,4096]{1,0:T(8,128)(2,1)} custom-call(f32[128,16]{1,0:T(8,128)S(1)} %get-tuple-element.100.low_ref, f32[128,16]{1,0:T(8,128)S(1)} %collective-permute-done.16.low_other_ref, bf16[16,4096]{1,0:T(8,128)(2,1)S(1)} %bitcast.25), custom_call_target="tpu_custom_call" | custom-call | flops 16777216 | bytes 1196032 | tf_op jit(solution)/shard_map/pallas_call | solution.py:153
  68.7 3.5 %collective-permute-done.17.got_ref = bf16[16,3072]{1,0:T(8,128)(2,1)S(1)} collective-permute-done((bf16[16,3072]{1,0:T(8,128)(2,1)S(1)}, bf16[16,3072]{1,0:T(8,128)(2,1)S(1)}, u32[]{:S(2)}, u32[]{:S(2)}) %collective-permute-start.17) | collective-permute-done | bytes 98336 | tf_op jit(solution)/shard_map/ppermute | solution.py:147
  72.2 1.2 %collective-permute-start.18 = (bf16[16,3072]{1,0:T(8,128)(2,1)S(1)}, bf16[16,3072]{1,0:T(8,128)(2,1)S(1)}, u32[]{:S(2)}, u32[]{:S(2)}) collective-permute-start(bf16[16,3072]{1,0:T(8,128)(2,1)S(1)} %shard_map.125.own_ref), channel_id=1, source_target_pairs={{0,4},{2,6},{4,0},{6,2},{1,5},{3,7},{5,1},{7,3},{8,12},{10,14},{12... | collective-permute-start | bytes 294920 | tf_op jit(solution)/shard_map/ppermute | solution.py:147
  73.4 5.8 %collective-permute-done.18.got_ref = bf16[16,3072]{1,0:T(8,128)(2,1)S(1)} collective-permute-done((bf16[16,3072]{1,0:T(8,128)(2,1)S(1)}, bf16[16,3072]{1,0:T(8,128)(2,1)S(1)}, u32[]{:S(2)}, u32[]{:S(2)}) %collective-permute-start.18) | collective-permute-done | bytes 98336 | tf_op jit(solution)/shard_map/ppermute | solution.py:147
  80.7 1.5 %collective-permute-start.21 = (f32[8,128]{1,0:T(8,128)S(1)}, f32[8,128]{1,0:T(8,128)S(1)}, u32[]{:S(2)}, u32[]{:S(2)}) collective-permute-start(f32[8,128]{1,0:T(8,128)S(1)} %add.30), channel_id=1, source_target_pairs={{0,8},{1,17},{8,0},{9,25},{16,24},{17,1},{24,16},{25,9},{2,10},{3,... | collective-permute-start | bytes 12296 | tf_op jit(solution)/shard_map/ppermute | solution.py:641
  82.2 1.5 %collective-permute-start.20 = (f32[8,128]{1,0:T(8,128)S(1)}, f32[8,128]{1,0:T(8,128)S(1)}, u32[]{:S(2)}, u32[]{:S(2)}) collective-permute-start(f32[8,128]{1,0:T(8,128)S(1)} %add.30), channel_id=1, source_target_pairs={{0,24},{8,16},{16,8},{24,0},{1,25},{9,17},{17,9},{25,1},{2,26},{10... | collective-permute-start | bytes 12296 | tf_op jit(solution)/shard_map/ppermute | solution.py:147
  84.3 2.4 %collective-permute-done.20 = f32[8,128]{1,0:T(8,128)S(1)} collective-permute-done((f32[8,128]{1,0:T(8,128)S(1)}, f32[8,128]{1,0:T(8,128)S(1)}, u32[]{:S(2)}, u32[]{:S(2)}) %collective-permute-start.20) | collective-permute-done | bytes 4128 | tf_op jit(solution)/shard_map/ppermute | solution.py:147
  86.7 3.6 %collective-permute-done.22 = f32[8,128]{1,0:T(8,128)S(1)} collective-permute-done((f32[8,128]{1,0:T(8,128)S(1)}, f32[8,128]{1,0:T(8,128)S(1)}, u32[]{:S(2)}, u32[]{:S(2)}) %collective-permute-start.22) | collective-permute-done | bytes 4128 | tf_op jit(solution)/shard_map/ppermute | solution.py:147
  90.3 1.2 %collective-permute-done.23.other_ref = f32[8,128]{1,0:T(8,128)S(1)} collective-permute-done((f32[8,128]{1,0:T(8,128)S(1)}, f32[8,128]{1,0:T(8,128)S(1)}, u32[]{:S(2)}, u32[]{:S(2)}) %collective-permute-start.23) | collective-permute-done | bytes 4128 | tf_op jit(solution)/shard_map/ppermute | solution.py:147
  (66 shorter events, 13.1 us)
Async XLA Ops:
  0.6 10.6 %copy-start.3 = (bf16[1,128,4096]{2,1,0:T(8,128)(2,1)S(1)}, bf16[1,128,4096]{2,1,0:T(8,128)(2,1)}, u32[]{:S(2)}) copy-start(bf16[1,128,4096]{2,1,0:T(8,128)(2,1)} %param.20) | copy-start | bytes 3145732
  0.7 10.5 %copy-start.5 = (bf16[1,16,4096]{2,1,0:T(8,128)(2,1)S(1)}, bf16[1,16,4096]{2,1,0:T(8,128)(2,1)}, u32[]{:S(2)}) copy-start(bf16[1,16,4096]{2,1,0:T(8,128)(2,1)} %param.19) | copy-start | bytes 393220
  0.7 10.5 %copy-start.9 = (s32[128]{0:T(128)S(1)}, s32[128]{0:T(128)}, u32[]{:S(2)}) copy-start(s32[128]{0:T(128)} %param.21) | copy-start | bytes 1540
  0.7 10.5 %copy-start.8 = (bf16[1,128,16,128]{3,2,1,0:T(8,128)(2,1)S(1)}, bf16[1,128,16,128]{3,2,1,0:T(8,128)(2,1)}, u32[]{:S(2)}) copy-start(bf16[1,128,16,128]{3,2,1,0:T(8,128)(2,1)} %param.16) | copy-start | bytes 1572868
  2.1 2.1 %collective-permute-start.2 = (bf16[64,4096]{1,0:T(8,128)(2,1)S(1)}, bf16[64,4096]{1,0:T(8,128)(2,1)S(1)}, u32[]{:S(2)}, u32[]{:S(2)}) collective-permute-start(bf16[64,4096]{1,0:T(8,128)(2,1)S(1)} %get-tuple-element.121), channel_id=1, source_target_pairs={{0,1},{1,0},{2,3},{3,2},{4,5},{5,4},{6,7},{7,6},{8,9},{9,8},{10,11... | collective-permute-start | bytes 1572872 | tf_op jit(solution)/shard_map/ppermute | solution.py:147
  2.6 1.6 %collective-permute-start.3 = (bf16[1,4096]{1,0:T(2,128)(2,1)S(1)}, bf16[1,4096]{1,0:T(2,128)(2,1)S(1)}, u32[]{:S(2)}, u32[]{:S(2)}) collective-permute-start(bf16[1,4096]{1,0:T(2,128)(2,1)S(1)} %copy-done.1), channel_id=1, source_target_pairs={{0,1},{1,0},{2,3},{3,2},{4,5},{5,4},{6,7},{7,6},{8,9},{9,8},{10,11... | collective-permute-start | bytes 24584 | tf_op jit(solution)/shard_map/ppermute | solution.py:147
  5.5 14.1 %collective-permute-start.7 = (bf16[64,2048]{1,0:T(8,128)(2,1)S(1)}, bf16[64,2048]{1,0:T(8,128)(2,1)S(1)}, u32[]{:S(2)}, u32[]{:S(2)}) collective-permute-start(bf16[64,2048]{1,0:T(8,128)(2,1)S(1)} %get-tuple-element.75.even_ref), channel_id=1, source_target_pairs={{0,1},{1,0},{2,3},{3,2},{4,5},{5,4},{6,7},{7,6},{8,9},{9,8},{10,11... | collective-permute-start | bytes 786440 | tf_op jit(solution)/shard_map/ppermute | solution.py:147
  5.9 15.7 %collective-permute-start.6 = (bf16[64,2048]{1,0:T(8,128)(2,1)}, bf16[64,2048]{1,0:T(8,128)(2,1)}, u32[]{:S(2)}, u32[]{:S(2)}) collective-permute-start(bf16[64,2048]{1,0:T(8,128)(2,1)} %get-tuple-element.74), channel_id=1, source_target_pairs={{0,6},{2,4},{4,2},{6,0},{1,7},{3,5},{5,3},{7,1},{8,14},{10,12},{12... | collective-permute-start | bytes 786440 | tf_op jit(solution)/shard_map/ppermute | solution.py:147
  10.6 15.7 %collective-permute-start.4 = (bf16[64,2048]{1,0:T(8,128)(2,1)}, bf16[64,2048]{1,0:T(8,128)(2,1)S(1)}, u32[]{:S(2)}, u32[]{:S(2)}) collective-permute-start(bf16[64,2048]{1,0:T(8,128)(2,1)} %get-tuple-element.72), channel_id=1, source_target_pairs={{0,2},{1,5},{2,0},{3,7},{4,6},{5,1},{6,4},{7,3},{8,10},{9,13},{10,... | collective-permute-start | bytes 786440 | tf_op jit(solution)/shard_map/ppermute | solution.py:481
  10.6 23.0 %collective-permute-start.5 = (bf16[64,2048]{1,0:T(8,128)(2,1)}, bf16[64,2048]{1,0:T(8,128)(2,1)S(1)}, u32[]{:S(2)}, u32[]{:S(2)}) collective-permute-start(bf16[64,2048]{1,0:T(8,128)(2,1)} %get-tuple-element.73), channel_id=1, source_target_pairs={{0,4},{1,3},{2,6},{3,1},{4,0},{5,7},{6,2},{7,5},{8,12},{9,11},{10,... | collective-permute-start | bytes 786440 | tf_op jit(solution)/shard_map/ppermute | solution.py:486
  12.2 2.4 %collective-permute-start.1 = (f32[128,16]{1,0:T(8,128)}, f32[128,16]{1,0:T(8,128)}, u32[]{:S(2)}, u32[]{:S(2)}) collective-permute-start(f32[128,16]{1,0:T(8,128)} %branch_1_fun.4), channel_id=1, source_target_pairs={{0,1},{1,0},{2,3},{3,2},{4,5},{5,4},{6,7},{7,6},{8,9},{9,8},{10,11... | collective-permute-start | bytes 24584 | tf_op jit(solution)/shard_map/cond/branch_1_fun/ppermute | solution.py:147
  21.6 1.9 %collective-permute-start = (bf16[64,2048]{1,0:T(8,128)(2,1)}, bf16[64,2048]{1,0:T(8,128)(2,1)S(1)}, u32[]{:S(2)}, u32[]{:S(2)}) collective-permute-start(bf16[64,2048]{1,0:T(8,128)(2,1)} %get-tuple-element.26.got_ref), channel_id=1, source_target_pairs={{0,1},{1,0},{2,3},{3,2},{4,5},{5,4},{6,7},{7,6},{8,9},{9,8},{10,11... | collective-permute-start | bytes 786440 | tf_op jit(solution)/shard_map/cond/branch_1_fun/ppermute | solution.py:147
  26.4 16.6 %copy-start = (bf16[1,16,2048]{2,1,0:T(8,128)(2,1)S(1)}, bf16[1,16,2048]{2,1,0:T(8,128)(2,1)}, u32[]{:S(2)}) copy-start(bf16[1,16,2048]{2,1,0:T(8,128)(2,1)} %param.18) | copy-start | bytes 196612
  33.7 3.0 %collective-permute-start.8 = (bf16[64,2048]{1,0:T(8,128)(2,1)S(1)}, bf16[64,2048]{1,0:T(8,128)(2,1)S(1)}, u32[]{:S(2)}, u32[]{:S(2)}) collective-permute-start(bf16[64,2048]{1,0:T(8,128)(2,1)S(1)} %collective-permute-done.4.got_a_ref), channel_id=1, source_target_pairs={{0,1},{1,0},{2,3},{3,2},{4,5},{5,4},{6,7},{7,6},{8,9},{9,8},{10,11... | collective-permute-start | bytes 786440 | tf_op jit(solution)/shard_map/ppermute | solution.py:147
  33.7 3.0 %collective-permute-start.9 = (bf16[64,2048]{1,0:T(8,128)(2,1)S(1)}, bf16[64,2048]{1,0:T(8,128)(2,1)S(1)}, u32[]{:S(2)}, u32[]{:S(2)}) collective-permute-start(bf16[64,2048]{1,0:T(8,128)(2,1)S(1)} %collective-permute-done.5.got_b_ref), channel_id=1, source_target_pairs={{0,1},{1,0},{2,3},{3,2},{4,5},{5,4},{6,7},{7,6},{8,9},{9,8},{10,11... | collective-permute-start | bytes 786440 | tf_op jit(solution)/shard_map/ppermute | solution.py:147
  34.2 8.8 %collective-permute-start.12 = (bf16[144,512]{1,0:T(8,128)(2,1)}, bf16[144,512]{1,0:T(8,128)(2,1)S(1)}, u32[]{:S(2)}, u32[]{:S(2)}) collective-permute-start(bf16[144,512]{1,0:T(8,128)(2,1)} %get-tuple-element.136), channel_id=1, source_target_pairs={{0,6},{2,4},{4,2},{6,0},{1,7},{3,5},{5,3},{7,1},{8,14},{10,12},{12... | collective-permute-start | bytes 442376 | tf_op jit(solution)/shard_map/ppermute | solution.py:147
  36.7 26.7 %copy-start.7 = (bf16[2048,128]{1,0:T(8,128)(2,1)S(1)}, bf16[2048,128]{1,0:T(8,128)(2,1)}, u32[]{:S(2)}) copy-start(bf16[2048,128]{1,0:T(8,128)(2,1)} %copy-done.6) | copy-start | bytes 1572868
  37.5 29.5 %copy-start.4 = (bf16[1,128,4096]{2,1,0:T(8,128)(2,1)S(1)}, bf16[1,128,4096]{2,1,0:T(8,128)(2,1)}, u32[]{:S(2)}) copy-start(bf16[1,128,4096]{2,1,0:T(8,128)(2,1)} %param.20) | copy-start | bytes 3145732
  37.5 10.5 %collective-permute-start.10 = (bf16[144,512]{1,0:T(8,128)(2,1)S(1)}, bf16[144,512]{1,0:T(8,128)(2,1)S(1)}, u32[]{:S(2)}, u32[]{:S(2)}) collective-permute-start(bf16[144,512]{1,0:T(8,128)(2,1)S(1)} %get-tuple-element.82), channel_id=1, source_target_pairs={{0,2},{1,5},{2,0},{3,7},{4,6},{5,1},{6,4},{7,3},{8,10},{9,13},{10,... | collective-permute-start | bytes 442376 | tf_op jit(solution)/shard_map/ppermute | solution.py:481
  37.5 11.3 %collective-permute-start.11 = (bf16[144,512]{1,0:T(8,128)(2,1)S(1)}, bf16[144,512]{1,0:T(8,128)(2,1)S(1)}, u32[]{:S(2)}, u32[]{:S(2)}) collective-permute-start(bf16[144,512]{1,0:T(8,128)(2,1)S(1)} %get-tuple-element.83), channel_id=1, source_target_pairs={{0,4},{1,3},{2,6},{3,1},{4,0},{5,7},{6,2},{7,5},{8,12},{9,11},{10,... | collective-permute-start | bytes 442376 | tf_op jit(solution)/shard_map/ppermute | solution.py:486
  49.0 8.7 %collective-permute-start.15 = (bf16[144,512]{1,0:T(8,128)(2,1)S(1)}, bf16[144,512]{1,0:T(8,128)(2,1)S(1)}, u32[]{:S(2)}, u32[]{:S(2)}) collective-permute-start(bf16[144,512]{1,0:T(8,128)(2,1)S(1)} %shard_map.121.block_0_ref), channel_id=1, source_target_pairs={{0,6},{2,4},{4,2},{6,0},{1,7},{3,5},{5,3},{7,1},{8,14},{10,12},{12... | collective-permute-start | bytes 442376 | tf_op jit(solution)/shard_map/ppermute | solution.py:147
  51.0 12.3 %collective-permute-start.14 = (bf16[144,512]{1,0:T(8,128)(2,1)S(1)}, bf16[144,512]{1,0:T(8,128)(2,1)S(1)}, u32[]{:S(2)}, u32[]{:S(2)}) collective-permute-start(bf16[144,512]{1,0:T(8,128)(2,1)S(1)} %shard_map.121.block_0_ref), channel_id=1, source_target_pairs={{0,4},{1,3},{2,6},{3,1},{4,0},{5,7},{6,2},{7,5},{8,12},{9,11},{10,... | collective-permute-start | bytes 442376 | tf_op jit(solution)/shard_map/ppermute | solution.py:486
  51.0 12.3 %collective-permute-start.13 = (bf16[144,512]{1,0:T(8,128)(2,1)S(1)}, bf16[144,512]{1,0:T(8,128)(2,1)S(1)}, u32[]{:S(2)}, u32[]{:S(2)}) collective-permute-start(bf16[144,512]{1,0:T(8,128)(2,1)S(1)} %shard_map.121.block_0_ref), channel_id=1, source_target_pairs={{0,2},{1,5},{2,0},{3,7},{4,6},{5,1},{6,4},{7,3},{8,10},{9,13},{10,... | collective-permute-start | bytes 442376 | tf_op jit(solution)/shard_map/ppermute | solution.py:481
  65.7 1.3 %collective-permute-start.16 = (f32[128,16]{1,0:T(8,128)S(1)}, f32[128,16]{1,0:T(8,128)S(1)}, u32[]{:S(2)}, u32[]{:S(2)}) collective-permute-start(f32[128,16]{1,0:T(8,128)S(1)} %get-tuple-element.100.low_ref), channel_id=1, source_target_pairs={{0,1},{1,0},{2,3},{3,2},{4,5},{5,4},{6,7},{7,6},{8,9},{9,8},{10,11... | collective-permute-start | bytes 24584 | tf_op jit(solution)/shard_map/ppermute | solution.py:147
  67.3 4.9 %collective-permute-start.17 = (bf16[16,3072]{1,0:T(8,128)(2,1)S(1)}, bf16[16,3072]{1,0:T(8,128)(2,1)S(1)}, u32[]{:S(2)}, u32[]{:S(2)}) collective-permute-start(bf16[16,3072]{1,0:T(8,128)(2,1)S(1)} %get-tuple-element.102), channel_id=1, source_target_pairs={{0,2},{2,0},{4,6},{6,4},{1,3},{3,1},{5,7},{7,5},{8,10},{10,8},{12,... | collective-permute-start | bytes 294920 | tf_op jit(solution)/shard_map/ppermute | solution.py:147
  72.2 7.1 %collective-permute-start.18 = (bf16[16,3072]{1,0:T(8,128)(2,1)S(1)}, bf16[16,3072]{1,0:T(8,128)(2,1)S(1)}, u32[]{:S(2)}, u32[]{:S(2)}) collective-permute-start(bf16[16,3072]{1,0:T(8,128)(2,1)S(1)} %shard_map.125.own_ref), channel_id=1, source_target_pairs={{0,4},{2,6},{4,0},{6,2},{1,5},{3,7},{5,1},{7,3},{8,12},{10,14},{12... | collective-permute-start | bytes 294920 | tf_op jit(solution)/shard_map/ppermute | solution.py:147
  79.5 1.2 %collective-permute-start.19 = (f32[8,128]{1,0:T(8,128)S(1)}, f32[8,128]{1,0:T(8,128)S(1)}, u32[]{:S(2)}, u32[]{:S(2)}) collective-permute-start(f32[8,128]{1,0:T(8,128)S(1)} %get-tuple-element.106), channel_id=1, source_target_pairs={{0,1},{1,0},{2,3},{3,2},{4,5},{5,4},{6,7},{7,6},{8,9},{9,8},{10,11... | collective-permute-start | bytes 12296 | tf_op jit(solution)/shard_map/ppermute | solution.py:147
  80.7 3.6 %collective-permute-start.21 = (f32[8,128]{1,0:T(8,128)S(1)}, f32[8,128]{1,0:T(8,128)S(1)}, u32[]{:S(2)}, u32[]{:S(2)}) collective-permute-start(f32[8,128]{1,0:T(8,128)S(1)} %add.30), channel_id=1, source_target_pairs={{0,8},{1,17},{8,0},{9,25},{16,24},{17,1},{24,16},{25,9},{2,10},{3,... | collective-permute-start | bytes 12296 | tf_op jit(solution)/shard_map/ppermute | solution.py:641
  82.2 4.5 %collective-permute-start.20 = (f32[8,128]{1,0:T(8,128)S(1)}, f32[8,128]{1,0:T(8,128)S(1)}, u32[]{:S(2)}, u32[]{:S(2)}) collective-permute-start(f32[8,128]{1,0:T(8,128)S(1)} %add.30), channel_id=1, source_target_pairs={{0,24},{8,16},{16,8},{24,0},{1,25},{9,17},{17,9},{25,1},{2,26},{10... | collective-permute-start | bytes 12296 | tf_op jit(solution)/shard_map/ppermute | solution.py:147
  83.7 7.8 %collective-permute-start.24 = (bf16[16,3072]{1,0:T(8,128)(2,1)S(1)}, bf16[16,3072]{1,0:T(8,128)(2,1)S(1)}, u32[]{:S(2)}, u32[]{:S(2)}) collective-permute-start(bf16[16,3072]{1,0:T(8,128)(2,1)S(1)} %get-tuple-element.107.own_ref), channel_id=1, source_target_pairs={{0,2},{2,0},{4,6},{6,4},{1,3},{3,1},{5,7},{7,5},{8,10},{10,8},{12,... | collective-permute-start | bytes 294920 | tf_op jit(solution)/shard_map/ppermute | solution.py:147
  86.7 3.6 %collective-permute-start.22 = (f32[8,128]{1,0:T(8,128)S(1)}, f32[8,128]{1,0:T(8,128)S(1)}, u32[]{:S(2)}, u32[]{:S(2)}) collective-permute-start(f32[8,128]{1,0:T(8,128)S(1)} %add_select_fusion), channel_id=1, source_target_pairs={{0,2},{2,0},{4,6},{6,4},{1,3},{3,1},{5,7},{7,5},{8,10},{10,8},{12,... | collective-permute-start | bytes 12296 | tf_op jit(solution)/shard_map/ppermute | solution.py:147
  90.3 1.2 %collective-permute-start.23 = (f32[8,128]{1,0:T(8,128)S(1)}, f32[8,128]{1,0:T(8,128)S(1)}, u32[]{:S(2)}, u32[]{:S(2)}) collective-permute-start(f32[8,128]{1,0:T(8,128)S(1)} %add.33.square_ref), channel_id=1, source_target_pairs={{0,1},{1,0},{2,3},{3,2},{4,5},{5,4},{6,7},{7,6},{8,9},{9,8},{10,11... | collective-permute-start | bytes 12296 | tf_op jit(solution)/shard_map/ppermute | solution.py:147
  (3 other events, 4.1 us)

commit v10 on v9

--- a/solution.py
+++ b/solution.py
@@ -535,11 +535,15 @@
     docs, cosine, sine, query, back_part, back_other = step(
         prepare_attention, queries, out_grad, adapt_up, doc_ids, weight
     )
+    def swap_own(even):
+        return swap(even, "tp", 1)
+
+    even_other = step(swap_own, even)
     part_0, weight_near = call(
         functools.partial(own_kernel, head),
         [summed, (weight.shape, BF16)],
         even,
-        swap(even, "tp", 1),
+        even_other,
         weight,
         flops=part_flops,
         scratch=[pltpu.VMEM((rows, slice_width), BF16), pltpu.SemaphoreType.DMA],

time: 92.7 us -> 92.2 us (level)
  local copies, waits for them, and re-layouts: 6.44 us -> 5.12 us
    ppermute x3, waiting for transfers between devices: 13.8 us -> 12.3 us  [send_b(): lax.ppermute(value, ('ctx', 'tp'), [(2 * a + t, 2 * (a ^ (1 if t else 2))...]
    unnamed x20 -> x24, local copies, waits for them, and re-layouts: 2.16 us -> 0.84 us
    ppermute x18, waiting for transfers between devices: 29.5 us -> 30.7 us  [swap(): return lax.ppermute(value, axis, [(i, i ^ distance) for i in range(count)])]
  transfers between devices with their start and end apart: 25 -> 25, of which waited for: 16 -> 17; matrix products, arithmetic and copies ran while one was open for 4% -> 4% of each run, Pallas kernels for 11% -> 12%
where the time goes in v10:
time: 92.2 us; the launch traced here: 91.8 us
  waiting for transfers between devices  47.2 us (51%)
  starting transfers between devices  21.2 us (23%)
  Pallas kernels  16.2 us (18%)
  local copies, waits for them, and re-layouts  5.12 us (6%)
  other arithmetic  1.09 us (1%)
    ppermute x18, waiting for transfers between devices, swap(): return lax.ppermute(value, axis, [(i, i ^ distance) for i in range(count)])  30.7 us
    pallas_call x14, Pallas kernels, call(): pl.pallas_call(kernel, out_shape=shapes, in_specs=[ANYWHERE if i in loose...  16.2 us
    ppermute x18, starting transfers between devices, swap(): return lax.ppermute(value, axis, [(i, i ^ distance) for i in range(count)])  14.3 us
    ppermute x3, waiting for transfers between devices, send_b(): lax.ppermute(value, ('ctx', 'tp'), [(2 * a + t, 2 * (a ^ (1 if t else 2))...  12.3 us
    ppermute x3, waiting for transfers between devices, send_a(): lax.ppermute(value, ('ctx', 'tp'), [(2 * a + t, 2 * (a ^ (2 if t else 1))...  3.61 us
    ppermute x3, starting transfers between devices, send_a(): lax.ppermute(value, ('ctx', 'tp'), [(2 * a + t, 2 * (a ^ (2 if t else 1))...  2.83 us
    squeeze x1, local copies, waits for them, and re-layouts, prepare(): return key_value_weight[0].reshape(slice_width, kv_width)  2.75 us
    ppermute x3, starting transfers between devices, send_b(): lax.ppermute(value, ('ctx', 'tp'), [(2 * a + t, 2 * (a ^ (1 if t else 2))...  2.58 us
  transfers between devices with their start and end apart: 25, of which 17 were waited for; matrix products, arithmetic and copies ran while one was open for 4% of the time, Pallas kernels for 12%

profile of v10, /device:TPU:0, one launch (start us, length us, event | category | flops | bytes accessed | tf_op | source)
XLA Modules:
  0.0 91.8 jit_solution(11717526818530838034)
XLA Ops:
  0.7 1.4 %dynamic-slice_bitcast_fusion = (bf16[64,4096]{1,0:T(8,128)(2,1)S(1)}, bf16[64,4096]{1,0:T(8,128)(2,1)S(1)}) fusion(bf16[1,128,4096]{2,1,0:T(8,128)(2,1)} %param.16, s32[]{:T(128)S(6)} %select_n.15, s32[]{:T(128)S(6)} %select_n.14), kind=kLoop, calls=%fused_computation.9 | loop fusion | bytes 2097160 | tf_op jit(solution)/shard_map/dynamic_slice | solution.py:467
  2.7 1.5 %collective-permute-done.4.gain_other_ref = bf16[1,4096]{1,0:T(2,128)(2,1)S(1)} collective-permute-done((bf16[1,4096]{1,0:T(2,128)(2,1)S(1)}, bf16[1,4096]{1,0:T(2,128)(2,1)S(1)}, u32[]{:S(2)}, u32[]{:S(2)}) %collective-permute-start.4) | collective-permute-done | bytes 8224 | tf_op jit(solution)/shard_map/ppermute | solution.py:147
  5.3 5.0 %collective-permute-start.7 = (bf16[64,2048]{1,0:T(8,128)(2,1)}, bf16[64,2048]{1,0:T(8,128)(2,1)}, u32[]{:S(2)}, u32[]{:S(2)}) collective-permute-start(bf16[64,2048]{1,0:T(8,128)(2,1)} %get-tuple-element.78), channel_id=1, source_target_pairs={{0,6},{2,4},{4,2},{6,0},{1,7},{3,5},{5,3},{7,1},{8,14},{10,12},{12... | collective-permute-start | bytes 786440 | tf_op jit(solution)/shard_map/ppermute | solution.py:147
  11.0 3.4 %conditional.4 = (f32[1,128]{1,0:T(1,128)S(1)}, f32[128,128]{1,0:T(8,128)}, f32[128,128]{1,0:T(8,128)}, bf16[2048,128]{1,0:T(8,128)(2,1)S(1)}, f32[128,16]{1,0:T(8,128)}, /*index=5*/f32[128,16]{1,0:T(8,128)}) conditional(s32[]{:T(128)} %convert_element_type.16, () %tuple.38, (s32[128]{0:T(128)S(1)}, s32[]{:T(128)}, ...), branch_computations={%region_0.0_spmd, %region_1.0_spmd} | conditional | flops 16826880 | bytes 3779176 | solution.py:499
  15.2 2.7 %conditional.6 = (bf16[2048,512]{1,0:T(8,128)(2,1)S(1)}) conditional(s32[]{:T(128)} %convert_element_type.16, () %tuple.42, (bf16[1,2048,2,2,128]{4,3,2,1,0:T(2,128)(2,1)}) %tuple.49), branch_computations={%region_4.0_spmd, %region_5.0_spmd} | conditional | bytes 4194312 | solution.py:499
  15.2 2.7 %squeeze.19 = bf16[2048,512]{1,0:T(8,128)(2,1)S(1)} reshape(bf16[1,2048,2,2,128]{4,3,2,1,0:T(2,128)(2,1)} %get-tuple-element.119) | data formatting | bytes 4194304 | tf_op jit(solution)/shard_map/cond/branch_1_fun/reshape;cond/branch_1_fun/squeeze | solution.py:507
  18.0 1.9 %conditional.5 = (bf16[64,2048]{1,0:T(8,128)(2,1)}) conditional(s32[]{:T(128)} %convert_element_type.16, () %tuple.41, bf16[64,2048]{1,0:T(8,128)(2,1)S(1)} %get-tuple-element.79.even_ref), branch_computations={%region_2.0_spmd, %region_3.0_spmd} | conditional | bytes 1048624 | solution.py:499
  18.5 1.3 %collective-permute-done = bf16[64,2048]{1,0:T(8,128)(2,1)} collective-permute-done((bf16[64,2048]{1,0:T(8,128)(2,1)S(1)}, bf16[64,2048]{1,0:T(8,128)(2,1)}, u32[]{:S(2)}, u32[]{:S(2)}) %collective-permute-start) | collective-permute-done | bytes 262176 | tf_op jit(solution)/shard_map/cond/branch_1_fun/ppermute | solution.py:147
  19.8 3.1 %shard_map.118 = (f32[128,512]{1,0:T(8,128)S(1)}, bf16[2048,512]{1,0:T(8,128)(2,1)S(1)}) custom-call(bf16[64,2048]{1,0:T(8,128)(2,1)} %copy-done.10, bf16[64,2048]{1,0:T(8,128)(2,1)} %get-tuple-element.139.even_other_ref, bf16[2048,512]{1,0:T(8,128)(2,1)} %copy-done.2), custom_call_target="tpu_custom_call" | custom-call | flops 268435456 | bytes 4980736 | tf_op jit(solution)/shard_map/pallas_call | solution.py:153
  22.9 4.7 %conditional.7 = (bf16[144,512]{1,0:T(8,128)(2,1)}) conditional(s32[]{:T(128)} %convert_element_type.16, () %tuple.40, (bf16[64,2048]{1,0:T(8,128)(2,1)}, bf16[2048,512]{1,0:T(8,128)(2,1)}) %tuple.62), branch_computations={%region_6.0_spmd, %region_7.0_spmd} | conditional | flops 268435456 | bytes 3817520 | solution.py:499
  23.4 1.4 %collective-permute-done.1.got_other_ref = bf16[64,2048]{1,0:T(8,128)(2,1)S(1)} collective-permute-done((bf16[64,2048]{1,0:T(8,128)(2,1)}, bf16[64,2048]{1,0:T(8,128)(2,1)S(1)}, u32[]{:S(2)}, u32[]{:S(2)}) %collective-permute-start.1) | collective-permute-done | bytes 262176 | tf_op jit(solution)/shard_map/cond/branch_1_fun/ppermute | solution.py:147
  24.8 2.8 %branch_1_fun.5 = bf16[144,512]{1,0:T(8,128)(2,1)} custom-call(bf16[64,2048]{1,0:T(8,128)(2,1)} %get-tuple-element.30.got_ref, bf16[64,2048]{1,0:T(8,128)(2,1)S(1)} %collective-permute-done.1.got_other_ref, bf16[2048,512]{1,0:T(8,128)(2,1)} %get-tuple-element.31.weight_ref), custom_call_target="tpu_custom_call" | custom-call | flops 268435456 | bytes 2768896 | tf_op jit(solution)/shard_map/cond/branch_1_fun/pallas_call | solution.py:153
  27.6 5.5 %collective-permute-done.6.got_b_ref = bf16[64,2048]{1,0:T(8,128)(2,1)S(1)} collective-permute-done((bf16[64,2048]{1,0:T(8,128)(2,1)S(1)}, bf16[64,2048]{1,0:T(8,128)(2,1)S(1)}, u32[]{:S(2)}, u32[]{:S(2)}) %collective-permute-start.6) | collective-permute-done | bytes 262176 | tf_op jit(solution)/shard_map/ppermute | solution.py:486
  33.6 2.5 %collective-permute-start.12 = (bf16[144,512]{1,0:T(8,128)(2,1)}, bf16[144,512]{1,0:T(8,128)(2,1)S(1)}, u32[]{:S(2)}, u32[]{:S(2)}) collective-permute-start(bf16[144,512]{1,0:T(8,128)(2,1)} %get-tuple-element.141), channel_id=1, source_target_pairs={{0,6},{2,4},{4,2},{6,0},{1,7},{3,5},{5,3},{7,1},{8,14},{10,12},{12... | collective-permute-start | bytes 442376 | tf_op jit(solution)/shard_map/ppermute | solution.py:147
  37.0 1.9 %collective-permute-start.11 = (bf16[144,512]{1,0:T(8,128)(2,1)S(1)}, bf16[144,512]{1,0:T(8,128)(2,1)S(1)}, u32[]{:S(2)}, u32[]{:S(2)}) collective-permute-start(bf16[144,512]{1,0:T(8,128)(2,1)S(1)} %get-tuple-element.87), channel_id=1, source_target_pairs={{0,4},{1,3},{2,6},{3,1},{4,0},{5,7},{6,2},{7,5},{8,12},{9,11},{10,... | collective-permute-start | bytes 442376 | tf_op jit(solution)/shard_map/ppermute | solution.py:486
  39.0 3.5 %collective-permute-done.12.got_ref = bf16[144,512]{1,0:T(8,128)(2,1)S(1)} collective-permute-done((bf16[144,512]{1,0:T(8,128)(2,1)}, bf16[144,512]{1,0:T(8,128)(2,1)S(1)}, u32[]{:S(2)}, u32[]{:S(2)}) %collective-permute-start.12) | collective-permute-done | bytes 147488 | tf_op jit(solution)/shard_map/ppermute | solution.py:147
  43.5 3.6 %collective-permute-done.10.got_a_ref = bf16[144,512]{1,0:T(8,128)(2,1)S(1)} collective-permute-done((bf16[144,512]{1,0:T(8,128)(2,1)S(1)}, bf16[144,512]{1,0:T(8,128)(2,1)S(1)}, u32[]{:S(2)}, u32[]{:S(2)}) %collective-permute-start.10) | collective-permute-done | bytes 147488 | tf_op jit(solution)/shard_map/ppermute | solution.py:481
  47.1 1.5 %collective-permute-done.11.got_b_ref = bf16[144,512]{1,0:T(8,128)(2,1)S(1)} collective-permute-done((bf16[144,512]{1,0:T(8,128)(2,1)S(1)}, bf16[144,512]{1,0:T(8,128)(2,1)S(1)}, u32[]{:S(2)}, u32[]{:S(2)}) %collective-permute-start.11) | collective-permute-done | bytes 147488 | tf_op jit(solution)/shard_map/ppermute | solution.py:486
  48.8 1.7 %collective-permute-start.15 = (bf16[144,512]{1,0:T(8,128)(2,1)S(1)}, bf16[144,512]{1,0:T(8,128)(2,1)S(1)}, u32[]{:S(2)}, u32[]{:S(2)}) collective-permute-start(bf16[144,512]{1,0:T(8,128)(2,1)S(1)} %shard_map.121.block_0_ref), channel_id=1, source_target_pairs={{0,6},{2,4},{4,2},{6,0},{1,7},{3,5},{5,3},{7,1},{8,14},{10,12},{12... | collective-permute-start | bytes 442376 | tf_op jit(solution)/shard_map/ppermute | solution.py:147
  50.5 2.8 %collective-permute-start.13 = (bf16[144,512]{1,0:T(8,128)(2,1)S(1)}, bf16[144,512]{1,0:T(8,128)(2,1)S(1)}, u32[]{:S(2)}, u32[]{:S(2)}) collective-permute-start(bf16[144,512]{1,0:T(8,128)(2,1)S(1)} %shard_map.121.block_0_ref), channel_id=1, source_target_pairs={{0,2},{1,5},{2,0},{3,7},{4,6},{5,1},{6,4},{7,3},{8,10},{9,13},{10,... | collective-permute-start | bytes 442376 | tf_op jit(solution)/shard_map/ppermute | solution.py:481
  53.3 4.2 %collective-permute-done.15.block_c_ref = bf16[144,512]{1,0:T(8,128)(2,1)S(1)} collective-permute-done((bf16[144,512]{1,0:T(8,128)(2,1)S(1)}, bf16[144,512]{1,0:T(8,128)(2,1)S(1)}, u32[]{:S(2)}, u32[]{:S(2)}) %collective-permute-start.15) | collective-permute-done | bytes 147488 | tf_op jit(solution)/shard_map/ppermute | solution.py:147
  57.5 5.3 %collective-permute-done.14.block_b_ref = bf16[144,512]{1,0:T(8,128)(2,1)S(1)} collective-permute-done((bf16[144,512]{1,0:T(8,128)(2,1)S(1)}, bf16[144,512]{1,0:T(8,128)(2,1)S(1)}, u32[]{:S(2)}, u32[]{:S(2)}) %collective-permute-start.14) | collective-permute-done | bytes 147488 | tf_op jit(solution)/shard_map/ppermute | solution.py:486
  62.8 2.3 %shard_map.122 = (bf16[128,2048]{1,0:T(8,128)(2,1)}, f32[128,16]{1,0:T(8,128)S(1)}, f32[16,2048]{1,0:T(8,128)S(1)}) custom-call(bf16[2048,128]{1,0:T(8,128)(2,1)S(1)} %copy-done.8, bf16[144,512]{1,0:T(8,128)(2,1)S(1)} %shard_map.121.block_0_ref, bf16[144,512]{1,0:T(8,128)(2,1)S(1)} %collective-permute-done.13.block_a_ref, ...), custom_call_target="tpu_custom_call" | custom-call | flops 536870912 | bytes 1847296 | tf_op jit(solution)/shard_map/pallas_call | solution.py:153
  65.2 1.2 %collective-permute-done.16.low_other_ref = f32[128,16]{1,0:T(8,128)S(1)} collective-permute-done((f32[128,16]{1,0:T(8,128)S(1)}, f32[128,16]{1,0:T(8,128)S(1)}, u32[]{:S(2)}, u32[]{:S(2)}) %collective-permute-start.16) | collective-permute-done | bytes 8224 | tf_op jit(solution)/shard_map/ppermute | solution.py:147
  66.8 1.4 %shard_map.124 = bf16[128,4096]{1,0:T(8,128)(2,1)} custom-call(f32[128,16]{1,0:T(8,128)S(1)} %get-tuple-element.104.low_ref, f32[128,16]{1,0:T(8,128)S(1)} %collective-permute-done.16.low_other_ref, bf16[16,4096]{1,0:T(8,128)(2,1)S(1)} %bitcast.25), custom_call_target="tpu_custom_call" | custom-call | flops 16777216 | bytes 1196032 | tf_op jit(solution)/shard_map/pallas_call | solution.py:153
  68.2 3.5 %collective-permute-done.17.got_ref = bf16[16,3072]{1,0:T(8,128)(2,1)S(1)} collective-permute-done((bf16[16,3072]{1,0:T(8,128)(2,1)S(1)}, bf16[16,3072]{1,0:T(8,128)(2,1)S(1)}, u32[]{:S(2)}, u32[]{:S(2)}) %collective-permute-start.17) | collective-permute-done | bytes 98336 | tf_op jit(solution)/shard_map/ppermute | solution.py:147
  71.6 1.3 %collective-permute-start.18 = (bf16[16,3072]{1,0:T(8,128)(2,1)S(1)}, bf16[16,3072]{1,0:T(8,128)(2,1)S(1)}, u32[]{:S(2)}, u32[]{:S(2)}) collective-permute-start(bf16[16,3072]{1,0:T(8,128)(2,1)S(1)} %shard_map.125.own_ref), channel_id=1, source_target_pairs={{0,4},{2,6},{4,0},{6,2},{1,5},{3,7},{5,1},{7,3},{8,12},{10,14},{12... | collective-permute-start | bytes 294920 | tf_op jit(solution)/shard_map/ppermute | solution.py:147
  72.9 5.8 %collective-permute-done.18.got_ref = bf16[16,3072]{1,0:T(8,128)(2,1)S(1)} collective-permute-done((bf16[16,3072]{1,0:T(8,128)(2,1)S(1)}, bf16[16,3072]{1,0:T(8,128)(2,1)S(1)}, u32[]{:S(2)}, u32[]{:S(2)}) %collective-permute-start.18) | collective-permute-done | bytes 98336 | tf_op jit(solution)/shard_map/ppermute | solution.py:147
  80.2 1.5 %collective-permute-start.21 = (f32[8,128]{1,0:T(8,128)S(1)}, f32[8,128]{1,0:T(8,128)S(1)}, u32[]{:S(2)}, u32[]{:S(2)}) collective-permute-start(f32[8,128]{1,0:T(8,128)S(1)} %add.30), channel_id=1, source_target_pairs={{0,8},{1,17},{8,0},{9,25},{16,24},{17,1},{24,16},{25,9},{2,10},{3,... | collective-permute-start | bytes 12296 | tf_op jit(solution)/shard_map/ppermute | solution.py:645
  81.7 1.5 %collective-permute-start.20 = (f32[8,128]{1,0:T(8,128)S(1)}, f32[8,128]{1,0:T(8,128)S(1)}, u32[]{:S(2)}, u32[]{:S(2)}) collective-permute-start(f32[8,128]{1,0:T(8,128)S(1)} %add.30), channel_id=1, source_target_pairs={{0,24},{8,16},{16,8},{24,0},{1,25},{9,17},{17,9},{25,1},{2,26},{10... | collective-permute-start | bytes 12296 | tf_op jit(solution)/shard_map/ppermute | solution.py:147
  83.8 2.4 %collective-permute-done.20 = f32[8,128]{1,0:T(8,128)S(1)} collective-permute-done((f32[8,128]{1,0:T(8,128)S(1)}, f32[8,128]{1,0:T(8,128)S(1)}, u32[]{:S(2)}, u32[]{:S(2)}) %collective-permute-start.20) | collective-permute-done | bytes 4128 | tf_op jit(solution)/shard_map/ppermute | solution.py:147
  86.2 3.6 %collective-permute-done.22 = f32[8,128]{1,0:T(8,128)S(1)} collective-permute-done((f32[8,128]{1,0:T(8,128)S(1)}, f32[8,128]{1,0:T(8,128)S(1)}, u32[]{:S(2)}, u32[]{:S(2)}) %collective-permute-start.22) | collective-permute-done | bytes 4128 | tf_op jit(solution)/shard_map/ppermute | solution.py:147
  (71 shorter events, 14.6 us)
Async XLA Ops:
  0.6 10.3 %copy-start.3 = (bf16[1,128,4096]{2,1,0:T(8,128)(2,1)S(1)}, bf16[1,128,4096]{2,1,0:T(8,128)(2,1)}, u32[]{:S(2)}) copy-start(bf16[1,128,4096]{2,1,0:T(8,128)(2,1)} %param.22) | copy-start | bytes 3145732
  0.7 10.3 %copy-start.5 = (bf16[1,16,4096]{2,1,0:T(8,128)(2,1)S(1)}, bf16[1,16,4096]{2,1,0:T(8,128)(2,1)}, u32[]{:S(2)}) copy-start(bf16[1,16,4096]{2,1,0:T(8,128)(2,1)} %param.21) | copy-start | bytes 393220
  2.1 2.1 %collective-permute-start.3 = (bf16[64,4096]{1,0:T(8,128)(2,1)S(1)}, bf16[64,4096]{1,0:T(8,128)(2,1)S(1)}, u32[]{:S(2)}, u32[]{:S(2)}) collective-permute-start(bf16[64,4096]{1,0:T(8,128)(2,1)S(1)} %get-tuple-element.125), channel_id=1, source_target_pairs={{0,1},{1,0},{2,3},{3,2},{4,5},{5,4},{6,7},{7,6},{8,9},{9,8},{10,11... | collective-permute-start | bytes 1572872 | tf_op jit(solution)/shard_map/ppermute | solution.py:147
  2.6 1.6 %collective-permute-start.4 = (bf16[1,4096]{1,0:T(2,128)(2,1)S(1)}, bf16[1,4096]{1,0:T(2,128)(2,1)S(1)}, u32[]{:S(2)}, u32[]{:S(2)}) collective-permute-start(bf16[1,4096]{1,0:T(2,128)(2,1)S(1)} %copy-done.1), channel_id=1, source_target_pairs={{0,1},{1,0},{2,3},{3,2},{4,5},{5,4},{6,7},{7,6},{8,9},{9,8},{10,11... | collective-permute-start | bytes 24584 | tf_op jit(solution)/shard_map/ppermute | solution.py:147
  5.3 12.7 %copy-start.10 = (bf16[64,2048]{1,0:T(8,128)(2,1)}, bf16[64,2048]{1,0:T(8,128)(2,1)S(1)}, u32[]{:S(2)}) copy-start(bf16[64,2048]{1,0:T(8,128)(2,1)S(1)} %get-tuple-element.79.even_ref) | copy-start | bytes 786436
  5.3 17.6 %collective-permute-start.7 = (bf16[64,2048]{1,0:T(8,128)(2,1)}, bf16[64,2048]{1,0:T(8,128)(2,1)}, u32[]{:S(2)}, u32[]{:S(2)}) collective-permute-start(bf16[64,2048]{1,0:T(8,128)(2,1)} %get-tuple-element.78), channel_id=1, source_target_pairs={{0,6},{2,4},{4,2},{6,0},{1,7},{3,5},{5,3},{7,1},{8,14},{10,12},{12... | collective-permute-start | bytes 786440 | tf_op jit(solution)/shard_map/ppermute | solution.py:147
  10.3 17.3 %collective-permute-start.5 = (bf16[64,2048]{1,0:T(8,128)(2,1)S(1)}, bf16[64,2048]{1,0:T(8,128)(2,1)S(1)}, u32[]{:S(2)}, u32[]{:S(2)}) collective-permute-start(bf16[64,2048]{1,0:T(8,128)(2,1)S(1)} %get-tuple-element.76), channel_id=1, source_target_pairs={{0,2},{1,5},{2,0},{3,7},{4,6},{5,1},{6,4},{7,3},{8,10},{9,13},{10,... | collective-permute-start | bytes 786440 | tf_op jit(solution)/shard_map/ppermute | solution.py:481
  10.3 22.8 %collective-permute-start.6 = (bf16[64,2048]{1,0:T(8,128)(2,1)S(1)}, bf16[64,2048]{1,0:T(8,128)(2,1)S(1)}, u32[]{:S(2)}, u32[]{:S(2)}) collective-permute-start(bf16[64,2048]{1,0:T(8,128)(2,1)S(1)} %get-tuple-element.77), channel_id=1, source_target_pairs={{0,4},{1,3},{2,6},{3,1},{4,0},{5,7},{6,2},{7,5},{8,12},{9,11},{10,... | collective-permute-start | bytes 786440 | tf_op jit(solution)/shard_map/ppermute | solution.py:486
  12.0 2.4 %collective-permute-start.2 = (f32[128,16]{1,0:T(8,128)}, f32[128,16]{1,0:T(8,128)}, u32[]{:S(2)}, u32[]{:S(2)}) collective-permute-start(f32[128,16]{1,0:T(8,128)} %branch_1_fun.4), channel_id=1, source_target_pairs={{0,1},{1,0},{2,3},{3,2},{4,5},{5,4},{6,7},{7,6},{8,9},{9,8},{10,11... | collective-permute-start | bytes 24584 | tf_op jit(solution)/shard_map/cond/branch_1_fun/ppermute | solution.py:147
  18.0 1.9 %collective-permute-start = (bf16[64,2048]{1,0:T(8,128)(2,1)S(1)}, bf16[64,2048]{1,0:T(8,128)(2,1)}, u32[]{:S(2)}, u32[]{:S(2)}) collective-permute-start(bf16[64,2048]{1,0:T(8,128)(2,1)S(1)} %param.3), channel_id=1, source_target_pairs={{0,1},{1,0},{2,3},{3,2},{4,5},{5,4},{6,7},{7,6},{8,9},{9,8},{10,11... | collective-permute-start | bytes 786440 | tf_op jit(solution)/shard_map/cond/branch_1_fun/ppermute | solution.py:147
  22.9 1.8 %collective-permute-start.1 = (bf16[64,2048]{1,0:T(8,128)(2,1)}, bf16[64,2048]{1,0:T(8,128)(2,1)S(1)}, u32[]{:S(2)}, u32[]{:S(2)}) collective-permute-start(bf16[64,2048]{1,0:T(8,128)(2,1)} %get-tuple-element.30.got_ref), channel_id=1, source_target_pairs={{0,1},{1,0},{2,3},{3,2},{4,5},{5,4},{6,7},{7,6},{8,9},{9,8},{10,11... | collective-permute-start | bytes 786440 | tf_op jit(solution)/shard_map/cond/branch_1_fun/ppermute | solution.py:147
  27.6 14.9 %copy-start = (bf16[1,16,2048]{2,1,0:T(8,128)(2,1)S(1)}, bf16[1,16,2048]{2,1,0:T(8,128)(2,1)}, u32[]{:S(2)}) copy-start(bf16[1,16,2048]{2,1,0:T(8,128)(2,1)} %param.20) | copy-start | bytes 196612
  33.1 3.0 %collective-permute-start.8 = (bf16[64,2048]{1,0:T(8,128)(2,1)S(1)}, bf16[64,2048]{1,0:T(8,128)(2,1)S(1)}, u32[]{:S(2)}, u32[]{:S(2)}) collective-permute-start(bf16[64,2048]{1,0:T(8,128)(2,1)S(1)} %collective-permute-done.5.got_a_ref), channel_id=1, source_target_pairs={{0,1},{1,0},{2,3},{3,2},{4,5},{5,4},{6,7},{7,6},{8,9},{9,8},{10,11... | collective-permute-start | bytes 786440 | tf_op jit(solution)/shard_map/ppermute | solution.py:147
  33.1 3.0 %collective-permute-start.9 = (bf16[64,2048]{1,0:T(8,128)(2,1)S(1)}, bf16[64,2048]{1,0:T(8,128)(2,1)S(1)}, u32[]{:S(2)}, u32[]{:S(2)}) collective-permute-start(bf16[64,2048]{1,0:T(8,128)(2,1)S(1)} %collective-permute-done.6.got_b_ref), channel_id=1, source_target_pairs={{0,1},{1,0},{2,3},{3,2},{4,5},{5,4},{6,7},{7,6},{8,9},{9,8},{10,11... | collective-permute-start | bytes 786440 | tf_op jit(solution)/shard_map/ppermute | solution.py:147
  33.6 8.8 %collective-permute-start.12 = (bf16[144,512]{1,0:T(8,128)(2,1)}, bf16[144,512]{1,0:T(8,128)(2,1)S(1)}, u32[]{:S(2)}, u32[]{:S(2)}) collective-permute-start(bf16[144,512]{1,0:T(8,128)(2,1)} %get-tuple-element.141), channel_id=1, source_target_pairs={{0,6},{2,4},{4,2},{6,0},{1,7},{3,5},{5,3},{7,1},{8,14},{10,12},{12... | collective-permute-start | bytes 442376 | tf_op jit(solution)/shard_map/ppermute | solution.py:147
  36.1 26.6 %copy-start.8 = (bf16[2048,128]{1,0:T(8,128)(2,1)S(1)}, bf16[2048,128]{1,0:T(8,128)(2,1)}, u32[]{:S(2)}) copy-start(bf16[2048,128]{1,0:T(8,128)(2,1)} %copy-done.7) | copy-start | bytes 1572868
  36.9 29.5 %copy-start.4 = (bf16[1,128,4096]{2,1,0:T(8,128)(2,1)S(1)}, bf16[1,128,4096]{2,1,0:T(8,128)(2,1)}, u32[]{:S(2)}) copy-start(bf16[1,128,4096]{2,1,0:T(8,128)(2,1)} %param.22) | copy-start | bytes 3145732
  37.0 10.1 %collective-permute-start.10 = (bf16[144,512]{1,0:T(8,128)(2,1)S(1)}, bf16[144,512]{1,0:T(8,128)(2,1)S(1)}, u32[]{:S(2)}, u32[]{:S(2)}) collective-permute-start(bf16[144,512]{1,0:T(8,128)(2,1)S(1)} %get-tuple-element.86), channel_id=1, source_target_pairs={{0,2},{1,5},{2,0},{3,7},{4,6},{5,1},{6,4},{7,3},{8,10},{9,13},{10,... | collective-permute-start | bytes 442376 | tf_op jit(solution)/shard_map/ppermute | solution.py:481
  37.0 11.6 %collective-permute-start.11 = (bf16[144,512]{1,0:T(8,128)(2,1)S(1)}, bf16[144,512]{1,0:T(8,128)(2,1)S(1)}, u32[]{:S(2)}, u32[]{:S(2)}) collective-permute-start(bf16[144,512]{1,0:T(8,128)(2,1)S(1)} %get-tuple-element.87), channel_id=1, source_target_pairs={{0,4},{1,3},{2,6},{3,1},{4,0},{5,7},{6,2},{7,5},{8,12},{9,11},{10,... | collective-permute-start | bytes 442376 | tf_op jit(solution)/shard_map/ppermute | solution.py:486
  43.5 23.3 %copy-start.6 = (bf16[1,16,4096]{2,1,0:T(8,128)(2,1)S(1)}, bf16[1,16,4096]{2,1,0:T(8,128)(2,1)}, u32[]{:S(2)}) copy-start(bf16[1,16,4096]{2,1,0:T(8,128)(2,1)} %param.21) | copy-start | bytes 393220
  48.8 8.7 %collective-permute-start.15 = (bf16[144,512]{1,0:T(8,128)(2,1)S(1)}, bf16[144,512]{1,0:T(8,128)(2,1)S(1)}, u32[]{:S(2)}, u32[]{:S(2)}) collective-permute-start(bf16[144,512]{1,0:T(8,128)(2,1)S(1)} %shard_map.121.block_0_ref), channel_id=1, source_target_pairs={{0,6},{2,4},{4,2},{6,0},{1,7},{3,5},{5,3},{7,1},{8,14},{10,12},{12... | collective-permute-start | bytes 442376 | tf_op jit(solution)/shard_map/ppermute | solution.py:147
  50.5 12.3 %collective-permute-start.14 = (bf16[144,512]{1,0:T(8,128)(2,1)S(1)}, bf16[144,512]{1,0:T(8,128)(2,1)S(1)}, u32[]{:S(2)}, u32[]{:S(2)}) collective-permute-start(bf16[144,512]{1,0:T(8,128)(2,1)S(1)} %shard_map.121.block_0_ref), channel_id=1, source_target_pairs={{0,4},{1,3},{2,6},{3,1},{4,0},{5,7},{6,2},{7,5},{8,12},{9,11},{10,... | collective-permute-start | bytes 442376 | tf_op jit(solution)/shard_map/ppermute | solution.py:486
  50.5 12.3 %collective-permute-start.13 = (bf16[144,512]{1,0:T(8,128)(2,1)S(1)}, bf16[144,512]{1,0:T(8,128)(2,1)S(1)}, u32[]{:S(2)}, u32[]{:S(2)}) collective-permute-start(bf16[144,512]{1,0:T(8,128)(2,1)S(1)} %shard_map.121.block_0_ref), channel_id=1, source_target_pairs={{0,2},{1,5},{2,0},{3,7},{4,6},{5,1},{6,4},{7,3},{8,10},{9,13},{10,... | collective-permute-start | bytes 442376 | tf_op jit(solution)/shard_map/ppermute | solution.py:481
  65.1 1.3 %collective-permute-start.16 = (f32[128,16]{1,0:T(8,128)S(1)}, f32[128,16]{1,0:T(8,128)S(1)}, u32[]{:S(2)}, u32[]{:S(2)}) collective-permute-start(f32[128,16]{1,0:T(8,128)S(1)} %get-tuple-element.104.low_ref), channel_id=1, source_target_pairs={{0,1},{1,0},{2,3},{3,2},{4,5},{5,4},{6,7},{7,6},{8,9},{9,8},{10,11... | collective-permute-start | bytes 24584 | tf_op jit(solution)/shard_map/ppermute | solution.py:147
  66.7 4.9 %collective-permute-start.17 = (bf16[16,3072]{1,0:T(8,128)(2,1)S(1)}, bf16[16,3072]{1,0:T(8,128)(2,1)S(1)}, u32[]{:S(2)}, u32[]{:S(2)}) collective-permute-start(bf16[16,3072]{1,0:T(8,128)(2,1)S(1)} %get-tuple-element.106), channel_id=1, source_target_pairs={{0,2},{2,0},{4,6},{6,4},{1,3},{3,1},{5,7},{7,5},{8,10},{10,8},{12,... | collective-permute-start | bytes 294920 | tf_op jit(solution)/shard_map/ppermute | solution.py:147
  71.6 7.1 %collective-permute-start.18 = (bf16[16,3072]{1,0:T(8,128)(2,1)S(1)}, bf16[16,3072]{1,0:T(8,128)(2,1)S(1)}, u32[]{:S(2)}, u32[]{:S(2)}) collective-permute-start(bf16[16,3072]{1,0:T(8,128)(2,1)S(1)} %shard_map.125.own_ref), channel_id=1, source_target_pairs={{0,4},{2,6},{4,0},{6,2},{1,5},{3,7},{5,1},{7,3},{8,12},{10,14},{12... | collective-permute-start | bytes 294920 | tf_op jit(solution)/shard_map/ppermute | solution.py:147
  78.9 1.2 %collective-permute-start.19 = (f32[8,128]{1,0:T(8,128)S(1)}, f32[8,128]{1,0:T(8,128)S(1)}, u32[]{:S(2)}, u32[]{:S(2)}) collective-permute-start(f32[8,128]{1,0:T(8,128)S(1)} %get-tuple-element.110), channel_id=1, source_target_pairs={{0,1},{1,0},{2,3},{3,2},{4,5},{5,4},{6,7},{7,6},{8,9},{9,8},{10,11... | collective-permute-start | bytes 12296 | tf_op jit(solution)/shard_map/ppermute | solution.py:147
  80.2 3.6 %collective-permute-start.21 = (f32[8,128]{1,0:T(8,128)S(1)}, f32[8,128]{1,0:T(8,128)S(1)}, u32[]{:S(2)}, u32[]{:S(2)}) collective-permute-start(f32[8,128]{1,0:T(8,128)S(1)} %add.30), channel_id=1, source_target_pairs={{0,8},{1,17},{8,0},{9,25},{16,24},{17,1},{24,16},{25,9},{2,10},{3,... | collective-permute-start | bytes 12296 | tf_op jit(solution)/shard_map/ppermute | solution.py:645
  81.7 4.5 %collective-permute-start.20 = (f32[8,128]{1,0:T(8,128)S(1)}, f32[8,128]{1,0:T(8,128)S(1)}, u32[]{:S(2)}, u32[]{:S(2)}) collective-permute-start(f32[8,128]{1,0:T(8,128)S(1)} %add.30), channel_id=1, source_target_pairs={{0,24},{8,16},{16,8},{24,0},{1,25},{9,17},{17,9},{25,1},{2,26},{10... | collective-permute-start | bytes 12296 | tf_op jit(solution)/shard_map/ppermute | solution.py:147
  83.2 7.8 %collective-permute-start.24 = (bf16[16,3072]{1,0:T(8,128)(2,1)S(1)}, bf16[16,3072]{1,0:T(8,128)(2,1)S(1)}, u32[]{:S(2)}, u32[]{:S(2)}) collective-permute-start(bf16[16,3072]{1,0:T(8,128)(2,1)S(1)} %get-tuple-element.111.own_ref), channel_id=1, source_target_pairs={{0,2},{2,0},{4,6},{6,4},{1,3},{3,1},{5,7},{7,5},{8,10},{10,8},{12,... | collective-permute-start | bytes 294920 | tf_op jit(solution)/shard_map/ppermute | solution.py:147
  86.2 3.6 %collective-permute-start.22 = (f32[8,128]{1,0:T(8,128)S(1)}, f32[8,128]{1,0:T(8,128)S(1)}, u32[]{:S(2)}, u32[]{:S(2)}) collective-permute-start(f32[8,128]{1,0:T(8,128)S(1)} %add_select_fusion), channel_id=1, source_target_pairs={{0,2},{2,0},{4,6},{6,4},{1,3},{3,1},{5,7},{7,5},{8,10},{10,8},{12,... | collective-permute-start | bytes 12296 | tf_op jit(solution)/shard_map/ppermute | solution.py:147
  89.8 1.2 %collective-permute-start.23 = (f32[8,128]{1,0:T(8,128)S(1)}, f32[8,128]{1,0:T(8,128)S(1)}, u32[]{:S(2)}, u32[]{:S(2)}) collective-permute-start(f32[8,128]{1,0:T(8,128)S(1)} %add.33.square_ref), channel_id=1, source_target_pairs={{0,1},{1,0},{2,3},{3,2},{4,5},{5,4},{6,7},{7,6},{8,9},{9,8},{10,11... | collective-permute-start | bytes 12296 | tf_op jit(solution)/shard_map/ppermute | solution.py:147
  (5 other events, 25.3 us)

commit v11 on v10

--- a/solution.py
+++ b/solution.py
@@ -436,8 +436,8 @@
     square_ref[...] = jnp.broadcast_to(squares, square_ref.shape)
 
 
-def clip_kernel(ceiling, square_ref, other_ref, own_ref, got_ref, up_ref, down_ref):
-    squares = square_ref[:1, :1] + other_ref[:1, :1]
+def clip_kernel(ceiling, square_ref, own_ref, got_ref, up_ref, down_ref):
+    squares = square_ref[:1, :1]
     factor = jnp.minimum(1.0, ceiling / (jnp.sqrt(squares) + 1e-06))
     parity = lax.axis_index("ctx") % 2
     up_step, down_step = up_ref.shape[1] // 2, down_ref.shape[1] // 2
@@ -642,20 +642,14 @@
     )
     total_other = swap(total, "ctx", 1)
     squares = squares + swap(squares, "tp", 1)
-    beside = lax.ppermute(
-        squares,
-        ("section", "tp"),
-        [(2 * i + t, 2 * (i ^ (2 if t else 1)) + t) for i in range(4) for t in range(2)],
-    )
-    across = swap(squares, "section", 3)
-    squares = jnp.where(core == 0, squares + across + beside, beside)
+    squares = squares + swap(squares, "section", 1)
+    squares = squares + swap(squares, "section", 2)
     squares = squares + swap(squares, "ctx", 1)
     ceiling = 0.5 * math.sqrt(lax.axis_size("section") * rank * (local_query + local_width) * 2)
     grad_up, grad_down = call(
         functools.partial(clip_kernel, ceiling),
         [((rank, local_width), F32), ((rank, local_query), F32)],
         squares,
-        swap(squares, "tp", 1),
         total,
         total_other,
     )

time: 92.2 us -> 92.3 us (level)
  starting transfers between devices: 21.2 us -> 23.2 us
  waiting for transfers between devices: 47.2 us -> 45.3 us
    ppermute x18, starting transfers between devices: 14.3 us -> 17.8 us  [swap(): return lax.ppermute(value, axis, [(i, i ^ distance) for i in range(count)])]
    ppermute x1 -> x0, starting transfers between devices: 1.49 us -> none  [split_model_width(): lax.ppermute(squares, ('section', 'tp'), [(2 * i + t, 2 * (i ^ (2 if t el...]
    ppermute x18, waiting for transfers between devices: 30.7 us -> 29.4 us  [swap(): return lax.ppermute(value, axis, [(i, i ^ distance) for i in range(count)])]
  transfers between devices with their start and end apart: 25 -> 24, of which waited for: 17 -> 16; matrix products, arithmetic and copies ran while one was open for 4% -> 4% of each run, Pallas kernels for 12% -> 12%
where the time goes in v11:
time: 92.3 us; the launch traced here: 91.9 us
  waiting for transfers between devices  45.3 us (49%)
  starting transfers between devices  23.2 us (25%)
  Pallas kernels  16.2 us (18%)
  local copies, waits for them, and re-layouts  5.12 us (6%)
  other arithmetic  1.08 us (1%)
    ppermute x18, waiting for transfers between devices, swap(): return lax.ppermute(value, axis, [(i, i ^ distance) for i in range(count)])  29.4 us
    ppermute x18, starting transfers between devices, swap(): return lax.ppermute(value, axis, [(i, i ^ distance) for i in range(count)])  17.8 us
    pallas_call x14, Pallas kernels, call(): pl.pallas_call(kernel, out_shape=shapes, in_specs=[ANYWHERE if i in loose...  16.2 us
    ppermute x3, waiting for transfers between devices, send_b(): lax.ppermute(value, ('ctx', 'tp'), [(2 * a + t, 2 * (a ^ (1 if t else 2))...  12.3 us
    ppermute x3, waiting for transfers between devices, send_a(): lax.ppermute(value, ('ctx', 'tp'), [(2 * a + t, 2 * (a ^ (2 if t else 1))...  3.61 us
    ppermute x3, starting transfers between devices, send_a(): lax.ppermute(value, ('ctx', 'tp'), [(2 * a + t, 2 * (a ^ (2 if t else 1))...  2.83 us
    squeeze x1, local copies, waits for them, and re-layouts, prepare(): return key_value_weight[0].reshape(slice_width, kv_width)  2.75 us
    ppermute x3, starting transfers between devices, send_b(): lax.ppermute(value, ('ctx', 'tp'), [(2 * a + t, 2 * (a ^ (1 if t else 2))...  2.58 us
  transfers between devices with their start and end apart: 24, of which 16 were waited for; matrix products, arithmetic and copies ran while one was open for 4% of the time, Pallas kernels for 12%

profile of v11, /device:TPU:0, one launch (start us, length us, event | category | flops | bytes accessed | tf_op | source)
XLA Modules:
  0.0 91.9 jit_solution(6537730666265178201)
XLA Ops:
  0.7 1.4 %dynamic-slice_bitcast_fusion = (bf16[64,4096]{1,0:T(8,128)(2,1)S(1)}, bf16[64,4096]{1,0:T(8,128)(2,1)S(1)}) fusion(bf16[1,128,4096]{2,1,0:T(8,128)(2,1)} %param.16, s32[]{:T(128)S(6)} %select_n.7, s32[]{:T(128)S(6)} %select_n.6), kind=kLoop, calls=%fused_computation.9 | loop fusion | bytes 2097160 | tf_op jit(solution)/shard_map/dynamic_slice | solution.py:467
  2.7 1.5 %collective-permute-done.4.gain_other_ref = bf16[1,4096]{1,0:T(2,128)(2,1)S(1)} collective-permute-done((bf16[1,4096]{1,0:T(2,128)(2,1)S(1)}, bf16[1,4096]{1,0:T(2,128)(2,1)S(1)}, u32[]{:S(2)}, u32[]{:S(2)}) %collective-permute-start.4) | collective-permute-done | bytes 8224 | tf_op jit(solution)/shard_map/ppermute | solution.py:147
  5.3 5.0 %collective-permute-start.7 = (bf16[64,2048]{1,0:T(8,128)(2,1)}, bf16[64,2048]{1,0:T(8,128)(2,1)}, u32[]{:S(2)}, u32[]{:S(2)}) collective-permute-start(bf16[64,2048]{1,0:T(8,128)(2,1)} %get-tuple-element.78), channel_id=1, source_target_pairs={{0,6},{2,4},{4,2},{6,0},{1,7},{3,5},{5,3},{7,1},{8,14},{10,12},{12... | collective-permute-start | bytes 786440 | tf_op jit(solution)/shard_map/ppermute | solution.py:147
  11.0 3.4 %conditional.4 = (f32[1,128]{1,0:T(1,128)S(1)}, f32[128,128]{1,0:T(8,128)}, f32[128,128]{1,0:T(8,128)}, bf16[2048,128]{1,0:T(8,128)(2,1)S(1)}, f32[128,16]{1,0:T(8,128)}, /*index=5*/f32[128,16]{1,0:T(8,128)}) conditional(s32[]{:T(128)} %convert_element_type.16, () %tuple.38, (s32[128]{0:T(128)S(1)}, s32[]{:T(128)}, ...), branch_computations={%region_0.0_spmd, %region_1.0_spmd} | conditional | flops 16826880 | bytes 3779176 | solution.py:499
  15.2 2.7 %conditional.6 = (bf16[2048,512]{1,0:T(8,128)(2,1)S(1)}) conditional(s32[]{:T(128)} %convert_element_type.16, () %tuple.42, (bf16[1,2048,2,2,128]{4,3,2,1,0:T(2,128)(2,1)}) %tuple.49), branch_computations={%region_4.0_spmd, %region_5.0_spmd} | conditional | bytes 4194312 | solution.py:499
  15.2 2.7 %squeeze.19 = bf16[2048,512]{1,0:T(8,128)(2,1)S(1)} reshape(bf16[1,2048,2,2,128]{4,3,2,1,0:T(2,128)(2,1)} %get-tuple-element.119) | data formatting | bytes 4194304 | tf_op jit(solution)/shard_map/cond/branch_1_fun/reshape;cond/branch_1_fun/squeeze | solution.py:507
  18.0 1.9 %conditional.5 = (bf16[64,2048]{1,0:T(8,128)(2,1)}) conditional(s32[]{:T(128)} %convert_element_type.16, () %tuple.41, bf16[64,2048]{1,0:T(8,128)(2,1)S(1)} %get-tuple-element.79.even_ref), branch_computations={%region_2.0_spmd, %region_3.0_spmd} | conditional | bytes 1048624 | solution.py:499
  18.5 1.3 %collective-permute-done = bf16[64,2048]{1,0:T(8,128)(2,1)} collective-permute-done((bf16[64,2048]{1,0:T(8,128)(2,1)S(1)}, bf16[64,2048]{1,0:T(8,128)(2,1)}, u32[]{:S(2)}, u32[]{:S(2)}) %collective-permute-start) | collective-permute-done | bytes 262176 | tf_op jit(solution)/shard_map/cond/branch_1_fun/ppermute | solution.py:147
  19.8 3.1 %shard_map.118 = (f32[128,512]{1,0:T(8,128)S(1)}, bf16[2048,512]{1,0:T(8,128)(2,1)S(1)}) custom-call(bf16[64,2048]{1,0:T(8,128)(2,1)} %copy-done.10, bf16[64,2048]{1,0:T(8,128)(2,1)} %get-tuple-element.139.even_other_ref, bf16[2048,512]{1,0:T(8,128)(2,1)} %copy-done.2), custom_call_target="tpu_custom_call" | custom-call | flops 268435456 | bytes 4980736 | tf_op jit(solution)/shard_map/pallas_call | solution.py:153
  22.9 4.7 %conditional.7 = (bf16[144,512]{1,0:T(8,128)(2,1)}) conditional(s32[]{:T(128)} %convert_element_type.16, () %tuple.40, (bf16[64,2048]{1,0:T(8,128)(2,1)}, bf16[2048,512]{1,0:T(8,128)(2,1)}) %tuple.62), branch_computations={%region_6.0_spmd, %region_7.0_spmd} | conditional | flops 268435456 | bytes 3817520 | solution.py:499
  23.4 1.4 %collective-permute-done.1.got_other_ref = bf16[64,2048]{1,0:T(8,128)(2,1)S(1)} collective-permute-done((bf16[64,2048]{1,0:T(8,128)(2,1)}, bf16[64,2048]{1,0:T(8,128)(2,1)S(1)}, u32[]{:S(2)}, u32[]{:S(2)}) %collective-permute-start.1) | collective-permute-done | bytes 262176 | tf_op jit(solution)/shard_map/cond/branch_1_fun/ppermute | solution.py:147
  24.8 2.8 %branch_1_fun.5 = bf16[144,512]{1,0:T(8,128)(2,1)} custom-call(bf16[64,2048]{1,0:T(8,128)(2,1)} %get-tuple-element.30.got_ref, bf16[64,2048]{1,0:T(8,128)(2,1)S(1)} %collective-permute-done.1.got_other_ref, bf16[2048,512]{1,0:T(8,128)(2,1)} %get-tuple-element.31.weight_ref), custom_call_target="tpu_custom_call" | custom-call | flops 268435456 | bytes 2768896 | tf_op jit(solution)/shard_map/cond/branch_1_fun/pallas_call | solution.py:153
  27.6 5.5 %collective-permute-done.6.got_b_ref = bf16[64,2048]{1,0:T(8,128)(2,1)S(1)} collective-permute-done((bf16[64,2048]{1,0:T(8,128)(2,1)S(1)}, bf16[64,2048]{1,0:T(8,128)(2,1)S(1)}, u32[]{:S(2)}, u32[]{:S(2)}) %collective-permute-start.6) | collective-permute-done | bytes 262176 | tf_op jit(solution)/shard_map/ppermute | solution.py:486
  33.6 2.5 %collective-permute-start.12 = (bf16[144,512]{1,0:T(8,128)(2,1)}, bf16[144,512]{1,0:T(8,128)(2,1)S(1)}, u32[]{:S(2)}, u32[]{:S(2)}) collective-permute-start(bf16[144,512]{1,0:T(8,128)(2,1)} %get-tuple-element.141), channel_id=1, source_target_pairs={{0,6},{2,4},{4,2},{6,0},{1,7},{3,5},{5,3},{7,1},{8,14},{10,12},{12... | collective-permute-start | bytes 442376 | tf_op jit(solution)/shard_map/ppermute | solution.py:147
  37.0 1.9 %collective-permute-start.11 = (bf16[144,512]{1,0:T(8,128)(2,1)S(1)}, bf16[144,512]{1,0:T(8,128)(2,1)S(1)}, u32[]{:S(2)}, u32[]{:S(2)}) collective-permute-start(bf16[144,512]{1,0:T(8,128)(2,1)S(1)} %get-tuple-element.87), channel_id=1, source_target_pairs={{0,4},{1,3},{2,6},{3,1},{4,0},{5,7},{6,2},{7,5},{8,12},{9,11},{10,... | collective-permute-start | bytes 442376 | tf_op jit(solution)/shard_map/ppermute | solution.py:486
  39.0 3.5 %collective-permute-done.12.got_ref = bf16[144,512]{1,0:T(8,128)(2,1)S(1)} collective-permute-done((bf16[144,512]{1,0:T(8,128)(2,1)}, bf16[144,512]{1,0:T(8,128)(2,1)S(1)}, u32[]{:S(2)}, u32[]{:S(2)}) %collective-permute-start.12) | collective-permute-done | bytes 147488 | tf_op jit(solution)/shard_map/ppermute | solution.py:147
  43.5 3.6 %collective-permute-done.10.got_a_ref = bf16[144,512]{1,0:T(8,128)(2,1)S(1)} collective-permute-done((bf16[144,512]{1,0:T(8,128)(2,1)S(1)}, bf16[144,512]{1,0:T(8,128)(2,1)S(1)}, u32[]{:S(2)}, u32[]{:S(2)}) %collective-permute-start.10) | collective-permute-done | bytes 147488 | tf_op jit(solution)/shard_map/ppermute | solution.py:481
  47.1 1.5 %collective-permute-done.11.got_b_ref = bf16[144,512]{1,0:T(8,128)(2,1)S(1)} collective-permute-done((bf16[144,512]{1,0:T(8,128)(2,1)S(1)}, bf16[144,512]{1,0:T(8,128)(2,1)S(1)}, u32[]{:S(2)}, u32[]{:S(2)}) %collective-permute-start.11) | collective-permute-done | bytes 147488 | tf_op jit(solution)/shard_map/ppermute | solution.py:486
  48.8 1.7 %collective-permute-start.15 = (bf16[144,512]{1,0:T(8,128)(2,1)S(1)}, bf16[144,512]{1,0:T(8,128)(2,1)S(1)}, u32[]{:S(2)}, u32[]{:S(2)}) collective-permute-start(bf16[144,512]{1,0:T(8,128)(2,1)S(1)} %shard_map.121.block_0_ref), channel_id=1, source_target_pairs={{0,6},{2,4},{4,2},{6,0},{1,7},{3,5},{5,3},{7,1},{8,14},{10,12},{12... | collective-permute-start | bytes 442376 | tf_op jit(solution)/shard_map/ppermute | solution.py:147
  50.5 2.8 %collective-permute-start.13 = (bf16[144,512]{1,0:T(8,128)(2,1)S(1)}, bf16[144,512]{1,0:T(8,128)(2,1)S(1)}, u32[]{:S(2)}, u32[]{:S(2)}) collective-permute-start(bf16[144,512]{1,0:T(8,128)(2,1)S(1)} %shard_map.121.block_0_ref), channel_id=1, source_target_pairs={{0,2},{1,5},{2,0},{3,7},{4,6},{5,1},{6,4},{7,3},{8,10},{9,13},{10,... | collective-permute-start | bytes 442376 | tf_op jit(solution)/shard_map/ppermute | solution.py:481
  53.3 4.2 %collective-permute-done.15.block_c_ref = bf16[144,512]{1,0:T(8,128)(2,1)S(1)} collective-permute-done((bf16[144,512]{1,0:T(8,128)(2,1)S(1)}, bf16[144,512]{1,0:T(8,128)(2,1)S(1)}, u32[]{:S(2)}, u32[]{:S(2)}) %collective-permute-start.15) | collective-permute-done | bytes 147488 | tf_op jit(solution)/shard_map/ppermute | solution.py:147
  57.5 5.3 %collective-permute-done.14.block_b_ref = bf16[144,512]{1,0:T(8,128)(2,1)S(1)} collective-permute-done((bf16[144,512]{1,0:T(8,128)(2,1)S(1)}, bf16[144,512]{1,0:T(8,128)(2,1)S(1)}, u32[]{:S(2)}, u32[]{:S(2)}) %collective-permute-start.14) | collective-permute-done | bytes 147488 | tf_op jit(solution)/shard_map/ppermute | solution.py:486
  62.8 2.3 %shard_map.122 = (bf16[128,2048]{1,0:T(8,128)(2,1)}, f32[128,16]{1,0:T(8,128)S(1)}, f32[16,2048]{1,0:T(8,128)S(1)}) custom-call(bf16[2048,128]{1,0:T(8,128)(2,1)S(1)} %copy-done.8, bf16[144,512]{1,0:T(8,128)(2,1)S(1)} %shard_map.121.block_0_ref, bf16[144,512]{1,0:T(8,128)(2,1)S(1)} %collective-permute-done.13.block_a_ref, ...), custom_call_target="tpu_custom_call" | custom-call | flops 536870912 | bytes 1847296 | tf_op jit(solution)/shard_map/pallas_call | solution.py:153
  66.8 1.4 %shard_map.124 = bf16[128,4096]{1,0:T(8,128)(2,1)} custom-call(f32[128,16]{1,0:T(8,128)S(1)} %get-tuple-element.104.low_ref, f32[128,16]{1,0:T(8,128)S(1)} %collective-permute-done.16.low_other_ref, bf16[16,4096]{1,0:T(8,128)(2,1)S(1)} %bitcast.25), custom_call_target="tpu_custom_call" | custom-call | flops 16777216 | bytes 1196032 | tf_op jit(solution)/shard_map/pallas_call | solution.py:153
  68.2 3.5 %collective-permute-done.17.got_ref = bf16[16,3072]{1,0:T(8,128)(2,1)S(1)} collective-permute-done((bf16[16,3072]{1,0:T(8,128)(2,1)S(1)}, bf16[16,3072]{1,0:T(8,128)(2,1)S(1)}, u32[]{:S(2)}, u32[]{:S(2)}) %collective-permute-start.17) | collective-permute-done | bytes 98336 | tf_op jit(solution)/shard_map/ppermute | solution.py:147
  72.9 5.8 %collective-permute-done.18.got_ref = bf16[16,3072]{1,0:T(8,128)(2,1)S(1)} collective-permute-done((bf16[16,3072]{1,0:T(8,128)(2,1)S(1)}, bf16[16,3072]{1,0:T(8,128)(2,1)S(1)}, u32[]{:S(2)}, u32[]{:S(2)}) %collective-permute-start.18) | collective-permute-done | bytes 98336 | tf_op jit(solution)/shard_map/ppermute | solution.py:147
  80.2 1.5 %collective-permute-start.20 = (f32[8,128]{1,0:T(8,128)S(1)}, f32[8,128]{1,0:T(8,128)S(1)}, u32[]{:S(2)}, u32[]{:S(2)}) collective-permute-start(f32[8,128]{1,0:T(8,128)S(1)} %add.30), channel_id=1, source_target_pairs={{0,8},{8,0},{16,24},{24,16},{1,9},{9,1},{17,25},{25,17},{2,10},{10... | collective-permute-start | bytes 12296 | tf_op jit(solution)/shard_map/ppermute | solution.py:147
  81.7 2.1 %collective-permute-done.20 = f32[8,128]{1,0:T(8,128)S(1)} collective-permute-done((f32[8,128]{1,0:T(8,128)S(1)}, f32[8,128]{1,0:T(8,128)S(1)}, u32[]{:S(2)}, u32[]{:S(2)}) %collective-permute-start.20) | collective-permute-done | bytes 4128 | tf_op jit(solution)/shard_map/ppermute | solution.py:147
  83.9 1.5 %collective-permute-start.21 = (f32[8,128]{1,0:T(8,128)S(1)}, f32[8,128]{1,0:T(8,128)S(1)}, u32[]{:S(2)}, u32[]{:S(2)}) collective-permute-start(f32[8,128]{1,0:T(8,128)S(1)} %add.31), channel_id=1, source_target_pairs={{0,16},{8,24},{16,0},{24,8},{1,17},{9,25},{17,1},{25,9},{2,18},{10... | collective-permute-start | bytes 12296 | tf_op jit(solution)/shard_map/ppermute | solution.py:147
  85.4 2.1 %collective-permute-done.21 = f32[8,128]{1,0:T(8,128)S(1)} collective-permute-done((f32[8,128]{1,0:T(8,128)S(1)}, f32[8,128]{1,0:T(8,128)S(1)}, u32[]{:S(2)}, u32[]{:S(2)}) %collective-permute-start.21) | collective-permute-done | bytes 4128 | tf_op jit(solution)/shard_map/ppermute | solution.py:147
  87.5 1.9 %collective-permute-start.22 = (f32[8,128]{1,0:T(8,128)S(1)}, f32[8,128]{1,0:T(8,128)S(1)}, u32[]{:S(2)}, u32[]{:S(2)}) collective-permute-start(f32[8,128]{1,0:T(8,128)S(1)} %add.32), channel_id=1, source_target_pairs={{0,2},{2,0},{4,6},{6,4},{1,3},{3,1},{5,7},{7,5},{8,10},{10,8},{12,... | collective-permute-start | bytes 12296 | tf_op jit(solution)/shard_map/ppermute | solution.py:147
  89.4 1.7 %collective-permute-done.22 = f32[8,128]{1,0:T(8,128)S(1)} collective-permute-done((f32[8,128]{1,0:T(8,128)S(1)}, f32[8,128]{1,0:T(8,128)S(1)}, u32[]{:S(2)}, u32[]{:S(2)}) %collective-permute-start.22) | collective-permute-done | bytes 4128 | tf_op jit(solution)/shard_map/ppermute | solution.py:147
  (70 shorter events, 15.4 us)
Async XLA Ops:
  0.6 10.3 %copy-start.3 = (bf16[1,128,4096]{2,1,0:T(8,128)(2,1)S(1)}, bf16[1,128,4096]{2,1,0:T(8,128)(2,1)}, u32[]{:S(2)}) copy-start(bf16[1,128,4096]{2,1,0:T(8,128)(2,1)} %param.22) | copy-start | bytes 3145732
  0.7 10.3 %copy-start.5 = (bf16[1,16,4096]{2,1,0:T(8,128)(2,1)S(1)}, bf16[1,16,4096]{2,1,0:T(8,128)(2,1)}, u32[]{:S(2)}) copy-start(bf16[1,16,4096]{2,1,0:T(8,128)(2,1)} %param.21) | copy-start | bytes 393220
  0.7 10.3 %copy-start.11 = (s32[128]{0:T(128)S(1)}, s32[128]{0:T(128)}, u32[]{:S(2)}) copy-start(s32[128]{0:T(128)} %param.23) | copy-start | bytes 1540
  2.1 2.1 %collective-permute-start.3 = (bf16[64,4096]{1,0:T(8,128)(2,1)S(1)}, bf16[64,4096]{1,0:T(8,128)(2,1)S(1)}, u32[]{:S(2)}, u32[]{:S(2)}) collective-permute-start(bf16[64,4096]{1,0:T(8,128)(2,1)S(1)} %get-tuple-element.125), channel_id=1, source_target_pairs={{0,1},{1,0},{2,3},{3,2},{4,5},{5,4},{6,7},{7,6},{8,9},{9,8},{10,11... | collective-permute-start | bytes 1572872 | tf_op jit(solution)/shard_map/ppermute | solution.py:147
  2.6 1.6 %collective-permute-start.4 = (bf16[1,4096]{1,0:T(2,128)(2,1)S(1)}, bf16[1,4096]{1,0:T(2,128)(2,1)S(1)}, u32[]{:S(2)}, u32[]{:S(2)}) collective-permute-start(bf16[1,4096]{1,0:T(2,128)(2,1)S(1)} %copy-done.1), channel_id=1, source_target_pairs={{0,1},{1,0},{2,3},{3,2},{4,5},{5,4},{6,7},{7,6},{8,9},{9,8},{10,11... | collective-permute-start | bytes 24584 | tf_op jit(solution)/shard_map/ppermute | solution.py:147
  5.3 12.7 %copy-start.10 = (bf16[64,2048]{1,0:T(8,128)(2,1)}, bf16[64,2048]{1,0:T(8,128)(2,1)S(1)}, u32[]{:S(2)}) copy-start(bf16[64,2048]{1,0:T(8,128)(2,1)S(1)} %get-tuple-element.79.even_ref) | copy-start | bytes 786436
  5.3 17.6 %collective-permute-start.7 = (bf16[64,2048]{1,0:T(8,128)(2,1)}, bf16[64,2048]{1,0:T(8,128)(2,1)}, u32[]{:S(2)}, u32[]{:S(2)}) collective-permute-start(bf16[64,2048]{1,0:T(8,128)(2,1)} %get-tuple-element.78), channel_id=1, source_target_pairs={{0,6},{2,4},{4,2},{6,0},{1,7},{3,5},{5,3},{7,1},{8,14},{10,12},{12... | collective-permute-start | bytes 786440 | tf_op jit(solution)/shard_map/ppermute | solution.py:147
  10.3 17.3 %collective-permute-start.5 = (bf16[64,2048]{1,0:T(8,128)(2,1)S(1)}, bf16[64,2048]{1,0:T(8,128)(2,1)S(1)}, u32[]{:S(2)}, u32[]{:S(2)}) collective-permute-start(bf16[64,2048]{1,0:T(8,128)(2,1)S(1)} %get-tuple-element.76), channel_id=1, source_target_pairs={{0,2},{1,5},{2,0},{3,7},{4,6},{5,1},{6,4},{7,3},{8,10},{9,13},{10,... | collective-permute-start | bytes 786440 | tf_op jit(solution)/shard_map/ppermute | solution.py:481
  10.3 22.8 %collective-permute-start.6 = (bf16[64,2048]{1,0:T(8,128)(2,1)S(1)}, bf16[64,2048]{1,0:T(8,128)(2,1)S(1)}, u32[]{:S(2)}, u32[]{:S(2)}) collective-permute-start(bf16[64,2048]{1,0:T(8,128)(2,1)S(1)} %get-tuple-element.77), channel_id=1, source_target_pairs={{0,4},{1,3},{2,6},{3,1},{4,0},{5,7},{6,2},{7,5},{8,12},{9,11},{10,... | collective-permute-start | bytes 786440 | tf_op jit(solution)/shard_map/ppermute | solution.py:486
  12.0 2.4 %collective-permute-start.2 = (f32[128,16]{1,0:T(8,128)}, f32[128,16]{1,0:T(8,128)}, u32[]{:S(2)}, u32[]{:S(2)}) collective-permute-start(f32[128,16]{1,0:T(8,128)} %branch_1_fun.4), channel_id=1, source_target_pairs={{0,1},{1,0},{2,3},{3,2},{4,5},{5,4},{6,7},{7,6},{8,9},{9,8},{10,11... | collective-permute-start | bytes 24584 | tf_op jit(solution)/shard_map/cond/branch_1_fun/ppermute | solution.py:147
  18.0 1.9 %collective-permute-start = (bf16[64,2048]{1,0:T(8,128)(2,1)S(1)}, bf16[64,2048]{1,0:T(8,128)(2,1)}, u32[]{:S(2)}, u32[]{:S(2)}) collective-permute-start(bf16[64,2048]{1,0:T(8,128)(2,1)S(1)} %param.3), channel_id=1, source_target_pairs={{0,1},{1,0},{2,3},{3,2},{4,5},{5,4},{6,7},{7,6},{8,9},{9,8},{10,11... | collective-permute-start | bytes 786440 | tf_op jit(solution)/shard_map/cond/branch_1_fun/ppermute | solution.py:147
  22.9 1.8 %collective-permute-start.1 = (bf16[64,2048]{1,0:T(8,128)(2,1)}, bf16[64,2048]{1,0:T(8,128)(2,1)S(1)}, u32[]{:S(2)}, u32[]{:S(2)}) collective-permute-start(bf16[64,2048]{1,0:T(8,128)(2,1)} %get-tuple-element.30.got_ref), channel_id=1, source_target_pairs={{0,1},{1,0},{2,3},{3,2},{4,5},{5,4},{6,7},{7,6},{8,9},{9,8},{10,11... | collective-permute-start | bytes 786440 | tf_op jit(solution)/shard_map/cond/branch_1_fun/ppermute | solution.py:147
  27.6 14.9 %copy-start = (bf16[1,16,2048]{2,1,0:T(8,128)(2,1)S(1)}, bf16[1,16,2048]{2,1,0:T(8,128)(2,1)}, u32[]{:S(2)}) copy-start(bf16[1,16,2048]{2,1,0:T(8,128)(2,1)} %param.20) | copy-start | bytes 196612
  33.1 3.0 %collective-permute-start.8 = (bf16[64,2048]{1,0:T(8,128)(2,1)S(1)}, bf16[64,2048]{1,0:T(8,128)(2,1)S(1)}, u32[]{:S(2)}, u32[]{:S(2)}) collective-permute-start(bf16[64,2048]{1,0:T(8,128)(2,1)S(1)} %collective-permute-done.5.got_a_ref), channel_id=1, source_target_pairs={{0,1},{1,0},{2,3},{3,2},{4,5},{5,4},{6,7},{7,6},{8,9},{9,8},{10,11... | collective-permute-start | bytes 786440 | tf_op jit(solution)/shard_map/ppermute | solution.py:147
  33.1 3.0 %collective-permute-start.9 = (bf16[64,2048]{1,0:T(8,128)(2,1)S(1)}, bf16[64,2048]{1,0:T(8,128)(2,1)S(1)}, u32[]{:S(2)}, u32[]{:S(2)}) collective-permute-start(bf16[64,2048]{1,0:T(8,128)(2,1)S(1)} %collective-permute-done.6.got_b_ref), channel_id=1, source_target_pairs={{0,1},{1,0},{2,3},{3,2},{4,5},{5,4},{6,7},{7,6},{8,9},{9,8},{10,11... | collective-permute-start | bytes 786440 | tf_op jit(solution)/shard_map/ppermute | solution.py:147
  33.6 8.8 %collective-permute-start.12 = (bf16[144,512]{1,0:T(8,128)(2,1)}, bf16[144,512]{1,0:T(8,128)(2,1)S(1)}, u32[]{:S(2)}, u32[]{:S(2)}) collective-permute-start(bf16[144,512]{1,0:T(8,128)(2,1)} %get-tuple-element.141), channel_id=1, source_target_pairs={{0,6},{2,4},{4,2},{6,0},{1,7},{3,5},{5,3},{7,1},{8,14},{10,12},{12... | collective-permute-start | bytes 442376 | tf_op jit(solution)/shard_map/ppermute | solution.py:147
  36.1 26.6 %copy-start.8 = (bf16[2048,128]{1,0:T(8,128)(2,1)S(1)}, bf16[2048,128]{1,0:T(8,128)(2,1)}, u32[]{:S(2)}) copy-start(bf16[2048,128]{1,0:T(8,128)(2,1)} %copy-done.7) | copy-start | bytes 1572868
  36.9 29.5 %copy-start.4 = (bf16[1,128,4096]{2,1,0:T(8,128)(2,1)S(1)}, bf16[1,128,4096]{2,1,0:T(8,128)(2,1)}, u32[]{:S(2)}) copy-start(bf16[1,128,4096]{2,1,0:T(8,128)(2,1)} %param.22) | copy-start | bytes 3145732
  37.0 10.1 %collective-permute-start.10 = (bf16[144,512]{1,0:T(8,128)(2,1)S(1)}, bf16[144,512]{1,0:T(8,128)(2,1)S(1)}, u32[]{:S(2)}, u32[]{:S(2)}) collective-permute-start(bf16[144,512]{1,0:T(8,128)(2,1)S(1)} %get-tuple-element.86), channel_id=1, source_target_pairs={{0,2},{1,5},{2,0},{3,7},{4,6},{5,1},{6,4},{7,3},{8,10},{9,13},{10,... | collective-permute-start | bytes 442376 | tf_op jit(solution)/shard_map/ppermute | solution.py:481
  37.0 11.6 %collective-permute-start.11 = (bf16[144,512]{1,0:T(8,128)(2,1)S(1)}, bf16[144,512]{1,0:T(8,128)(2,1)S(1)}, u32[]{:S(2)}, u32[]{:S(2)}) collective-permute-start(bf16[144,512]{1,0:T(8,128)(2,1)S(1)} %get-tuple-element.87), channel_id=1, source_target_pairs={{0,4},{1,3},{2,6},{3,1},{4,0},{5,7},{6,2},{7,5},{8,12},{9,11},{10,... | collective-permute-start | bytes 442376 | tf_op jit(solution)/shard_map/ppermute | solution.py:486
  43.5 23.3 %copy-start.6 = (bf16[1,16,4096]{2,1,0:T(8,128)(2,1)S(1)}, bf16[1,16,4096]{2,1,0:T(8,128)(2,1)}, u32[]{:S(2)}) copy-start(bf16[1,16,4096]{2,1,0:T(8,128)(2,1)} %param.21) | copy-start | bytes 393220
  48.8 8.7 %collective-permute-start.15 = (bf16[144,512]{1,0:T(8,128)(2,1)S(1)}, bf16[144,512]{1,0:T(8,128)(2,1)S(1)}, u32[]{:S(2)}, u32[]{:S(2)}) collective-permute-start(bf16[144,512]{1,0:T(8,128)(2,1)S(1)} %shard_map.121.block_0_ref), channel_id=1, source_target_pairs={{0,6},{2,4},{4,2},{6,0},{1,7},{3,5},{5,3},{7,1},{8,14},{10,12},{12... | collective-permute-start | bytes 442376 | tf_op jit(solution)/shard_map/ppermute | solution.py:147
  50.5 12.3 %collective-permute-start.14 = (bf16[144,512]{1,0:T(8,128)(2,1)S(1)}, bf16[144,512]{1,0:T(8,128)(2,1)S(1)}, u32[]{:S(2)}, u32[]{:S(2)}) collective-permute-start(bf16[144,512]{1,0:T(8,128)(2,1)S(1)} %shard_map.121.block_0_ref), channel_id=1, source_target_pairs={{0,4},{1,3},{2,6},{3,1},{4,0},{5,7},{6,2},{7,5},{8,12},{9,11},{10,... | collective-permute-start | bytes 442376 | tf_op jit(solution)/shard_map/ppermute | solution.py:486
  50.5 12.3 %collective-permute-start.13 = (bf16[144,512]{1,0:T(8,128)(2,1)S(1)}, bf16[144,512]{1,0:T(8,128)(2,1)S(1)}, u32[]{:S(2)}, u32[]{:S(2)}) collective-permute-start(bf16[144,512]{1,0:T(8,128)(2,1)S(1)} %shard_map.121.block_0_ref), channel_id=1, source_target_pairs={{0,2},{1,5},{2,0},{3,7},{4,6},{5,1},{6,4},{7,3},{8,10},{9,13},{10,... | collective-permute-start | bytes 442376 | tf_op jit(solution)/shard_map/ppermute | solution.py:481
  65.1 1.3 %collective-permute-start.16 = (f32[128,16]{1,0:T(8,128)S(1)}, f32[128,16]{1,0:T(8,128)S(1)}, u32[]{:S(2)}, u32[]{:S(2)}) collective-permute-start(f32[128,16]{1,0:T(8,128)S(1)} %get-tuple-element.104.low_ref), channel_id=1, source_target_pairs={{0,1},{1,0},{2,3},{3,2},{4,5},{5,4},{6,7},{7,6},{8,9},{9,8},{10,11... | collective-permute-start | bytes 24584 | tf_op jit(solution)/shard_map/ppermute | solution.py:147
  66.7 4.9 %collective-permute-start.17 = (bf16[16,3072]{1,0:T(8,128)(2,1)S(1)}, bf16[16,3072]{1,0:T(8,128)(2,1)S(1)}, u32[]{:S(2)}, u32[]{:S(2)}) collective-permute-start(bf16[16,3072]{1,0:T(8,128)(2,1)S(1)} %get-tuple-element.106), channel_id=1, source_target_pairs={{0,2},{2,0},{4,6},{6,4},{1,3},{3,1},{5,7},{7,5},{8,10},{10,8},{12,... | collective-permute-start | bytes 294920 | tf_op jit(solution)/shard_map/ppermute | solution.py:147
  71.6 7.1 %collective-permute-start.18 = (bf16[16,3072]{1,0:T(8,128)(2,1)S(1)}, bf16[16,3072]{1,0:T(8,128)(2,1)S(1)}, u32[]{:S(2)}, u32[]{:S(2)}) collective-permute-start(bf16[16,3072]{1,0:T(8,128)(2,1)S(1)} %shard_map.125.own_ref), channel_id=1, source_target_pairs={{0,4},{2,6},{4,0},{6,2},{1,5},{3,7},{5,1},{7,3},{8,12},{10,14},{12... | collective-permute-start | bytes 294920 | tf_op jit(solution)/shard_map/ppermute | solution.py:147
  78.9 12.2 %collective-permute-start.23 = (bf16[16,3072]{1,0:T(8,128)(2,1)S(1)}, bf16[16,3072]{1,0:T(8,128)(2,1)S(1)}, u32[]{:S(2)}, u32[]{:S(2)}) collective-permute-start(bf16[16,3072]{1,0:T(8,128)(2,1)S(1)} %get-tuple-element.111.own_ref), channel_id=1, source_target_pairs={{0,2},{2,0},{4,6},{6,4},{1,3},{3,1},{5,7},{7,5},{8,10},{10,8},{12,... | collective-permute-start | bytes 294920 | tf_op jit(solution)/shard_map/ppermute | solution.py:147
  79.0 1.2 %collective-permute-start.19 = (f32[8,128]{1,0:T(8,128)S(1)}, f32[8,128]{1,0:T(8,128)S(1)}, u32[]{:S(2)}, u32[]{:S(2)}) collective-permute-start(f32[8,128]{1,0:T(8,128)S(1)} %get-tuple-element.110), channel_id=1, source_target_pairs={{0,1},{1,0},{2,3},{3,2},{4,5},{5,4},{6,7},{7,6},{8,9},{9,8},{10,11... | collective-permute-start | bytes 12296 | tf_op jit(solution)/shard_map/ppermute | solution.py:147
  80.2 3.6 %collective-permute-start.20 = (f32[8,128]{1,0:T(8,128)S(1)}, f32[8,128]{1,0:T(8,128)S(1)}, u32[]{:S(2)}, u32[]{:S(2)}) collective-permute-start(f32[8,128]{1,0:T(8,128)S(1)} %add.30), channel_id=1, source_target_pairs={{0,8},{8,0},{16,24},{24,16},{1,9},{9,1},{17,25},{25,17},{2,10},{10... | collective-permute-start | bytes 12296 | tf_op jit(solution)/shard_map/ppermute | solution.py:147
  83.9 3.6 %collective-permute-start.21 = (f32[8,128]{1,0:T(8,128)S(1)}, f32[8,128]{1,0:T(8,128)S(1)}, u32[]{:S(2)}, u32[]{:S(2)}) collective-permute-start(f32[8,128]{1,0:T(8,128)S(1)} %add.31), channel_id=1, source_target_pairs={{0,16},{8,24},{16,0},{24,8},{1,17},{9,25},{17,1},{25,9},{2,18},{10... | collective-permute-start | bytes 12296 | tf_op jit(solution)/shard_map/ppermute | solution.py:147
  87.5 3.6 %collective-permute-start.22 = (f32[8,128]{1,0:T(8,128)S(1)}, f32[8,128]{1,0:T(8,128)S(1)}, u32[]{:S(2)}, u32[]{:S(2)}) collective-permute-start(f32[8,128]{1,0:T(8,128)S(1)} %add.32), channel_id=1, source_target_pairs={{0,2},{2,0},{4,6},{6,4},{1,3},{3,1},{5,7},{7,5},{8,10},{10,8},{12,... | collective-permute-start | bytes 12296 | tf_op jit(solution)/shard_map/ppermute | solution.py:147
  (4 other events, 15.0 us)
